TPU v7x, 32 devices: a whole 2x2x4 slice. The times are simulated.
32 devices in a mesh: grp: 2 (over y), seq: 4 (over z), fsdp: 2 (over x), chan: 2 (over core).
Axes of the slice: x: 2, y: 2, z: 4, core: 2. Of those that a mesh axis runs over, the one named last changes fastest.
Arguments:
- tokens: bfloat16 [2048, 4096], P(('grp', 'seq', 'fsdp'), 'chan'), parts along dimension 0, may hold values from -6 to 6
- proj_weight: bfloat16 [4096, 3, 512], P('fsdp', None, 'chan'), may hold values from -0.09375 to 0.09375
- short_weight: float32 [3, 3, 512], P(None, None, 'chan'), may hold values from -3 to 3
- skip_gain: float32 [512], P('chan'), may hold values from -4 to 4
- filter_taps: bfloat16 [1024, 512], P(('seq', 'fsdp'), 'chan'), may hold values from -0.1875 to 0.1875
Outputs:
- mixed_out: bfloat16 [2048, 512], P(('grp', 'seq', 'fsdp'), 'chan'), parts along dimension 0
There are 2 independent parts, one for each index of `grp`. A program takes and returns all parts, laid end to end along the dimension named above; an argument that names none is the same for every part. Nothing has to cross between parts.
All inputs are finite; a program needn't handle non-finite values.
Results may differ from a plain program's by a relative error of at most 0.009.
Values may be sent and summed in bfloat16 or wider, within the bound.
No kernel may reach another device: no remote copies, remote signals or barrier semaphores. Data moves between devices by JAX's collectives and lax.ppermute only.
A program may use at most 64 MiB of HBM per device.

v0:
```python
import math

import jax
import jax.numpy as jnp
from jax import lax
from jax.sharding import PartitionSpec as P


def shifted(value, axis, steps):
    count = lax.axis_size(axis)
    initial, last = (max(0, -steps), min(count, count - steps))
    return lax.ppermute(value, axis, [(source, source + steps) for source in range(initial, last)])


def index_grid(row_count, col_count):
    return (
        lax.broadcasted_iota(jnp.int32, (row_count, col_count), 0),
        lax.broadcasted_iota(jnp.int32, (row_count, col_count), 1),
    )


def phase_pair(row_ids, col_ids, period):
    wrapped = row_ids * col_ids % period
    phase = wrapped.astype(jnp.float32) * (2.0 * math.pi / period)
    return (jnp.cos(phase), jnp.sin(phase))


def multiply(real_x, imag_x):
    sig_real = real_x[0].astype(jnp.float32)
    sig_imag = imag_x[0].astype(jnp.float32)
    tap_real = real_x[1].astype(jnp.float32)
    tap_imag = imag_x[1].astype(jnp.float32)
    real_z = (sig_real * tap_real - sig_imag * tap_imag).astype(jnp.bfloat16)
    imag_z = (sig_real * tap_imag + sig_imag * tap_real).astype(jnp.bfloat16)
    return (real_z, imag_z)


def spread(stacked, groups, inner_shape):
    shaped = stacked.reshape((2, groups, 1) + inner_shape)
    moved = lax.all_to_all(shaped, ("seq", "fsdp"), split_axis=1, concat_axis=2, tiled=True)
    return moved.reshape((2, groups) + inner_shape)


def per_device(tokens, proj_weight, short_weight, skip_gain, filter_taps):
    whole = lax.all_gather(tokens, "chan", axis=1, tiled=True)
    row_count = whole.shape[0]
    width = proj_weight.shape[2]
    flat_width = 3 * width
    piece = lax.all_gather(proj_weight, "fsdp", axis=0, tiled=True)
    summed = jnp.dot(
        whole, piece.reshape(piece.shape[0], flat_width), preferred_element_type=jnp.float32
    )
    projected = summed.astype(jnp.bfloat16).reshape(row_count, 3, width)
    earlier = shifted(projected[row_count - 2 :], ("seq", "fsdp"), 1)
    extended = jnp.concatenate([earlier, projected], axis=0).astype(jnp.float32)
    mixed = (
        short_weight[0] * extended[2:]
        + short_weight[1] * extended[1:-1]
        + short_weight[2] * extended[:-2]
    )
    query = mixed[:, 0]
    product = (mixed[:, 1] * mixed[:, 2]).astype(jnp.bfloat16)
    groups = lax.axis_size(("seq", "fsdp"))
    position = lax.axis_index(("seq", "fsdp"))
    period_rows = 2 * groups
    length = period_rows * row_count
    scale = 1.0 / length
    bin_ids, tap_ids = index_grid(period_rows, groups)
    first_cos, first_sin = phase_pair(bin_ids, tap_ids, period_rows)
    first_cos = first_cos.astype(jnp.bfloat16)
    first_sin = first_sin.astype(jnp.bfloat16)
    col_ids, freq_ids = index_grid(row_count, row_count)
    last_cos, last_sin = phase_pair(col_ids, freq_ids, row_count)
    last_cos = last_cos.astype(jnp.bfloat16)
    last_sin = last_sin.astype(jnp.bfloat16)
    stacked = jnp.stack([product, filter_taps])
    f32 = jnp.float32
    per_dev = row_count // groups
    per_bins = period_rows // groups
    arrived = spread(stacked.reshape(2, groups, per_dev, width), groups, (per_dev, width))
    real_a = jnp.einsum("qp,kpmc->kqmc", first_cos, arrived, preferred_element_type=f32)
    imag_a = -jnp.einsum("qp,kpmc->kqmc", first_sin, arrived, preferred_element_type=f32)
    row_ids, mid_ids = index_grid(period_rows, per_dev)
    twist_cos, twist_sin = phase_pair(row_ids, mid_ids + position * per_dev, length)
    twist_cos = twist_cos[:, :, None]
    twist_sin = twist_sin[:, :, None]
    real_b = (real_a * twist_cos + imag_a * twist_sin).astype(jnp.bfloat16)
    imag_b = (imag_a * twist_cos - real_a * twist_sin).astype(jnp.bfloat16)
    outgoing = jnp.stack([real_b, imag_b]).reshape(2, 2, groups, per_bins, 1, per_dev, width)
    turned = lax.all_to_all(outgoing, ("seq", "fsdp"), split_axis=2, concat_axis=4, tiled=True)
    turned = turned.reshape(2, 2, per_bins, row_count, width)
    real_b = turned[0]
    imag_b = turned[1]
    real_x = (
        jnp.einsum("kqmc,mr->kqrc", real_b, last_cos, preferred_element_type=f32)
        + jnp.einsum("kqmc,mr->kqrc", imag_b, last_sin, preferred_element_type=f32)
    ).astype(jnp.bfloat16)
    imag_x = (
        jnp.einsum("kqmc,mr->kqrc", imag_b, last_cos, preferred_element_type=f32)
        - jnp.einsum("kqmc,mr->kqrc", real_b, last_sin, preferred_element_type=f32)
    ).astype(jnp.bfloat16)
    real_z, imag_z = multiply(real_x, imag_x)
    real_v = jnp.einsum("qrc,mr->qmc", real_z, last_cos, preferred_element_type=f32) - jnp.einsum(
        "qrc,mr->qmc", imag_z, last_sin, preferred_element_type=f32
    )
    imag_v = jnp.einsum("qrc,mr->qmc", imag_z, last_cos, preferred_element_type=f32) + jnp.einsum(
        "qrc,mr->qmc", real_z, last_sin, preferred_element_type=f32
    )
    row_ids, mid_ids = index_grid(per_bins, row_count)
    twist_cos, twist_sin = phase_pair(row_ids + position * per_bins, mid_ids, length)
    twist_cos = twist_cos[:, :, None]
    twist_sin = twist_sin[:, :, None]
    real_w = (real_v * twist_cos - imag_v * twist_sin).astype(jnp.bfloat16)
    imag_w = (imag_v * twist_cos + real_v * twist_sin).astype(jnp.bfloat16)
    backward = jnp.stack([real_w, imag_w]).reshape(2, 1, per_bins, groups, per_dev, width)
    returned = lax.all_to_all(backward, ("seq", "fsdp"), split_axis=3, concat_axis=1, tiled=True)
    returned = returned.reshape(2, period_rows, per_dev, width)
    conv_rows = jnp.einsum(
        "qp,qmc->pmc", first_cos, returned[0], preferred_element_type=f32
    ) - jnp.einsum("qp,qmc->pmc", first_sin, returned[1], preferred_element_type=f32)
    conv_rows = (conv_rows * scale).astype(jnp.bfloat16)
    homed = lax.all_to_all(
        conv_rows.reshape(groups, 1, per_dev, width),
        ("seq", "fsdp"),
        split_axis=0,
        concat_axis=1,
        tiled=True,
    )
    conv = homed.reshape(row_count, width)
    result = query * (conv.astype(jnp.float32) + skip_gain * product.astype(jnp.float32))
    return result.astype(jnp.bfloat16)


def solution(mesh):
    in_specs = (
        P(("grp", "seq", "fsdp"), "chan"),
        P("fsdp", None, "chan"),
        P(None, None, "chan"),
        P("chan"),
        P(("seq", "fsdp"), "chan"),
    )
    out_specs = P(("grp", "seq", "fsdp"), "chan")
    return jax.shard_map(
        per_device, mesh=mesh, in_specs=in_specs, out_specs=out_specs, check_vma=False
    )
```

profile of v0, /device:TPU:0, one launch (start us, length us, event | category | flops | bytes accessed | tf_op | source)
XLA Modules:
  0.0 182.0 jit_solution(7906080105272334590)
XLA Ops:
  6.5 0.7 all-gather.3.cloned.1.call-update
  7.3 4.7 %copy.33 = bf16[2048,3,256]{0,2,1:T(8,128)(2,1)} copy(bf16[2048,3,256]{2,0,1:T(8,128)(2,1)} %param.6) | data formatting | bytes 6291456 | tf_op args[1]
  12.1 8.6 %all-gather.3.cloned.1.call-done = bf16[128,4096]{1,0:T(8,128)(2,1)} async-done(((bf16[128,2048]{1,0:T(8,128)(2,1)}), bf16[128,4096]{1,0:T(8,128)(2,1)}) %all-gather.3.cloned.1.call-update) | async-done | bytes 1048592 | tf_op jit(solution)/shard_map/all_gather | solution.py:45
  20.7 83.1 %all-gather.5.cloned.1.call-done = bf16[4096,3,256]{0,2,1:T(8,128)(2,1)} async-done(((bf16[2048,3,256]{0,2,1:T(8,128)(2,1)}), bf16[4096,3,256]{0,2,1:T(8,128)(2,1)}) %all-gather.5.cloned.1.call-update) | async-done | bytes 6291472 | tf_op jit(solution)/shard_map/all_gather | solution.py:49
  103.8 5.3 %convolution_convert_fusion = bf16[128,768]{1,0:T(8,128)(2,1)S(1)} fusion(bf16[128,4096]{1,0:T(8,128)(2,1)} %all-gather.3.cloned.1.call-done, bf16[4096,768]{0,1:T(8,128)(2,1)} %bitcast.121), kind=kOutput, calls=%fused_computation.7 | convolution fusion | flops 805404672 | bytes 7536640 | tf_op jit(solution)/shard_map/dot_general | solution.py:50
  109.2 2.2 %collective-permute-start = (bf16[2,3,256]{2,1,0:T(4,128)(2,1)S(1)}, bf16[2,3,256]{2,1,0:T(4,128)(2,1)S(1)}, u32[]{:S(2)}, u32[]{:S(2)}) collective-permute-start(bf16[2,3,256]{2,1,0:T(4,128)(2,1)S(1)} %slice.63), channel_id=1, source_target_pairs={{0,2},{2,4},{4,6},{6,8},{8,10},{10,12},{12,14},{1,3},{3,5},{5,7},{... | collective-permute-start | bytes 9224 | tf_op jit(solution)/shard_map/ppermute | solution.py:12
  111.6 1.1 collective-permute-done
  112.7 0.2 copy.35
  113.1 0.6 fusion.10
  113.8 0.7 copy.37
  114.5 7.5 %all-to-all-start = ((bf16[2,8,1,16,256]{4,3,0,2,1:T(8,128)(2,1)}), bf16[2,8,1,16,256]{4,3,0,2,1:T(8,128)(2,1)S(1)}, u32[]{:S(2)}, u32[]{:S(2)}) async-start(bf16[2,8,1,16,256]{4,3,0,2,1:T(8,128)(2,1)} %copy.37), calls=%async_computation | async-start | bytes 262144 | tf_op jit(solution)/shard_map/all_to_all | solution.py:40
  122.1 7.2 %all-to-all-done = bf16[2,8,1,16,256]{4,3,0,2,1:T(8,128)(2,1)S(1)} async-done(((bf16[2,8,1,16,256]{4,3,0,2,1:T(8,128)(2,1)}), bf16[2,8,1,16,256]{4,3,0,2,1:T(8,128)(2,1)S(1)}, u32[]{:S(2)}, u32[]{:S(2)}) %all-to-all-start) | async-done | bytes 131104 | tf_op jit(solution)/shard_map/all_to_all | solution.py:40
  129.3 0.3 convolution_bitcast_fusion
  129.6 0.4 add_convert_fusion
  130.2 0.7 pad_maximum_fusion
  131.0 1.4 copy.62
  132.4 3.5 %all-to-all-start.1 = ((bf16[2,2,8,2,1,16,256]{6,3,5,1,4,0,2:T(2,128)(2,1)}), bf16[2,2,8,2,1,16,256]{6,3,5,1,4,0,2:T(2,128)(2,1)S(1)}, u32[]{:S(2)}, u32[]{:S(2)}) async-start(bf16[2,2,8,2,1,16,256]{6,3,5,1,4,0,2:T(2,128)(2,1)} %copy.62), calls=%async_computation.1 | async-start | bytes 1048576 | tf_op jit(solution)/shard_map/all_to_all | solution.py:90
  136.0 12.0 %all-to-all-done.1 = bf16[2,2,8,2,1,16,256]{6,3,5,1,4,0,2:T(2,128)(2,1)S(1)} async-done(((bf16[2,2,8,2,1,16,256]{6,3,5,1,4,0,2:T(2,128)(2,1)}), bf16[2,2,8,2,1,16,256]{6,3,5,1,4,0,2:T(2,128)(2,1)S(1)}, u32[]{:S(2)}, u32[]{:S(2)}) %all-to-all-start.1) | async-done | bytes 524320 | tf_op jit(solution)/shard_map/all_to_all | solution.py:90
  148.0 0.6 fusion.118
  148.6 0.5 fusion.41
  149.1 0.5 fusion.39
  149.6 0.5 fusion.4
  150.1 0.5 fusion.3
  150.7 0.4 fusion.45
  151.1 0.4 fusion.43
  151.5 0.4 fusion.6
  151.9 0.4 subtract_convert_fusion.1
  152.3 11.7 %all_to_all.48 = bf16[2,1,2,8,16,256]{5,4,2,1,0,3:T(8,128)(2,1)S(1)} all-to-all(bf16[2,1,2,8,16,256]{5,4,2,1,0,3:T(8,128)(2,1)S(1)} %copy.66), channel_id=1, replica_groups=mesh['grp'=2,'seq'=4,'fsdp'=2,'chan'=2] {'seq','fsdp'}, dimensions={3} | all-to-all | bytes 524288 | tf_op jit(solution)/shard_map/all_to_all | solution.py:116
  164.0 0.2 fusion.23
  164.2 0.2 fusion.9
  164.5 9.7 %all_to_all.49 = bf16[8,1,16,256]{3,2,1,0:T(8,128)(2,1)S(1)} all-to-all(bf16[8,1,16,256]{3,2,1,0:T(8,128)(2,1)S(1)} %copy.51), channel_id=1, replica_groups=mesh['grp'=2,'seq'=4,'fsdp'=2,'chan'=2] {'seq','fsdp'}, dimensions={0} | all-to-all | bytes 131072 | tf_op jit(solution)/shard_map/all_to_all | solution.py:122
  174.4 0.7 copy.54
  (33 shorter events, 1.5 us)
Async XLA Ops:
  6.5 14.1 %all-gather.3.cloned.1.call-start = ((), (), s32[]{:S(2)}) async-start(), calls=%async_computation.4 | async-start | bytes 1572864 | tf_op jit(solution)/shard_map/all_gather | solution.py:45
  7.3 96.5 %all-gather.5.cloned.1.call-start = ((), (), s32[]{:S(2)}) async-start(), calls=%async_computation.5 | async-start | bytes 9437184 | tf_op jit(solution)/shard_map/all_gather | solution.py:49
  12.0 99.4 %copy-start.1 = (f32[3,3,256]{2,1,0:T(4,128)S(1)}, f32[3,3,256]{2,1,0:T(4,128)}, u32[]{:S(2)}) copy-start(f32[3,3,256]{2,1,0:T(4,128)} %param.7) | copy-start | bytes 27652
  12.0 101.7 %copy-start = (bf16[128,256]{1,0:T(8,128)(2,1)S(1)}, bf16[128,256]{1,0:T(8,128)(2,1)}, u32[]{:S(2)}) copy-start(bf16[128,256]{1,0:T(8,128)(2,1)} %param.9) | copy-start | bytes 196612
  109.2 3.5 %collective-permute-start = (bf16[2,3,256]{2,1,0:T(4,128)(2,1)S(1)}, bf16[2,3,256]{2,1,0:T(4,128)(2,1)S(1)}, u32[]{:S(2)}, u32[]{:S(2)}) collective-permute-start(bf16[2,3,256]{2,1,0:T(4,128)(2,1)S(1)} %slice.63), channel_id=1, source_target_pairs={{0,2},{2,4},{4,6},{6,8},{8,10},{10,12},{12,14},{1,3},{3,5},{5,7},{... | collective-permute-start | bytes 9224 | tf_op jit(solution)/shard_map/ppermute | solution.py:12
  114.5 14.8 %all-to-all-start = ((bf16[2,8,1,16,256]{4,3,0,2,1:T(8,128)(2,1)}), bf16[2,8,1,16,256]{4,3,0,2,1:T(8,128)(2,1)S(1)}, u32[]{:S(2)}, u32[]{:S(2)}) async-start(bf16[2,8,1,16,256]{4,3,0,2,1:T(8,128)(2,1)} %copy.37), calls=%async_computation | async-start | bytes 262144 | tf_op jit(solution)/shard_map/all_to_all | solution.py:40
  132.4 15.6 %all-to-all-start.1 = ((bf16[2,2,8,2,1,16,256]{6,3,5,1,4,0,2:T(2,128)(2,1)}), bf16[2,2,8,2,1,16,256]{6,3,5,1,4,0,2:T(2,128)(2,1)S(1)}, u32[]{:S(2)}, u32[]{:S(2)}) async-start(bf16[2,2,8,2,1,16,256]{6,3,5,1,4,0,2:T(2,128)(2,1)} %copy.62), calls=%async_computation.1 | async-start | bytes 1048576 | tf_op jit(solution)/shard_map/all_to_all | solution.py:90
  135.9 38.5 %copy-start.2 = (f32[256]{0:T(256)S(1)}, f32[256]{0:T(256)}, u32[]{:S(2)}) copy-start(f32[256]{0:T(256)} %param.8) | copy-start | bytes 3076
Sparse Core Ops, SparseCore 0:
  8.9 11.7 all-gather.2
  22.2 81.5 all-gather.4
where the time goes:
time: 182 us
  waiting for transfers between devices  113 us (62%)
  blocking collectives  21.4 us (12%)
  between operations  13.7 us (8%)
  starting transfers between devices  13.2 us (7%)
  matrix products  9.98 us (5%)
  local copies, waits for them, and re-layouts  8.96 us (5%)
  other arithmetic  2.03 us (1%)
    all_gather x1, waiting for transfers between devices, per_device(): piece = lax.all_gather(proj_weight, 'fsdp', axis=0, tiled=True)  83.1 us
    all_to_all x1, waiting for transfers between devices, per_device(): lax.all_to_all(outgoing, ('seq', 'fsdp'), split_axis=2, concat_axis=4, ti...  12 us
    all_to_all x1, blocking collectives, per_device(): lax.all_to_all(backward, ('seq', 'fsdp'), split_axis=3, concat_axis=1, ti...  11.7 us
    all_to_all x1, blocking collectives, per_device(): lax.all_to_all(conv_rows.reshape(groups, 1, per_dev, width), ('seq', 'fsd...  9.74 us
    all_gather x1, waiting for transfers between devices, per_device(): whole = lax.all_gather(tokens, 'chan', axis=1, tiled=True)  8.61 us
    all_to_all x1, starting transfers between devices, spread(): lax.all_to_all(shaped, ('seq', 'fsdp'), split_axis=1, concat_axis=2, tile...  7.46 us
    all_to_all x1, waiting for transfers between devices, spread(): lax.all_to_all(shaped, ('seq', 'fsdp'), split_axis=1, concat_axis=2, tile...  7.21 us
    dot_general x1, matrix products, per_device(): jnp.dot(whole, piece.reshape(piece.shape[0], flat_width), preferred_eleme...  5.33 us
  transfers between devices with their start and end apart: 5, of which 5 were waited for; matrix products, arithmetic and copies ran while one was open for 3% of the time, Pallas kernels for 0%

commit v1 on v0

--- a/solution.py
+++ b/solution.py
@@ -1,9 +1,17 @@
+import functools
 import math
 
 import jax
 import jax.numpy as jnp
+import numpy as np
 from jax import lax
+from jax.experimental import pallas as pl
+from jax.experimental.pallas import tpu as pltpu
 from jax.sharding import PartitionSpec as P
+
+HALO = 16
+F32 = jnp.float32
+BF16 = jnp.bfloat16
 
 
 def shifted(value, axis, steps):
@@ -41,7 +49,7 @@
     return moved.reshape((2, groups) + inner_shape)
 
 
-def per_device(tokens, proj_weight, short_weight, skip_gain, filter_taps):
+def any_mesh(tokens, proj_weight, short_weight, skip_gain, filter_taps):
     whole = lax.all_gather(tokens, "chan", axis=1, tiled=True)
     row_count = whole.shape[0]
     width = proj_weight.shape[2]
@@ -131,6 +139,224 @@
     return result.astype(jnp.bfloat16)
 
 
+def wave_table(size):
+    freq, time = np.meshgrid(np.arange(size), np.arange(size), indexing="ij")
+    angle = ((2 * freq + 1) * time % (4 * size)) * (math.pi / (2 * size))
+    return np.concatenate([np.cos(angle), np.sin(angle)], axis=0)
+
+
+def exchange(value, axis):
+    return lax.ppermute(value, axis, [(0, 1), (1, 0)])
+
+
+def whole_specs(count):
+    return [pl.BlockSpec(memory_space=pltpu.VMEM)] * count
+
+
+def split_channels(summed, own_half):
+    half = summed.shape[1] // 2
+    low, high = (summed[:, :half], summed[:, half:])
+    first = own_half == 0
+    return (jnp.where(first, low, high), jnp.where(first, high, low))
+
+
+def project_body(rows_ref, hop_ref, weight_ref, keep_ref, send_ref):
+    own_half = lax.axis_index("fsdp")
+    here = lax.axis_index("chan") == own_half
+    rows = jnp.where(here, rows_ref[...], hop_ref[...])
+    half = keep_ref.shape[1] // 3
+    for branch in range(3):
+        summed = jnp.dot(rows, weight_ref[branch], preferred_element_type=F32)
+        keep, send = split_channels(summed, own_half)
+        keep_ref[:, branch * half : (branch + 1) * half] = keep
+        send_ref[:, branch * half : (branch + 1) * half] = send.astype(BF16)
+
+
+def project_first_body(rows_ref, hop_ref, halo_ref, halo_hop_ref, weight_ref, keep_ref, send_ref):
+    own_half = lax.axis_index("fsdp")
+    here = lax.axis_index("chan") == own_half
+    rows = jnp.where(here, rows_ref[...], hop_ref[...])
+    halo = jnp.where(here, halo_ref[...], halo_hop_ref[...])
+    rows = jnp.concatenate([halo, rows], axis=0)
+    half = keep_ref.shape[1] // 3
+    for branch in range(3):
+        summed = jnp.dot(rows, weight_ref[branch], preferred_element_type=F32)
+        keep, send = split_channels(summed, own_half)
+        keep_ref[:, branch * half : (branch + 1) * half] = keep
+        send_ref[:, branch * half : (branch + 1) * half] = send.astype(BF16)
+
+
+def taps_body(table_ref, *refs):
+    tap_refs = refs[:4]
+    real_ref, imag_ref, ordered = refs[4:]
+    position = lax.axis_index("seq")
+    blocks = len(tap_refs)
+    size = table_ref.shape[1]
+    for step in range(blocks):
+        ordered[lax.rem(position - step + blocks, blocks)] = tap_refs[step][...]
+    sign = 1.0 - 2.0 * (lax.broadcasted_iota(jnp.int32, (size, 1), 0) % 2).astype(F32)
+    sign = sign * (1.0 / size)
+    before_real = before_imag = None
+    for block in range(blocks):
+        waves = jnp.dot(table_ref[...], ordered[block], preferred_element_type=F32)
+        real, imag = (waves[:size], -waves[size:])
+        if block == 0:
+            real_ref[block] = real * (1.0 / size)
+            imag_ref[block] = imag * (1.0 / size)
+        else:
+            real_ref[block] = real * (1.0 / size) - sign * before_imag
+            imag_ref[block] = imag * (1.0 / size) + sign * before_real
+        before_real, before_imag = (real, imag)
+
+
+def mix_body(keep_first, keep_second, got_first, got_second, short_ref, product_ref, query_ref, joined):
+    own = lax.axis_index("fsdp")
+    rows = keep_second.shape[0]
+    half = keep_second.shape[1] // 3
+    joined[:HALO, :] = keep_first[:HALO, :] + got_first[:HALO, :].astype(F32)
+    own_start = pl.multiple_of(HALO + own * rows, HALO)
+    other_start = pl.multiple_of(HALO + (1 - own) * rows, HALO)
+    joined[pl.ds(own_start, rows), :] = keep_first[HALO:, :] + got_second[...].astype(F32)
+    joined[pl.ds(other_start, rows), :] = keep_second[...] + got_first[HALO:, :].astype(F32)
+    count = 2 * rows
+    mixed = []
+    for branch in range(3):
+        lanes = slice(branch * half, (branch + 1) * half)
+        total = None
+        for tap in range(3):
+            term = short_ref[tap, branch][None, :] * joined[pl.ds(HALO - tap, count), lanes]
+            total = term if total is None else total + term
+        mixed.append(total)
+    query_ref[...] = mixed[0]
+    product_ref[...] = (mixed[1] * mixed[2]).astype(BF16)
+
+
+def conv_body(own_ref, one_ref, two_ref, three_ref, real_ref, imag_ref, table_ref, turned_ref,
+              query_ref, gain_ref, stay_ref, go_ref, result):
+    position = lax.axis_index("seq")
+    own = lax.axis_index("fsdp")
+    size = table_ref.shape[1]
+    total_real = total_imag = None
+    for step, block_ref in enumerate((own_ref, one_ref, two_ref, three_ref)):
+        block = block_ref[...]
+        if step:
+            block = jnp.where(position >= step, block, jnp.zeros_like(block))
+        waves = jnp.dot(table_ref[...], block, preferred_element_type=F32)
+        real, imag = (waves[:size], -waves[size:])
+        term_real = real * real_ref[step] - imag * imag_ref[step]
+        term_imag = real * imag_ref[step] + imag * real_ref[step]
+        total_real = term_real if total_real is None else total_real + term_real
+        total_imag = term_imag if total_imag is None else total_imag + term_imag
+    stacked = jnp.concatenate([total_real, -total_imag], axis=0).astype(BF16)
+    conv = jnp.dot(turned_ref[...], stacked, preferred_element_type=F32)
+    gated = query_ref[...] * (conv + gain_ref[...] * own_ref[...].astype(F32))
+    result[...] = gated.astype(BF16)
+    rows = stay_ref.shape[0]
+    stay_ref[...] = result[pl.ds(pl.multiple_of(own * rows, rows), rows), :]
+    go_ref[...] = result[pl.ds(pl.multiple_of((1 - own) * rows, rows), rows), :]
+
+
+def join_body(stay_ref, got_ref, out_ref):
+    first = lax.axis_index("fsdp") == 0
+    half = stay_ref.shape[1]
+    out_ref[:, :half] = jnp.where(first, stay_ref[...], got_ref[...])
+    out_ref[:, half:] = jnp.where(first, got_ref[...], stay_ref[...])
+
+
+def shape(dims, kind):
+    return jax.ShapeDtypeStruct(dims, kind)
+
+
+def pair_mesh(tokens, proj_weight, short_weight, skip_gain, filter_taps):
+    rows = tokens.shape[0]
+    features = proj_weight.shape[0]
+    width = proj_weight.shape[2]
+    half = width // 2
+    size = 2 * rows
+    blocks = lax.axis_size("seq")
+    fsdp = lax.axis_index("fsdp")
+    weight = jnp.transpose(proj_weight, (1, 0, 2))
+    call = functools.partial(
+        pl.pallas_call, compiler_params=pltpu.CompilerParams(vmem_limit_bytes=32 * 1024 * 1024)
+    )
+
+    got = lax.ppermute(tokens, ("fsdp", "chan"), [(1, 3), (2, 0)])
+    own_hop = exchange(tokens, "chan")
+    halo = lax.ppermute(
+        tokens[rows - HALO :],
+        ("seq", "fsdp", "chan"),
+        [(4 * s + 2 + c, 4 * (s + 1) + 2 * c + c) for s in range(blocks - 1) for c in range(2)],
+    )
+    halo_hop = exchange(halo, "chan")
+
+    keep_first, send_first = call(
+        project_first_body,
+        in_specs=whole_specs(5),
+        out_specs=whole_specs(2),
+        out_shape=(shape((HALO + rows, 3 * half), F32), shape((HALO + rows, 3 * half), BF16)),
+    )(tokens, own_hop, halo, halo_hop, weight)
+
+    table = wave_table(size)
+    forward = jnp.asarray(table, dtype=BF16)
+    inverse = jnp.asarray(table.T, dtype=BF16)
+    tap_low, tap_high = (filter_taps[:, :half], filter_taps[:, half:])
+    first = fsdp == 0
+    tap_keep = jnp.where(first, tap_low, tap_high)
+    tap_got = exchange(jnp.where(first, tap_high, tap_low), "fsdp")
+    taps = jnp.where(
+        first,
+        jnp.concatenate([tap_keep, tap_got], axis=0),
+        jnp.concatenate([tap_got, tap_keep], axis=0),
+    )
+    ring = [
+        [(s, (s + step) % blocks) for s in range(blocks)] for step in range(blocks)
+    ]
+    tap_blocks = [taps] + [lax.ppermute(taps, "seq", ring[step]) for step in range(1, blocks)]
+    tap_real, tap_imag = call(
+        taps_body,
+        in_specs=whole_specs(1 + blocks),
+        out_specs=whole_specs(2),
+        out_shape=(shape((blocks, size, half), F32), shape((blocks, size, half), F32)),
+        scratch_shapes=[pltpu.VMEM((blocks, size, half), BF16)],
+    )(forward, *tap_blocks)
+
+    got_first = exchange(send_first, "fsdp")
+    got_hop = exchange(got, "chan")
+    keep_second, send_second = call(
+        project_body,
+        in_specs=whole_specs(3),
+        out_specs=whole_specs(2),
+        out_shape=(shape((rows, 3 * half), F32), shape((rows, 3 * half), BF16)),
+    )(got, got_hop, weight)
+    got_second = exchange(send_second, "fsdp")
+
+    short_half = lax.dynamic_slice_in_dim(short_weight, fsdp * half, half, axis=2)
+    gain_half = lax.dynamic_slice_in_dim(skip_gain, fsdp * half, half, axis=0)[None, :]
+    product, query = call(
+        mix_body,
+        in_specs=whole_specs(5),
+        out_specs=whole_specs(2),
+        out_shape=(shape((size, half), BF16), shape((size, half), F32)),
+        scratch_shapes=[pltpu.VMEM((HALO + size, 3 * half), F32)],
+    )(keep_first, keep_second, got_first, got_second, short_half)
+
+    products = [product] + [lax.ppermute(product, "seq", ring[step]) for step in range(1, blocks)]
+    stay, go = call(
+        conv_body,
+        in_specs=whole_specs(10),
+        out_specs=whole_specs(2),
+        out_shape=(shape((rows, half), BF16), shape((rows, half), BF16)),
+        scratch_shapes=[pltpu.VMEM((size, half), BF16)],
+    )(*products, tap_real, tap_imag, forward, inverse, query, gain_half)
+    back = exchange(go, "fsdp")
+    return call(
+        join_body,
+        in_specs=whole_specs(2),
+        out_specs=whole_specs(1)[0],
+        out_shape=shape((rows, width), BF16),
+    )(stay, back)
+
+
 def solution(mesh):
     in_specs = (
         P(("grp", "seq", "fsdp"), "chan"),
@@ -140,6 +366,9 @@
         P(("seq", "fsdp"), "chan"),
     )
     out_specs = P(("grp", "seq", "fsdp"), "chan")
+    sizes = mesh.shape
+    paired = sizes["fsdp"] == 2 and sizes["chan"] == 2 and sizes["seq"] == 4
+    per_device = pair_mesh if paired else any_mesh
     return jax.shard_map(
         per_device, mesh=mesh, in_specs=in_specs, out_specs=out_specs, check_vma=False
     )

time: 182 us -> 48.1 us (0.26)
  waiting for transfers between devices: 113 us -> 14.4 us
  blocking collectives: 21.4 us -> 0 us
  between operations: 13.7 us -> 0.11 us
  starting transfers between devices: 13.2 us -> 25.2 us
  matrix products: 9.98 us -> 0 us
  local copies, waits for them, and re-layouts: 8.96 us -> 3.88 us
  Pallas kernels: 0 us -> 3.31 us
    all_gather x2 -> x0, waiting for transfers between devices: 91.7 us -> none  [the longest x1 83.1 us: per_device(): piece = lax.all_gather(proj_weight, 'fsdp', axis=0, tiled=True)]
    ppermute x1 -> x15, starting transfers between devices: 2.22 us -> 25.2 us  [the longest x7 13.2 us: exchange(): return lax.ppermute(value, axis, [(0, 1), (1, 0)])]
    all_to_all x2 -> x0, blocking collectives: 21.4 us -> none  [the longest x1 11.7 us: per_device(): lax.all_to_all(backward, ('seq', 'fsdp'), split_axis=3, concat_axis=1, ti...]
    all_to_all x2 -> x0, waiting for transfers between devices: 19.2 us -> none  [the longest x1 12 us: per_device(): lax.all_to_all(outgoing, ('seq', 'fsdp'), split_axis=2, concat_axis=4, ti...]
    ppermute x1 -> x15, waiting for transfers between devices: 1.12 us -> 14.4 us  [the longest x1 7.08 us: pair_mesh(): got = lax.ppermute(tokens, ('fsdp', 'chan'), [(1, 3), (2, 0)])]
    all_to_all x2 -> x0, starting transfers between devices: 11 us -> none  [the longest x1 7.46 us: spread(): lax.all_to_all(shaped, ('seq', 'fsdp'), split_axis=1, concat_axis=2, tile...]
    dot_general x13 -> x0, matrix products: 9.98 us -> none  [the longest x1 5.33 us: per_device(): jnp.dot(whole, piece.reshape(piece.shape[0], flat_width), preferred_eleme...]
    pallas_call x0 -> x6, Pallas kernels: none -> 3.31 us  [the longest x1 0.7 us: pair_mesh(): call(conv_body, in_specs=whole_specs(10), out_specs=whole_specs(2), out_s...]
  transfers between devices with their start and end apart: 5 -> 15, of which waited for: 5 -> 5; matrix products, arithmetic and copies ran while one was open for 3% -> 4% of each run, Pallas kernels for 0% -> 4%
where the time goes in v1:
time: 48.1 us; the launch traced here: 47.8 us
  starting transfers between devices  25.2 us (52%)
  waiting for transfers between devices  14.4 us (30%)
  local copies, waits for them, and re-layouts  3.88 us (8%)
  Pallas kernels  3.31 us (7%)
  other arithmetic  0.8 us (2%)
    ppermute x7, starting transfers between devices, exchange(): return lax.ppermute(value, axis, [(0, 1), (1, 0)])  13.2 us
    ppermute x1, waiting for transfers between devices, pair_mesh(): got = lax.ppermute(tokens, ('fsdp', 'chan'), [(1, 3), (2, 0)])  7.08 us
    ppermute x3, starting transfers between devices, pair_mesh(): lax.ppermute(taps, 'seq', ring[step])  5.56 us
    ppermute x7, waiting for transfers between devices, exchange(): return lax.ppermute(value, axis, [(0, 1), (1, 0)])  4.65 us
    ppermute x3, starting transfers between devices, pair_mesh(): lax.ppermute(product, 'seq', ring[step])  4.4 us
    unnamed x14, local copies, waits for them, and re-layouts  2.96 us
    ppermute x3, waiting for transfers between devices, pair_mesh(): lax.ppermute(product, 'seq', ring[step])  2.69 us
    ppermute x1, starting transfers between devices, pair_mesh(): got = lax.ppermute(tokens, ('fsdp', 'chan'), [(1, 3), (2, 0)])  1.41 us
  transfers between devices with their start and end apart: 15, of which 5 were waited for; matrix products, arithmetic and copies ran while one was open for 4% of the time, Pallas kernels for 4%

profile of v1, /device:TPU:0, one launch (start us, length us, event | category | flops | bytes accessed | tf_op | source)
XLA Modules:
  0.0 47.8 jit_solution(1177398178002632309)
XLA Ops:
  0.0 1.4 %collective-permute-start.3 = (bf16[128,2048]{1,0:T(8,128)(2,1)}, bf16[128,2048]{1,0:T(8,128)(2,1)S(1)}, u32[]{:S(2)}, u32[]{:S(2)}) collective-permute-start(bf16[128,2048]{1,0:T(8,128)(2,1)} %rows_ref.1), channel_id=1, source_target_pairs={{1,3},{2,0},{5,7},{6,4},{9,11},{10,8},{13,15},{14,12},{17,19},{18,... | collective-permute-start | bytes 1572872 | tf_op jit(solution)/shard_map/ppermute | solution.py:283
  1.4 3.2 %collective-permute-start = (bf16[128,2048]{1,0:T(8,128)(2,1)}, bf16[128,2048]{1,0:T(8,128)(2,1)S(1)}, u32[]{:S(2)}, u32[]{:S(2)}) collective-permute-start(bf16[128,2048]{1,0:T(8,128)(2,1)} %rows_ref.1), channel_id=1, source_target_pairs={{0,1},{1,0},{2,3},{3,2},{4,5},{5,4},{6,7},{7,6},{8,9},{9,8},{10,11... | collective-permute-start | bytes 1572872 | tf_op jit(solution)/shard_map/ppermute | solution.py:149
  4.6 7.1 %collective-permute-done.3.rows_ref = bf16[128,2048]{1,0:T(8,128)(2,1)S(1)} collective-permute-done((bf16[128,2048]{1,0:T(8,128)(2,1)}, bf16[128,2048]{1,0:T(8,128)(2,1)S(1)}, u32[]{:S(2)}, u32[]{:S(2)}) %collective-permute-start.3) | collective-permute-done | bytes 524320 | tf_op jit(solution)/shard_map/ppermute | solution.py:283
  11.7 0.8 %slice.9 = bf16[16,2048]{1,0:T(8,128)(2,1)S(1)} slice(bf16[128,2048]{1,0:T(8,128)(2,1)} %rows_ref.1), slice={[112:128], [0:2048]} | slice | bytes 131072 | tf_op jit(solution)/shard_map/slice | solution.py:286
  12.6 0.7 %collective-permute-start.1 = (bf16[16,2048]{1,0:T(8,128)(2,1)S(1)}, bf16[16,2048]{1,0:T(8,128)(2,1)S(1)}, u32[]{:S(2)}, u32[]{:S(2)}) collective-permute-start(bf16[16,2048]{1,0:T(8,128)(2,1)S(1)} %slice.9), channel_id=1, source_target_pairs={{2,4},{3,7},{6,8},{7,11},{10,12},{11,15},{18,20},{19,23},{22,24},{... | collective-permute-start | bytes 196616 | tf_op jit(solution)/shard_map/ppermute | solution.py:285
  13.2 0.8 %broadcast_select_fusion.1 = (bf16[128,128]{1,0:T(8,128)(2,1)S(1)}, bf16[128,128]{1,0:T(8,128)(2,1)S(1)}) fusion(pred[]{:T(512)S(6)} %eq.3, bf16[128,256]{1,0:T(8,128)(2,1)} %param.11), kind=kLoop, calls=%fused_computation.2 | loop fusion | flops 32768 | bytes 131073 | tf_op jit(solution)/shard_map/jit(_where)/select_n | solution.py:304
  14.0 5.5 %collective-permute-start.10 = (bf16[128,128]{1,0:T(8,128)(2,1)S(1)}, bf16[128,128]{1,0:T(8,128)(2,1)S(1)}, u32[]{:S(2)}, u32[]{:S(2)}) collective-permute-start(bf16[128,128]{1,0:T(8,128)(2,1)S(1)} %get-tuple-element.26), channel_id=1, source_target_pairs={{0,2},{2,0},{1,3},{3,1},{4,6},{6,4},{5,7},{7,5},{8,10},{10,8},{9,1... | collective-permute-start | bytes 98312 | tf_op jit(solution)/shard_map/ppermute | solution.py:149
  19.5 1.9 %collective-permute-done.10 = bf16[128,128]{1,0:T(8,128)(2,1)S(1)} collective-permute-done((bf16[128,128]{1,0:T(8,128)(2,1)S(1)}, bf16[128,128]{1,0:T(8,128)(2,1)S(1)}, u32[]{:S(2)}, u32[]{:S(2)}) %collective-permute-start.10) | collective-permute-done | bytes 32800 | tf_op jit(solution)/shard_map/ppermute | solution.py:149
  21.4 1.6 %collective-permute-start.11 = (bf16[256,128]{1,0:T(8,128)(2,1)S(1)}, bf16[256,128]{1,0:T(8,128)(2,1)S(1)}, u32[]{:S(2)}, u32[]{:S(2)}) collective-permute-start(bf16[256,128]{1,0:T(8,128)(2,1)S(1)} %maximum_select_fusion.refs_0_), channel_id=1, source_target_pairs={{0,4},{4,8},{8,12},{12,0},{1,5},{5,9},{9,13},{13,1},{2,6},{6,10},{... | collective-permute-start | bytes 196616 | tf_op jit(solution)/shard_map/ppermute | solution.py:314
  23.1 1.9 %copy-done.1 = bf16[2048,3,256]{2,0,1:T(8,128)(2,1)S(1)} copy-done((bf16[2048,3,256]{2,0,1:T(8,128)(2,1)S(1)}, bf16[2048,3,256]{2,0,1:T(8,128)(2,1)}, u32[]{:S(2)}) %copy-start.1) | copy-done | bytes 3145752
  24.9 1.0 %copy-done.4 = bf16[128,2048]{1,0:T(8,128)(2,1)S(1)} copy-done((bf16[128,2048]{1,0:T(8,128)(2,1)S(1)}, bf16[128,2048]{1,0:T(8,128)(2,1)}, u32[]{:S(2)}) %copy-start.4) | copy-done | bytes 524312
  26.0 0.6 %shard_map.73 = (f32[144,384]{1,0:T(8,128)S(1)}, bf16[144,384]{1,0:T(8,128)(2,1)S(1)}) custom-call(bf16[128,2048]{1,0:T(8,128)(2,1)S(1)} %copy-done.4, bf16[128,2048]{1,0:T(8,128)(2,1)S(1)} %collective-permute-done.hop_ref, bf16[16,2048]{1,0:T(8,128)(2,1)S(1)} %collective-permute-done.1.halo_ref, bf16[16,2048]{1,0:T(8,128)(2,1)S(1)} %collective-permute-done.2.halo_hop_ref, ...), custom_call_target="tpu_custom_call" | custom-call | tf_op jit(solution)/shard_map/pallas_call | solution.py:292
  26.6 0.0 copy-start.6
  26.7 0.0 copy-start.3
  26.7 0.0 copy-start.5
  26.7 2.1 %collective-permute-start.5 = (bf16[144,384]{1,0:T(8,128)(2,1)S(1)}, bf16[144,384]{1,0:T(8,128)(2,1)S(1)}, u32[]{:S(2)}, u32[]{:S(2)}) collective-permute-start(bf16[144,384]{1,0:T(8,128)(2,1)S(1)} %get-tuple-element.17), channel_id=1, source_target_pairs={{0,2},{2,0},{1,3},{3,1},{4,6},{6,4},{5,7},{7,5},{8,10},{10,8},{9,1... | collective-permute-start | bytes 331784 | tf_op jit(solution)/shard_map/ppermute | solution.py:149
  28.8 0.7 %shard_map.74 = (f32[128,384]{1,0:T(8,128)S(1)}, bf16[128,384]{1,0:T(8,128)(2,1)S(1)}) custom-call(bf16[128,2048]{1,0:T(8,128)(2,1)S(1)} %collective-permute-done.3.rows_ref, bf16[128,2048]{1,0:T(8,128)(2,1)S(1)} %collective-permute-done.4.hop_ref, bf16[3,2048,256]{2,1,0:T(8,128)(2,1)S(1)} %bitcast.4), custom_call_target="tpu_custom_call" | custom-call | tf_op jit(solution)/shard_map/pallas_call | solution.py:325
  29.4 1.2 %collective-permute-start.6 = (bf16[128,384]{1,0:T(8,128)(2,1)S(1)}, bf16[128,384]{1,0:T(8,128)(2,1)S(1)}, u32[]{:S(2)}, u32[]{:S(2)}) collective-permute-start(bf16[128,384]{1,0:T(8,128)(2,1)S(1)} %get-tuple-element.18), channel_id=1, source_target_pairs={{0,2},{2,0},{1,3},{3,1},{4,6},{6,4},{5,7},{7,5},{8,10},{10,8},{9,1... | collective-permute-start | bytes 294920 | tf_op jit(solution)/shard_map/ppermute | solution.py:149
  30.6 1.0 %collective-permute-start.12 = (bf16[256,128]{1,0:T(8,128)(2,1)S(1)}, bf16[256,128]{1,0:T(8,128)(2,1)S(1)}, u32[]{:S(2)}, u32[]{:S(2)}) collective-permute-start(bf16[256,128]{1,0:T(8,128)(2,1)S(1)} %maximum_select_fusion.refs_0_), channel_id=1, source_target_pairs={{0,8},{4,12},{8,0},{12,4},{1,9},{5,13},{9,1},{13,5},{2,10},{6,14},... | collective-permute-start | bytes 196616 | tf_op jit(solution)/shard_map/ppermute | solution.py:314
  31.7 2.9 %collective-permute-start.13 = (bf16[256,128]{1,0:T(8,128)(2,1)S(1)}, bf16[256,128]{1,0:T(8,128)(2,1)S(1)}, u32[]{:S(2)}, u32[]{:S(2)}) collective-permute-start(bf16[256,128]{1,0:T(8,128)(2,1)S(1)} %maximum_select_fusion.refs_0_), channel_id=1, source_target_pairs={{0,12},{4,0},{8,4},{12,8},{1,13},{5,1},{9,5},{13,9},{2,14},{6,2},{... | collective-permute-start | bytes 196616 | tf_op jit(solution)/shard_map/ppermute | solution.py:314
  34.6 0.2 shard_map.75
  34.8 1.2 %collective-permute-start.7 = (bf16[256,128]{1,0:T(8,128)(2,1)S(1)}, bf16[256,128]{1,0:T(8,128)(2,1)S(1)}, u32[]{:S(2)}, u32[]{:S(2)}) collective-permute-start(bf16[256,128]{1,0:T(8,128)(2,1)S(1)} %get-tuple-element.19.own_ref), channel_id=1, source_target_pairs={{0,4},{4,8},{8,12},{12,0},{1,5},{5,9},{9,13},{13,1},{2,6},{6,10},{... | collective-permute-start | bytes 196616 | tf_op jit(solution)/shard_map/ppermute | solution.py:343
  35.9 1.4 %collective-permute-start.8 = (bf16[256,128]{1,0:T(8,128)(2,1)S(1)}, bf16[256,128]{1,0:T(8,128)(2,1)S(1)}, u32[]{:S(2)}, u32[]{:S(2)}) collective-permute-start(bf16[256,128]{1,0:T(8,128)(2,1)S(1)} %get-tuple-element.19.own_ref), channel_id=1, source_target_pairs={{0,8},{4,12},{8,0},{12,4},{1,9},{5,13},{9,1},{13,5},{2,10},{6,14},... | collective-permute-start | bytes 196616 | tf_op jit(solution)/shard_map/ppermute | solution.py:343
  37.3 1.8 %collective-permute-start.9 = (bf16[256,128]{1,0:T(8,128)(2,1)S(1)}, bf16[256,128]{1,0:T(8,128)(2,1)S(1)}, u32[]{:S(2)}, u32[]{:S(2)}) collective-permute-start(bf16[256,128]{1,0:T(8,128)(2,1)S(1)} %get-tuple-element.19.own_ref), channel_id=1, source_target_pairs={{0,12},{4,0},{8,4},{12,8},{1,13},{5,1},{9,5},{13,9},{2,14},{6,2},{... | collective-permute-start | bytes 196616 | tf_op jit(solution)/shard_map/ppermute | solution.py:343
  39.2 0.1 dynamic-slice_bitcast_fusion.gain_ref
  39.3 0.5 shard_map.76
  39.7 1.5 %collective-permute-done.7.one_ref = bf16[256,128]{1,0:T(8,128)(2,1)S(1)} collective-permute-done((bf16[256,128]{1,0:T(8,128)(2,1)S(1)}, bf16[256,128]{1,0:T(8,128)(2,1)S(1)}, u32[]{:S(2)}, u32[]{:S(2)}) %collective-permute-start.7) | collective-permute-done | bytes 65568 | tf_op jit(solution)/shard_map/ppermute | solution.py:343
  41.2 1.2 %collective-permute-done.8.two_ref = bf16[256,128]{1,0:T(8,128)(2,1)S(1)} collective-permute-done((bf16[256,128]{1,0:T(8,128)(2,1)S(1)}, bf16[256,128]{1,0:T(8,128)(2,1)S(1)}, u32[]{:S(2)}, u32[]{:S(2)}) %collective-permute-start.8) | collective-permute-done | bytes 65568 | tf_op jit(solution)/shard_map/ppermute | solution.py:343
  42.4 0.7 %shard_map.77 = (bf16[128,128]{1,0:T(8,128)(2,1)S(1)}, bf16[128,128]{1,0:T(8,128)(2,1)S(1)}) custom-call(bf16[256,128]{1,0:T(8,128)(2,1)S(1)} %get-tuple-element.19.own_ref, bf16[256,128]{1,0:T(8,128)(2,1)S(1)} %collective-permute-done.7.one_ref, bf16[256,128]{1,0:T(8,128)(2,1)S(1)} %collective-permute-done.8.two_ref, ...), custom_call_target="tpu_custom_call" | custom-call | tf_op jit(solution)/shard_map/pallas_call | solution.py:344
  43.1 1.2 %collective-permute-start.14 = (bf16[128,128]{1,0:T(8,128)(2,1)S(1)}, bf16[128,128]{1,0:T(8,128)(2,1)S(1)}, u32[]{:S(2)}, u32[]{:S(2)}) collective-permute-start(bf16[128,128]{1,0:T(8,128)(2,1)S(1)} %get-tuple-element.24), channel_id=1, source_target_pairs={{0,2},{2,0},{1,3},{3,1},{4,6},{6,4},{5,7},{7,5},{8,10},{10,8},{9,1... | collective-permute-start | bytes 98312 | tf_op jit(solution)/shard_map/ppermute | solution.py:149
  44.4 2.8 %collective-permute-done.14.got_ref = bf16[128,128]{1,0:T(8,128)(2,1)S(1)} collective-permute-done((bf16[128,128]{1,0:T(8,128)(2,1)S(1)}, bf16[128,128]{1,0:T(8,128)(2,1)S(1)}, u32[]{:S(2)}, u32[]{:S(2)}) %collective-permute-start.14) | collective-permute-done | bytes 32800 | tf_op jit(solution)/shard_map/ppermute | solution.py:149
  47.1 0.6 %shard_map.78 = bf16[128,256]{1,0:T(8,128)(2,1)} custom-call(bf16[128,128]{1,0:T(8,128)(2,1)S(1)} %get-tuple-element.23.stay_ref, bf16[128,128]{1,0:T(8,128)(2,1)S(1)} %collective-permute-done.14.got_ref), custom_call_target="tpu_custom_call" | custom-call | tf_op jit(solution)/shard_map/pallas_call | solution.py:352
  (23 shorter events, 0.1 us)
Async XLA Ops:
  0.0 30.6 %copy-start = (f32[3,3,256]{2,1,0:T(4,128)S(1)}, f32[3,3,256]{2,1,0:T(4,128)}, u32[]{:S(2)}) copy-start(f32[3,3,256]{2,1,0:T(4,128)} %param.9) | copy-start | bytes 27652
  0.0 11.7 %collective-permute-start.3 = (bf16[128,2048]{1,0:T(8,128)(2,1)}, bf16[128,2048]{1,0:T(8,128)(2,1)S(1)}, u32[]{:S(2)}, u32[]{:S(2)}) collective-permute-start(bf16[128,2048]{1,0:T(8,128)(2,1)} %rows_ref.1), channel_id=1, source_target_pairs={{1,3},{2,0},{5,7},{6,4},{9,11},{10,8},{13,15},{14,12},{17,19},{18,... | collective-permute-start | bytes 1572872 | tf_op jit(solution)/shard_map/ppermute | solution.py:283
  1.4 21.6 %collective-permute-start = (bf16[128,2048]{1,0:T(8,128)(2,1)}, bf16[128,2048]{1,0:T(8,128)(2,1)S(1)}, u32[]{:S(2)}, u32[]{:S(2)}) collective-permute-start(bf16[128,2048]{1,0:T(8,128)(2,1)} %rows_ref.1), channel_id=1, source_target_pairs={{0,1},{1,0},{2,3},{3,2},{4,5},{5,4},{6,7},{7,6},{8,9},{9,8},{10,11... | collective-permute-start | bytes 1572872 | tf_op jit(solution)/shard_map/ppermute | solution.py:149
  11.7 17.1 %collective-permute-start.4 = (bf16[128,2048]{1,0:T(8,128)(2,1)S(1)}, bf16[128,2048]{1,0:T(8,128)(2,1)S(1)}, u32[]{:S(2)}, u32[]{:S(2)}) collective-permute-start(bf16[128,2048]{1,0:T(8,128)(2,1)S(1)} %collective-permute-done.3.rows_ref), channel_id=1, source_target_pairs={{0,1},{1,0},{2,3},{3,2},{4,5},{5,4},{6,7},{7,6},{8,9},{9,8},{10,11... | collective-permute-start | bytes 1572872 | tf_op jit(solution)/shard_map/ppermute | solution.py:149
  12.6 6.9 %collective-permute-start.1 = (bf16[16,2048]{1,0:T(8,128)(2,1)S(1)}, bf16[16,2048]{1,0:T(8,128)(2,1)S(1)}, u32[]{:S(2)}, u32[]{:S(2)}) collective-permute-start(bf16[16,2048]{1,0:T(8,128)(2,1)S(1)} %slice.9), channel_id=1, source_target_pairs={{2,4},{3,7},{6,8},{7,11},{10,12},{11,15},{18,20},{19,23},{22,24},{... | collective-permute-start | bytes 196616 | tf_op jit(solution)/shard_map/ppermute | solution.py:285
  14.0 7.4 %collective-permute-start.10 = (bf16[128,128]{1,0:T(8,128)(2,1)S(1)}, bf16[128,128]{1,0:T(8,128)(2,1)S(1)}, u32[]{:S(2)}, u32[]{:S(2)}) collective-permute-start(bf16[128,128]{1,0:T(8,128)(2,1)S(1)} %get-tuple-element.26), channel_id=1, source_target_pairs={{0,2},{2,0},{1,3},{3,1},{4,6},{6,4},{5,7},{7,5},{8,10},{10,8},{9,1... | collective-permute-start | bytes 98312 | tf_op jit(solution)/shard_map/ppermute | solution.py:149
  19.5 3.5 %collective-permute-start.2 = (bf16[16,2048]{1,0:T(8,128)(2,1)S(1)}, bf16[16,2048]{1,0:T(8,128)(2,1)S(1)}, u32[]{:S(2)}, u32[]{:S(2)}) collective-permute-start(bf16[16,2048]{1,0:T(8,128)(2,1)S(1)} %collective-permute-done.1.halo_ref), channel_id=1, source_target_pairs={{0,1},{1,0},{2,3},{3,2},{4,5},{5,4},{6,7},{7,6},{8,9},{9,8},{10,11... | collective-permute-start | bytes 196616 | tf_op jit(solution)/shard_map/ppermute | solution.py:149
  21.4 15.9 %collective-permute-start.11 = (bf16[256,128]{1,0:T(8,128)(2,1)S(1)}, bf16[256,128]{1,0:T(8,128)(2,1)S(1)}, u32[]{:S(2)}, u32[]{:S(2)}) collective-permute-start(bf16[256,128]{1,0:T(8,128)(2,1)S(1)} %maximum_select_fusion.refs_0_), channel_id=1, source_target_pairs={{0,4},{4,8},{8,12},{12,0},{1,5},{5,9},{9,13},{13,1},{2,6},{6,10},{... | collective-permute-start | bytes 196616 | tf_op jit(solution)/shard_map/ppermute | solution.py:314
  23.1 1.9 %copy-start.1 = (bf16[2048,3,256]{2,0,1:T(8,128)(2,1)S(1)}, bf16[2048,3,256]{2,0,1:T(8,128)(2,1)}, u32[]{:S(2)}) copy-start(bf16[2048,3,256]{2,0,1:T(8,128)(2,1)} %param.8) | copy-start | bytes 9437188
  24.9 1.0 %copy-start.4 = (bf16[128,2048]{1,0:T(8,128)(2,1)S(1)}, bf16[128,2048]{1,0:T(8,128)(2,1)}, u32[]{:S(2)}) copy-start(bf16[128,2048]{1,0:T(8,128)(2,1)} %rows_ref.1) | copy-start | bytes 1572868
  26.0 2.8 %copy-start.2 = (bf16[2048,3,256]{2,0,1:T(8,128)(2,1)S(1)}, bf16[2048,3,256]{2,0,1:T(8,128)(2,1)}, u32[]{:S(2)}) copy-start(bf16[2048,3,256]{2,0,1:T(8,128)(2,1)} %param.8) | copy-start | bytes 9437188
  26.6 12.5 %copy-start.6 = (f32[256]{0:T(256)S(1)}, f32[256]{0:T(256)}, u32[]{:S(2)}) copy-start(f32[256]{0:T(256)} %param.10) | copy-start | bytes 3076
  26.7 12.6 %copy-start.3 = (bf16[512,256]{1,0:T(8,128)(2,1)S(1)}, bf16[512,256]{1,0:T(8,128)(2,1)}, u32[]{:S(2)}) copy-start(bf16[512,256]{1,0:T(8,128)(2,1)} %constant.14.clone.table_ref) | copy-start | bytes 786436
  26.7 15.8 %copy-start.5 = (bf16[256,512]{1,0:T(8,128)(2,1)S(1)}, bf16[256,512]{1,0:T(8,128)(2,1)}, u32[]{:S(2)}) copy-start(bf16[256,512]{1,0:T(8,128)(2,1)} %constant.15.clone.turned_ref) | copy-start | bytes 786436
  26.7 7.9 %collective-permute-start.5 = (bf16[144,384]{1,0:T(8,128)(2,1)S(1)}, bf16[144,384]{1,0:T(8,128)(2,1)S(1)}, u32[]{:S(2)}, u32[]{:S(2)}) collective-permute-start(bf16[144,384]{1,0:T(8,128)(2,1)S(1)} %get-tuple-element.17), channel_id=1, source_target_pairs={{0,2},{2,0},{1,3},{3,1},{4,6},{6,4},{5,7},{7,5},{8,10},{10,8},{9,1... | collective-permute-start | bytes 331784 | tf_op jit(solution)/shard_map/ppermute | solution.py:149
  29.4 5.1 %collective-permute-start.6 = (bf16[128,384]{1,0:T(8,128)(2,1)S(1)}, bf16[128,384]{1,0:T(8,128)(2,1)S(1)}, u32[]{:S(2)}, u32[]{:S(2)}) collective-permute-start(bf16[128,384]{1,0:T(8,128)(2,1)S(1)} %get-tuple-element.18), channel_id=1, source_target_pairs={{0,2},{2,0},{1,3},{3,1},{4,6},{6,4},{5,7},{7,5},{8,10},{10,8},{9,1... | collective-permute-start | bytes 294920 | tf_op jit(solution)/shard_map/ppermute | solution.py:149
  30.6 8.6 %collective-permute-start.12 = (bf16[256,128]{1,0:T(8,128)(2,1)S(1)}, bf16[256,128]{1,0:T(8,128)(2,1)S(1)}, u32[]{:S(2)}, u32[]{:S(2)}) collective-permute-start(bf16[256,128]{1,0:T(8,128)(2,1)S(1)} %maximum_select_fusion.refs_0_), channel_id=1, source_target_pairs={{0,8},{4,12},{8,0},{12,4},{1,9},{5,13},{9,1},{13,5},{2,10},{6,14},... | collective-permute-start | bytes 196616 | tf_op jit(solution)/shard_map/ppermute | solution.py:314
  31.7 7.6 %collective-permute-start.13 = (bf16[256,128]{1,0:T(8,128)(2,1)S(1)}, bf16[256,128]{1,0:T(8,128)(2,1)S(1)}, u32[]{:S(2)}, u32[]{:S(2)}) collective-permute-start(bf16[256,128]{1,0:T(8,128)(2,1)S(1)} %maximum_select_fusion.refs_0_), channel_id=1, source_target_pairs={{0,12},{4,0},{8,4},{12,8},{1,13},{5,1},{9,5},{13,9},{2,14},{6,2},{... | collective-permute-start | bytes 196616 | tf_op jit(solution)/shard_map/ppermute | solution.py:314
  34.8 6.4 %collective-permute-start.7 = (bf16[256,128]{1,0:T(8,128)(2,1)S(1)}, bf16[256,128]{1,0:T(8,128)(2,1)S(1)}, u32[]{:S(2)}, u32[]{:S(2)}) collective-permute-start(bf16[256,128]{1,0:T(8,128)(2,1)S(1)} %get-tuple-element.19.own_ref), channel_id=1, source_target_pairs={{0,4},{4,8},{8,12},{12,0},{1,5},{5,9},{9,13},{13,1},{2,6},{6,10},{... | collective-permute-start | bytes 196616 | tf_op jit(solution)/shard_map/ppermute | solution.py:343
  35.9 6.5 %collective-permute-start.8 = (bf16[256,128]{1,0:T(8,128)(2,1)S(1)}, bf16[256,128]{1,0:T(8,128)(2,1)S(1)}, u32[]{:S(2)}, u32[]{:S(2)}) collective-permute-start(bf16[256,128]{1,0:T(8,128)(2,1)S(1)} %get-tuple-element.19.own_ref), channel_id=1, source_target_pairs={{0,8},{4,12},{8,0},{12,4},{1,9},{5,13},{9,1},{13,5},{2,10},{6,14},... | collective-permute-start | bytes 196616 | tf_op jit(solution)/shard_map/ppermute | solution.py:343
  37.3 5.1 %collective-permute-start.9 = (bf16[256,128]{1,0:T(8,128)(2,1)S(1)}, bf16[256,128]{1,0:T(8,128)(2,1)S(1)}, u32[]{:S(2)}, u32[]{:S(2)}) collective-permute-start(bf16[256,128]{1,0:T(8,128)(2,1)S(1)} %get-tuple-element.19.own_ref), channel_id=1, source_target_pairs={{0,12},{4,0},{8,4},{12,8},{1,13},{5,1},{9,5},{13,9},{2,14},{6,2},{... | collective-permute-start | bytes 196616 | tf_op jit(solution)/shard_map/ppermute | solution.py:343
  43.1 4.0 %collective-permute-start.14 = (bf16[128,128]{1,0:T(8,128)(2,1)S(1)}, bf16[128,128]{1,0:T(8,128)(2,1)S(1)}, u32[]{:S(2)}, u32[]{:S(2)}) collective-permute-start(bf16[128,128]{1,0:T(8,128)(2,1)S(1)} %get-tuple-element.24), channel_id=1, source_target_pairs={{0,2},{2,0},{1,3},{3,1},{4,6},{6,4},{5,7},{7,5},{8,10},{10,8},{9,1... | collective-permute-start | bytes 98312 | tf_op jit(solution)/shard_map/ppermute | solution.py:149

commit v2 on v1

--- a/solution.py
+++ b/solution.py
@@ -10,6 +10,7 @@
 from jax.sharding import PartitionSpec as P
 
 HALO = 16
+LOAD_MIB = 48
 F32 = jnp.float32
 BF16 = jnp.bfloat16
 
@@ -160,10 +161,52 @@
     return (jnp.where(first, low, high), jnp.where(first, high, low))
 
 
-def project_body(rows_ref, hop_ref, weight_ref, keep_ref, send_ref):
-    own_half = lax.axis_index("fsdp")
-    here = lax.axis_index("chan") == own_half
-    rows = jnp.where(here, rows_ref[...], hop_ref[...])
+def pick_rows(source, target):
+    lines = lax.broadcasted_iota(jnp.int32, (HALO, HALO), 0)
+    places = lax.broadcasted_iota(jnp.int32, (HALO, HALO), 1)
+    wanted = (lines - target == places - source) & (places >= source) & (places < source + 2)
+    return wanted.astype(F32).astype(BF16)
+
+
+def pack_body(rows_ref, pack_ref, done_ref):
+    width = pack_ref.shape[1]
+    last = rows_ref[rows_ref.shape[0] - HALO :, :]
+    total = jnp.zeros((HALO, width), F32)
+    for piece in range(last.shape[1] // width):
+        part = last[:, piece * width : (piece + 1) * width]
+        total += jnp.dot(pick_rows(HALO - 2, 2 * piece), part, preferred_element_type=F32)
+    pack_ref[...] = total.astype(BF16)
+    done_ref[...] = jnp.zeros_like(done_ref)
+
+
+def unpack_halo(pieces, count):
+    parts = [
+        jnp.dot(pick_rows(2 * piece, HALO - 2), pieces, preferred_element_type=F32).astype(BF16)
+        for piece in range(count)
+    ]
+    return jnp.concatenate(parts, axis=1)
+
+
+def choose_body(rows_ref, hop_ref, order_ref, send_ref):
+    core = lax.axis_index("chan")
+    count = send_ref.shape[0]
+    lines = pl.ds(pl.multiple_of(core * count, count), count)
+    here = core != lax.axis_index("fsdp")
+    send_ref[...] = jnp.where(here, rows_ref[lines, :], hop_ref[lines, :])
+
+
+def load_body(weight_ref, order_ref, weight_out, sems):
+    copies = [
+        pltpu.make_async_copy(weight_ref.at[branch], weight_out.at[branch], sems.at[branch])
+        for branch in range(3)
+    ]
+    for copy in copies:
+        copy.start()
+    for copy in copies:
+        copy.wait()
+
+
+def project(rows, weight_ref, own_half, keep_ref, send_ref):
     half = keep_ref.shape[1] // 3
     for branch in range(3):
         summed = jnp.dot(rows, weight_ref[branch], preferred_element_type=F32)
@@ -172,33 +215,77 @@
         send_ref[:, branch * half : (branch + 1) * half] = send.astype(BF16)
 
 
-def project_first_body(rows_ref, hop_ref, halo_ref, halo_hop_ref, weight_ref, keep_ref, send_ref):
+def project_first_body(
+    rows_ref, hop_ref, pack_ref, pack_hop_ref, weight_ref, keep_ref, send_ref, done_ref
+):
     own_half = lax.axis_index("fsdp")
     here = lax.axis_index("chan") == own_half
+    pieces = rows_ref.shape[1] // pack_ref.shape[1]
     rows = jnp.where(here, rows_ref[...], hop_ref[...])
-    halo = jnp.where(here, halo_ref[...], halo_hop_ref[...])
+    halo = unpack_halo(jnp.where(here, pack_ref[...], pack_hop_ref[...]), pieces)
+    halo = jnp.where(lax.axis_index("seq") > 0, halo, jnp.zeros_like(halo))
     rows = jnp.concatenate([halo, rows], axis=0)
-    half = keep_ref.shape[1] // 3
-    for branch in range(3):
-        summed = jnp.dot(rows, weight_ref[branch], preferred_element_type=F32)
-        keep, send = split_channels(summed, own_half)
-        keep_ref[:, branch * half : (branch + 1) * half] = keep
-        send_ref[:, branch * half : (branch + 1) * half] = send.astype(BF16)
-
-
-def taps_body(table_ref, *refs):
-    tap_refs = refs[:4]
-    real_ref, imag_ref, ordered = refs[4:]
+    project(rows, weight_ref, own_half, keep_ref, send_ref)
+    done_ref[...] = jnp.zeros_like(done_ref)
+
+
+def project_second_body(got_ref, hop_ref, weight_ref, keep_ref, send_ref, done_ref):
+    own_half = lax.axis_index("fsdp")
+    first = lax.axis_index("chan") == 0
+    got, hop = (got_ref[...], hop_ref[...])
+    rows = jnp.concatenate([jnp.where(first, got, hop), jnp.where(first, hop, got)], axis=0)
+    project(rows, weight_ref, own_half, keep_ref, send_ref)
+    done_ref[...] = jnp.zeros_like(done_ref)
+
+
+def pair_taps_body(own_ref, got_ref, *refs):
+    pair_ref = refs[-1]
+    pair_ref[0] = own_ref[...]
+    pair_ref[1] = got_ref[...]
+
+
+def sort_taps_body(pair_ref, far_ref, *refs):
+    keep_ref, send_ref, done_ref = refs[-3:]
     position = lax.axis_index("seq")
-    blocks = len(tap_refs)
+    first = lax.axis_index("fsdp") == 0
+    blocks, rows, half = keep_ref.shape
+    for step in range(blocks):
+        block = lax.rem(position - step + blocks, blocks)
+        taps = (pair_ref if step < 2 else far_ref)[step % 2]
+        low, high = (taps[:, :half], taps[:, half:])
+        keep_ref[block] = jnp.where(first, low, high)
+        send_ref[block] = jnp.where(first, high, low)
+    done_ref[...] = jnp.zeros_like(done_ref)
+
+
+def after_body(*refs):
+    pass
+
+
+def after(value, *orders):
+    return pl.pallas_call(
+        after_body,
+        in_specs=whole_specs(1 + len(orders)),
+        out_specs=whole_specs(1)[0],
+        out_shape=shape(value.shape, value.dtype),
+        input_output_aliases={0: 0},
+        compiler_params=pltpu.CompilerParams(vmem_limit_bytes=32 * 1024 * 1024),
+    )(value, *orders)
+
+
+def taps_body(table_ref, keep_ref, got_ref, real_ref, imag_ref):
+    first = lax.axis_index("fsdp") == 0
+    blocks = keep_ref.shape[0]
     size = table_ref.shape[1]
-    for step in range(blocks):
-        ordered[lax.rem(position - step + blocks, blocks)] = tap_refs[step][...]
     sign = 1.0 - 2.0 * (lax.broadcasted_iota(jnp.int32, (size, 1), 0) % 2).astype(F32)
     sign = sign * (1.0 / size)
     before_real = before_imag = None
     for block in range(blocks):
-        waves = jnp.dot(table_ref[...], ordered[block], preferred_element_type=F32)
+        keep, got = (keep_ref[block], got_ref[block])
+        taps = jnp.concatenate(
+            [jnp.where(first, keep, got), jnp.where(first, got, keep)], axis=0
+        )
+        waves = jnp.dot(table_ref[...], taps, preferred_element_type=F32)
         real, imag = (waves[:size], -waves[size:])
         if block == 0:
             real_ref[block] = real * (1.0 / size)
@@ -209,22 +296,25 @@
         before_real, before_imag = (real, imag)
 
 
-def mix_body(keep_first, keep_second, got_first, got_second, short_ref, product_ref, query_ref, joined):
+def mix_body(keep_first, keep_second, got_first, got_second, short_ref, *refs):
+    product_ref, query_ref, joined = refs[-3:]
     own = lax.axis_index("fsdp")
-    rows = keep_second.shape[0]
-    half = keep_second.shape[1] // 3
+    rows = got_second.shape[0]
+    half = got_second.shape[1] // 3
     joined[:HALO, :] = keep_first[:HALO, :] + got_first[:HALO, :].astype(F32)
     own_start = pl.multiple_of(HALO + own * rows, HALO)
     other_start = pl.multiple_of(HALO + (1 - own) * rows, HALO)
-    joined[pl.ds(own_start, rows), :] = keep_first[HALO:, :] + got_second[...].astype(F32)
-    joined[pl.ds(other_start, rows), :] = keep_second[...] + got_first[HALO:, :].astype(F32)
+    joined[pl.ds(own_start, rows), :] = keep_first[HALO:, :] + got_second[:, :].astype(F32)
+    joined[pl.ds(other_start, rows), :] = keep_second[:, :] + got_first[HALO:, :].astype(F32)
     count = 2 * rows
     mixed = []
     for branch in range(3):
         lanes = slice(branch * half, (branch + 1) * half)
         total = None
         for tap in range(3):
-            term = short_ref[tap, branch][None, :] * joined[pl.ds(HALO - tap, count), lanes]
+            taps = short_ref[tap, branch : branch + 1, :]
+            taps = jnp.where(own == 0, taps[:, :half], taps[:, half:])
+            term = taps * joined[pl.ds(HALO - tap, count), lanes]
             total = term if total is None else total + term
         mixed.append(total)
     query_ref[...] = mixed[0]
@@ -249,7 +339,9 @@
         total_imag = term_imag if total_imag is None else total_imag + term_imag
     stacked = jnp.concatenate([total_real, -total_imag], axis=0).astype(BF16)
     conv = jnp.dot(turned_ref[...], stacked, preferred_element_type=F32)
-    gated = query_ref[...] * (conv + gain_ref[...] * own_ref[...].astype(F32))
+    half = own_ref.shape[1]
+    gain = jnp.where(own == 0, gain_ref[:, :half], gain_ref[:, half:])
+    gated = query_ref[...] * (conv + gain * own_ref[...].astype(F32))
     result[...] = gated.astype(BF16)
     rows = stay_ref.shape[0]
     stay_ref[...] = result[pl.ds(pl.multiple_of(own * rows, rows), rows), :]
@@ -274,80 +366,112 @@
     half = width // 2
     size = 2 * rows
     blocks = lax.axis_size("seq")
-    fsdp = lax.axis_index("fsdp")
     weight = jnp.transpose(proj_weight, (1, 0, 2))
+    ring = [[(s, (s + step) % blocks) for s in range(blocks)] for step in range(blocks)]
     call = functools.partial(
         pl.pallas_call, compiler_params=pltpu.CompilerParams(vmem_limit_bytes=32 * 1024 * 1024)
     )
 
-    got = lax.ppermute(tokens, ("fsdp", "chan"), [(1, 3), (2, 0)])
     own_hop = exchange(tokens, "chan")
-    halo = lax.ppermute(
-        tokens[rows - HALO :],
+    token = shape((8, 128), F32)
+    pack, pack_done = call(
+        pack_body,
+        in_specs=whole_specs(1),
+        out_specs=whole_specs(2),
+        out_shape=(shape((HALO, width), BF16), token),
+    )(tokens)
+    token_send = call(
+        choose_body,
+        in_specs=whole_specs(3),
+        out_specs=whole_specs(1)[0],
+        out_shape=shape((rows // 2, features), BF16),
+    )(tokens, own_hop, pack_done)
+    got = exchange(token_send, "fsdp")
+    tap_near = lax.ppermute(filter_taps, "seq", ring[1])
+    weight = pl.pallas_call(
+        load_body,
+        in_specs=[pl.BlockSpec(memory_space=pltpu.HBM), *whole_specs(1)],
+        out_specs=whole_specs(1)[0],
+        out_shape=shape(weight.shape, BF16),
+        scratch_shapes=[pltpu.SemaphoreType.DMA((3,))],
+        compiler_params=pltpu.CompilerParams(vmem_limit_bytes=LOAD_MIB * 1024 * 1024),
+    )(weight, pack_done)
+    pack_got = lax.ppermute(
+        pack,
         ("seq", "fsdp", "chan"),
-        [(4 * s + 2 + c, 4 * (s + 1) + 2 * c + c) for s in range(blocks - 1) for c in range(2)],
-    )
-    halo_hop = exchange(halo, "chan")
-
-    keep_first, send_first = call(
+        [
+            (4 * s + 2 * f + c, 4 * ((s + 1) % blocks) + 2 * (f ^ (1 - c)) + c)
+            for s in range(blocks)
+            for f in range(2)
+            for c in range(2)
+        ],
+    )
+    tap_pair = call(
+        pair_taps_body,
+        in_specs=whole_specs(2),
+        out_specs=whole_specs(1)[0],
+        out_shape=shape((2, rows, width), BF16),
+    )(filter_taps, tap_near)
+    pack_got = after(pack_got, weight)
+    pack_hop = exchange(pack_got, "chan")
+    keep_first, send_first, first_done = call(
         project_first_body,
         in_specs=whole_specs(5),
-        out_specs=whole_specs(2),
-        out_shape=(shape((HALO + rows, 3 * half), F32), shape((HALO + rows, 3 * half), BF16)),
-    )(tokens, own_hop, halo, halo_hop, weight)
-
+        out_specs=whole_specs(3),
+        out_shape=(
+            shape((HALO + rows, 3 * half), F32),
+            shape((HALO + rows, 3 * half), BF16),
+            token,
+        ),
+    )(tokens, own_hop, pack_got, pack_hop, weight)
+    got = after(got, first_done, tap_pair)
+    got_hop = exchange(got, "chan")
+    got_first = exchange(send_first, "fsdp")
+    keep_second, send_second, second_done = call(
+        project_second_body,
+        in_specs=whole_specs(3),
+        out_specs=whole_specs(3),
+        out_shape=(shape((rows, 3 * half), F32), shape((rows, 3 * half), BF16), token),
+    )(got, got_hop, weight)
+    got_second = exchange(send_second, "fsdp")
+    tap_far = lax.ppermute(tap_pair, "seq", ring[2])
+
+    tap_keep, tap_send, tap_done = call(
+        sort_taps_body,
+        in_specs=whole_specs(2 + 1),
+        out_specs=whole_specs(3),
+        out_shape=(
+            shape((blocks, rows, half), BF16),
+            shape((blocks, rows, half), BF16),
+            token,
+        ),
+    )(tap_pair, tap_far, second_done)
+    tap_got = exchange(tap_send, "fsdp")
     table = wave_table(size)
     forward = jnp.asarray(table, dtype=BF16)
     inverse = jnp.asarray(table.T, dtype=BF16)
-    tap_low, tap_high = (filter_taps[:, :half], filter_taps[:, half:])
-    first = fsdp == 0
-    tap_keep = jnp.where(first, tap_low, tap_high)
-    tap_got = exchange(jnp.where(first, tap_high, tap_low), "fsdp")
-    taps = jnp.where(
-        first,
-        jnp.concatenate([tap_keep, tap_got], axis=0),
-        jnp.concatenate([tap_got, tap_keep], axis=0),
-    )
-    ring = [
-        [(s, (s + step) % blocks) for s in range(blocks)] for step in range(blocks)
-    ]
-    tap_blocks = [taps] + [lax.ppermute(taps, "seq", ring[step]) for step in range(1, blocks)]
-    tap_real, tap_imag = call(
-        taps_body,
-        in_specs=whole_specs(1 + blocks),
-        out_specs=whole_specs(2),
-        out_shape=(shape((blocks, size, half), F32), shape((blocks, size, half), F32)),
-        scratch_shapes=[pltpu.VMEM((blocks, size, half), BF16)],
-    )(forward, *tap_blocks)
-
-    got_first = exchange(send_first, "fsdp")
-    got_hop = exchange(got, "chan")
-    keep_second, send_second = call(
-        project_body,
-        in_specs=whole_specs(3),
-        out_specs=whole_specs(2),
-        out_shape=(shape((rows, 3 * half), F32), shape((rows, 3 * half), BF16)),
-    )(got, got_hop, weight)
-    got_second = exchange(send_second, "fsdp")
-
-    short_half = lax.dynamic_slice_in_dim(short_weight, fsdp * half, half, axis=2)
-    gain_half = lax.dynamic_slice_in_dim(skip_gain, fsdp * half, half, axis=0)[None, :]
     product, query = call(
         mix_body,
-        in_specs=whole_specs(5),
+        in_specs=whole_specs(6),
         out_specs=whole_specs(2),
         out_shape=(shape((size, half), BF16), shape((size, half), F32)),
         scratch_shapes=[pltpu.VMEM((HALO + size, 3 * half), F32)],
-    )(keep_first, keep_second, got_first, got_second, short_half)
+    )(keep_first, keep_second, got_first, got_second, short_weight, tap_done)
 
     products = [product] + [lax.ppermute(product, "seq", ring[step]) for step in range(1, blocks)]
+    tap_real, tap_imag = call(
+        taps_body,
+        in_specs=whole_specs(3),
+        out_specs=whole_specs(2),
+        out_shape=(shape((blocks, size, half), F32), shape((blocks, size, half), F32)),
+    )(forward, tap_keep, tap_got)
     stay, go = call(
         conv_body,
         in_specs=whole_specs(10),
         out_specs=whole_specs(2),
         out_shape=(shape((rows, half), BF16), shape((rows, half), BF16)),
         scratch_shapes=[pltpu.VMEM((size, half), BF16)],
-    )(*products, tap_real, tap_imag, forward, inverse, query, gain_half)
+    )(*products, tap_real, tap_imag, forward, inverse, query, skip_gain.reshape(1, width))
     back = exchange(go, "fsdp")
     return call(
         join_body,

time: 48.1 us -> 38.8 us (0.81)
  starting transfers between devices: 25.2 us -> 13.8 us
  waiting for transfers between devices: 14.4 us -> 18.2 us
  local copies, waits for them, and re-layouts: 3.88 us -> 1.08 us
  Pallas kernels: 3.31 us -> 5.45 us
  other arithmetic: 0.8 us -> 0 us
    ppermute x7 -> x8, starting transfers between devices: 13.2 us -> 7 us  [exchange(): return lax.ppermute(value, axis, [(0, 1), (1, 0)])]
    ppermute x5 -> x3, starting transfers between devices: 7.63 us -> 4.03 us  [the longest x1 1.58 us: pair_mesh(): tap_near = lax.ppermute(filter_taps, 'seq', ring[1])]
    ppermute x7 -> x8, waiting for transfers between devices: 4.65 us -> 6.9 us  [exchange(): return lax.ppermute(value, axis, [(0, 1), (1, 0)])]
    pallas_call x4 -> x11, Pallas kernels: 1.96 us -> 4.1 us  [the longest x1 1.88 us: pair_mesh(): pl.pallas_call(load_body, in_specs=[pl.BlockSpec(memory_space=pltpu.HBM),...]
    unnamed x14, local copies, waits for them, and re-layouts: 2.96 us -> 1.08 us
    ppermute x3, starting transfers between devices: 4.4 us -> 2.81 us  [pair_mesh(): lax.ppermute(product, 'seq', ring[step])]
    ppermute x5 -> x3, waiting for transfers between devices: 7.09 us -> 8.08 us  [the longest x1 5.19 us: pair_mesh(): tap_far = lax.ppermute(tap_pair, 'seq', ring[2])]
    slice x1 -> x0, local copies, waits for them, and re-layouts: 0.84 us -> none  [pair_mesh(): tokens[rows - HALO:]]
  transfers between devices with their start and end apart: 15 -> 14, of which waited for: 5 -> 8; matrix products, arithmetic and copies ran while one was open for 4% -> 0% of each run, Pallas kernels for 4% -> 10%
where the time goes in v2:
time: 38.8 us; the launch traced here: 38.7 us
  waiting for transfers between devices  18.2 us (47%)
  starting transfers between devices  13.8 us (36%)
  Pallas kernels  5.45 us (14%)
  local copies, waits for them, and re-layouts  1.08 us (3%)
    ppermute x8, starting transfers between devices, exchange(): return lax.ppermute(value, axis, [(0, 1), (1, 0)])  7 us
    ppermute x8, waiting for transfers between devices, exchange(): return lax.ppermute(value, axis, [(0, 1), (1, 0)])  6.9 us
    ppermute x1, waiting for transfers between devices, pair_mesh(): tap_far = lax.ppermute(tap_pair, 'seq', ring[2])  5.19 us
    ppermute x3, waiting for transfers between devices, pair_mesh(): lax.ppermute(product, 'seq', ring[step])  3.19 us
    ppermute x1, waiting for transfers between devices, pair_mesh(): lax.ppermute(pack, ('seq', 'fsdp', 'chan'), [(4 * s + 2 * f + c, 4 * ((s...  2.89 us
    ppermute x3, starting transfers between devices, pair_mesh(): lax.ppermute(product, 'seq', ring[step])  2.81 us
    pallas_call x1, Pallas kernels, pair_mesh(): pl.pallas_call(load_body, in_specs=[pl.BlockSpec(memory_space=pltpu.HBM),...  1.88 us
    ppermute x1, starting transfers between devices, pair_mesh(): tap_near = lax.ppermute(filter_taps, 'seq', ring[1])  1.58 us
  transfers between devices with their start and end apart: 14, of which 8 were waited for; matrix products, arithmetic and copies ran while one was open for 0% of the time, Pallas kernels for 10%

profile of v2, /device:TPU:0, one launch (start us, length us, event | category | flops | bytes accessed | tf_op | source)
XLA Modules:
  0.0 38.7 jit_solution(7917803393184279425)
XLA Ops:
  0.0 0.5 %collective-permute-start = (bf16[128,2048]{1,0:T(8,128)(2,1)}, bf16[128,2048]{1,0:T(8,128)(2,1)S(1)}, u32[]{:S(2)}, u32[]{:S(2)}) collective-permute-start(bf16[128,2048]{1,0:T(8,128)(2,1)} %rows_ref.5), channel_id=1, source_target_pairs={{0,1},{1,0},{2,3},{3,2},{4,5},{5,4},{6,7},{7,6},{8,9},{9,8},{10,11... | collective-permute-start | bytes 1572872 | tf_op jit(solution)/shard_map/ppermute | solution.py:150
  0.5 1.0 %copy-done = bf16[128,2048]{1,0:T(8,128)(2,1)S(1)} copy-done((bf16[128,2048]{1,0:T(8,128)(2,1)S(1)}, bf16[128,2048]{1,0:T(8,128)(2,1)}, u32[]{:S(2)}) %copy-start) | copy-done | bytes 524312
  1.5 0.1 shard_map.73
  1.6 0.6 %collective-permute-done.hop_ref = bf16[128,2048]{1,0:T(8,128)(2,1)S(1)} collective-permute-done((bf16[128,2048]{1,0:T(8,128)(2,1)}, bf16[128,2048]{1,0:T(8,128)(2,1)S(1)}, u32[]{:S(2)}, u32[]{:S(2)}) %collective-permute-start) | collective-permute-done | bytes 524320 | tf_op jit(solution)/shard_map/ppermute | solution.py:150
  2.2 2.9 %collective-permute-start.3 = (bf16[64,2048]{1,0:T(8,128)(2,1)S(1)}, bf16[64,2048]{1,0:T(8,128)(2,1)S(1)}, u32[]{:S(2)}, u32[]{:S(2)}) collective-permute-start(bf16[64,2048]{1,0:T(8,128)(2,1)S(1)} %shard_map.77), channel_id=1, source_target_pairs={{0,2},{2,0},{1,3},{3,1},{4,6},{6,4},{5,7},{7,5},{8,10},{10,8},{9,1... | collective-permute-start | bytes 786440 | tf_op jit(solution)/shard_map/ppermute | solution.py:150
  5.2 1.6 %collective-permute-start.4 = (bf16[128,256]{1,0:T(8,128)(2,1)}, bf16[128,256]{1,0:T(8,128)(2,1)S(1)}, u32[]{:S(2)}, u32[]{:S(2)}) collective-permute-start(bf16[128,256]{1,0:T(8,128)(2,1)} %own_ref.1), channel_id=1, source_target_pairs={{0,4},{4,8},{8,12},{12,0},{1,5},{5,9},{9,13},{13,1},{2,6},{6,10},{... | collective-permute-start | bytes 196616 | tf_op jit(solution)/shard_map/ppermute | solution.py:390
  6.7 1.5 %collective-permute-start.1 = (bf16[16,256]{1,0:T(8,128)(2,1)S(1)}, bf16[16,256]{1,0:T(8,128)(2,1)S(1)}, u32[]{:S(2)}, u32[]{:S(2)}) collective-permute-start(bf16[16,256]{1,0:T(8,128)(2,1)S(1)} %get-tuple-element.22), channel_id=1, source_target_pairs={{0,6},{1,5},{2,4},{3,7},{4,10},{5,9},{6,8},{7,11},{8,14},{9,13},{1... | collective-permute-start | bytes 24584 | tf_op jit(solution)/shard_map/ppermute | solution.py:399
  8.3 1.9 %shard_map.74.refs_1_.weight_ref = bf16[3,2048,256]{2,1,0:T(8,128)(2,1)S(1)} custom-call(bf16[3,2048,256]{2,1,0:T(8,128)(2,1)} %bitcast.3, f32[8,128]{1,0:T(8,128)S(1)} %get-tuple-element.23.order_ref), custom_call_target="tpu_custom_call" | custom-call | tf_op jit(solution)/shard_map/pallas_call | solution.py:391
  10.2 2.9 %collective-permute-done.1.refs_0_ = bf16[16,256]{1,0:T(8,128)(2,1)S(1)} collective-permute-done((bf16[16,256]{1,0:T(8,128)(2,1)S(1)}, bf16[16,256]{1,0:T(8,128)(2,1)S(1)}, u32[]{:S(2)}, u32[]{:S(2)}) %collective-permute-start.1) | collective-permute-done | bytes 8224 | tf_op jit(solution)/shard_map/ppermute | solution.py:399
  13.1 1.1 %collective-permute-done.2.pack_hop_ref = bf16[16,256]{1,0:T(8,128)(2,1)S(1)} collective-permute-done((bf16[16,256]{1,0:T(8,128)(2,1)S(1)}, bf16[16,256]{1,0:T(8,128)(2,1)S(1)}, u32[]{:S(2)}, u32[]{:S(2)}) %collective-permute-start.2) | collective-permute-done | bytes 8224 | tf_op jit(solution)/shard_map/ppermute | solution.py:150
  14.3 0.8 %shard_map.76 = (f32[144,384]{1,0:T(8,128)S(1)}, bf16[144,384]{1,0:T(8,128)(2,1)S(1)}, f32[8,128]{1,0:T(8,128)S(1)}) custom-call(bf16[128,2048]{1,0:T(8,128)(2,1)S(1)} %copy-done.1, bf16[128,2048]{1,0:T(8,128)(2,1)S(1)} %collective-permute-done.hop_ref, bf16[16,256]{1,0:T(8,128)(2,1)S(1)} %shard_map.75.pack_ref, ...), custom_call_target="tpu_custom_call" | custom-call | tf_op jit(solution)/shard_map/pallas_call | solution.py:417
  15.0 0.0 copy-start.2
  15.1 0.2 collective-permute-start.5
  15.3 0.9 %collective-permute-start.8 = (bf16[2,128,256]{2,1,0:T(8,128)(2,1)S(1)}, bf16[2,128,256]{2,1,0:T(8,128)(2,1)S(1)}, u32[]{:S(2)}, u32[]{:S(2)}) collective-permute-start(bf16[2,128,256]{2,1,0:T(8,128)(2,1)S(1)} %shard_map.78.refs_2_.pair_ref), channel_id=1, source_target_pairs={{0,8},{4,12},{8,0},{12,4},{1,9},{5,13},{9,1},{13,5},{2,10},{6,14},... | collective-permute-start | bytes 393224 | tf_op jit(solution)/shard_map/ppermute | solution.py:437
  16.2 0.5 %collective-permute-start.6 = (bf16[144,384]{1,0:T(8,128)(2,1)S(1)}, bf16[144,384]{1,0:T(8,128)(2,1)S(1)}, u32[]{:S(2)}, u32[]{:S(2)}) collective-permute-start(bf16[144,384]{1,0:T(8,128)(2,1)S(1)} %get-tuple-element.27), channel_id=1, source_target_pairs={{0,2},{2,0},{1,3},{3,1},{4,6},{6,4},{5,7},{7,5},{8,10},{10,8},{9,1... | collective-permute-start | bytes 331784 | tf_op jit(solution)/shard_map/ppermute | solution.py:150
  16.8 0.6 %shard_map.80 = (f32[128,384]{1,0:T(8,128)S(1)}, bf16[128,384]{1,0:T(8,128)(2,1)S(1)}, f32[8,128]{1,0:T(8,128)S(1)}) custom-call(bf16[64,2048]{1,0:T(8,128)(2,1)S(1)} %shard_map.79.got_ref, bf16[64,2048]{1,0:T(8,128)(2,1)S(1)} %collective-permute-done.5.hop_ref, bf16[3,2048,256]{2,1,0:T(8,128)(2,1)S(1)} %shard_map.74.refs_1_.weight_ref), custom_call_target="tpu_custom_call" | custom-call | tf_op jit(solution)/shard_map/pallas_call | solution.py:430
  17.4 1.6 %collective-permute-start.7 = (bf16[128,384]{1,0:T(8,128)(2,1)S(1)}, bf16[128,384]{1,0:T(8,128)(2,1)S(1)}, u32[]{:S(2)}, u32[]{:S(2)}) collective-permute-start(bf16[128,384]{1,0:T(8,128)(2,1)S(1)} %get-tuple-element.28), channel_id=1, source_target_pairs={{0,2},{2,0},{1,3},{3,1},{4,6},{6,4},{5,7},{7,5},{8,10},{10,8},{9,1... | collective-permute-start | bytes 294920 | tf_op jit(solution)/shard_map/ppermute | solution.py:150
  18.9 5.2 %collective-permute-done.8.far_ref = bf16[2,128,256]{2,1,0:T(8,128)(2,1)S(1)} collective-permute-done((bf16[2,128,256]{2,1,0:T(8,128)(2,1)S(1)}, bf16[2,128,256]{2,1,0:T(8,128)(2,1)S(1)}, u32[]{:S(2)}, u32[]{:S(2)}) %collective-permute-start.8) | collective-permute-done | bytes 131104 | tf_op jit(solution)/shard_map/ppermute | solution.py:437
  24.1 0.1 shard_map.81
  24.2 0.6 %collective-permute-start.12 = (bf16[4,128,128]{2,1,0:T(8,128)(2,1)S(1)}, bf16[4,128,128]{2,1,0:T(8,128)(2,1)S(1)}, u32[]{:S(2)}, u32[]{:S(2)}) collective-permute-start(bf16[4,128,128]{2,1,0:T(8,128)(2,1)S(1)} %get-tuple-element.33), channel_id=1, source_target_pairs={{0,2},{2,0},{1,3},{3,1},{4,6},{6,4},{5,7},{7,5},{8,10},{10,8},{9,1... | collective-permute-start | bytes 393224 | tf_op jit(solution)/shard_map/ppermute | solution.py:150
  24.8 0.2 shard_map.82
  25.0 0.7 %collective-permute-start.10 = (bf16[256,128]{1,0:T(8,128)(2,1)S(1)}, bf16[256,128]{1,0:T(8,128)(2,1)S(1)}, u32[]{:S(2)}, u32[]{:S(2)}) collective-permute-start(bf16[256,128]{1,0:T(8,128)(2,1)S(1)} %get-tuple-element.31.own_ref), channel_id=1, source_target_pairs={{0,8},{4,12},{8,0},{12,4},{1,9},{5,13},{9,1},{13,5},{2,10},{6,14},... | collective-permute-start | bytes 196616 | tf_op jit(solution)/shard_map/ppermute | solution.py:461
  25.7 1.6 %collective-permute-start.11 = (bf16[256,128]{1,0:T(8,128)(2,1)S(1)}, bf16[256,128]{1,0:T(8,128)(2,1)S(1)}, u32[]{:S(2)}, u32[]{:S(2)}) collective-permute-start(bf16[256,128]{1,0:T(8,128)(2,1)S(1)} %get-tuple-element.31.own_ref), channel_id=1, source_target_pairs={{0,12},{4,0},{8,4},{12,8},{1,13},{5,1},{9,5},{13,9},{2,14},{6,2},{... | collective-permute-start | bytes 196616 | tf_op jit(solution)/shard_map/ppermute | solution.py:461
  27.3 0.5 %collective-permute-start.9 = (bf16[256,128]{1,0:T(8,128)(2,1)S(1)}, bf16[256,128]{1,0:T(8,128)(2,1)S(1)}, u32[]{:S(2)}, u32[]{:S(2)}) collective-permute-start(bf16[256,128]{1,0:T(8,128)(2,1)S(1)} %get-tuple-element.31.own_ref), channel_id=1, source_target_pairs={{0,4},{4,8},{8,12},{12,0},{1,5},{5,9},{9,13},{13,1},{2,6},{6,10},{... | collective-permute-start | bytes 196616 | tf_op jit(solution)/shard_map/ppermute | solution.py:461
  27.8 1.9 %collective-permute-done.12.got_ref = bf16[4,128,128]{2,1,0:T(8,128)(2,1)S(1)} collective-permute-done((bf16[4,128,128]{2,1,0:T(8,128)(2,1)S(1)}, bf16[4,128,128]{2,1,0:T(8,128)(2,1)S(1)}, u32[]{:S(2)}, u32[]{:S(2)}) %collective-permute-start.12) | collective-permute-done | bytes 131104 | tf_op jit(solution)/shard_map/ppermute | solution.py:150
  29.7 0.5 %shard_map.83 = (f32[4,256,128]{2,1,0:T(8,128)S(1)}, f32[4,256,128]{2,1,0:T(8,128)S(1)}) custom-call(bf16[512,256]{1,0:T(8,128)(2,1)S(1)} %copy-done.2, bf16[4,128,128]{2,1,0:T(8,128)(2,1)S(1)} %get-tuple-element.32.keep_ref, bf16[4,128,128]{2,1,0:T(8,128)(2,1)S(1)} %collective-permute-done.12.got_ref), custom_call_target="tpu_custom_call" | custom-call | tf_op jit(solution)/shard_map/pallas_call | solution.py:462
  30.2 0.8 %collective-permute-done.10.two_ref = bf16[256,128]{1,0:T(8,128)(2,1)S(1)} collective-permute-done((bf16[256,128]{1,0:T(8,128)(2,1)S(1)}, bf16[256,128]{1,0:T(8,128)(2,1)S(1)}, u32[]{:S(2)}, u32[]{:S(2)}) %collective-permute-start.10) | collective-permute-done | bytes 65568 | tf_op jit(solution)/shard_map/ppermute | solution.py:461
  31.0 2.3 %collective-permute-done.9.one_ref = bf16[256,128]{1,0:T(8,128)(2,1)S(1)} collective-permute-done((bf16[256,128]{1,0:T(8,128)(2,1)S(1)}, bf16[256,128]{1,0:T(8,128)(2,1)S(1)}, u32[]{:S(2)}, u32[]{:S(2)}) %collective-permute-start.9) | collective-permute-done | bytes 65568 | tf_op jit(solution)/shard_map/ppermute | solution.py:461
  33.4 0.7 %shard_map.84 = (bf16[128,128]{1,0:T(8,128)(2,1)S(1)}, bf16[128,128]{1,0:T(8,128)(2,1)S(1)}) custom-call(bf16[256,128]{1,0:T(8,128)(2,1)S(1)} %get-tuple-element.31.own_ref, bf16[256,128]{1,0:T(8,128)(2,1)S(1)} %collective-permute-done.9.one_ref, bf16[256,128]{1,0:T(8,128)(2,1)S(1)} %collective-permute-done.10.two_ref, ...), custom_call_target="tpu_custom_call" | custom-call | tf_op jit(solution)/shard_map/pallas_call | solution.py:468
  34.1 0.7 %collective-permute-start.13 = (bf16[128,128]{1,0:T(8,128)(2,1)S(1)}, bf16[128,128]{1,0:T(8,128)(2,1)S(1)}, u32[]{:S(2)}, u32[]{:S(2)}) collective-permute-start(bf16[128,128]{1,0:T(8,128)(2,1)S(1)} %get-tuple-element.38), channel_id=1, source_target_pairs={{0,2},{2,0},{1,3},{3,1},{4,6},{6,4},{5,7},{7,5},{8,10},{10,8},{9,1... | collective-permute-start | bytes 98312 | tf_op jit(solution)/shard_map/ppermute | solution.py:150
  34.8 3.3 %collective-permute-done.13.got_ref = bf16[128,128]{1,0:T(8,128)(2,1)S(1)} collective-permute-done((bf16[128,128]{1,0:T(8,128)(2,1)S(1)}, bf16[128,128]{1,0:T(8,128)(2,1)S(1)}, u32[]{:S(2)}, u32[]{:S(2)}) %collective-permute-start.13) | collective-permute-done | bytes 32800 | tf_op jit(solution)/shard_map/ppermute | solution.py:150
  38.0 0.6 %shard_map.85 = bf16[128,256]{1,0:T(8,128)(2,1)} custom-call(bf16[128,128]{1,0:T(8,128)(2,1)S(1)} %get-tuple-element.37.stay_ref, bf16[128,128]{1,0:T(8,128)(2,1)S(1)} %collective-permute-done.13.got_ref), custom_call_target="tpu_custom_call" | custom-call | tf_op jit(solution)/shard_map/pallas_call | solution.py:476
  (23 shorter events, 0.1 us)
Async XLA Ops:
  0.0 2.2 %collective-permute-start = (bf16[128,2048]{1,0:T(8,128)(2,1)}, bf16[128,2048]{1,0:T(8,128)(2,1)S(1)}, u32[]{:S(2)}, u32[]{:S(2)}) collective-permute-start(bf16[128,2048]{1,0:T(8,128)(2,1)} %rows_ref.5), channel_id=1, source_target_pairs={{0,1},{1,0},{2,3},{3,2},{4,5},{5,4},{6,7},{7,6},{8,9},{9,8},{10,11... | collective-permute-start | bytes 1572872 | tf_op jit(solution)/shard_map/ppermute | solution.py:150
  0.5 1.0 %copy-start = (bf16[128,2048]{1,0:T(8,128)(2,1)S(1)}, bf16[128,2048]{1,0:T(8,128)(2,1)}, u32[]{:S(2)}) copy-start(bf16[128,2048]{1,0:T(8,128)(2,1)} %rows_ref.5) | copy-start | bytes 1572868
  2.2 12.8 %collective-permute-start.3 = (bf16[64,2048]{1,0:T(8,128)(2,1)S(1)}, bf16[64,2048]{1,0:T(8,128)(2,1)S(1)}, u32[]{:S(2)}, u32[]{:S(2)}) collective-permute-start(bf16[64,2048]{1,0:T(8,128)(2,1)S(1)} %shard_map.77), channel_id=1, source_target_pairs={{0,2},{2,0},{1,3},{3,1},{4,6},{6,4},{5,7},{7,5},{8,10},{10,8},{9,1... | collective-permute-start | bytes 786440 | tf_op jit(solution)/shard_map/ppermute | solution.py:150
  5.2 7.9 %collective-permute-start.4 = (bf16[128,256]{1,0:T(8,128)(2,1)}, bf16[128,256]{1,0:T(8,128)(2,1)S(1)}, u32[]{:S(2)}, u32[]{:S(2)}) collective-permute-start(bf16[128,256]{1,0:T(8,128)(2,1)} %own_ref.1), channel_id=1, source_target_pairs={{0,4},{4,8},{8,12},{12,0},{1,5},{5,9},{9,13},{13,1},{2,6},{6,10},{... | collective-permute-start | bytes 196616 | tf_op jit(solution)/shard_map/ppermute | solution.py:390
  6.7 6.3 %collective-permute-start.1 = (bf16[16,256]{1,0:T(8,128)(2,1)S(1)}, bf16[16,256]{1,0:T(8,128)(2,1)S(1)}, u32[]{:S(2)}, u32[]{:S(2)}) collective-permute-start(bf16[16,256]{1,0:T(8,128)(2,1)S(1)} %get-tuple-element.22), channel_id=1, source_target_pairs={{0,6},{1,5},{2,4},{3,7},{4,10},{5,9},{6,8},{7,11},{8,14},{9,13},{1... | collective-permute-start | bytes 24584 | tf_op jit(solution)/shard_map/ppermute | solution.py:399
  10.2 2.9 %copy-start.4 = (bf16[128,256]{1,0:T(8,128)(2,1)S(1)}, bf16[128,256]{1,0:T(8,128)(2,1)}, u32[]{:S(2)}) copy-start(bf16[128,256]{1,0:T(8,128)(2,1)} %own_ref.1) | copy-start | bytes 196612
  10.2 4.1 %copy-start.1 = (bf16[128,2048]{1,0:T(8,128)(2,1)S(1)}, bf16[128,2048]{1,0:T(8,128)(2,1)}, u32[]{:S(2)}) copy-start(bf16[128,2048]{1,0:T(8,128)(2,1)} %rows_ref.5) | copy-start | bytes 1572868
  13.1 1.2 %collective-permute-start.2 = (bf16[16,256]{1,0:T(8,128)(2,1)S(1)}, bf16[16,256]{1,0:T(8,128)(2,1)S(1)}, u32[]{:S(2)}, u32[]{:S(2)}) collective-permute-start(bf16[16,256]{1,0:T(8,128)(2,1)S(1)} %shard_map.75.pack_ref), channel_id=1, source_target_pairs={{0,1},{1,0},{2,3},{3,2},{4,5},{5,4},{6,7},{7,6},{8,9},{9,8},{10,11... | collective-permute-start | bytes 24584 | tf_op jit(solution)/shard_map/ppermute | solution.py:150
  15.0 9.7 %copy-start.5 = (f32[3,3,256]{2,1,0:T(4,128)S(1)}, f32[3,3,256]{2,1,0:T(4,128)}, u32[]{:S(2)}) copy-start(f32[3,3,256]{2,1,0:T(4,128)} %short_ref.1) | copy-start | bytes 27652
  15.0 14.7 %copy-start.2 = (bf16[512,256]{1,0:T(8,128)(2,1)S(1)}, bf16[512,256]{1,0:T(8,128)(2,1)}, u32[]{:S(2)}) copy-start(bf16[512,256]{1,0:T(8,128)(2,1)} %constant.4.clone.table_ref) | copy-start | bytes 786436
  15.1 18.3 %copy-start.3 = (bf16[256,512]{1,0:T(8,128)(2,1)S(1)}, bf16[256,512]{1,0:T(8,128)(2,1)}, u32[]{:S(2)}) copy-start(bf16[256,512]{1,0:T(8,128)(2,1)} %constant.5.clone.turned_ref) | copy-start | bytes 786436
  15.1 18.3 %copy-start.6 = (f32[256]{0:T(256)S(1)}, f32[256]{0:T(256)}, u32[]{:S(2)}) copy-start(f32[256]{0:T(256)} %param.10) | copy-start | bytes 3076
  15.1 1.7 %collective-permute-start.5 = (bf16[64,2048]{1,0:T(8,128)(2,1)S(1)}, bf16[64,2048]{1,0:T(8,128)(2,1)S(1)}, u32[]{:S(2)}, u32[]{:S(2)}) collective-permute-start(bf16[64,2048]{1,0:T(8,128)(2,1)S(1)} %shard_map.79.got_ref), channel_id=1, source_target_pairs={{0,1},{1,0},{2,3},{3,2},{4,5},{5,4},{6,7},{7,6},{8,9},{9,8},{10,11... | collective-permute-start | bytes 786440 | tf_op jit(solution)/shard_map/ppermute | solution.py:150
  15.3 8.8 %collective-permute-start.8 = (bf16[2,128,256]{2,1,0:T(8,128)(2,1)S(1)}, bf16[2,128,256]{2,1,0:T(8,128)(2,1)S(1)}, u32[]{:S(2)}, u32[]{:S(2)}) collective-permute-start(bf16[2,128,256]{2,1,0:T(8,128)(2,1)S(1)} %shard_map.78.refs_2_.pair_ref), channel_id=1, source_target_pairs={{0,8},{4,12},{8,0},{12,4},{1,9},{5,13},{9,1},{13,5},{2,10},{6,14},... | collective-permute-start | bytes 393224 | tf_op jit(solution)/shard_map/ppermute | solution.py:437
  16.2 8.5 %collective-permute-start.6 = (bf16[144,384]{1,0:T(8,128)(2,1)S(1)}, bf16[144,384]{1,0:T(8,128)(2,1)S(1)}, u32[]{:S(2)}, u32[]{:S(2)}) collective-permute-start(bf16[144,384]{1,0:T(8,128)(2,1)S(1)} %get-tuple-element.27), channel_id=1, source_target_pairs={{0,2},{2,0},{1,3},{3,1},{4,6},{6,4},{5,7},{7,5},{8,10},{10,8},{9,1... | collective-permute-start | bytes 331784 | tf_op jit(solution)/shard_map/ppermute | solution.py:150
  17.4 7.4 %collective-permute-start.7 = (bf16[128,384]{1,0:T(8,128)(2,1)S(1)}, bf16[128,384]{1,0:T(8,128)(2,1)S(1)}, u32[]{:S(2)}, u32[]{:S(2)}) collective-permute-start(bf16[128,384]{1,0:T(8,128)(2,1)S(1)} %get-tuple-element.28), channel_id=1, source_target_pairs={{0,2},{2,0},{1,3},{3,1},{4,6},{6,4},{5,7},{7,5},{8,10},{10,8},{9,1... | collective-permute-start | bytes 294920 | tf_op jit(solution)/shard_map/ppermute | solution.py:150
  24.2 5.5 %collective-permute-start.12 = (bf16[4,128,128]{2,1,0:T(8,128)(2,1)S(1)}, bf16[4,128,128]{2,1,0:T(8,128)(2,1)S(1)}, u32[]{:S(2)}, u32[]{:S(2)}) collective-permute-start(bf16[4,128,128]{2,1,0:T(8,128)(2,1)S(1)} %get-tuple-element.33), channel_id=1, source_target_pairs={{0,2},{2,0},{1,3},{3,1},{4,6},{6,4},{5,7},{7,5},{8,10},{10,8},{9,1... | collective-permute-start | bytes 393224 | tf_op jit(solution)/shard_map/ppermute | solution.py:150
  25.0 6.0 %collective-permute-start.10 = (bf16[256,128]{1,0:T(8,128)(2,1)S(1)}, bf16[256,128]{1,0:T(8,128)(2,1)S(1)}, u32[]{:S(2)}, u32[]{:S(2)}) collective-permute-start(bf16[256,128]{1,0:T(8,128)(2,1)S(1)} %get-tuple-element.31.own_ref), channel_id=1, source_target_pairs={{0,8},{4,12},{8,0},{12,4},{1,9},{5,13},{9,1},{13,5},{2,10},{6,14},... | collective-permute-start | bytes 196616 | tf_op jit(solution)/shard_map/ppermute | solution.py:461
  25.7 5.4 %collective-permute-start.11 = (bf16[256,128]{1,0:T(8,128)(2,1)S(1)}, bf16[256,128]{1,0:T(8,128)(2,1)S(1)}, u32[]{:S(2)}, u32[]{:S(2)}) collective-permute-start(bf16[256,128]{1,0:T(8,128)(2,1)S(1)} %get-tuple-element.31.own_ref), channel_id=1, source_target_pairs={{0,12},{4,0},{8,4},{12,8},{1,13},{5,1},{9,5},{13,9},{2,14},{6,2},{... | collective-permute-start | bytes 196616 | tf_op jit(solution)/shard_map/ppermute | solution.py:461
  27.3 6.1 %collective-permute-start.9 = (bf16[256,128]{1,0:T(8,128)(2,1)S(1)}, bf16[256,128]{1,0:T(8,128)(2,1)S(1)}, u32[]{:S(2)}, u32[]{:S(2)}) collective-permute-start(bf16[256,128]{1,0:T(8,128)(2,1)S(1)} %get-tuple-element.31.own_ref), channel_id=1, source_target_pairs={{0,4},{4,8},{8,12},{12,0},{1,5},{5,9},{9,13},{13,1},{2,6},{6,10},{... | collective-permute-start | bytes 196616 | tf_op jit(solution)/shard_map/ppermute | solution.py:461
  34.1 4.0 %collective-permute-start.13 = (bf16[128,128]{1,0:T(8,128)(2,1)S(1)}, bf16[128,128]{1,0:T(8,128)(2,1)S(1)}, u32[]{:S(2)}, u32[]{:S(2)}) collective-permute-start(bf16[128,128]{1,0:T(8,128)(2,1)S(1)} %get-tuple-element.38), channel_id=1, source_target_pairs={{0,2},{2,0},{1,3},{3,1},{4,6},{6,4},{5,7},{7,5},{8,10},{10,8},{9,1... | collective-permute-start | bytes 98312 | tf_op jit(solution)/shard_map/ppermute | solution.py:150

commit v3 on v2

--- a/solution.py
+++ b/solution.py
@@ -10,7 +10,7 @@
 from jax.sharding import PartitionSpec as P
 
 HALO = 16
-LOAD_MIB = 48
+PAD = 32
 F32 = jnp.float32
 BF16 = jnp.bfloat16
 
@@ -168,7 +168,7 @@
     return wanted.astype(F32).astype(BF16)
 
 
-def pack_body(rows_ref, pack_ref, done_ref):
+def pack_body(rows_ref, pack_ref):
     width = pack_ref.shape[1]
     last = rows_ref[rows_ref.shape[0] - HALO :, :]
     total = jnp.zeros((HALO, width), F32)
@@ -176,7 +176,6 @@
         part = last[:, piece * width : (piece + 1) * width]
         total += jnp.dot(pick_rows(HALO - 2, 2 * piece), part, preferred_element_type=F32)
     pack_ref[...] = total.astype(BF16)
-    done_ref[...] = jnp.zeros_like(done_ref)
 
 
 def unpack_halo(pieces, count):
@@ -187,41 +186,30 @@
     return jnp.concatenate(parts, axis=1)
 
 
-def choose_body(rows_ref, hop_ref, order_ref, send_ref):
-    core = lax.axis_index("chan")
-    count = send_ref.shape[0]
-    lines = pl.ds(pl.multiple_of(core * count, count), count)
-    here = core != lax.axis_index("fsdp")
-    send_ref[...] = jnp.where(here, rows_ref[lines, :], hop_ref[lines, :])
-
-
-def load_body(weight_ref, order_ref, weight_out, sems):
-    copies = [
-        pltpu.make_async_copy(weight_ref.at[branch], weight_out.at[branch], sems.at[branch])
-        for branch in range(3)
-    ]
-    for copy in copies:
-        copy.start()
-    for copy in copies:
-        copy.wait()
-
-
 def project(rows, weight_ref, own_half, keep_ref, send_ref):
     half = keep_ref.shape[1] // 3
     for branch in range(3):
         summed = jnp.dot(rows, weight_ref[branch], preferred_element_type=F32)
         keep, send = split_channels(summed, own_half)
-        keep_ref[:, branch * half : (branch + 1) * half] = keep
-        send_ref[:, branch * half : (branch + 1) * half] = send.astype(BF16)
-
-
-def project_first_body(
-    rows_ref, hop_ref, pack_ref, pack_hop_ref, weight_ref, keep_ref, send_ref, done_ref
+        lanes = slice(branch * half, (branch + 1) * half)
+        keep_ref[:, lanes] = keep
+        send_ref[: send.shape[0], lanes] = send.astype(BF16)
+
+
+def project_first_body(rows_ref, cycled_ref, weight_ref, keep_ref, send_ref):
+    own_half = lax.axis_index("fsdp")
+    here = lax.axis_index("chan") == own_half
+    rows = jnp.where(here, rows_ref[...], cycled_ref[...])
+    project(rows, weight_ref, own_half, keep_ref, send_ref)
+
+
+def project_second_body(
+    cycled_ref, hop_ref, pack_ref, pack_hop_ref, weight_ref, keep_ref, send_ref, done_ref
 ):
     own_half = lax.axis_index("fsdp")
     here = lax.axis_index("chan") == own_half
-    pieces = rows_ref.shape[1] // pack_ref.shape[1]
-    rows = jnp.where(here, rows_ref[...], hop_ref[...])
+    pieces = cycled_ref.shape[1] // pack_ref.shape[1]
+    rows = jnp.where(here, cycled_ref[...], hop_ref[...])
     halo = unpack_halo(jnp.where(here, pack_ref[...], pack_hop_ref[...]), pieces)
     halo = jnp.where(lax.axis_index("seq") > 0, halo, jnp.zeros_like(halo))
     rows = jnp.concatenate([halo, rows], axis=0)
@@ -229,29 +217,14 @@
     done_ref[...] = jnp.zeros_like(done_ref)
 
 
-def project_second_body(got_ref, hop_ref, weight_ref, keep_ref, send_ref, done_ref):
-    own_half = lax.axis_index("fsdp")
-    first = lax.axis_index("chan") == 0
-    got, hop = (got_ref[...], hop_ref[...])
-    rows = jnp.concatenate([jnp.where(first, got, hop), jnp.where(first, hop, got)], axis=0)
-    project(rows, weight_ref, own_half, keep_ref, send_ref)
-    done_ref[...] = jnp.zeros_like(done_ref)
-
-
-def pair_taps_body(own_ref, got_ref, *refs):
-    pair_ref = refs[-1]
-    pair_ref[0] = own_ref[...]
-    pair_ref[1] = got_ref[...]
-
-
-def sort_taps_body(pair_ref, far_ref, *refs):
+def sort_taps_body(*refs):
     keep_ref, send_ref, done_ref = refs[-3:]
     position = lax.axis_index("seq")
     first = lax.axis_index("fsdp") == 0
-    blocks, rows, half = keep_ref.shape
+    blocks, _, half = keep_ref.shape
     for step in range(blocks):
         block = lax.rem(position - step + blocks, blocks)
-        taps = (pair_ref if step < 2 else far_ref)[step % 2]
+        taps = refs[step][...]
         low, high = (taps[:, :half], taps[:, half:])
         keep_ref[block] = jnp.where(first, low, high)
         send_ref[block] = jnp.where(first, high, low)
@@ -296,16 +269,16 @@
         before_real, before_imag = (real, imag)
 
 
-def mix_body(keep_first, keep_second, got_first, got_second, short_ref, *refs):
-    product_ref, query_ref, joined = refs[-3:]
+def mix_body(keep_first, keep_second, got_first, got_second, short_ref, order_ref,
+             product_ref, query_ref, joined):
     own = lax.axis_index("fsdp")
-    rows = got_second.shape[0]
-    half = got_second.shape[1] // 3
-    joined[:HALO, :] = keep_first[:HALO, :] + got_first[:HALO, :].astype(F32)
+    rows = keep_first.shape[0]
+    half = keep_first.shape[1] // 3
+    joined[:HALO, :] = keep_second[:HALO, :] + got_second[:HALO, :].astype(F32)
     own_start = pl.multiple_of(HALO + own * rows, HALO)
     other_start = pl.multiple_of(HALO + (1 - own) * rows, HALO)
-    joined[pl.ds(own_start, rows), :] = keep_first[HALO:, :] + got_second[:, :].astype(F32)
-    joined[pl.ds(other_start, rows), :] = keep_second[:, :] + got_first[HALO:, :].astype(F32)
+    joined[pl.ds(own_start, rows), :] = keep_first[...] + got_second[HALO:, :].astype(F32)
+    joined[pl.ds(other_start, rows), :] = keep_second[HALO:, :] + got_first[:rows, :].astype(F32)
     count = 2 * rows
     mixed = []
     for branch in range(3):
@@ -361,7 +334,6 @@
 
 def pair_mesh(tokens, proj_weight, short_weight, skip_gain, filter_taps):
     rows = tokens.shape[0]
-    features = proj_weight.shape[0]
     width = proj_weight.shape[2]
     half = width // 2
     size = 2 * rows
@@ -372,30 +344,15 @@
         pl.pallas_call, compiler_params=pltpu.CompilerParams(vmem_limit_bytes=32 * 1024 * 1024)
     )
 
-    own_hop = exchange(tokens, "chan")
+    cycled = lax.ppermute(tokens, ("fsdp", "chan"), [(1, 3), (3, 2), (2, 0), (0, 1)])
     token = shape((8, 128), F32)
-    pack, pack_done = call(
+    pack = call(
         pack_body,
+        cost_estimate=pl.CostEstimate(flops=10_000_000_000, bytes_accessed=40_000_000, transcendentals=0),
         in_specs=whole_specs(1),
-        out_specs=whole_specs(2),
-        out_shape=(shape((HALO, width), BF16), token),
+        out_specs=whole_specs(1)[0],
+        out_shape=shape((HALO, width), BF16),
     )(tokens)
-    token_send = call(
-        choose_body,
-        in_specs=whole_specs(3),
-        out_specs=whole_specs(1)[0],
-        out_shape=shape((rows // 2, features), BF16),
-    )(tokens, own_hop, pack_done)
-    got = exchange(token_send, "fsdp")
-    tap_near = lax.ppermute(filter_taps, "seq", ring[1])
-    weight = pl.pallas_call(
-        load_body,
-        in_specs=[pl.BlockSpec(memory_space=pltpu.HBM), *whole_specs(1)],
-        out_specs=whole_specs(1)[0],
-        out_shape=shape(weight.shape, BF16),
-        scratch_shapes=[pltpu.SemaphoreType.DMA((3,))],
-        compiler_params=pltpu.CompilerParams(vmem_limit_bytes=LOAD_MIB * 1024 * 1024),
-    )(weight, pack_done)
     pack_got = lax.ppermute(
         pack,
         ("seq", "fsdp", "chan"),
@@ -406,16 +363,22 @@
             for c in range(2)
         ],
     )
-    tap_pair = call(
-        pair_taps_body,
-        in_specs=whole_specs(2),
-        out_specs=whole_specs(1)[0],
-        out_shape=shape((2, rows, width), BF16),
-    )(filter_taps, tap_near)
-    pack_got = after(pack_got, weight)
+    tap_blocks = [filter_taps] + [
+        lax.ppermute(filter_taps, "seq", ring[step]) for step in range(1, blocks)
+    ]
+    cycled = after(cycled, pack_got)
+    hop = exchange(cycled, "chan")
     pack_hop = exchange(pack_got, "chan")
-    keep_first, send_first, first_done = call(
+    keep_first, send_first = call(
         project_first_body,
+        cost_estimate=pl.CostEstimate(flops=10_000_000_000, bytes_accessed=40_000_000, transcendentals=0),
+        in_specs=whole_specs(3),
+        out_specs=whole_specs(2),
+        out_shape=(shape((rows, 3 * half), F32), shape((rows + PAD, 3 * half), BF16)),
+    )(tokens, cycled, weight)
+    got_first = exchange(send_first, "fsdp")
+    keep_second, send_second, second_done = call(
+        project_second_body,
         in_specs=whole_specs(5),
         out_specs=whole_specs(3),
         out_shape=(
@@ -423,33 +386,20 @@
             shape((HALO + rows, 3 * half), BF16),
             token,
         ),
-    )(tokens, own_hop, pack_got, pack_hop, weight)
-    got = after(got, first_done, tap_pair)
-    got_hop = exchange(got, "chan")
-    got_first = exchange(send_first, "fsdp")
-    keep_second, send_second, second_done = call(
-        project_second_body,
-        in_specs=whole_specs(3),
-        out_specs=whole_specs(3),
-        out_shape=(shape((rows, 3 * half), F32), shape((rows, 3 * half), BF16), token),
-    )(got, got_hop, weight)
+    )(cycled, hop, pack_got, pack_hop, weight)
     got_second = exchange(send_second, "fsdp")
-    tap_far = lax.ppermute(tap_pair, "seq", ring[2])
-
     tap_keep, tap_send, tap_done = call(
         sort_taps_body,
-        in_specs=whole_specs(2 + 1),
+        in_specs=whole_specs(1 + blocks),
         out_specs=whole_specs(3),
         out_shape=(
             shape((blocks, rows, half), BF16),
             shape((blocks, rows, half), BF16),
             token,
         ),
-    )(tap_pair, tap_far, second_done)
+    )(*tap_blocks, second_done)
     tap_got = exchange(tap_send, "fsdp")
-    table = wave_table(size)
-    forward = jnp.asarray(table, dtype=BF16)
-    inverse = jnp.asarray(table.T, dtype=BF16)
+
     product, query = call(
         mix_body,
         in_specs=whole_specs(6),
@@ -459,6 +409,9 @@
     )(keep_first, keep_second, got_first, got_second, short_weight, tap_done)
 
     products = [product] + [lax.ppermute(product, "seq", ring[step]) for step in range(1, blocks)]
+    table = wave_table(size)
+    forward = jnp.asarray(table, dtype=BF16)
+    inverse = jnp.asarray(table.T, dtype=BF16)
     tap_real, tap_imag = call(
         taps_body,
         in_specs=whole_specs(3),

time: 38.8 us -> 36 us (0.928)
  waiting for transfers between devices: 18.2 us -> 13.9 us
  starting transfers between devices: 13.8 us -> 16.9 us
  Pallas kernels: 5.45 us -> 3.61 us
    ppermute x2 -> x4, waiting for transfers between devices: 5.19 us -> 0.01 us  [the longest x3 0.01 us: pair_mesh(): lax.ppermute(filter_taps, 'seq', ring[step])]
    ppermute x8 -> x6, starting transfers between devices: 7 us -> 3.19 us  [exchange(): return lax.ppermute(value, axis, [(0, 1), (1, 0)])]
    ppermute x2 -> x4, starting transfers between devices: 2.48 us -> 5.97 us  [the longest x3 5.51 us: pair_mesh(): lax.ppermute(filter_taps, 'seq', ring[step])]
    ppermute x1, waiting for transfers between devices: 2.89 us -> 0.01 us  [pair_mesh(): lax.ppermute(pack, ('seq', 'fsdp', 'chan'), [(4 * s + 2 * f + c, 4 * ((s...]
    ppermute x1, starting transfers between devices: 1.55 us -> 4.09 us  [pair_mesh(): lax.ppermute(pack, ('seq', 'fsdp', 'chan'), [(4 * s + 2 * f + c, 4 * ((s...]
    ppermute x8 -> x6, waiting for transfers between devices: 6.9 us -> 8.94 us  [exchange(): return lax.ppermute(value, axis, [(0, 1), (1, 0)])]
    pallas_call x7 -> x4, Pallas kernels: 3.46 us -> 1.62 us  [the longest x1 0.77 us: pair_mesh(): call(project_second_body, in_specs=whole_specs(5), out_specs=whole_specs(...]
    ppermute x3, waiting for transfers between devices: 3.19 us -> 4.92 us  [pair_mesh(): lax.ppermute(product, 'seq', ring[step])]
  transfers between devices with their start and end apart: 14 -> 14, of which waited for: 8 -> 7; matrix products, arithmetic and copies ran while one was open for 0% -> 0% of each run, Pallas kernels for 10% -> 6%
where the time goes in v3:
time: 36 us; the launch traced here: 35.8 us
  starting transfers between devices  16.9 us (47%)
  waiting for transfers between devices  13.9 us (39%)
  Pallas kernels  3.61 us (10%)
  local copies, waits for them, and re-layouts  1.31 us (4%)
    ppermute x6, waiting for transfers between devices, exchange(): return lax.ppermute(value, axis, [(0, 1), (1, 0)])  8.94 us
    ppermute x3, starting transfers between devices, pair_mesh(): lax.ppermute(filter_taps, 'seq', ring[step])  5.51 us
    ppermute x3, waiting for transfers between devices, pair_mesh(): lax.ppermute(product, 'seq', ring[step])  4.92 us
    ppermute x1, starting transfers between devices, pair_mesh(): lax.ppermute(pack, ('seq', 'fsdp', 'chan'), [(4 * s + 2 * f + c, 4 * ((s...  4.09 us
    ppermute x3, starting transfers between devices, pair_mesh(): lax.ppermute(product, 'seq', ring[step])  3.67 us
    ppermute x6, starting transfers between devices, exchange(): return lax.ppermute(value, axis, [(0, 1), (1, 0)])  3.19 us
    unnamed x14, local copies, waits for them, and re-layouts  1.31 us
    pallas_call x1, Pallas kernels, pair_mesh(): call(project_second_body, in_specs=whole_specs(5), out_specs=whole_specs(...  0.77 us
  transfers between devices with their start and end apart: 14, of which 7 were waited for; matrix products, arithmetic and copies ran while one was open for 0% of the time, Pallas kernels for 6%

profile of v3, /device:TPU:0, one launch (start us, length us, event | category | flops | bytes accessed | tf_op | source)
XLA Modules:
  0.0 35.8 jit_solution(4762782665823488026)
XLA Ops:
  0.0 0.5 %collective-permute-start = (bf16[128,2048]{1,0:T(8,128)(2,1)}, bf16[128,2048]{1,0:T(8,128)(2,1)S(1)}, u32[]{:S(2)}, u32[]{:S(2)}) collective-permute-start(bf16[128,2048]{1,0:T(8,128)(2,1)} %rows_ref.3), channel_id=1, source_target_pairs={{1,3},{3,2},{2,0},{0,1},{5,7},{7,6},{6,4},{4,5},{9,11},{11,10},{10... | collective-permute-start | bytes 1572872 | tf_op jit(solution)/shard_map/ppermute | solution.py:347
  0.5 1.3 %copy-done.6 = bf16[128,2048]{1,0:T(8,128)(2,1)S(1)} copy-done((bf16[128,2048]{1,0:T(8,128)(2,1)S(1)}, bf16[128,2048]{1,0:T(8,128)(2,1)}, u32[]{:S(2)}) %copy-start.6) | copy-done | bytes 524312
  1.7 0.1 shard_map.73
  1.9 4.1 %collective-permute-start.1 = (bf16[16,256]{1,0:T(8,128)(2,1)S(1)}, bf16[16,256]{1,0:T(8,128)(2,1)S(1)}, u32[]{:S(2)}, u32[]{:S(2)}) collective-permute-start(bf16[16,256]{1,0:T(8,128)(2,1)S(1)} %shard_map.73), channel_id=1, source_target_pairs={{0,6},{1,5},{2,4},{3,7},{4,10},{5,9},{6,8},{7,11},{8,14},{9,13},{1... | collective-permute-start | bytes 24584 | tf_op jit(solution)/shard_map/ppermute | solution.py:356
  6.0 1.6 %collective-permute-start.6 = (bf16[128,256]{1,0:T(8,128)(2,1)S(1)}, bf16[128,256]{1,0:T(8,128)(2,1)S(1)}, u32[]{:S(2)}, u32[]{:S(2)}) collective-permute-start(bf16[128,256]{1,0:T(8,128)(2,1)S(1)} %copy-done.3), channel_id=1, source_target_pairs={{0,4},{4,8},{8,12},{12,0},{1,5},{5,9},{9,13},{13,1},{2,6},{6,10},{... | collective-permute-start | bytes 196616 | tf_op jit(solution)/shard_map/ppermute | solution.py:367
  7.5 1.0 %collective-permute-start.7 = (bf16[128,256]{1,0:T(8,128)(2,1)S(1)}, bf16[128,256]{1,0:T(8,128)(2,1)S(1)}, u32[]{:S(2)}, u32[]{:S(2)}) collective-permute-start(bf16[128,256]{1,0:T(8,128)(2,1)S(1)} %copy-done.3), channel_id=1, source_target_pairs={{0,8},{4,12},{8,0},{12,4},{1,9},{5,13},{9,1},{13,5},{2,10},{6,14},... | collective-permute-start | bytes 196616 | tf_op jit(solution)/shard_map/ppermute | solution.py:367
  8.6 2.9 %collective-permute-start.8 = (bf16[128,256]{1,0:T(8,128)(2,1)S(1)}, bf16[128,256]{1,0:T(8,128)(2,1)S(1)}, u32[]{:S(2)}, u32[]{:S(2)}) collective-permute-start(bf16[128,256]{1,0:T(8,128)(2,1)S(1)} %copy-done.3), channel_id=1, source_target_pairs={{0,12},{4,0},{8,4},{12,8},{1,13},{5,1},{9,5},{13,9},{2,14},{6,2},{... | collective-permute-start | bytes 196616 | tf_op jit(solution)/shard_map/ppermute | solution.py:367
  11.5 0.5 %collective-permute-start.2 = (bf16[128,2048]{1,0:T(8,128)(2,1)S(1)}, bf16[128,2048]{1,0:T(8,128)(2,1)S(1)}, u32[]{:S(2)}, u32[]{:S(2)}) collective-permute-start(bf16[128,2048]{1,0:T(8,128)(2,1)S(1)} %shard_map.74.cycled_ref), channel_id=1, source_target_pairs={{0,1},{1,0},{2,3},{3,2},{4,5},{5,4},{6,7},{7,6},{8,9},{9,8},{10,11... | collective-permute-start | bytes 1572872 | tf_op jit(solution)/shard_map/ppermute | solution.py:150
  12.0 0.7 %shard_map.75 = (f32[128,384]{1,0:T(8,128)S(1)}, bf16[160,384]{1,0:T(8,128)(2,1)S(1)}) custom-call(bf16[128,2048]{1,0:T(8,128)(2,1)S(1)} %copy-done.6, bf16[128,2048]{1,0:T(8,128)(2,1)S(1)} %shard_map.74.cycled_ref, bf16[3,2048,256]{2,1,0:T(8,128)(2,1)S(1)} %bitcast.2), custom_call_target="tpu_custom_call" | custom-call | flops 10000000000 | bytes 40000000 | tf_op jit(solution)/shard_map/pallas_call | solution.py:372
  12.7 0.0 copy-start.1
  12.7 0.0 copy-start.2
  12.7 0.0 copy-start.5
  12.7 0.1 collective-permute-start.4
  12.8 0.7 %collective-permute-done.2.hop_ref = bf16[128,2048]{1,0:T(8,128)(2,1)S(1)} collective-permute-done((bf16[128,2048]{1,0:T(8,128)(2,1)S(1)}, bf16[128,2048]{1,0:T(8,128)(2,1)S(1)}, u32[]{:S(2)}, u32[]{:S(2)}) %collective-permute-start.2) | collective-permute-done | bytes 524320 | tf_op jit(solution)/shard_map/ppermute | solution.py:150
  13.5 0.8 %shard_map.76 = (f32[144,384]{1,0:T(8,128)S(1)}, bf16[144,384]{1,0:T(8,128)(2,1)S(1)}, f32[8,128]{1,0:T(8,128)S(1)}) custom-call(bf16[128,2048]{1,0:T(8,128)(2,1)S(1)} %shard_map.74.cycled_ref, bf16[128,2048]{1,0:T(8,128)(2,1)S(1)} %collective-permute-done.2.hop_ref, bf16[16,256]{1,0:T(8,128)(2,1)S(1)} %collective-permute-done.1.refs_1_.pack_ref, ...), custom_call_target="tpu_custom_call" | custom-call | tf_op jit(solution)/shard_map/pallas_call | solution.py:380
  14.3 1.4 %collective-permute-start.5 = (bf16[144,384]{1,0:T(8,128)(2,1)S(1)}, bf16[144,384]{1,0:T(8,128)(2,1)S(1)}, u32[]{:S(2)}, u32[]{:S(2)}) collective-permute-start(bf16[144,384]{1,0:T(8,128)(2,1)S(1)} %get-tuple-element.22), channel_id=1, source_target_pairs={{0,2},{2,0},{1,3},{3,1},{4,6},{6,4},{5,7},{7,5},{8,10},{10,8},{9,1... | collective-permute-start | bytes 331784 | tf_op jit(solution)/shard_map/ppermute | solution.py:150
  15.7 0.1 shard_map.77
  15.8 0.8 %collective-permute-start.12 = (bf16[4,128,128]{2,1,0:T(8,128)(2,1)S(1)}, bf16[4,128,128]{2,1,0:T(8,128)(2,1)S(1)}, u32[]{:S(2)}, u32[]{:S(2)}) collective-permute-start(bf16[4,128,128]{2,1,0:T(8,128)(2,1)S(1)} %get-tuple-element.27), channel_id=1, source_target_pairs={{0,2},{2,0},{1,3},{3,1},{4,6},{6,4},{5,7},{7,5},{8,10},{10,8},{9,1... | collective-permute-start | bytes 393224 | tf_op jit(solution)/shard_map/ppermute | solution.py:150
  16.6 2.3 %collective-permute-done.4.got_first = bf16[160,384]{1,0:T(8,128)(2,1)S(1)} collective-permute-done((bf16[160,384]{1,0:T(8,128)(2,1)S(1)}, bf16[160,384]{1,0:T(8,128)(2,1)S(1)}, u32[]{:S(2)}, u32[]{:S(2)}) %collective-permute-start.4) | collective-permute-done | bytes 122912 | tf_op jit(solution)/shard_map/ppermute | solution.py:150
  18.9 2.4 %collective-permute-done.5.got_second = bf16[144,384]{1,0:T(8,128)(2,1)S(1)} collective-permute-done((bf16[144,384]{1,0:T(8,128)(2,1)S(1)}, bf16[144,384]{1,0:T(8,128)(2,1)S(1)}, u32[]{:S(2)}, u32[]{:S(2)}) %collective-permute-start.5) | collective-permute-done | bytes 110624 | tf_op jit(solution)/shard_map/ppermute | solution.py:150
  21.2 0.2 shard_map.78
  21.4 1.6 %collective-permute-start.10 = (bf16[256,128]{1,0:T(8,128)(2,1)S(1)}, bf16[256,128]{1,0:T(8,128)(2,1)S(1)}, u32[]{:S(2)}, u32[]{:S(2)}) collective-permute-start(bf16[256,128]{1,0:T(8,128)(2,1)S(1)} %get-tuple-element.25.own_ref), channel_id=1, source_target_pairs={{0,8},{4,12},{8,0},{12,4},{1,9},{5,13},{9,1},{13,5},{2,10},{6,14},... | collective-permute-start | bytes 196616 | tf_op jit(solution)/shard_map/ppermute | solution.py:411
  23.1 1.3 %collective-permute-start.11 = (bf16[256,128]{1,0:T(8,128)(2,1)S(1)}, bf16[256,128]{1,0:T(8,128)(2,1)S(1)}, u32[]{:S(2)}, u32[]{:S(2)}) collective-permute-start(bf16[256,128]{1,0:T(8,128)(2,1)S(1)} %get-tuple-element.25.own_ref), channel_id=1, source_target_pairs={{0,12},{4,0},{8,4},{12,8},{1,13},{5,1},{9,5},{13,9},{2,14},{6,2},{... | collective-permute-start | bytes 196616 | tf_op jit(solution)/shard_map/ppermute | solution.py:411
  24.4 0.7 %collective-permute-start.9 = (bf16[256,128]{1,0:T(8,128)(2,1)S(1)}, bf16[256,128]{1,0:T(8,128)(2,1)S(1)}, u32[]{:S(2)}, u32[]{:S(2)}) collective-permute-start(bf16[256,128]{1,0:T(8,128)(2,1)S(1)} %get-tuple-element.25.own_ref), channel_id=1, source_target_pairs={{0,4},{4,8},{8,12},{12,0},{1,5},{5,9},{9,13},{13,1},{2,6},{6,10},{... | collective-permute-start | bytes 196616 | tf_op jit(solution)/shard_map/ppermute | solution.py:411
  25.1 0.5 %shard_map.79 = (f32[4,256,128]{2,1,0:T(8,128)S(1)}, f32[4,256,128]{2,1,0:T(8,128)S(1)}) custom-call(bf16[512,256]{1,0:T(8,128)(2,1)S(1)} %copy-done.1, bf16[4,128,128]{2,1,0:T(8,128)(2,1)S(1)} %get-tuple-element.26.keep_ref, bf16[4,128,128]{2,1,0:T(8,128)(2,1)S(1)} %collective-permute-done.12.got_ref), custom_call_target="tpu_custom_call" | custom-call | tf_op jit(solution)/shard_map/pallas_call | solution.py:415
  25.6 2.6 %collective-permute-done.10.two_ref = bf16[256,128]{1,0:T(8,128)(2,1)S(1)} collective-permute-done((bf16[256,128]{1,0:T(8,128)(2,1)S(1)}, bf16[256,128]{1,0:T(8,128)(2,1)S(1)}, u32[]{:S(2)}, u32[]{:S(2)}) %collective-permute-start.10) | collective-permute-done | bytes 65568 | tf_op jit(solution)/shard_map/ppermute | solution.py:411
  28.2 0.2 collective-permute-done.11.three_ref
  28.4 2.1 %collective-permute-done.9.one_ref = bf16[256,128]{1,0:T(8,128)(2,1)S(1)} collective-permute-done((bf16[256,128]{1,0:T(8,128)(2,1)S(1)}, bf16[256,128]{1,0:T(8,128)(2,1)S(1)}, u32[]{:S(2)}, u32[]{:S(2)}) %collective-permute-start.9) | collective-permute-done | bytes 65568 | tf_op jit(solution)/shard_map/ppermute | solution.py:411
  30.5 0.7 %shard_map.80 = (bf16[128,128]{1,0:T(8,128)(2,1)S(1)}, bf16[128,128]{1,0:T(8,128)(2,1)S(1)}) custom-call(bf16[256,128]{1,0:T(8,128)(2,1)S(1)} %get-tuple-element.25.own_ref, bf16[256,128]{1,0:T(8,128)(2,1)S(1)} %collective-permute-done.9.one_ref, bf16[256,128]{1,0:T(8,128)(2,1)S(1)} %collective-permute-done.10.two_ref, ...), custom_call_target="tpu_custom_call" | custom-call | tf_op jit(solution)/shard_map/pallas_call | solution.py:421
  31.2 0.4 %collective-permute-start.13 = (bf16[128,128]{1,0:T(8,128)(2,1)S(1)}, bf16[128,128]{1,0:T(8,128)(2,1)S(1)}, u32[]{:S(2)}, u32[]{:S(2)}) collective-permute-start(bf16[128,128]{1,0:T(8,128)(2,1)S(1)} %get-tuple-element.32), channel_id=1, source_target_pairs={{0,2},{2,0},{1,3},{3,1},{4,6},{6,4},{5,7},{7,5},{8,10},{10,8},{9,1... | collective-permute-start | bytes 98312 | tf_op jit(solution)/shard_map/ppermute | solution.py:150
  31.6 3.5 %collective-permute-done.13.got_ref = bf16[128,128]{1,0:T(8,128)(2,1)S(1)} collective-permute-done((bf16[128,128]{1,0:T(8,128)(2,1)S(1)}, bf16[128,128]{1,0:T(8,128)(2,1)S(1)}, u32[]{:S(2)}, u32[]{:S(2)}) %collective-permute-start.13) | collective-permute-done | bytes 32800 | tf_op jit(solution)/shard_map/ppermute | solution.py:150
  35.2 0.6 %shard_map.81 = bf16[128,256]{1,0:T(8,128)(2,1)} custom-call(bf16[128,128]{1,0:T(8,128)(2,1)S(1)} %get-tuple-element.31.stay_ref, bf16[128,128]{1,0:T(8,128)(2,1)S(1)} %collective-permute-done.13.got_ref), custom_call_target="tpu_custom_call" | custom-call | tf_op jit(solution)/shard_map/pallas_call | solution.py:429
  (19 shorter events, 0.0 us)
Async XLA Ops:
  0.0 6.0 %copy-start.3 = (bf16[128,256]{1,0:T(8,128)(2,1)S(1)}, bf16[128,256]{1,0:T(8,128)(2,1)}, u32[]{:S(2)}) copy-start(bf16[128,256]{1,0:T(8,128)(2,1)} %refs_0_.1) | copy-start | bytes 196612
  0.0 12.0 %copy-start = (bf16[2048,3,256]{2,0,1:T(8,128)(2,1)S(1)}, bf16[2048,3,256]{2,0,1:T(8,128)(2,1)}, u32[]{:S(2)}) copy-start(bf16[2048,3,256]{2,0,1:T(8,128)(2,1)} %param.8) | copy-start | bytes 9437188
  0.0 11.5 %collective-permute-start = (bf16[128,2048]{1,0:T(8,128)(2,1)}, bf16[128,2048]{1,0:T(8,128)(2,1)S(1)}, u32[]{:S(2)}, u32[]{:S(2)}) collective-permute-start(bf16[128,2048]{1,0:T(8,128)(2,1)} %rows_ref.3), channel_id=1, source_target_pairs={{1,3},{3,2},{2,0},{0,1},{5,7},{7,6},{6,4},{4,5},{9,11},{11,10},{10... | collective-permute-start | bytes 1572872 | tf_op jit(solution)/shard_map/ppermute | solution.py:347
  0.5 1.3 %copy-start.6 = (bf16[128,2048]{1,0:T(8,128)(2,1)S(1)}, bf16[128,2048]{1,0:T(8,128)(2,1)}, u32[]{:S(2)}) copy-start(bf16[128,2048]{1,0:T(8,128)(2,1)} %rows_ref.3) | copy-start | bytes 1572868
  1.9 9.6 %collective-permute-start.1 = (bf16[16,256]{1,0:T(8,128)(2,1)S(1)}, bf16[16,256]{1,0:T(8,128)(2,1)S(1)}, u32[]{:S(2)}, u32[]{:S(2)}) collective-permute-start(bf16[16,256]{1,0:T(8,128)(2,1)S(1)} %shard_map.73), channel_id=1, source_target_pairs={{0,6},{1,5},{2,4},{3,7},{4,10},{5,9},{6,8},{7,11},{8,14},{9,13},{1... | collective-permute-start | bytes 24584 | tf_op jit(solution)/shard_map/ppermute | solution.py:356
  6.0 9.7 %collective-permute-start.6 = (bf16[128,256]{1,0:T(8,128)(2,1)S(1)}, bf16[128,256]{1,0:T(8,128)(2,1)S(1)}, u32[]{:S(2)}, u32[]{:S(2)}) collective-permute-start(bf16[128,256]{1,0:T(8,128)(2,1)S(1)} %copy-done.3), channel_id=1, source_target_pairs={{0,4},{4,8},{8,12},{12,0},{1,5},{5,9},{9,13},{13,1},{2,6},{6,10},{... | collective-permute-start | bytes 196616 | tf_op jit(solution)/shard_map/ppermute | solution.py:367
  7.5 8.1 %collective-permute-start.7 = (bf16[128,256]{1,0:T(8,128)(2,1)S(1)}, bf16[128,256]{1,0:T(8,128)(2,1)S(1)}, u32[]{:S(2)}, u32[]{:S(2)}) collective-permute-start(bf16[128,256]{1,0:T(8,128)(2,1)S(1)} %copy-done.3), channel_id=1, source_target_pairs={{0,8},{4,12},{8,0},{12,4},{1,9},{5,13},{9,1},{13,5},{2,10},{6,14},... | collective-permute-start | bytes 196616 | tf_op jit(solution)/shard_map/ppermute | solution.py:367
  8.6 7.1 %collective-permute-start.8 = (bf16[128,256]{1,0:T(8,128)(2,1)S(1)}, bf16[128,256]{1,0:T(8,128)(2,1)S(1)}, u32[]{:S(2)}, u32[]{:S(2)}) collective-permute-start(bf16[128,256]{1,0:T(8,128)(2,1)S(1)} %copy-done.3), channel_id=1, source_target_pairs={{0,12},{4,0},{8,4},{12,8},{1,13},{5,1},{9,5},{13,9},{2,14},{6,2},{... | collective-permute-start | bytes 196616 | tf_op jit(solution)/shard_map/ppermute | solution.py:367
  11.5 1.2 %collective-permute-start.3 = (bf16[16,256]{1,0:T(8,128)(2,1)S(1)}, bf16[16,256]{1,0:T(8,128)(2,1)S(1)}, u32[]{:S(2)}, u32[]{:S(2)}) collective-permute-start(bf16[16,256]{1,0:T(8,128)(2,1)S(1)} %collective-permute-done.1.refs_1_.pack_ref), channel_id=1, source_target_pairs={{0,1},{1,0},{2,3},{3,2},{4,5},{5,4},{6,7},{7,6},{8,9},{9,8},{10,11... | collective-permute-start | bytes 24584 | tf_op jit(solution)/shard_map/ppermute | solution.py:150
  11.5 2.0 %collective-permute-start.2 = (bf16[128,2048]{1,0:T(8,128)(2,1)S(1)}, bf16[128,2048]{1,0:T(8,128)(2,1)S(1)}, u32[]{:S(2)}, u32[]{:S(2)}) collective-permute-start(bf16[128,2048]{1,0:T(8,128)(2,1)S(1)} %shard_map.74.cycled_ref), channel_id=1, source_target_pairs={{0,1},{1,0},{2,3},{3,2},{4,5},{5,4},{6,7},{7,6},{8,9},{9,8},{10,11... | collective-permute-start | bytes 1572872 | tf_op jit(solution)/shard_map/ppermute | solution.py:150
  12.7 8.6 %copy-start.4 = (f32[3,3,256]{2,1,0:T(4,128)S(1)}, f32[3,3,256]{2,1,0:T(4,128)}, u32[]{:S(2)}) copy-start(f32[3,3,256]{2,1,0:T(4,128)} %short_ref.1) | copy-start | bytes 27652
  12.7 12.4 %copy-start.1 = (bf16[512,256]{1,0:T(8,128)(2,1)S(1)}, bf16[512,256]{1,0:T(8,128)(2,1)}, u32[]{:S(2)}) copy-start(bf16[512,256]{1,0:T(8,128)(2,1)} %constant.4.clone.table_ref) | copy-start | bytes 786436
  12.7 17.8 %copy-start.2 = (bf16[256,512]{1,0:T(8,128)(2,1)S(1)}, bf16[256,512]{1,0:T(8,128)(2,1)}, u32[]{:S(2)}) copy-start(bf16[256,512]{1,0:T(8,128)(2,1)} %constant.5.clone.turned_ref) | copy-start | bytes 786436
  12.7 17.8 %copy-start.5 = (f32[256]{0:T(256)S(1)}, f32[256]{0:T(256)}, u32[]{:S(2)}) copy-start(f32[256]{0:T(256)} %param.10) | copy-start | bytes 3076
  12.7 6.1 %collective-permute-start.4 = (bf16[160,384]{1,0:T(8,128)(2,1)S(1)}, bf16[160,384]{1,0:T(8,128)(2,1)S(1)}, u32[]{:S(2)}, u32[]{:S(2)}) collective-permute-start(bf16[160,384]{1,0:T(8,128)(2,1)S(1)} %get-tuple-element.21), channel_id=1, source_target_pairs={{0,2},{2,0},{1,3},{3,1},{4,6},{6,4},{5,7},{7,5},{8,10},{10,8},{9,1... | collective-permute-start | bytes 368648 | tf_op jit(solution)/shard_map/ppermute | solution.py:150
  14.3 6.9 %collective-permute-start.5 = (bf16[144,384]{1,0:T(8,128)(2,1)S(1)}, bf16[144,384]{1,0:T(8,128)(2,1)S(1)}, u32[]{:S(2)}, u32[]{:S(2)}) collective-permute-start(bf16[144,384]{1,0:T(8,128)(2,1)S(1)} %get-tuple-element.22), channel_id=1, source_target_pairs={{0,2},{2,0},{1,3},{3,1},{4,6},{6,4},{5,7},{7,5},{8,10},{10,8},{9,1... | collective-permute-start | bytes 331784 | tf_op jit(solution)/shard_map/ppermute | solution.py:150
  15.8 9.4 %collective-permute-start.12 = (bf16[4,128,128]{2,1,0:T(8,128)(2,1)S(1)}, bf16[4,128,128]{2,1,0:T(8,128)(2,1)S(1)}, u32[]{:S(2)}, u32[]{:S(2)}) collective-permute-start(bf16[4,128,128]{2,1,0:T(8,128)(2,1)S(1)} %get-tuple-element.27), channel_id=1, source_target_pairs={{0,2},{2,0},{1,3},{3,1},{4,6},{6,4},{5,7},{7,5},{8,10},{10,8},{9,1... | collective-permute-start | bytes 393224 | tf_op jit(solution)/shard_map/ppermute | solution.py:150
  21.4 6.7 %collective-permute-start.10 = (bf16[256,128]{1,0:T(8,128)(2,1)S(1)}, bf16[256,128]{1,0:T(8,128)(2,1)S(1)}, u32[]{:S(2)}, u32[]{:S(2)}) collective-permute-start(bf16[256,128]{1,0:T(8,128)(2,1)S(1)} %get-tuple-element.25.own_ref), channel_id=1, source_target_pairs={{0,8},{4,12},{8,0},{12,4},{1,9},{5,13},{9,1},{13,5},{2,10},{6,14},... | collective-permute-start | bytes 196616 | tf_op jit(solution)/shard_map/ppermute | solution.py:411
  23.1 5.3 %collective-permute-start.11 = (bf16[256,128]{1,0:T(8,128)(2,1)S(1)}, bf16[256,128]{1,0:T(8,128)(2,1)S(1)}, u32[]{:S(2)}, u32[]{:S(2)}) collective-permute-start(bf16[256,128]{1,0:T(8,128)(2,1)S(1)} %get-tuple-element.25.own_ref), channel_id=1, source_target_pairs={{0,12},{4,0},{8,4},{12,8},{1,13},{5,1},{9,5},{13,9},{2,14},{6,2},{... | collective-permute-start | bytes 196616 | tf_op jit(solution)/shard_map/ppermute | solution.py:411
  24.4 6.1 %collective-permute-start.9 = (bf16[256,128]{1,0:T(8,128)(2,1)S(1)}, bf16[256,128]{1,0:T(8,128)(2,1)S(1)}, u32[]{:S(2)}, u32[]{:S(2)}) collective-permute-start(bf16[256,128]{1,0:T(8,128)(2,1)S(1)} %get-tuple-element.25.own_ref), channel_id=1, source_target_pairs={{0,4},{4,8},{8,12},{12,0},{1,5},{5,9},{9,13},{13,1},{2,6},{6,10},{... | collective-permute-start | bytes 196616 | tf_op jit(solution)/shard_map/ppermute | solution.py:411
  31.2 4.0 %collective-permute-start.13 = (bf16[128,128]{1,0:T(8,128)(2,1)S(1)}, bf16[128,128]{1,0:T(8,128)(2,1)S(1)}, u32[]{:S(2)}, u32[]{:S(2)}) collective-permute-start(bf16[128,128]{1,0:T(8,128)(2,1)S(1)} %get-tuple-element.32), channel_id=1, source_target_pairs={{0,2},{2,0},{1,3},{3,1},{4,6},{6,4},{5,7},{7,5},{8,10},{10,8},{9,1... | collective-permute-start | bytes 98312 | tf_op jit(solution)/shard_map/ppermute | solution.py:150

commit v4 on v3

--- a/solution.py
+++ b/solution.py
@@ -10,7 +10,7 @@
 from jax.sharding import PartitionSpec as P
 
 HALO = 16
-PAD = 32
+LONG = pl.CostEstimate(flops=10_000_000_000, bytes_accessed=40_000_000, transcendentals=0)
 F32 = jnp.float32
 BF16 = jnp.bfloat16
 
@@ -186,35 +186,35 @@
     return jnp.concatenate(parts, axis=1)
 
 
-def project(rows, weight_ref, own_half, keep_ref, send_ref):
-    half = keep_ref.shape[1] // 3
-    for branch in range(3):
+def project(rows, weight_ref, branches, keep_ref, send_ref):
+    own_half = lax.axis_index("fsdp")
+    half = weight_ref.shape[2] // 2
+    for place, branch in enumerate(branches):
         summed = jnp.dot(rows, weight_ref[branch], preferred_element_type=F32)
         keep, send = split_channels(summed, own_half)
-        lanes = slice(branch * half, (branch + 1) * half)
+        lanes = slice(place * half, (place + 1) * half)
         keep_ref[:, lanes] = keep
-        send_ref[: send.shape[0], lanes] = send.astype(BF16)
+        send_ref[:, lanes] = send.astype(BF16)
 
 
 def project_first_body(rows_ref, cycled_ref, weight_ref, keep_ref, send_ref):
-    own_half = lax.axis_index("fsdp")
-    here = lax.axis_index("chan") == own_half
+    here = lax.axis_index("chan") == lax.axis_index("fsdp")
     rows = jnp.where(here, rows_ref[...], cycled_ref[...])
-    project(rows, weight_ref, own_half, keep_ref, send_ref)
+    project(rows, weight_ref, (0, 1, 2), keep_ref, send_ref)
 
 
 def project_second_body(
-    cycled_ref, hop_ref, pack_ref, pack_hop_ref, weight_ref, keep_ref, send_ref, done_ref
+    branches, cycled_ref, hop_ref, pack_ref, pack_hop_ref, weight_ref, keep_ref, send_ref, *done_refs
 ):
-    own_half = lax.axis_index("fsdp")
-    here = lax.axis_index("chan") == own_half
+    here = lax.axis_index("chan") == lax.axis_index("fsdp")
     pieces = cycled_ref.shape[1] // pack_ref.shape[1]
     rows = jnp.where(here, cycled_ref[...], hop_ref[...])
     halo = unpack_halo(jnp.where(here, pack_ref[...], pack_hop_ref[...]), pieces)
     halo = jnp.where(lax.axis_index("seq") > 0, halo, jnp.zeros_like(halo))
     rows = jnp.concatenate([halo, rows], axis=0)
-    project(rows, weight_ref, own_half, keep_ref, send_ref)
-    done_ref[...] = jnp.zeros_like(done_ref)
+    project(rows, weight_ref, branches, keep_ref, send_ref)
+    for done_ref in done_refs:
+        done_ref[...] = jnp.zeros_like(done_ref)
 
 
 def sort_taps_body(*refs):
@@ -269,29 +269,47 @@
         before_real, before_imag = (real, imag)
 
 
-def mix_body(keep_first, keep_second, got_first, got_second, short_ref, order_ref,
-             product_ref, query_ref, joined):
+def mixed_branches(branches, keep_first, keep_second, got_first, got_second, short_ref, joined):
     own = lax.axis_index("fsdp")
     rows = keep_first.shape[0]
-    half = keep_first.shape[1] // 3
+    half = keep_second.shape[1] // len(branches)
+    first_lanes = slice(branches[0] * half, (branches[-1] + 1) * half)
     joined[:HALO, :] = keep_second[:HALO, :] + got_second[:HALO, :].astype(F32)
     own_start = pl.multiple_of(HALO + own * rows, HALO)
     other_start = pl.multiple_of(HALO + (1 - own) * rows, HALO)
-    joined[pl.ds(own_start, rows), :] = keep_first[...] + got_second[HALO:, :].astype(F32)
-    joined[pl.ds(other_start, rows), :] = keep_second[HALO:, :] + got_first[:rows, :].astype(F32)
-    count = 2 * rows
+    joined[pl.ds(own_start, rows), :] = (
+        keep_first[:, first_lanes] + got_second[HALO:, :].astype(F32)
+    )
+    joined[pl.ds(other_start, rows), :] = (
+        keep_second[HALO:, :] + got_first[:, first_lanes].astype(F32)
+    )
     mixed = []
-    for branch in range(3):
-        lanes = slice(branch * half, (branch + 1) * half)
+    for place, branch in enumerate(branches):
+        lanes = slice(place * half, (place + 1) * half)
         total = None
         for tap in range(3):
             taps = short_ref[tap, branch : branch + 1, :]
             taps = jnp.where(own == 0, taps[:, :half], taps[:, half:])
-            term = taps * joined[pl.ds(HALO - tap, count), lanes]
+            term = taps * joined[pl.ds(HALO - tap, 2 * rows), lanes]
             total = term if total is None else total + term
         mixed.append(total)
-    query_ref[...] = mixed[0]
-    product_ref[...] = (mixed[1] * mixed[2]).astype(BF16)
+    return mixed
+
+
+def product_body(
+    keep_first, keep_second, got_first, got_second, short_ref, order_ref, product_ref, joined
+):
+    key, value = mixed_branches(
+        (1, 2), keep_first, keep_second, got_first, got_second, short_ref, joined
+    )
+    product_ref[...] = (key * value).astype(BF16)
+
+
+def query_body(keep_first, keep_second, got_first, got_second, short_ref, query_ref, joined):
+    (query,) = mixed_branches(
+        (0,), keep_first, keep_second, got_first, got_second, short_ref, joined
+    )
+    query_ref[...] = query
 
 
 def conv_body(own_ref, one_ref, two_ref, three_ref, real_ref, imag_ref, table_ref, turned_ref,
@@ -348,7 +366,7 @@
     token = shape((8, 128), F32)
     pack = call(
         pack_body,
-        cost_estimate=pl.CostEstimate(flops=10_000_000_000, bytes_accessed=40_000_000, transcendentals=0),
+        cost_estimate=LONG,
         in_specs=whole_specs(1),
         out_specs=whole_specs(1)[0],
         out_shape=shape((HALO, width), BF16),
@@ -371,23 +389,28 @@
     pack_hop = exchange(pack_got, "chan")
     keep_first, send_first = call(
         project_first_body,
-        cost_estimate=pl.CostEstimate(flops=10_000_000_000, bytes_accessed=40_000_000, transcendentals=0),
+        cost_estimate=LONG,
         in_specs=whole_specs(3),
         out_specs=whole_specs(2),
-        out_shape=(shape((rows, 3 * half), F32), shape((rows + PAD, 3 * half), BF16)),
+        out_shape=(shape((rows, 3 * half), F32), shape((rows, 3 * half), BF16)),
     )(tokens, cycled, weight)
     got_first = exchange(send_first, "fsdp")
-    keep_second, send_second, second_done = call(
-        project_second_body,
+    keep_product, send_product, second_done = call(
+        functools.partial(project_second_body, (1, 2)),
         in_specs=whole_specs(5),
         out_specs=whole_specs(3),
         out_shape=(
-            shape((HALO + rows, 3 * half), F32),
-            shape((HALO + rows, 3 * half), BF16),
+            shape((HALO + rows, 2 * half), F32),
+            shape((HALO + rows, 2 * half), BF16),
             token,
         ),
     )(cycled, hop, pack_got, pack_hop, weight)
-    got_second = exchange(send_second, "fsdp")
+    keep_query, send_query = call(
+        functools.partial(project_second_body, (0,)),
+        in_specs=whole_specs(5),
+        out_specs=whole_specs(2),
+        out_shape=(shape((HALO + rows, half), F32), shape((HALO + rows, half), BF16)),
+    )(cycled, hop, pack_got, pack_hop, weight)
     tap_keep, tap_send, tap_done = call(
         sort_taps_body,
         in_specs=whole_specs(1 + blocks),
@@ -398,16 +421,24 @@
             token,
         ),
     )(*tap_blocks, second_done)
+    got_product = exchange(send_product, "fsdp")
+    got_query = exchange(send_query, "fsdp")
+
+    product = call(
+        product_body,
+        in_specs=whole_specs(6),
+        out_specs=whole_specs(1)[0],
+        out_shape=shape((size, half), BF16),
+        scratch_shapes=[pltpu.VMEM((HALO + size, 2 * half), F32)],
+    )(keep_first, keep_product, got_first, got_product, short_weight, tap_done)
+    query = call(
+        query_body,
+        in_specs=whole_specs(5),
+        out_specs=whole_specs(1)[0],
+        out_shape=shape((size, half), F32),
+        scratch_shapes=[pltpu.VMEM((HALO + size, half), F32)],
+    )(keep_first, keep_query, got_first, got_query, short_weight)
     tap_got = exchange(tap_send, "fsdp")
-
-    product, query = call(
-        mix_body,
-        in_specs=whole_specs(6),
-        out_specs=whole_specs(2),
-        out_shape=(shape((size, half), BF16), shape((size, half), F32)),
-        scratch_shapes=[pltpu.VMEM((HALO + size, 3 * half), F32)],
-    )(keep_first, keep_second, got_first, got_second, short_weight, tap_done)
-
     products = [product] + [lax.ppermute(product, "seq", ring[step]) for step in range(1, blocks)]
     table = wave_table(size)
     forward = jnp.asarray(table, dtype=BF16)

time: 36 us -> 34.5 us (0.958)
  waiting for transfers between devices: 13.9 us -> 11 us
  starting transfers between devices: 16.9 us -> 18.1 us
    ppermute x3, waiting for transfers between devices: 4.92 us -> 0.35 us  [pair_mesh(): lax.ppermute(product, 'seq', ring[step])]
    ppermute x6 -> x7, waiting for transfers between devices: 8.94 us -> 10.6 us  [exchange(): return lax.ppermute(value, axis, [(0, 1), (1, 0)])]
    ppermute x6 -> x7, starting transfers between devices: 3.19 us -> 3.97 us  [exchange(): return lax.ppermute(value, axis, [(0, 1), (1, 0)])]
    ppermute x3, starting transfers between devices: 3.67 us -> 4.05 us  [pair_mesh(): lax.ppermute(product, 'seq', ring[step])]
    pallas_call x4 -> x6, Pallas kernels: 1.76 us -> 1.95 us  [the longest x1 0.59 us: pair_mesh(): call(functools.partial(project_second_body, (1, 2)), in_specs=whole_specs...]
  transfers between devices with their start and end apart: 14 -> 15, of which waited for: 7 -> 6; matrix products, arithmetic and copies ran while one was open for 0% -> 0% of each run, Pallas kernels for 6% -> 7%
where the time goes in v4:
time: 34.5 us; the launch traced here: 34.3 us
  starting transfers between devices  18.1 us (52%)
  waiting for transfers between devices  11 us (32%)
  Pallas kernels  3.79 us (11%)
  local copies, waits for them, and re-layouts  1.31 us (4%)
    ppermute x7, waiting for transfers between devices, exchange(): return lax.ppermute(value, axis, [(0, 1), (1, 0)])  10.6 us
    ppermute x3, starting transfers between devices, pair_mesh(): lax.ppermute(filter_taps, 'seq', ring[step])  5.51 us
    ppermute x1, starting transfers between devices, pair_mesh(): lax.ppermute(pack, ('seq', 'fsdp', 'chan'), [(4 * s + 2 * f + c, 4 * ((s...  4.09 us
    ppermute x3, starting transfers between devices, pair_mesh(): lax.ppermute(product, 'seq', ring[step])  4.05 us
    ppermute x7, starting transfers between devices, exchange(): return lax.ppermute(value, axis, [(0, 1), (1, 0)])  3.97 us
    unnamed x14, local copies, waits for them, and re-layouts  1.31 us
  transfers between devices with their start and end apart: 15, of which 6 were waited for; matrix products, arithmetic and copies ran while one was open for 0% of the time, Pallas kernels for 7%

profile of v4, /device:TPU:0, one launch (start us, length us, event | category | flops | bytes accessed | tf_op | source)
XLA Modules:
  0.0 34.3 jit_solution(2675589476530405836)
XLA Ops:
  0.0 0.5 %collective-permute-start = (bf16[128,2048]{1,0:T(8,128)(2,1)}, bf16[128,2048]{1,0:T(8,128)(2,1)S(1)}, u32[]{:S(2)}, u32[]{:S(2)}) collective-permute-start(bf16[128,2048]{1,0:T(8,128)(2,1)} %rows_ref.3), channel_id=1, source_target_pairs={{1,3},{3,2},{2,0},{0,1},{5,7},{7,6},{6,4},{4,5},{9,11},{11,10},{10... | collective-permute-start | bytes 1572872 | tf_op jit(solution)/shard_map/ppermute | solution.py:365
  0.5 1.3 %copy-done.6 = bf16[128,2048]{1,0:T(8,128)(2,1)S(1)} copy-done((bf16[128,2048]{1,0:T(8,128)(2,1)S(1)}, bf16[128,2048]{1,0:T(8,128)(2,1)}, u32[]{:S(2)}) %copy-start.6) | copy-done | bytes 524312
  1.7 0.1 shard_map.73
  1.9 4.1 %collective-permute-start.1 = (bf16[16,256]{1,0:T(8,128)(2,1)S(1)}, bf16[16,256]{1,0:T(8,128)(2,1)S(1)}, u32[]{:S(2)}, u32[]{:S(2)}) collective-permute-start(bf16[16,256]{1,0:T(8,128)(2,1)S(1)} %shard_map.73), channel_id=1, source_target_pairs={{0,6},{1,5},{2,4},{3,7},{4,10},{5,9},{6,8},{7,11},{8,14},{9,13},{1... | collective-permute-start | bytes 24584 | tf_op jit(solution)/shard_map/ppermute | solution.py:374
  6.0 1.6 %collective-permute-start.6 = (bf16[128,256]{1,0:T(8,128)(2,1)S(1)}, bf16[128,256]{1,0:T(8,128)(2,1)S(1)}, u32[]{:S(2)}, u32[]{:S(2)}) collective-permute-start(bf16[128,256]{1,0:T(8,128)(2,1)S(1)} %copy-done.3), channel_id=1, source_target_pairs={{0,4},{4,8},{8,12},{12,0},{1,5},{5,9},{9,13},{13,1},{2,6},{6,10},{... | collective-permute-start | bytes 196616 | tf_op jit(solution)/shard_map/ppermute | solution.py:385
  7.5 1.0 %collective-permute-start.7 = (bf16[128,256]{1,0:T(8,128)(2,1)S(1)}, bf16[128,256]{1,0:T(8,128)(2,1)S(1)}, u32[]{:S(2)}, u32[]{:S(2)}) collective-permute-start(bf16[128,256]{1,0:T(8,128)(2,1)S(1)} %copy-done.3), channel_id=1, source_target_pairs={{0,8},{4,12},{8,0},{12,4},{1,9},{5,13},{9,1},{13,5},{2,10},{6,14},... | collective-permute-start | bytes 196616 | tf_op jit(solution)/shard_map/ppermute | solution.py:385
  8.6 2.9 %collective-permute-start.8 = (bf16[128,256]{1,0:T(8,128)(2,1)S(1)}, bf16[128,256]{1,0:T(8,128)(2,1)S(1)}, u32[]{:S(2)}, u32[]{:S(2)}) collective-permute-start(bf16[128,256]{1,0:T(8,128)(2,1)S(1)} %copy-done.3), channel_id=1, source_target_pairs={{0,12},{4,0},{8,4},{12,8},{1,13},{5,1},{9,5},{13,9},{2,14},{6,2},{... | collective-permute-start | bytes 196616 | tf_op jit(solution)/shard_map/ppermute | solution.py:385
  11.5 0.5 %collective-permute-start.2 = (bf16[128,2048]{1,0:T(8,128)(2,1)S(1)}, bf16[128,2048]{1,0:T(8,128)(2,1)S(1)}, u32[]{:S(2)}, u32[]{:S(2)}) collective-permute-start(bf16[128,2048]{1,0:T(8,128)(2,1)S(1)} %shard_map.74.cycled_ref), channel_id=1, source_target_pairs={{0,1},{1,0},{2,3},{3,2},{4,5},{5,4},{6,7},{7,6},{8,9},{9,8},{10,11... | collective-permute-start | bytes 1572872 | tf_op jit(solution)/shard_map/ppermute | solution.py:150
  12.0 0.6 %shard_map.75 = (f32[128,384]{1,0:T(8,128)S(1)}, bf16[128,384]{1,0:T(8,128)(2,1)S(1)}) custom-call(bf16[128,2048]{1,0:T(8,128)(2,1)S(1)} %copy-done.6, bf16[128,2048]{1,0:T(8,128)(2,1)S(1)} %shard_map.74.cycled_ref, bf16[3,2048,256]{2,1,0:T(8,128)(2,1)S(1)} %bitcast.2), custom_call_target="tpu_custom_call" | custom-call | flops 10000000000 | bytes 40000000 | tf_op jit(solution)/shard_map/pallas_call | solution.py:390
  12.6 0.0 collective-permute-done.3.pack_hop_ref
  12.7 0.0 collective-permute-start.4
  12.7 0.8 %collective-permute-done.2.hop_ref = bf16[128,2048]{1,0:T(8,128)(2,1)S(1)} collective-permute-done((bf16[128,2048]{1,0:T(8,128)(2,1)S(1)}, bf16[128,2048]{1,0:T(8,128)(2,1)S(1)}, u32[]{:S(2)}, u32[]{:S(2)}) %collective-permute-start.2) | collective-permute-done | bytes 524320 | tf_op jit(solution)/shard_map/ppermute | solution.py:150
  13.5 0.6 %shard_map.76 = (f32[144,256]{1,0:T(8,128)S(1)}, bf16[144,256]{1,0:T(8,128)(2,1)S(1)}, f32[8,128]{1,0:T(8,128)S(1)}) custom-call(bf16[128,2048]{1,0:T(8,128)(2,1)S(1)} %shard_map.74.cycled_ref, bf16[128,2048]{1,0:T(8,128)(2,1)S(1)} %collective-permute-done.2.hop_ref, bf16[16,256]{1,0:T(8,128)(2,1)S(1)} %collective-permute-done.1.refs_1_.pack_ref, ...), custom_call_target="tpu_custom_call" | custom-call | tf_op jit(solution)/shard_map/pallas_call | solution.py:398
  14.2 1.2 %collective-permute-start.5 = (bf16[144,256]{1,0:T(8,128)(2,1)S(1)}, bf16[144,256]{1,0:T(8,128)(2,1)S(1)}, u32[]{:S(2)}, u32[]{:S(2)}) collective-permute-start(bf16[144,256]{1,0:T(8,128)(2,1)S(1)} %get-tuple-element.22), channel_id=1, source_target_pairs={{0,2},{2,0},{1,3},{3,1},{4,6},{6,4},{5,7},{7,5},{8,10},{10,8},{9,1... | collective-permute-start | bytes 221192 | tf_op jit(solution)/shard_map/ppermute | solution.py:150
  15.4 0.1 shard_map.77
  15.5 0.9 %collective-permute-start.12 = (bf16[4,128,128]{2,1,0:T(8,128)(2,1)S(1)}, bf16[4,128,128]{2,1,0:T(8,128)(2,1)S(1)}, u32[]{:S(2)}, u32[]{:S(2)}) collective-permute-start(bf16[4,128,128]{2,1,0:T(8,128)(2,1)S(1)} %get-tuple-element.26), channel_id=1, source_target_pairs={{0,2},{2,0},{1,3},{3,1},{4,6},{6,4},{5,7},{7,5},{8,10},{10,8},{9,1... | collective-permute-start | bytes 393224 | tf_op jit(solution)/shard_map/ppermute | solution.py:150
  16.4 1.4 %collective-permute-done.4.got_first = bf16[128,384]{1,0:T(8,128)(2,1)S(1)} collective-permute-done((bf16[128,384]{1,0:T(8,128)(2,1)S(1)}, bf16[128,384]{1,0:T(8,128)(2,1)S(1)}, u32[]{:S(2)}, u32[]{:S(2)}) %collective-permute-start.4) | collective-permute-done | bytes 98336 | tf_op jit(solution)/shard_map/ppermute | solution.py:150
  17.8 1.6 %collective-permute-done.5.got_second = bf16[144,256]{1,0:T(8,128)(2,1)S(1)} collective-permute-done((bf16[144,256]{1,0:T(8,128)(2,1)S(1)}, bf16[144,256]{1,0:T(8,128)(2,1)S(1)}, u32[]{:S(2)}, u32[]{:S(2)}) %collective-permute-start.5) | collective-permute-done | bytes 73760 | tf_op jit(solution)/shard_map/ppermute | solution.py:150
  19.4 0.1 shard_map.78.own_ref
  19.6 2.0 %collective-permute-start.10 = (bf16[256,128]{1,0:T(8,128)(2,1)S(1)}, bf16[256,128]{1,0:T(8,128)(2,1)S(1)}, u32[]{:S(2)}, u32[]{:S(2)}) collective-permute-start(bf16[256,128]{1,0:T(8,128)(2,1)S(1)} %shard_map.78.own_ref), channel_id=1, source_target_pairs={{0,8},{4,12},{8,0},{12,4},{1,9},{5,13},{9,1},{13,5},{2,10},{6,14},... | collective-permute-start | bytes 196616 | tf_op jit(solution)/shard_map/ppermute | solution.py:442
  21.6 1.3 %collective-permute-start.11 = (bf16[256,128]{1,0:T(8,128)(2,1)S(1)}, bf16[256,128]{1,0:T(8,128)(2,1)S(1)}, u32[]{:S(2)}, u32[]{:S(2)}) collective-permute-start(bf16[256,128]{1,0:T(8,128)(2,1)S(1)} %shard_map.78.own_ref), channel_id=1, source_target_pairs={{0,12},{4,0},{8,4},{12,8},{1,13},{5,1},{9,5},{13,9},{2,14},{6,2},{... | collective-permute-start | bytes 196616 | tf_op jit(solution)/shard_map/ppermute | solution.py:442
  22.9 0.7 %collective-permute-start.9 = (bf16[256,128]{1,0:T(8,128)(2,1)S(1)}, bf16[256,128]{1,0:T(8,128)(2,1)S(1)}, u32[]{:S(2)}, u32[]{:S(2)}) collective-permute-start(bf16[256,128]{1,0:T(8,128)(2,1)S(1)} %shard_map.78.own_ref), channel_id=1, source_target_pairs={{0,4},{4,8},{8,12},{12,0},{1,5},{5,9},{9,13},{13,1},{2,6},{6,10},{... | collective-permute-start | bytes 196616 | tf_op jit(solution)/shard_map/ppermute | solution.py:442
  23.6 0.4 %shard_map.80 = (f32[144,128]{1,0:T(8,128)S(1)}, bf16[144,128]{1,0:T(8,128)(2,1)S(1)}) custom-call(bf16[128,2048]{1,0:T(8,128)(2,1)S(1)} %shard_map.74.cycled_ref, bf16[128,2048]{1,0:T(8,128)(2,1)S(1)} %collective-permute-done.2.hop_ref, bf16[16,256]{1,0:T(8,128)(2,1)S(1)} %collective-permute-done.1.refs_1_.pack_ref, ...), custom_call_target="tpu_custom_call" | custom-call | tf_op jit(solution)/shard_map/pallas_call | solution.py:408
  24.1 0.6 %collective-permute-start.13 = (bf16[144,128]{1,0:T(8,128)(2,1)S(1)}, bf16[144,128]{1,0:T(8,128)(2,1)S(1)}, u32[]{:S(2)}, u32[]{:S(2)}) collective-permute-start(bf16[144,128]{1,0:T(8,128)(2,1)S(1)} %get-tuple-element.30), channel_id=1, source_target_pairs={{0,2},{2,0},{1,3},{3,1},{4,6},{6,4},{5,7},{7,5},{8,10},{10,8},{9,1... | collective-permute-start | bytes 110600 | tf_op jit(solution)/shard_map/ppermute | solution.py:150
  24.7 3.4 %collective-permute-done.13.got_second = bf16[144,128]{1,0:T(8,128)(2,1)S(1)} collective-permute-done((bf16[144,128]{1,0:T(8,128)(2,1)S(1)}, bf16[144,128]{1,0:T(8,128)(2,1)S(1)}, u32[]{:S(2)}, u32[]{:S(2)}) %collective-permute-start.13) | collective-permute-done | bytes 36896 | tf_op jit(solution)/shard_map/ppermute | solution.py:150
  28.1 0.1 shard_map.81.query_ref
  28.2 0.5 %shard_map.79 = (f32[4,256,128]{2,1,0:T(8,128)S(1)}, f32[4,256,128]{2,1,0:T(8,128)S(1)}) custom-call(bf16[512,256]{1,0:T(8,128)(2,1)S(1)} %copy-done.1, bf16[4,128,128]{2,1,0:T(8,128)(2,1)S(1)} %get-tuple-element.25.keep_ref, bf16[4,128,128]{2,1,0:T(8,128)(2,1)S(1)} %collective-permute-done.12.got_ref), custom_call_target="tpu_custom_call" | custom-call | tf_op jit(solution)/shard_map/pallas_call | solution.py:446
  28.7 0.3 %collective-permute-done.9.one_ref = bf16[256,128]{1,0:T(8,128)(2,1)S(1)} collective-permute-done((bf16[256,128]{1,0:T(8,128)(2,1)S(1)}, bf16[256,128]{1,0:T(8,128)(2,1)S(1)}, u32[]{:S(2)}, u32[]{:S(2)}) %collective-permute-start.9) | collective-permute-done | bytes 65568 | tf_op jit(solution)/shard_map/ppermute | solution.py:442
  29.0 0.7 %shard_map.82 = (bf16[128,128]{1,0:T(8,128)(2,1)S(1)}, bf16[128,128]{1,0:T(8,128)(2,1)S(1)}) custom-call(bf16[256,128]{1,0:T(8,128)(2,1)S(1)} %shard_map.78.own_ref, bf16[256,128]{1,0:T(8,128)(2,1)S(1)} %collective-permute-done.9.one_ref, bf16[256,128]{1,0:T(8,128)(2,1)S(1)} %collective-permute-done.10.two_ref, ...), custom_call_target="tpu_custom_call" | custom-call | tf_op jit(solution)/shard_map/pallas_call | solution.py:452
  29.7 0.6 %collective-permute-start.14 = (bf16[128,128]{1,0:T(8,128)(2,1)S(1)}, bf16[128,128]{1,0:T(8,128)(2,1)S(1)}, u32[]{:S(2)}, u32[]{:S(2)}) collective-permute-start(bf16[128,128]{1,0:T(8,128)(2,1)S(1)} %get-tuple-element.32), channel_id=1, source_target_pairs={{0,2},{2,0},{1,3},{3,1},{4,6},{6,4},{5,7},{7,5},{8,10},{10,8},{9,1... | collective-permute-start | bytes 98312 | tf_op jit(solution)/shard_map/ppermute | solution.py:150
  30.3 3.4 %collective-permute-done.14.got_ref = bf16[128,128]{1,0:T(8,128)(2,1)S(1)} collective-permute-done((bf16[128,128]{1,0:T(8,128)(2,1)S(1)}, bf16[128,128]{1,0:T(8,128)(2,1)S(1)}, u32[]{:S(2)}, u32[]{:S(2)}) %collective-permute-start.14) | collective-permute-done | bytes 32800 | tf_op jit(solution)/shard_map/ppermute | solution.py:150
  33.7 0.6 %shard_map.83 = bf16[128,256]{1,0:T(8,128)(2,1)} custom-call(bf16[128,128]{1,0:T(8,128)(2,1)S(1)} %get-tuple-element.31.stay_ref, bf16[128,128]{1,0:T(8,128)(2,1)S(1)} %collective-permute-done.14.got_ref), custom_call_target="tpu_custom_call" | custom-call | tf_op jit(solution)/shard_map/pallas_call | solution.py:460
  (23 shorter events, 0.1 us)
Async XLA Ops:
  0.0 6.0 %copy-start.3 = (bf16[128,256]{1,0:T(8,128)(2,1)S(1)}, bf16[128,256]{1,0:T(8,128)(2,1)}, u32[]{:S(2)}) copy-start(bf16[128,256]{1,0:T(8,128)(2,1)} %refs_0_.1) | copy-start | bytes 196612
  0.0 12.0 %copy-start = (bf16[2048,3,256]{2,0,1:T(8,128)(2,1)S(1)}, bf16[2048,3,256]{2,0,1:T(8,128)(2,1)}, u32[]{:S(2)}) copy-start(bf16[2048,3,256]{2,0,1:T(8,128)(2,1)} %param.8) | copy-start | bytes 9437188
  0.0 11.5 %collective-permute-start = (bf16[128,2048]{1,0:T(8,128)(2,1)}, bf16[128,2048]{1,0:T(8,128)(2,1)S(1)}, u32[]{:S(2)}, u32[]{:S(2)}) collective-permute-start(bf16[128,2048]{1,0:T(8,128)(2,1)} %rows_ref.3), channel_id=1, source_target_pairs={{1,3},{3,2},{2,0},{0,1},{5,7},{7,6},{6,4},{4,5},{9,11},{11,10},{10... | collective-permute-start | bytes 1572872 | tf_op jit(solution)/shard_map/ppermute | solution.py:365
  0.5 1.3 %copy-start.6 = (bf16[128,2048]{1,0:T(8,128)(2,1)S(1)}, bf16[128,2048]{1,0:T(8,128)(2,1)}, u32[]{:S(2)}) copy-start(bf16[128,2048]{1,0:T(8,128)(2,1)} %rows_ref.3) | copy-start | bytes 1572868
  1.9 9.6 %collective-permute-start.1 = (bf16[16,256]{1,0:T(8,128)(2,1)S(1)}, bf16[16,256]{1,0:T(8,128)(2,1)S(1)}, u32[]{:S(2)}, u32[]{:S(2)}) collective-permute-start(bf16[16,256]{1,0:T(8,128)(2,1)S(1)} %shard_map.73), channel_id=1, source_target_pairs={{0,6},{1,5},{2,4},{3,7},{4,10},{5,9},{6,8},{7,11},{8,14},{9,13},{1... | collective-permute-start | bytes 24584 | tf_op jit(solution)/shard_map/ppermute | solution.py:374
  6.0 9.5 %collective-permute-start.6 = (bf16[128,256]{1,0:T(8,128)(2,1)S(1)}, bf16[128,256]{1,0:T(8,128)(2,1)S(1)}, u32[]{:S(2)}, u32[]{:S(2)}) collective-permute-start(bf16[128,256]{1,0:T(8,128)(2,1)S(1)} %copy-done.3), channel_id=1, source_target_pairs={{0,4},{4,8},{8,12},{12,0},{1,5},{5,9},{9,13},{13,1},{2,6},{6,10},{... | collective-permute-start | bytes 196616 | tf_op jit(solution)/shard_map/ppermute | solution.py:385
  7.5 7.9 %collective-permute-start.7 = (bf16[128,256]{1,0:T(8,128)(2,1)S(1)}, bf16[128,256]{1,0:T(8,128)(2,1)S(1)}, u32[]{:S(2)}, u32[]{:S(2)}) collective-permute-start(bf16[128,256]{1,0:T(8,128)(2,1)S(1)} %copy-done.3), channel_id=1, source_target_pairs={{0,8},{4,12},{8,0},{12,4},{1,9},{5,13},{9,1},{13,5},{2,10},{6,14},... | collective-permute-start | bytes 196616 | tf_op jit(solution)/shard_map/ppermute | solution.py:385
  8.6 6.9 %collective-permute-start.8 = (bf16[128,256]{1,0:T(8,128)(2,1)S(1)}, bf16[128,256]{1,0:T(8,128)(2,1)S(1)}, u32[]{:S(2)}, u32[]{:S(2)}) collective-permute-start(bf16[128,256]{1,0:T(8,128)(2,1)S(1)} %copy-done.3), channel_id=1, source_target_pairs={{0,12},{4,0},{8,4},{12,8},{1,13},{5,1},{9,5},{13,9},{2,14},{6,2},{... | collective-permute-start | bytes 196616 | tf_op jit(solution)/shard_map/ppermute | solution.py:385
  11.5 1.2 %collective-permute-start.3 = (bf16[16,256]{1,0:T(8,128)(2,1)S(1)}, bf16[16,256]{1,0:T(8,128)(2,1)S(1)}, u32[]{:S(2)}, u32[]{:S(2)}) collective-permute-start(bf16[16,256]{1,0:T(8,128)(2,1)S(1)} %collective-permute-done.1.refs_1_.pack_ref), channel_id=1, source_target_pairs={{0,1},{1,0},{2,3},{3,2},{4,5},{5,4},{6,7},{7,6},{8,9},{9,8},{10,11... | collective-permute-start | bytes 24584 | tf_op jit(solution)/shard_map/ppermute | solution.py:150
  11.5 2.0 %collective-permute-start.2 = (bf16[128,2048]{1,0:T(8,128)(2,1)S(1)}, bf16[128,2048]{1,0:T(8,128)(2,1)S(1)}, u32[]{:S(2)}, u32[]{:S(2)}) collective-permute-start(bf16[128,2048]{1,0:T(8,128)(2,1)S(1)} %shard_map.74.cycled_ref), channel_id=1, source_target_pairs={{0,1},{1,0},{2,3},{3,2},{4,5},{5,4},{6,7},{7,6},{8,9},{9,8},{10,11... | collective-permute-start | bytes 1572872 | tf_op jit(solution)/shard_map/ppermute | solution.py:150
  12.6 6.8 %copy-start.4 = (f32[3,3,256]{2,1,0:T(4,128)S(1)}, f32[3,3,256]{2,1,0:T(4,128)}, u32[]{:S(2)}) copy-start(f32[3,3,256]{2,1,0:T(4,128)} %short_ref.3) | copy-start | bytes 27652
  12.7 5.2 %collective-permute-start.4 = (bf16[128,384]{1,0:T(8,128)(2,1)S(1)}, bf16[128,384]{1,0:T(8,128)(2,1)S(1)}, u32[]{:S(2)}, u32[]{:S(2)}) collective-permute-start(bf16[128,384]{1,0:T(8,128)(2,1)S(1)} %get-tuple-element.21), channel_id=1, source_target_pairs={{0,2},{2,0},{1,3},{3,1},{4,6},{6,4},{5,7},{7,5},{8,10},{10,8},{9,1... | collective-permute-start | bytes 294920 | tf_op jit(solution)/shard_map/ppermute | solution.py:150
  14.1 14.0 %copy-start.1 = (bf16[512,256]{1,0:T(8,128)(2,1)S(1)}, bf16[512,256]{1,0:T(8,128)(2,1)}, u32[]{:S(2)}) copy-start(bf16[512,256]{1,0:T(8,128)(2,1)} %constant.4.clone.table_ref) | copy-start | bytes 786436
  14.1 14.9 %copy-start.2 = (bf16[256,512]{1,0:T(8,128)(2,1)S(1)}, bf16[256,512]{1,0:T(8,128)(2,1)}, u32[]{:S(2)}) copy-start(bf16[256,512]{1,0:T(8,128)(2,1)} %constant.5.clone.turned_ref) | copy-start | bytes 786436
  14.2 14.8 %copy-start.5 = (f32[256]{0:T(256)S(1)}, f32[256]{0:T(256)}, u32[]{:S(2)}) copy-start(f32[256]{0:T(256)} %param.10) | copy-start | bytes 3076
  14.2 5.3 %collective-permute-start.5 = (bf16[144,256]{1,0:T(8,128)(2,1)S(1)}, bf16[144,256]{1,0:T(8,128)(2,1)S(1)}, u32[]{:S(2)}, u32[]{:S(2)}) collective-permute-start(bf16[144,256]{1,0:T(8,128)(2,1)S(1)} %get-tuple-element.22), channel_id=1, source_target_pairs={{0,2},{2,0},{1,3},{3,1},{4,6},{6,4},{5,7},{7,5},{8,10},{10,8},{9,1... | collective-permute-start | bytes 221192 | tf_op jit(solution)/shard_map/ppermute | solution.py:150
  15.5 12.7 %collective-permute-start.12 = (bf16[4,128,128]{2,1,0:T(8,128)(2,1)S(1)}, bf16[4,128,128]{2,1,0:T(8,128)(2,1)S(1)}, u32[]{:S(2)}, u32[]{:S(2)}) collective-permute-start(bf16[4,128,128]{2,1,0:T(8,128)(2,1)S(1)} %get-tuple-element.26), channel_id=1, source_target_pairs={{0,2},{2,0},{1,3},{3,1},{4,6},{6,4},{5,7},{7,5},{8,10},{10,8},{9,1... | collective-permute-start | bytes 393224 | tf_op jit(solution)/shard_map/ppermute | solution.py:150
  19.6 9.1 %collective-permute-start.10 = (bf16[256,128]{1,0:T(8,128)(2,1)S(1)}, bf16[256,128]{1,0:T(8,128)(2,1)S(1)}, u32[]{:S(2)}, u32[]{:S(2)}) collective-permute-start(bf16[256,128]{1,0:T(8,128)(2,1)S(1)} %shard_map.78.own_ref), channel_id=1, source_target_pairs={{0,8},{4,12},{8,0},{12,4},{1,9},{5,13},{9,1},{13,5},{2,10},{6,14},... | collective-permute-start | bytes 196616 | tf_op jit(solution)/shard_map/ppermute | solution.py:442
  21.6 7.1 %collective-permute-start.11 = (bf16[256,128]{1,0:T(8,128)(2,1)S(1)}, bf16[256,128]{1,0:T(8,128)(2,1)S(1)}, u32[]{:S(2)}, u32[]{:S(2)}) collective-permute-start(bf16[256,128]{1,0:T(8,128)(2,1)S(1)} %shard_map.78.own_ref), channel_id=1, source_target_pairs={{0,12},{4,0},{8,4},{12,8},{1,13},{5,1},{9,5},{13,9},{2,14},{6,2},{... | collective-permute-start | bytes 196616 | tf_op jit(solution)/shard_map/ppermute | solution.py:442
  22.9 6.1 %collective-permute-start.9 = (bf16[256,128]{1,0:T(8,128)(2,1)S(1)}, bf16[256,128]{1,0:T(8,128)(2,1)S(1)}, u32[]{:S(2)}, u32[]{:S(2)}) collective-permute-start(bf16[256,128]{1,0:T(8,128)(2,1)S(1)} %shard_map.78.own_ref), channel_id=1, source_target_pairs={{0,4},{4,8},{8,12},{12,0},{1,5},{5,9},{9,13},{13,1},{2,6},{6,10},{... | collective-permute-start | bytes 196616 | tf_op jit(solution)/shard_map/ppermute | solution.py:442
  24.1 4.0 %collective-permute-start.13 = (bf16[144,128]{1,0:T(8,128)(2,1)S(1)}, bf16[144,128]{1,0:T(8,128)(2,1)S(1)}, u32[]{:S(2)}, u32[]{:S(2)}) collective-permute-start(bf16[144,128]{1,0:T(8,128)(2,1)S(1)} %get-tuple-element.30), channel_id=1, source_target_pairs={{0,2},{2,0},{1,3},{3,1},{4,6},{6,4},{5,7},{7,5},{8,10},{10,8},{9,1... | collective-permute-start | bytes 110600 | tf_op jit(solution)/shard_map/ppermute | solution.py:150
  29.7 4.0 %collective-permute-start.14 = (bf16[128,128]{1,0:T(8,128)(2,1)S(1)}, bf16[128,128]{1,0:T(8,128)(2,1)S(1)}, u32[]{:S(2)}, u32[]{:S(2)}) collective-permute-start(bf16[128,128]{1,0:T(8,128)(2,1)S(1)} %get-tuple-element.32), channel_id=1, source_target_pairs={{0,2},{2,0},{1,3},{3,1},{4,6},{6,4},{5,7},{7,5},{8,10},{10,8},{9,1... | collective-permute-start | bytes 98312 | tf_op jit(solution)/shard_map/ppermute | solution.py:150

commit v5 on v4

--- a/solution.py
+++ b/solution.py
@@ -194,7 +194,7 @@
         keep, send = split_channels(summed, own_half)
         lanes = slice(place * half, (place + 1) * half)
         keep_ref[:, lanes] = keep
-        send_ref[:, lanes] = send.astype(BF16)
+        send_ref[:, lanes] = send.astype(send_ref.dtype)
 
 
 def project_first_body(rows_ref, cycled_ref, weight_ref, keep_ref, send_ref):
@@ -320,12 +320,14 @@
     total_real = total_imag = None
     for step, block_ref in enumerate((own_ref, one_ref, two_ref, three_ref)):
         block = block_ref[...]
+        source = position ^ step
+        back = jnp.maximum(position - source, 0)
         if step:
-            block = jnp.where(position >= step, block, jnp.zeros_like(block))
+            block = jnp.where(source < position, block, jnp.zeros_like(block))
         waves = jnp.dot(table_ref[...], block, preferred_element_type=F32)
         real, imag = (waves[:size], -waves[size:])
-        term_real = real * real_ref[step] - imag * imag_ref[step]
-        term_imag = real * imag_ref[step] + imag * real_ref[step]
+        term_real = real * real_ref[back] - imag * imag_ref[back]
+        term_imag = real * imag_ref[back] + imag * real_ref[back]
         total_real = term_real if total_real is None else total_real + term_real
         total_imag = term_imag if total_imag is None else total_imag + term_imag
     stacked = jnp.concatenate([total_real, -total_imag], axis=0).astype(BF16)
@@ -409,7 +411,7 @@
         functools.partial(project_second_body, (0,)),
         in_specs=whole_specs(5),
         out_specs=whole_specs(2),
-        out_shape=(shape((HALO + rows, half), F32), shape((HALO + rows, half), BF16)),
+        out_shape=(shape((HALO + rows, half), F32), shape((HALO + rows, half), F32)),
     )(cycled, hop, pack_got, pack_hop, weight)
     tap_keep, tap_send, tap_done = call(
         sort_taps_body,
@@ -439,7 +441,7 @@
         scratch_shapes=[pltpu.VMEM((HALO + size, half), F32)],
     )(keep_first, keep_query, got_first, got_query, short_weight)
     tap_got = exchange(tap_send, "fsdp")
-    products = [product] + [lax.ppermute(product, "seq", ring[step]) for step in range(1, blocks)]
+    products = [product] + [lax.ppermute(product, "seq", [(s, s ^ step) for s in range(blocks)]) for step in range(1, blocks)]
     table = wave_table(size)
     forward = jnp.asarray(table, dtype=BF16)
     inverse = jnp.asarray(table.T, dtype=BF16)

time: 34.5 us -> 33.4 us (0.968)
  waiting for transfers between devices: 11 us -> 9.94 us
    ppermute x7, waiting for transfers between devices: 10.6 us -> 5.95 us  [exchange(): return lax.ppermute(value, axis, [(0, 1), (1, 0)])]
    ppermute x3, waiting for transfers between devices: 0.35 us -> 3.98 us  [pair_mesh(): lax.ppermute(product, 'seq', [(s, s ^ step) for s in range(blocks)])]
    ppermute x7, starting transfers between devices: 3.97 us -> 4.47 us  [exchange(): return lax.ppermute(value, axis, [(0, 1), (1, 0)])]
    ppermute x3, starting transfers between devices: 4.05 us -> 3.61 us  [pair_mesh(): lax.ppermute(product, 'seq', [(s, s ^ step) for s in range(blocks)])]
  transfers between devices with their start and end apart: 15 -> 15, of which waited for: 6 -> 8; matrix products, arithmetic and copies ran while one was open for 0% -> 0% of each run, Pallas kernels for 7% -> 7%
where the time goes in v5:
time: 33.4 us; the launch traced here: 33.3 us
  starting transfers between devices  18.1 us (54%)
  waiting for transfers between devices  9.94 us (30%)
  Pallas kernels  3.77 us (11%)
  local copies, waits for them, and re-layouts  1.31 us (4%)
    ppermute x7, waiting for transfers between devices, exchange(): return lax.ppermute(value, axis, [(0, 1), (1, 0)])  5.95 us
    ppermute x3, starting transfers between devices, pair_mesh(): lax.ppermute(filter_taps, 'seq', ring[step])  5.51 us
    ppermute x7, starting transfers between devices, exchange(): return lax.ppermute(value, axis, [(0, 1), (1, 0)])  4.47 us
    ppermute x1, starting transfers between devices, pair_mesh(): lax.ppermute(pack, ('seq', 'fsdp', 'chan'), [(4 * s + 2 * f + c, 4 * ((s...  4.09 us
    ppermute x3, waiting for transfers between devices, pair_mesh(): lax.ppermute(product, 'seq', [(s, s ^ step) for s in range(blocks)])  3.98 us
    ppermute x3, starting transfers between devices, pair_mesh(): lax.ppermute(product, 'seq', [(s, s ^ step) for s in range(blocks)])  3.61 us
    unnamed x14, local copies, waits for them, and re-layouts  1.31 us
  transfers between devices with their start and end apart: 15, of which 8 were waited for; matrix products, arithmetic and copies ran while one was open for 0% of the time, Pallas kernels for 7%

profile of v5, /device:TPU:0, one launch (start us, length us, event | category | flops | bytes accessed | tf_op | source)
XLA Modules:
  0.0 33.3 jit_solution(13848793406619574066)
XLA Ops:
  0.0 0.5 %collective-permute-start = (bf16[128,2048]{1,0:T(8,128)(2,1)}, bf16[128,2048]{1,0:T(8,128)(2,1)S(1)}, u32[]{:S(2)}, u32[]{:S(2)}) collective-permute-start(bf16[128,2048]{1,0:T(8,128)(2,1)} %rows_ref.3), channel_id=1, source_target_pairs={{1,3},{3,2},{2,0},{0,1},{5,7},{7,6},{6,4},{4,5},{9,11},{11,10},{10... | collective-permute-start | bytes 1572872 | tf_op jit(solution)/shard_map/ppermute | solution.py:367
  0.5 1.3 %copy-done.6 = bf16[128,2048]{1,0:T(8,128)(2,1)S(1)} copy-done((bf16[128,2048]{1,0:T(8,128)(2,1)S(1)}, bf16[128,2048]{1,0:T(8,128)(2,1)}, u32[]{:S(2)}) %copy-start.6) | copy-done | bytes 524312
  1.7 0.1 shard_map.73
  1.9 4.1 %collective-permute-start.1 = (bf16[16,256]{1,0:T(8,128)(2,1)S(1)}, bf16[16,256]{1,0:T(8,128)(2,1)S(1)}, u32[]{:S(2)}, u32[]{:S(2)}) collective-permute-start(bf16[16,256]{1,0:T(8,128)(2,1)S(1)} %shard_map.73), channel_id=1, source_target_pairs={{0,6},{1,5},{2,4},{3,7},{4,10},{5,9},{6,8},{7,11},{8,14},{9,13},{1... | collective-permute-start | bytes 24584 | tf_op jit(solution)/shard_map/ppermute | solution.py:376
  6.0 1.6 %collective-permute-start.6 = (bf16[128,256]{1,0:T(8,128)(2,1)S(1)}, bf16[128,256]{1,0:T(8,128)(2,1)S(1)}, u32[]{:S(2)}, u32[]{:S(2)}) collective-permute-start(bf16[128,256]{1,0:T(8,128)(2,1)S(1)} %copy-done.3), channel_id=1, source_target_pairs={{0,4},{4,8},{8,12},{12,0},{1,5},{5,9},{9,13},{13,1},{2,6},{6,10},{... | collective-permute-start | bytes 196616 | tf_op jit(solution)/shard_map/ppermute | solution.py:387
  7.5 1.0 %collective-permute-start.7 = (bf16[128,256]{1,0:T(8,128)(2,1)S(1)}, bf16[128,256]{1,0:T(8,128)(2,1)S(1)}, u32[]{:S(2)}, u32[]{:S(2)}) collective-permute-start(bf16[128,256]{1,0:T(8,128)(2,1)S(1)} %copy-done.3), channel_id=1, source_target_pairs={{0,8},{4,12},{8,0},{12,4},{1,9},{5,13},{9,1},{13,5},{2,10},{6,14},... | collective-permute-start | bytes 196616 | tf_op jit(solution)/shard_map/ppermute | solution.py:387
  8.6 2.9 %collective-permute-start.8 = (bf16[128,256]{1,0:T(8,128)(2,1)S(1)}, bf16[128,256]{1,0:T(8,128)(2,1)S(1)}, u32[]{:S(2)}, u32[]{:S(2)}) collective-permute-start(bf16[128,256]{1,0:T(8,128)(2,1)S(1)} %copy-done.3), channel_id=1, source_target_pairs={{0,12},{4,0},{8,4},{12,8},{1,13},{5,1},{9,5},{13,9},{2,14},{6,2},{... | collective-permute-start | bytes 196616 | tf_op jit(solution)/shard_map/ppermute | solution.py:387
  11.5 0.5 %collective-permute-start.2 = (bf16[128,2048]{1,0:T(8,128)(2,1)S(1)}, bf16[128,2048]{1,0:T(8,128)(2,1)S(1)}, u32[]{:S(2)}, u32[]{:S(2)}) collective-permute-start(bf16[128,2048]{1,0:T(8,128)(2,1)S(1)} %shard_map.74.cycled_ref), channel_id=1, source_target_pairs={{0,1},{1,0},{2,3},{3,2},{4,5},{5,4},{6,7},{7,6},{8,9},{9,8},{10,11... | collective-permute-start | bytes 1572872 | tf_op jit(solution)/shard_map/ppermute | solution.py:150
  12.0 0.6 %shard_map.75 = (f32[128,384]{1,0:T(8,128)S(1)}, bf16[128,384]{1,0:T(8,128)(2,1)S(1)}) custom-call(bf16[128,2048]{1,0:T(8,128)(2,1)S(1)} %copy-done.6, bf16[128,2048]{1,0:T(8,128)(2,1)S(1)} %shard_map.74.cycled_ref, bf16[3,2048,256]{2,1,0:T(8,128)(2,1)S(1)} %bitcast.2), custom_call_target="tpu_custom_call" | custom-call | flops 10000000000 | bytes 40000000 | tf_op jit(solution)/shard_map/pallas_call | solution.py:392
  12.6 0.1 collective-permute-done.3.pack_hop_ref
  12.7 0.8 %collective-permute-done.2.hop_ref = bf16[128,2048]{1,0:T(8,128)(2,1)S(1)} collective-permute-done((bf16[128,2048]{1,0:T(8,128)(2,1)S(1)}, bf16[128,2048]{1,0:T(8,128)(2,1)S(1)}, u32[]{:S(2)}, u32[]{:S(2)}) %collective-permute-start.2) | collective-permute-done | bytes 524320 | tf_op jit(solution)/shard_map/ppermute | solution.py:150
  13.5 0.6 %shard_map.76 = (f32[144,256]{1,0:T(8,128)S(1)}, bf16[144,256]{1,0:T(8,128)(2,1)S(1)}, f32[8,128]{1,0:T(8,128)S(1)}) custom-call(bf16[128,2048]{1,0:T(8,128)(2,1)S(1)} %shard_map.74.cycled_ref, bf16[128,2048]{1,0:T(8,128)(2,1)S(1)} %collective-permute-done.2.hop_ref, bf16[16,256]{1,0:T(8,128)(2,1)S(1)} %collective-permute-done.1.refs_1_.pack_ref, ...), custom_call_target="tpu_custom_call" | custom-call | tf_op jit(solution)/shard_map/pallas_call | solution.py:400
  14.2 1.2 %collective-permute-start.5 = (bf16[144,256]{1,0:T(8,128)(2,1)S(1)}, bf16[144,256]{1,0:T(8,128)(2,1)S(1)}, u32[]{:S(2)}, u32[]{:S(2)}) collective-permute-start(bf16[144,256]{1,0:T(8,128)(2,1)S(1)} %get-tuple-element.22), channel_id=1, source_target_pairs={{0,2},{2,0},{1,3},{3,1},{4,6},{6,4},{5,7},{7,5},{8,10},{10,8},{9,1... | collective-permute-start | bytes 221192 | tf_op jit(solution)/shard_map/ppermute | solution.py:150
  15.4 0.1 shard_map.77
  15.5 0.9 %collective-permute-start.12 = (bf16[4,128,128]{2,1,0:T(8,128)(2,1)S(1)}, bf16[4,128,128]{2,1,0:T(8,128)(2,1)S(1)}, u32[]{:S(2)}, u32[]{:S(2)}) collective-permute-start(bf16[4,128,128]{2,1,0:T(8,128)(2,1)S(1)} %get-tuple-element.26), channel_id=1, source_target_pairs={{0,2},{2,0},{1,3},{3,1},{4,6},{6,4},{5,7},{7,5},{8,10},{10,8},{9,1... | collective-permute-start | bytes 393224 | tf_op jit(solution)/shard_map/ppermute | solution.py:150
  16.4 0.4 %shard_map.80 = (f32[144,128]{1,0:T(8,128)S(1)}, f32[144,128]{1,0:T(8,128)S(1)}) custom-call(bf16[128,2048]{1,0:T(8,128)(2,1)S(1)} %shard_map.74.cycled_ref, bf16[128,2048]{1,0:T(8,128)(2,1)S(1)} %collective-permute-done.2.hop_ref, bf16[16,256]{1,0:T(8,128)(2,1)S(1)} %collective-permute-done.1.refs_1_.pack_ref, ...), custom_call_target="tpu_custom_call" | custom-call | tf_op jit(solution)/shard_map/pallas_call | solution.py:410
  16.9 1.2 %collective-permute-start.13 = (f32[144,128]{1,0:T(8,128)S(1)}, f32[144,128]{1,0:T(8,128)S(1)}, u32[]{:S(2)}, u32[]{:S(2)}) collective-permute-start(f32[144,128]{1,0:T(8,128)S(1)} %get-tuple-element.30), channel_id=1, source_target_pairs={{0,2},{2,0},{1,3},{3,1},{4,6},{6,4},{5,7},{7,5},{8,10},{10,8},{9,1... | collective-permute-start | bytes 221192 | tf_op jit(solution)/shard_map/ppermute | solution.py:150
  18.1 1.3 %collective-permute-done.5.got_second = bf16[144,256]{1,0:T(8,128)(2,1)S(1)} collective-permute-done((bf16[144,256]{1,0:T(8,128)(2,1)S(1)}, bf16[144,256]{1,0:T(8,128)(2,1)S(1)}, u32[]{:S(2)}, u32[]{:S(2)}) %collective-permute-start.5) | collective-permute-done | bytes 73760 | tf_op jit(solution)/shard_map/ppermute | solution.py:150
  19.4 0.1 shard_map.78.own_ref
  19.5 2.0 %collective-permute-start.10 = (bf16[256,128]{1,0:T(8,128)(2,1)S(1)}, bf16[256,128]{1,0:T(8,128)(2,1)S(1)}, u32[]{:S(2)}, u32[]{:S(2)}) collective-permute-start(bf16[256,128]{1,0:T(8,128)(2,1)S(1)} %shard_map.78.own_ref), channel_id=1, source_target_pairs={{0,8},{4,12},{8,0},{12,4},{1,9},{5,13},{9,1},{13,5},{2,10},{6,14},... | collective-permute-start | bytes 196616 | tf_op jit(solution)/shard_map/ppermute | solution.py:444
  21.6 1.3 %collective-permute-start.11 = (bf16[256,128]{1,0:T(8,128)(2,1)S(1)}, bf16[256,128]{1,0:T(8,128)(2,1)S(1)}, u32[]{:S(2)}, u32[]{:S(2)}) collective-permute-start(bf16[256,128]{1,0:T(8,128)(2,1)S(1)} %shard_map.78.own_ref), channel_id=1, source_target_pairs={{0,12},{4,8},{8,4},{12,0},{1,13},{5,9},{9,5},{13,1},{2,14},{6,10},... | collective-permute-start | bytes 196616 | tf_op jit(solution)/shard_map/ppermute | solution.py:444
  22.9 0.2 collective-permute-start.9
  23.2 0.3 collective-permute-done.13.got_second
  23.5 0.1 shard_map.81.query_ref
  23.6 0.5 %shard_map.79 = (f32[4,256,128]{2,1,0:T(8,128)S(1)}, f32[4,256,128]{2,1,0:T(8,128)S(1)}) custom-call(bf16[512,256]{1,0:T(8,128)(2,1)S(1)} %copy-done.1, bf16[4,128,128]{2,1,0:T(8,128)(2,1)S(1)} %get-tuple-element.25.keep_ref, bf16[4,128,128]{2,1,0:T(8,128)(2,1)S(1)} %collective-permute-done.12.got_ref), custom_call_target="tpu_custom_call" | custom-call | tf_op jit(solution)/shard_map/pallas_call | solution.py:448
  24.0 2.7 %collective-permute-done.10.two_ref = bf16[256,128]{1,0:T(8,128)(2,1)S(1)} collective-permute-done((bf16[256,128]{1,0:T(8,128)(2,1)S(1)}, bf16[256,128]{1,0:T(8,128)(2,1)S(1)}, u32[]{:S(2)}, u32[]{:S(2)}) %collective-permute-start.10) | collective-permute-done | bytes 65568 | tf_op jit(solution)/shard_map/ppermute | solution.py:444
  26.7 1.1 %collective-permute-done.11.three_ref = bf16[256,128]{1,0:T(8,128)(2,1)S(1)} collective-permute-done((bf16[256,128]{1,0:T(8,128)(2,1)S(1)}, bf16[256,128]{1,0:T(8,128)(2,1)S(1)}, u32[]{:S(2)}, u32[]{:S(2)}) %collective-permute-start.11) | collective-permute-done | bytes 65568 | tf_op jit(solution)/shard_map/ppermute | solution.py:444
  27.8 0.2 collective-permute-done.9.one_ref
  28.0 0.7 %shard_map.82 = (bf16[128,128]{1,0:T(8,128)(2,1)S(1)}, bf16[128,128]{1,0:T(8,128)(2,1)S(1)}) custom-call(bf16[256,128]{1,0:T(8,128)(2,1)S(1)} %shard_map.78.own_ref, bf16[256,128]{1,0:T(8,128)(2,1)S(1)} %collective-permute-done.9.one_ref, bf16[256,128]{1,0:T(8,128)(2,1)S(1)} %collective-permute-done.10.two_ref, ...), custom_call_target="tpu_custom_call" | custom-call | tf_op jit(solution)/shard_map/pallas_call | solution.py:454
  28.7 0.6 %collective-permute-start.14 = (bf16[128,128]{1,0:T(8,128)(2,1)S(1)}, bf16[128,128]{1,0:T(8,128)(2,1)S(1)}, u32[]{:S(2)}, u32[]{:S(2)}) collective-permute-start(bf16[128,128]{1,0:T(8,128)(2,1)S(1)} %get-tuple-element.32), channel_id=1, source_target_pairs={{0,2},{2,0},{1,3},{3,1},{4,6},{6,4},{5,7},{7,5},{8,10},{10,8},{9,1... | collective-permute-start | bytes 98312 | tf_op jit(solution)/shard_map/ppermute | solution.py:150
  29.2 3.4 %collective-permute-done.14.got_ref = bf16[128,128]{1,0:T(8,128)(2,1)S(1)} collective-permute-done((bf16[128,128]{1,0:T(8,128)(2,1)S(1)}, bf16[128,128]{1,0:T(8,128)(2,1)S(1)}, u32[]{:S(2)}, u32[]{:S(2)}) %collective-permute-start.14) | collective-permute-done | bytes 32800 | tf_op jit(solution)/shard_map/ppermute | solution.py:150
  32.7 0.6 %shard_map.83 = bf16[128,256]{1,0:T(8,128)(2,1)} custom-call(bf16[128,128]{1,0:T(8,128)(2,1)S(1)} %get-tuple-element.31.stay_ref, bf16[128,128]{1,0:T(8,128)(2,1)S(1)} %collective-permute-done.14.got_ref), custom_call_target="tpu_custom_call" | custom-call | tf_op jit(solution)/shard_map/pallas_call | solution.py:462
  (23 shorter events, 0.1 us)
Async XLA Ops:
  0.0 6.0 %copy-start.3 = (bf16[128,256]{1,0:T(8,128)(2,1)S(1)}, bf16[128,256]{1,0:T(8,128)(2,1)}, u32[]{:S(2)}) copy-start(bf16[128,256]{1,0:T(8,128)(2,1)} %refs_0_.1) | copy-start | bytes 196612
  0.0 12.0 %copy-start = (bf16[2048,3,256]{2,0,1:T(8,128)(2,1)S(1)}, bf16[2048,3,256]{2,0,1:T(8,128)(2,1)}, u32[]{:S(2)}) copy-start(bf16[2048,3,256]{2,0,1:T(8,128)(2,1)} %param.8) | copy-start | bytes 9437188
  0.0 11.5 %collective-permute-start = (bf16[128,2048]{1,0:T(8,128)(2,1)}, bf16[128,2048]{1,0:T(8,128)(2,1)S(1)}, u32[]{:S(2)}, u32[]{:S(2)}) collective-permute-start(bf16[128,2048]{1,0:T(8,128)(2,1)} %rows_ref.3), channel_id=1, source_target_pairs={{1,3},{3,2},{2,0},{0,1},{5,7},{7,6},{6,4},{4,5},{9,11},{11,10},{10... | collective-permute-start | bytes 1572872 | tf_op jit(solution)/shard_map/ppermute | solution.py:367
  0.5 1.3 %copy-start.6 = (bf16[128,2048]{1,0:T(8,128)(2,1)S(1)}, bf16[128,2048]{1,0:T(8,128)(2,1)}, u32[]{:S(2)}) copy-start(bf16[128,2048]{1,0:T(8,128)(2,1)} %rows_ref.3) | copy-start | bytes 1572868
  1.9 9.6 %collective-permute-start.1 = (bf16[16,256]{1,0:T(8,128)(2,1)S(1)}, bf16[16,256]{1,0:T(8,128)(2,1)S(1)}, u32[]{:S(2)}, u32[]{:S(2)}) collective-permute-start(bf16[16,256]{1,0:T(8,128)(2,1)S(1)} %shard_map.73), channel_id=1, source_target_pairs={{0,6},{1,5},{2,4},{3,7},{4,10},{5,9},{6,8},{7,11},{8,14},{9,13},{1... | collective-permute-start | bytes 24584 | tf_op jit(solution)/shard_map/ppermute | solution.py:376
  6.0 9.5 %collective-permute-start.6 = (bf16[128,256]{1,0:T(8,128)(2,1)S(1)}, bf16[128,256]{1,0:T(8,128)(2,1)S(1)}, u32[]{:S(2)}, u32[]{:S(2)}) collective-permute-start(bf16[128,256]{1,0:T(8,128)(2,1)S(1)} %copy-done.3), channel_id=1, source_target_pairs={{0,4},{4,8},{8,12},{12,0},{1,5},{5,9},{9,13},{13,1},{2,6},{6,10},{... | collective-permute-start | bytes 196616 | tf_op jit(solution)/shard_map/ppermute | solution.py:387
  7.5 7.9 %collective-permute-start.7 = (bf16[128,256]{1,0:T(8,128)(2,1)S(1)}, bf16[128,256]{1,0:T(8,128)(2,1)S(1)}, u32[]{:S(2)}, u32[]{:S(2)}) collective-permute-start(bf16[128,256]{1,0:T(8,128)(2,1)S(1)} %copy-done.3), channel_id=1, source_target_pairs={{0,8},{4,12},{8,0},{12,4},{1,9},{5,13},{9,1},{13,5},{2,10},{6,14},... | collective-permute-start | bytes 196616 | tf_op jit(solution)/shard_map/ppermute | solution.py:387
  8.6 6.9 %collective-permute-start.8 = (bf16[128,256]{1,0:T(8,128)(2,1)S(1)}, bf16[128,256]{1,0:T(8,128)(2,1)S(1)}, u32[]{:S(2)}, u32[]{:S(2)}) collective-permute-start(bf16[128,256]{1,0:T(8,128)(2,1)S(1)} %copy-done.3), channel_id=1, source_target_pairs={{0,12},{4,0},{8,4},{12,8},{1,13},{5,1},{9,5},{13,9},{2,14},{6,2},{... | collective-permute-start | bytes 196616 | tf_op jit(solution)/shard_map/ppermute | solution.py:387
  11.5 1.2 %collective-permute-start.3 = (bf16[16,256]{1,0:T(8,128)(2,1)S(1)}, bf16[16,256]{1,0:T(8,128)(2,1)S(1)}, u32[]{:S(2)}, u32[]{:S(2)}) collective-permute-start(bf16[16,256]{1,0:T(8,128)(2,1)S(1)} %collective-permute-done.1.refs_1_.pack_ref), channel_id=1, source_target_pairs={{0,1},{1,0},{2,3},{3,2},{4,5},{5,4},{6,7},{7,6},{8,9},{9,8},{10,11... | collective-permute-start | bytes 24584 | tf_op jit(solution)/shard_map/ppermute | solution.py:150
  11.5 2.0 %collective-permute-start.2 = (bf16[128,2048]{1,0:T(8,128)(2,1)S(1)}, bf16[128,2048]{1,0:T(8,128)(2,1)S(1)}, u32[]{:S(2)}, u32[]{:S(2)}) collective-permute-start(bf16[128,2048]{1,0:T(8,128)(2,1)S(1)} %shard_map.74.cycled_ref), channel_id=1, source_target_pairs={{0,1},{1,0},{2,3},{3,2},{4,5},{5,4},{6,7},{7,6},{8,9},{9,8},{10,11... | collective-permute-start | bytes 1572872 | tf_op jit(solution)/shard_map/ppermute | solution.py:150
  12.7 5.5 %collective-permute-start.4 = (bf16[128,384]{1,0:T(8,128)(2,1)S(1)}, bf16[128,384]{1,0:T(8,128)(2,1)S(1)}, u32[]{:S(2)}, u32[]{:S(2)}) collective-permute-start(bf16[128,384]{1,0:T(8,128)(2,1)S(1)} %get-tuple-element.21), channel_id=1, source_target_pairs={{0,2},{2,0},{1,3},{3,1},{4,6},{6,4},{5,7},{7,5},{8,10},{10,8},{9,1... | collective-permute-start | bytes 294920 | tf_op jit(solution)/shard_map/ppermute | solution.py:150
  14.1 5.3 %copy-start.4 = (f32[3,3,256]{2,1,0:T(4,128)S(1)}, f32[3,3,256]{2,1,0:T(4,128)}, u32[]{:S(2)}) copy-start(f32[3,3,256]{2,1,0:T(4,128)} %short_ref.3) | copy-start | bytes 27652
  14.1 9.4 %copy-start.1 = (bf16[512,256]{1,0:T(8,128)(2,1)S(1)}, bf16[512,256]{1,0:T(8,128)(2,1)}, u32[]{:S(2)}) copy-start(bf16[512,256]{1,0:T(8,128)(2,1)} %constant.4.clone.table_ref) | copy-start | bytes 786436
  14.2 13.8 %copy-start.2 = (bf16[256,512]{1,0:T(8,128)(2,1)S(1)}, bf16[256,512]{1,0:T(8,128)(2,1)}, u32[]{:S(2)}) copy-start(bf16[256,512]{1,0:T(8,128)(2,1)} %constant.5.clone.turned_ref) | copy-start | bytes 786436
  14.2 13.8 %copy-start.5 = (f32[256]{0:T(256)S(1)}, f32[256]{0:T(256)}, u32[]{:S(2)}) copy-start(f32[256]{0:T(256)} %param.10) | copy-start | bytes 3076
  14.2 5.2 %collective-permute-start.5 = (bf16[144,256]{1,0:T(8,128)(2,1)S(1)}, bf16[144,256]{1,0:T(8,128)(2,1)S(1)}, u32[]{:S(2)}, u32[]{:S(2)}) collective-permute-start(bf16[144,256]{1,0:T(8,128)(2,1)S(1)} %get-tuple-element.22), channel_id=1, source_target_pairs={{0,2},{2,0},{1,3},{3,1},{4,6},{6,4},{5,7},{7,5},{8,10},{10,8},{9,1... | collective-permute-start | bytes 221192 | tf_op jit(solution)/shard_map/ppermute | solution.py:150
  15.5 8.1 %collective-permute-start.12 = (bf16[4,128,128]{2,1,0:T(8,128)(2,1)S(1)}, bf16[4,128,128]{2,1,0:T(8,128)(2,1)S(1)}, u32[]{:S(2)}, u32[]{:S(2)}) collective-permute-start(bf16[4,128,128]{2,1,0:T(8,128)(2,1)S(1)} %get-tuple-element.26), channel_id=1, source_target_pairs={{0,2},{2,0},{1,3},{3,1},{4,6},{6,4},{5,7},{7,5},{8,10},{10,8},{9,1... | collective-permute-start | bytes 393224 | tf_op jit(solution)/shard_map/ppermute | solution.py:150
  16.9 6.6 %collective-permute-start.13 = (f32[144,128]{1,0:T(8,128)S(1)}, f32[144,128]{1,0:T(8,128)S(1)}, u32[]{:S(2)}, u32[]{:S(2)}) collective-permute-start(f32[144,128]{1,0:T(8,128)S(1)} %get-tuple-element.30), channel_id=1, source_target_pairs={{0,2},{2,0},{1,3},{3,1},{4,6},{6,4},{5,7},{7,5},{8,10},{10,8},{9,1... | collective-permute-start | bytes 221192 | tf_op jit(solution)/shard_map/ppermute | solution.py:150
  19.5 7.2 %collective-permute-start.10 = (bf16[256,128]{1,0:T(8,128)(2,1)S(1)}, bf16[256,128]{1,0:T(8,128)(2,1)S(1)}, u32[]{:S(2)}, u32[]{:S(2)}) collective-permute-start(bf16[256,128]{1,0:T(8,128)(2,1)S(1)} %shard_map.78.own_ref), channel_id=1, source_target_pairs={{0,8},{4,12},{8,0},{12,4},{1,9},{5,13},{9,1},{13,5},{2,10},{6,14},... | collective-permute-start | bytes 196616 | tf_op jit(solution)/shard_map/ppermute | solution.py:444
  21.6 6.2 %collective-permute-start.11 = (bf16[256,128]{1,0:T(8,128)(2,1)S(1)}, bf16[256,128]{1,0:T(8,128)(2,1)S(1)}, u32[]{:S(2)}, u32[]{:S(2)}) collective-permute-start(bf16[256,128]{1,0:T(8,128)(2,1)S(1)} %shard_map.78.own_ref), channel_id=1, source_target_pairs={{0,12},{4,8},{8,4},{12,0},{1,13},{5,9},{9,5},{13,1},{2,14},{6,10},... | collective-permute-start | bytes 196616 | tf_op jit(solution)/shard_map/ppermute | solution.py:444
  22.9 5.1 %collective-permute-start.9 = (bf16[256,128]{1,0:T(8,128)(2,1)S(1)}, bf16[256,128]{1,0:T(8,128)(2,1)S(1)}, u32[]{:S(2)}, u32[]{:S(2)}) collective-permute-start(bf16[256,128]{1,0:T(8,128)(2,1)S(1)} %shard_map.78.own_ref), channel_id=1, source_target_pairs={{0,4},{4,0},{8,12},{12,8},{1,5},{5,1},{9,13},{13,9},{2,6},{6,2},{1... | collective-permute-start | bytes 196616 | tf_op jit(solution)/shard_map/ppermute | solution.py:444
  28.7 4.0 %collective-permute-start.14 = (bf16[128,128]{1,0:T(8,128)(2,1)S(1)}, bf16[128,128]{1,0:T(8,128)(2,1)S(1)}, u32[]{:S(2)}, u32[]{:S(2)}) collective-permute-start(bf16[128,128]{1,0:T(8,128)(2,1)S(1)} %get-tuple-element.32), channel_id=1, source_target_pairs={{0,2},{2,0},{1,3},{3,1},{4,6},{6,4},{5,7},{7,5},{8,10},{10,8},{9,1... | collective-permute-start | bytes 98312 | tf_op jit(solution)/shard_map/ppermute | solution.py:150

commit v6 on v5

--- a/solution.py
+++ b/solution.py
@@ -223,7 +223,7 @@
     first = lax.axis_index("fsdp") == 0
     blocks, _, half = keep_ref.shape
     for step in range(blocks):
-        block = lax.rem(position - step + blocks, blocks)
+        block = position ^ step
         taps = refs[step][...]
         low, high = (taps[:, :half], taps[:, half:])
         keep_ref[block] = jnp.where(first, low, high)
@@ -312,33 +312,56 @@
     query_ref[...] = query
 
 
-def conv_body(own_ref, one_ref, two_ref, three_ref, real_ref, imag_ref, table_ref, turned_ref,
-              query_ref, gain_ref, stay_ref, go_ref, result):
+def spectrum_term(step, block_ref, real_ref, imag_ref, table_ref):
     position = lax.axis_index("seq")
+    size = table_ref.shape[1]
+    source = position ^ step
+    back = jnp.maximum(position - source, 0)
+    block = block_ref[...]
+    if step:
+        block = jnp.where(source < position, block, jnp.zeros_like(block))
+    waves = jnp.dot(table_ref[...], block, preferred_element_type=F32)
+    real, imag = (waves[:size], -waves[size:])
+    tap_real, tap_imag = (real_ref[back], imag_ref[back])
+    return (real * tap_real - imag * tap_imag, real * tap_imag + imag * tap_real)
+
+
+def conv_early_body(own_ref, far_ref, near_ref, real_ref, imag_ref, table_ref, total_ref):
+    total_ref[0], total_ref[1] = spectrum_term(0, own_ref, real_ref, imag_ref, table_ref)
+    for step, block_ref in ((3, far_ref), (1, near_ref)):
+        real, imag = spectrum_term(step, block_ref, real_ref, imag_ref, table_ref)
+        total_ref[0] += real
+        total_ref[1] += imag
+
+
+def gated_rows(place, rows, stacked, turned_ref, query_ref, gain_ref, own_ref):
+    half = own_ref.shape[1]
+    lines = pl.ds(pl.multiple_of(place * rows, rows), rows)
+    conv = jnp.dot(turned_ref[lines, :], stacked, preferred_element_type=F32)
+    first = lax.axis_index("fsdp") == 0
+    gain = jnp.where(first, gain_ref[:, :half], gain_ref[:, half:])
+    gated = query_ref[lines, :] * (conv + gain * own_ref[lines, :].astype(F32))
+    return gated.astype(BF16)
+
+
+def conv_last_body(
+    last_ref, total_ref, real_ref, imag_ref, table_ref, turned_ref, query_ref, gain_ref, own_ref,
+    go_ref, stacked_ref
+):
+    real, imag = spectrum_term(2, last_ref, real_ref, imag_ref, table_ref)
+    stacked = jnp.concatenate([total_ref[0] + real, -(total_ref[1] + imag)], axis=0).astype(BF16)
+    stacked_ref[...] = stacked
+    other = 1 - lax.axis_index("fsdp")
+    go_ref[...] = gated_rows(
+        other, go_ref.shape[0], stacked, turned_ref, query_ref, gain_ref, own_ref
+    )
+
+
+def conv_stay_body(stacked_ref, turned_ref, query_ref, gain_ref, own_ref, stay_ref):
     own = lax.axis_index("fsdp")
-    size = table_ref.shape[1]
-    total_real = total_imag = None
-    for step, block_ref in enumerate((own_ref, one_ref, two_ref, three_ref)):
-        block = block_ref[...]
-        source = position ^ step
-        back = jnp.maximum(position - source, 0)
-        if step:
-            block = jnp.where(source < position, block, jnp.zeros_like(block))
-        waves = jnp.dot(table_ref[...], block, preferred_element_type=F32)
-        real, imag = (waves[:size], -waves[size:])
-        term_real = real * real_ref[back] - imag * imag_ref[back]
-        term_imag = real * imag_ref[back] + imag * real_ref[back]
-        total_real = term_real if total_real is None else total_real + term_real
-        total_imag = term_imag if total_imag is None else total_imag + term_imag
-    stacked = jnp.concatenate([total_real, -total_imag], axis=0).astype(BF16)
-    conv = jnp.dot(turned_ref[...], stacked, preferred_element_type=F32)
-    half = own_ref.shape[1]
-    gain = jnp.where(own == 0, gain_ref[:, :half], gain_ref[:, half:])
-    gated = query_ref[...] * (conv + gain * own_ref[...].astype(F32))
-    result[...] = gated.astype(BF16)
-    rows = stay_ref.shape[0]
-    stay_ref[...] = result[pl.ds(pl.multiple_of(own * rows, rows), rows), :]
-    go_ref[...] = result[pl.ds(pl.multiple_of((1 - own) * rows, rows), rows), :]
+    stay_ref[...] = gated_rows(
+        own, stay_ref.shape[0], stacked_ref[...], turned_ref, query_ref, gain_ref, own_ref
+    )
 
 
 def join_body(stay_ref, got_ref, out_ref):
@@ -359,7 +382,7 @@
     size = 2 * rows
     blocks = lax.axis_size("seq")
     weight = jnp.transpose(proj_weight, (1, 0, 2))
-    ring = [[(s, (s + step) % blocks) for s in range(blocks)] for step in range(blocks)]
+    pairs = [[(s, s ^ step) for s in range(blocks)] for step in range(blocks)]
     call = functools.partial(
         pl.pallas_call, compiler_params=pltpu.CompilerParams(vmem_limit_bytes=32 * 1024 * 1024)
     )
@@ -384,7 +407,7 @@
         ],
     )
     tap_blocks = [filter_taps] + [
-        lax.ppermute(filter_taps, "seq", ring[step]) for step in range(1, blocks)
+        lax.ppermute(filter_taps, "seq", pairs[step]) for step in range(1, blocks)
     ]
     cycled = after(cycled, pack_got)
     hop = exchange(cycled, "chan")
@@ -441,7 +464,7 @@
         scratch_shapes=[pltpu.VMEM((HALO + size, half), F32)],
     )(keep_first, keep_query, got_first, got_query, short_weight)
     tap_got = exchange(tap_send, "fsdp")
-    products = [product] + [lax.ppermute(product, "seq", [(s, s ^ step) for s in range(blocks)]) for step in range(1, blocks)]
+    last, far, near = (lax.ppermute(product, "seq", pairs[step]) for step in (2, 3, 1))
     table = wave_table(size)
     forward = jnp.asarray(table, dtype=BF16)
     inverse = jnp.asarray(table.T, dtype=BF16)
@@ -451,13 +474,25 @@
         out_specs=whole_specs(2),
         out_shape=(shape((blocks, size, half), F32), shape((blocks, size, half), F32)),
     )(forward, tap_keep, tap_got)
-    stay, go = call(
-        conv_body,
-        in_specs=whole_specs(10),
+    total = call(
+        conv_early_body,
+        in_specs=whole_specs(6),
+        out_specs=whole_specs(1)[0],
+        out_shape=shape((2, size, half), F32),
+    )(product, far, near, tap_real, tap_imag, forward)
+    ending = (inverse, query, skip_gain.reshape(1, width), product)
+    go, stacked = call(
+        conv_last_body,
+        in_specs=whole_specs(9),
         out_specs=whole_specs(2),
-        out_shape=(shape((rows, half), BF16), shape((rows, half), BF16)),
-        scratch_shapes=[pltpu.VMEM((size, half), BF16)],
-    )(*products, tap_real, tap_imag, forward, inverse, query, skip_gain.reshape(1, width))
+        out_shape=(shape((rows, half), BF16), shape((2 * size, half), BF16)),
+    )(last, total, tap_real, tap_imag, forward, *ending)
+    stay = call(
+        conv_stay_body,
+        in_specs=whole_specs(5),
+        out_specs=whole_specs(1)[0],
+        out_shape=shape((rows, half), BF16),
+    )(stacked, *ending)
     back = exchange(go, "fsdp")
     return call(
         join_body,

time: 33.4 us -> 33 us (0.988)
  waiting for transfers between devices: 9.94 us -> 8.73 us
  starting transfers between devices: 18.1 us -> 18.5 us
  Pallas kernels: 3.77 us -> 4.13 us
    ppermute x7, waiting for transfers between devices: 5.95 us -> 4.64 us  [exchange(): return lax.ppermute(value, axis, [(0, 1), (1, 0)])]
    pallas_call x1 -> x3, Pallas kernels: 0.67 us -> 1.03 us  [the longest x1 0.46 us: pair_mesh(): call(conv_last_body, in_specs=whole_specs(9), out_specs=whole_specs(2), o...]
    ppermute x7, starting transfers between devices: 4.47 us -> 4.83 us  [exchange(): return lax.ppermute(value, axis, [(0, 1), (1, 0)])]
  transfers between devices with their start and end apart: 15 -> 15, of which waited for: 8 -> 8; matrix products, arithmetic and copies ran while one was open for 0% -> 0% of each run, Pallas kernels for 7% -> 9%
where the time goes in v6:
time: 33 us; the launch traced here: 32.9 us
  starting transfers between devices  18.5 us (56%)
  waiting for transfers between devices  8.73 us (26%)
  Pallas kernels  4.13 us (13%)
  local copies, waits for them, and re-layouts  1.31 us (4%)
    ppermute x7, starting transfers between devices, exchange(): return lax.ppermute(value, axis, [(0, 1), (1, 0)])  4.83 us
    ppermute x3, starting transfers between devices, pair_mesh(): lax.ppermute(product, 'seq', pairs[step])  4.79 us
    ppermute x7, waiting for transfers between devices, exchange(): return lax.ppermute(value, axis, [(0, 1), (1, 0)])  4.64 us
    ppermute x3, starting transfers between devices, pair_mesh(): lax.ppermute(filter_taps, 'seq', pairs[step])  4.39 us
    ppermute x1, starting transfers between devices, pair_mesh(): lax.ppermute(pack, ('seq', 'fsdp', 'chan'), [(4 * s + 2 * f + c, 4 * ((s...  4.09 us
    ppermute x3, waiting for transfers between devices, pair_mesh(): lax.ppermute(product, 'seq', pairs[step])  3.58 us
    unnamed x14, local copies, waits for them, and re-layouts  1.31 us
  transfers between devices with their start and end apart: 15, of which 8 were waited for; matrix products, arithmetic and copies ran while one was open for 0% of the time, Pallas kernels for 9%

profile of v6, /device:TPU:0, one launch (start us, length us, event | category | flops | bytes accessed | tf_op | source)
XLA Modules:
  0.0 32.9 jit_solution(10180926749849304193)
XLA Ops:
  0.0 0.5 %collective-permute-start = (bf16[128,2048]{1,0:T(8,128)(2,1)}, bf16[128,2048]{1,0:T(8,128)(2,1)S(1)}, u32[]{:S(2)}, u32[]{:S(2)}) collective-permute-start(bf16[128,2048]{1,0:T(8,128)(2,1)} %rows_ref.3), channel_id=1, source_target_pairs={{1,3},{3,2},{2,0},{0,1},{5,7},{7,6},{6,4},{4,5},{9,11},{11,10},{10... | collective-permute-start | bytes 1572872 | tf_op jit(solution)/shard_map/ppermute | solution.py:390
  0.5 1.3 %copy-done.6 = bf16[128,2048]{1,0:T(8,128)(2,1)S(1)} copy-done((bf16[128,2048]{1,0:T(8,128)(2,1)S(1)}, bf16[128,2048]{1,0:T(8,128)(2,1)}, u32[]{:S(2)}) %copy-start.6) | copy-done | bytes 524312
  1.7 0.1 shard_map.73
  1.9 4.1 %collective-permute-start.1 = (bf16[16,256]{1,0:T(8,128)(2,1)S(1)}, bf16[16,256]{1,0:T(8,128)(2,1)S(1)}, u32[]{:S(2)}, u32[]{:S(2)}) collective-permute-start(bf16[16,256]{1,0:T(8,128)(2,1)S(1)} %shard_map.73), channel_id=1, source_target_pairs={{0,6},{1,5},{2,4},{3,7},{4,10},{5,9},{6,8},{7,11},{8,14},{9,13},{1... | collective-permute-start | bytes 24584 | tf_op jit(solution)/shard_map/ppermute | solution.py:399
  6.0 1.6 %collective-permute-start.6 = (bf16[128,256]{1,0:T(8,128)(2,1)S(1)}, bf16[128,256]{1,0:T(8,128)(2,1)S(1)}, u32[]{:S(2)}, u32[]{:S(2)}) collective-permute-start(bf16[128,256]{1,0:T(8,128)(2,1)S(1)} %copy-done.3), channel_id=1, source_target_pairs={{0,4},{4,0},{8,12},{12,8},{1,5},{5,1},{9,13},{13,9},{2,6},{6,2},{1... | collective-permute-start | bytes 196616 | tf_op jit(solution)/shard_map/ppermute | solution.py:410
  7.5 1.0 %collective-permute-start.7 = (bf16[128,256]{1,0:T(8,128)(2,1)S(1)}, bf16[128,256]{1,0:T(8,128)(2,1)S(1)}, u32[]{:S(2)}, u32[]{:S(2)}) collective-permute-start(bf16[128,256]{1,0:T(8,128)(2,1)S(1)} %copy-done.3), channel_id=1, source_target_pairs={{0,8},{4,12},{8,0},{12,4},{1,9},{5,13},{9,1},{13,5},{2,10},{6,14},... | collective-permute-start | bytes 196616 | tf_op jit(solution)/shard_map/ppermute | solution.py:410
  8.6 1.8 %collective-permute-start.8 = (bf16[128,256]{1,0:T(8,128)(2,1)S(1)}, bf16[128,256]{1,0:T(8,128)(2,1)S(1)}, u32[]{:S(2)}, u32[]{:S(2)}) collective-permute-start(bf16[128,256]{1,0:T(8,128)(2,1)S(1)} %copy-done.3), channel_id=1, source_target_pairs={{0,12},{4,8},{8,4},{12,0},{1,13},{5,9},{9,5},{13,1},{2,14},{6,10},... | collective-permute-start | bytes 196616 | tf_op jit(solution)/shard_map/ppermute | solution.py:410
  10.4 0.5 %collective-permute-start.2 = (bf16[128,2048]{1,0:T(8,128)(2,1)S(1)}, bf16[128,2048]{1,0:T(8,128)(2,1)S(1)}, u32[]{:S(2)}, u32[]{:S(2)}) collective-permute-start(bf16[128,2048]{1,0:T(8,128)(2,1)S(1)} %shard_map.74.cycled_ref), channel_id=1, source_target_pairs={{0,1},{1,0},{2,3},{3,2},{4,5},{5,4},{6,7},{7,6},{8,9},{9,8},{10,11... | collective-permute-start | bytes 1572872 | tf_op jit(solution)/shard_map/ppermute | solution.py:150
  10.9 0.6 %shard_map.75 = (f32[128,384]{1,0:T(8,128)S(1)}, bf16[128,384]{1,0:T(8,128)(2,1)S(1)}) custom-call(bf16[128,2048]{1,0:T(8,128)(2,1)S(1)} %copy-done.6, bf16[128,2048]{1,0:T(8,128)(2,1)S(1)} %shard_map.74.cycled_ref, bf16[3,2048,256]{2,1,0:T(8,128)(2,1)S(1)} %bitcast.2), custom_call_target="tpu_custom_call" | custom-call | flops 10000000000 | bytes 40000000 | tf_op jit(solution)/shard_map/pallas_call | solution.py:415
  11.5 0.1 collective-permute-done.3.pack_hop_ref
  11.5 0.4 %collective-permute-start.4 = (bf16[128,384]{1,0:T(8,128)(2,1)S(1)}, bf16[128,384]{1,0:T(8,128)(2,1)S(1)}, u32[]{:S(2)}, u32[]{:S(2)}) collective-permute-start(bf16[128,384]{1,0:T(8,128)(2,1)S(1)} %get-tuple-element.21), channel_id=1, source_target_pairs={{0,2},{2,0},{1,3},{3,1},{4,6},{6,4},{5,7},{7,5},{8,10},{10,8},{9,1... | collective-permute-start | bytes 294920 | tf_op jit(solution)/shard_map/ppermute | solution.py:150
  11.9 0.5 %collective-permute-done.2.hop_ref = bf16[128,2048]{1,0:T(8,128)(2,1)S(1)} collective-permute-done((bf16[128,2048]{1,0:T(8,128)(2,1)S(1)}, bf16[128,2048]{1,0:T(8,128)(2,1)S(1)}, u32[]{:S(2)}, u32[]{:S(2)}) %collective-permute-start.2) | collective-permute-done | bytes 524320 | tf_op jit(solution)/shard_map/ppermute | solution.py:150
  12.4 0.6 %shard_map.76 = (f32[144,256]{1,0:T(8,128)S(1)}, bf16[144,256]{1,0:T(8,128)(2,1)S(1)}, f32[8,128]{1,0:T(8,128)S(1)}) custom-call(bf16[128,2048]{1,0:T(8,128)(2,1)S(1)} %shard_map.74.cycled_ref, bf16[128,2048]{1,0:T(8,128)(2,1)S(1)} %collective-permute-done.2.hop_ref, bf16[16,256]{1,0:T(8,128)(2,1)S(1)} %collective-permute-done.1.refs_1_.pack_ref, ...), custom_call_target="tpu_custom_call" | custom-call | tf_op jit(solution)/shard_map/pallas_call | solution.py:423
  13.0 1.2 %collective-permute-start.5 = (bf16[144,256]{1,0:T(8,128)(2,1)S(1)}, bf16[144,256]{1,0:T(8,128)(2,1)S(1)}, u32[]{:S(2)}, u32[]{:S(2)}) collective-permute-start(bf16[144,256]{1,0:T(8,128)(2,1)S(1)} %get-tuple-element.22), channel_id=1, source_target_pairs={{0,2},{2,0},{1,3},{3,1},{4,6},{6,4},{5,7},{7,5},{8,10},{10,8},{9,1... | collective-permute-start | bytes 221192 | tf_op jit(solution)/shard_map/ppermute | solution.py:150
  14.3 0.5 %collective-permute-done.7.refs_2_ = bf16[128,256]{1,0:T(8,128)(2,1)S(1)} collective-permute-done((bf16[128,256]{1,0:T(8,128)(2,1)S(1)}, bf16[128,256]{1,0:T(8,128)(2,1)S(1)}, u32[]{:S(2)}, u32[]{:S(2)}) %collective-permute-start.7) | collective-permute-done | bytes 65568 | tf_op jit(solution)/shard_map/ppermute | solution.py:410
  14.8 1.2 %collective-permute-start.12 = (bf16[4,128,128]{2,1,0:T(8,128)(2,1)S(1)}, bf16[4,128,128]{2,1,0:T(8,128)(2,1)S(1)}, u32[]{:S(2)}, u32[]{:S(2)}) collective-permute-start(bf16[4,128,128]{2,1,0:T(8,128)(2,1)S(1)} %get-tuple-element.26), channel_id=1, source_target_pairs={{0,2},{2,0},{1,3},{3,1},{4,6},{6,4},{5,7},{7,5},{8,10},{10,8},{9,1... | collective-permute-start | bytes 393224 | tf_op jit(solution)/shard_map/ppermute | solution.py:150
  16.0 0.4 %shard_map.81 = (f32[144,128]{1,0:T(8,128)S(1)}, f32[144,128]{1,0:T(8,128)S(1)}) custom-call(bf16[128,2048]{1,0:T(8,128)(2,1)S(1)} %shard_map.74.cycled_ref, bf16[128,2048]{1,0:T(8,128)(2,1)S(1)} %collective-permute-done.2.hop_ref, bf16[16,256]{1,0:T(8,128)(2,1)S(1)} %collective-permute-done.1.refs_1_.pack_ref, ...), custom_call_target="tpu_custom_call" | custom-call | tf_op jit(solution)/shard_map/pallas_call | solution.py:433
  16.4 1.0 %collective-permute-start.13 = (f32[144,128]{1,0:T(8,128)S(1)}, f32[144,128]{1,0:T(8,128)S(1)}, u32[]{:S(2)}, u32[]{:S(2)}) collective-permute-start(f32[144,128]{1,0:T(8,128)S(1)} %get-tuple-element.30), channel_id=1, source_target_pairs={{0,2},{2,0},{1,3},{3,1},{4,6},{6,4},{5,7},{7,5},{8,10},{10,8},{9,1... | collective-permute-start | bytes 221192 | tf_op jit(solution)/shard_map/ppermute | solution.py:150
  17.4 0.9 %collective-permute-done.5.got_second = bf16[144,256]{1,0:T(8,128)(2,1)S(1)} collective-permute-done((bf16[144,256]{1,0:T(8,128)(2,1)S(1)}, bf16[144,256]{1,0:T(8,128)(2,1)S(1)}, u32[]{:S(2)}, u32[]{:S(2)}) %collective-permute-start.5) | collective-permute-done | bytes 73760 | tf_op jit(solution)/shard_map/ppermute | solution.py:150
  18.3 0.1 shard_map.78.own_ref
  18.4 4.1 %collective-permute-start.10 = (bf16[256,128]{1,0:T(8,128)(2,1)S(1)}, bf16[256,128]{1,0:T(8,128)(2,1)S(1)}, u32[]{:S(2)}, u32[]{:S(2)}) collective-permute-start(bf16[256,128]{1,0:T(8,128)(2,1)S(1)} %shard_map.78.own_ref), channel_id=1, source_target_pairs={{0,12},{4,8},{8,4},{12,0},{1,13},{5,9},{9,5},{13,1},{2,14},{6,10},... | collective-permute-start | bytes 196616 | tf_op jit(solution)/shard_map/ppermute | solution.py:467
  22.6 0.6 %collective-permute-start.9 = (bf16[256,128]{1,0:T(8,128)(2,1)S(1)}, bf16[256,128]{1,0:T(8,128)(2,1)S(1)}, u32[]{:S(2)}, u32[]{:S(2)}) collective-permute-start(bf16[256,128]{1,0:T(8,128)(2,1)S(1)} %shard_map.78.own_ref), channel_id=1, source_target_pairs={{0,8},{4,12},{8,0},{12,4},{1,9},{5,13},{9,1},{13,5},{2,10},{6,14},... | collective-permute-start | bytes 196616 | tf_op jit(solution)/shard_map/ppermute | solution.py:467
  23.3 0.5 %shard_map.79 = (f32[4,256,128]{2,1,0:T(8,128)S(1)}, f32[4,256,128]{2,1,0:T(8,128)S(1)}) custom-call(bf16[512,256]{1,0:T(8,128)(2,1)S(1)} %copy-done.1, bf16[4,128,128]{2,1,0:T(8,128)(2,1)S(1)} %get-tuple-element.25.keep_ref, bf16[4,128,128]{2,1,0:T(8,128)(2,1)S(1)} %collective-permute-done.12.got_ref), custom_call_target="tpu_custom_call" | custom-call | tf_op jit(solution)/shard_map/pallas_call | solution.py:471
  23.8 1.3 %collective-permute-done.10.far_ref = bf16[256,128]{1,0:T(8,128)(2,1)S(1)} collective-permute-done((bf16[256,128]{1,0:T(8,128)(2,1)S(1)}, bf16[256,128]{1,0:T(8,128)(2,1)S(1)}, u32[]{:S(2)}, u32[]{:S(2)}) %collective-permute-start.10) | collective-permute-done | bytes 65568 | tf_op jit(solution)/shard_map/ppermute | solution.py:467
  25.1 2.0 %collective-permute-done.11.near_ref = bf16[256,128]{1,0:T(8,128)(2,1)S(1)} collective-permute-done((bf16[256,128]{1,0:T(8,128)(2,1)S(1)}, bf16[256,128]{1,0:T(8,128)(2,1)S(1)}, u32[]{:S(2)}, u32[]{:S(2)}) %collective-permute-start.11) | collective-permute-done | bytes 65568 | tf_op jit(solution)/shard_map/ppermute | solution.py:467
  27.0 0.4 %shard_map.80.total_ref = f32[2,256,128]{2,1,0:T(8,128)S(1)} custom-call(bf16[256,128]{1,0:T(8,128)(2,1)S(1)} %shard_map.78.own_ref, bf16[256,128]{1,0:T(8,128)(2,1)S(1)} %collective-permute-done.10.far_ref, bf16[256,128]{1,0:T(8,128)(2,1)S(1)} %collective-permute-done.11.near_ref, f32[4,256,128]{2,1,0:T(8,128)S(1)} %get-tuple-element.27.real_ref, ...), custom_call_target="tpu_custom_call" | custom-call | tf_op jit(solution)/shard_map/pallas_call | solution.py:477
  27.4 0.3 collective-permute-done.9.last_ref
  27.8 0.5 %shard_map.83 = (bf16[128,128]{1,0:T(8,128)(2,1)S(1)}, bf16[512,128]{1,0:T(8,128)(2,1)S(1)}) custom-call(bf16[256,128]{1,0:T(8,128)(2,1)S(1)} %collective-permute-done.9.last_ref, f32[2,256,128]{2,1,0:T(8,128)S(1)} %shard_map.80.total_ref, f32[4,256,128]{2,1,0:T(8,128)S(1)} %get-tuple-element.27.real_ref, f32[4,256,128]{2,1,0:T(8,128)S(1)} %get-tuple-element.28.imag_ref, ...), custom_call_target="tpu_custom_call" | custom-call | tf_op jit(solution)/shard_map/pallas_call | solution.py:484
  28.2 0.6 %collective-permute-start.14 = (bf16[128,128]{1,0:T(8,128)(2,1)S(1)}, bf16[128,128]{1,0:T(8,128)(2,1)S(1)}, u32[]{:S(2)}, u32[]{:S(2)}) collective-permute-start(bf16[128,128]{1,0:T(8,128)(2,1)S(1)} %get-tuple-element.32), channel_id=1, source_target_pairs={{0,2},{2,0},{1,3},{3,1},{4,6},{6,4},{5,7},{7,5},{8,10},{10,8},{9,1... | collective-permute-start | bytes 98312 | tf_op jit(solution)/shard_map/ppermute | solution.py:150
  28.8 0.2 shard_map.84.stay_ref
  29.0 3.2 %collective-permute-done.14.got_ref = bf16[128,128]{1,0:T(8,128)(2,1)S(1)} collective-permute-done((bf16[128,128]{1,0:T(8,128)(2,1)S(1)}, bf16[128,128]{1,0:T(8,128)(2,1)S(1)}, u32[]{:S(2)}, u32[]{:S(2)}) %collective-permute-start.14) | collective-permute-done | bytes 32800 | tf_op jit(solution)/shard_map/ppermute | solution.py:150
  32.2 0.6 %shard_map.85 = bf16[128,256]{1,0:T(8,128)(2,1)} custom-call(bf16[128,128]{1,0:T(8,128)(2,1)S(1)} %shard_map.84.stay_ref, bf16[128,128]{1,0:T(8,128)(2,1)S(1)} %collective-permute-done.14.got_ref), custom_call_target="tpu_custom_call" | custom-call | tf_op jit(solution)/shard_map/pallas_call | solution.py:497
  (25 shorter events, 0.2 us)
Async XLA Ops:
  0.0 6.0 %copy-start.3 = (bf16[128,256]{1,0:T(8,128)(2,1)S(1)}, bf16[128,256]{1,0:T(8,128)(2,1)}, u32[]{:S(2)}) copy-start(bf16[128,256]{1,0:T(8,128)(2,1)} %refs_0_.1) | copy-start | bytes 196612
  0.0 10.9 %copy-start = (bf16[2048,3,256]{2,0,1:T(8,128)(2,1)S(1)}, bf16[2048,3,256]{2,0,1:T(8,128)(2,1)}, u32[]{:S(2)}) copy-start(bf16[2048,3,256]{2,0,1:T(8,128)(2,1)} %param.8) | copy-start | bytes 9437188
  0.0 10.4 %collective-permute-start = (bf16[128,2048]{1,0:T(8,128)(2,1)}, bf16[128,2048]{1,0:T(8,128)(2,1)S(1)}, u32[]{:S(2)}, u32[]{:S(2)}) collective-permute-start(bf16[128,2048]{1,0:T(8,128)(2,1)} %rows_ref.3), channel_id=1, source_target_pairs={{1,3},{3,2},{2,0},{0,1},{5,7},{7,6},{6,4},{4,5},{9,11},{11,10},{10... | collective-permute-start | bytes 1572872 | tf_op jit(solution)/shard_map/ppermute | solution.py:390
  0.5 1.3 %copy-start.6 = (bf16[128,2048]{1,0:T(8,128)(2,1)S(1)}, bf16[128,2048]{1,0:T(8,128)(2,1)}, u32[]{:S(2)}) copy-start(bf16[128,2048]{1,0:T(8,128)(2,1)} %rows_ref.3) | copy-start | bytes 1572868
  1.9 8.5 %collective-permute-start.1 = (bf16[16,256]{1,0:T(8,128)(2,1)S(1)}, bf16[16,256]{1,0:T(8,128)(2,1)S(1)}, u32[]{:S(2)}, u32[]{:S(2)}) collective-permute-start(bf16[16,256]{1,0:T(8,128)(2,1)S(1)} %shard_map.73), channel_id=1, source_target_pairs={{0,6},{1,5},{2,4},{3,7},{4,10},{5,9},{6,8},{7,11},{8,14},{9,13},{1... | collective-permute-start | bytes 24584 | tf_op jit(solution)/shard_map/ppermute | solution.py:399
  6.0 8.3 %collective-permute-start.6 = (bf16[128,256]{1,0:T(8,128)(2,1)S(1)}, bf16[128,256]{1,0:T(8,128)(2,1)S(1)}, u32[]{:S(2)}, u32[]{:S(2)}) collective-permute-start(bf16[128,256]{1,0:T(8,128)(2,1)S(1)} %copy-done.3), channel_id=1, source_target_pairs={{0,4},{4,0},{8,12},{12,8},{1,5},{5,1},{9,13},{13,9},{2,6},{6,2},{1... | collective-permute-start | bytes 196616 | tf_op jit(solution)/shard_map/ppermute | solution.py:410
  7.5 7.2 %collective-permute-start.7 = (bf16[128,256]{1,0:T(8,128)(2,1)S(1)}, bf16[128,256]{1,0:T(8,128)(2,1)S(1)}, u32[]{:S(2)}, u32[]{:S(2)}) collective-permute-start(bf16[128,256]{1,0:T(8,128)(2,1)S(1)} %copy-done.3), channel_id=1, source_target_pairs={{0,8},{4,12},{8,0},{12,4},{1,9},{5,13},{9,1},{13,5},{2,10},{6,14},... | collective-permute-start | bytes 196616 | tf_op jit(solution)/shard_map/ppermute | solution.py:410
  8.6 6.2 %collective-permute-start.8 = (bf16[128,256]{1,0:T(8,128)(2,1)S(1)}, bf16[128,256]{1,0:T(8,128)(2,1)S(1)}, u32[]{:S(2)}, u32[]{:S(2)}) collective-permute-start(bf16[128,256]{1,0:T(8,128)(2,1)S(1)} %copy-done.3), channel_id=1, source_target_pairs={{0,12},{4,8},{8,4},{12,0},{1,13},{5,9},{9,5},{13,1},{2,14},{6,10},... | collective-permute-start | bytes 196616 | tf_op jit(solution)/shard_map/ppermute | solution.py:410
  10.4 1.2 %collective-permute-start.3 = (bf16[16,256]{1,0:T(8,128)(2,1)S(1)}, bf16[16,256]{1,0:T(8,128)(2,1)S(1)}, u32[]{:S(2)}, u32[]{:S(2)}) collective-permute-start(bf16[16,256]{1,0:T(8,128)(2,1)S(1)} %collective-permute-done.1.refs_1_.pack_ref), channel_id=1, source_target_pairs={{0,1},{1,0},{2,3},{3,2},{4,5},{5,4},{6,7},{7,6},{8,9},{9,8},{10,11... | collective-permute-start | bytes 24584 | tf_op jit(solution)/shard_map/ppermute | solution.py:150
  10.4 2.0 %collective-permute-start.2 = (bf16[128,2048]{1,0:T(8,128)(2,1)S(1)}, bf16[128,2048]{1,0:T(8,128)(2,1)S(1)}, u32[]{:S(2)}, u32[]{:S(2)}) collective-permute-start(bf16[128,2048]{1,0:T(8,128)(2,1)S(1)} %shard_map.74.cycled_ref), channel_id=1, source_target_pairs={{0,1},{1,0},{2,3},{3,2},{4,5},{5,4},{6,7},{7,6},{8,9},{9,8},{10,11... | collective-permute-start | bytes 1572872 | tf_op jit(solution)/shard_map/ppermute | solution.py:150
  11.5 5.9 %collective-permute-start.4 = (bf16[128,384]{1,0:T(8,128)(2,1)S(1)}, bf16[128,384]{1,0:T(8,128)(2,1)S(1)}, u32[]{:S(2)}, u32[]{:S(2)}) collective-permute-start(bf16[128,384]{1,0:T(8,128)(2,1)S(1)} %get-tuple-element.21), channel_id=1, source_target_pairs={{0,2},{2,0},{1,3},{3,1},{4,6},{6,4},{5,7},{7,5},{8,10},{10,8},{9,1... | collective-permute-start | bytes 294920 | tf_op jit(solution)/shard_map/ppermute | solution.py:150
  13.0 5.3 %copy-start.4 = (f32[3,3,256]{2,1,0:T(4,128)S(1)}, f32[3,3,256]{2,1,0:T(4,128)}, u32[]{:S(2)}) copy-start(f32[3,3,256]{2,1,0:T(4,128)} %short_ref.3) | copy-start | bytes 27652
  13.0 10.3 %copy-start.1 = (bf16[512,256]{1,0:T(8,128)(2,1)S(1)}, bf16[512,256]{1,0:T(8,128)(2,1)}, u32[]{:S(2)}) copy-start(bf16[512,256]{1,0:T(8,128)(2,1)} %constant.4.clone.table_ref) | copy-start | bytes 786436
  13.0 5.3 %collective-permute-start.5 = (bf16[144,256]{1,0:T(8,128)(2,1)S(1)}, bf16[144,256]{1,0:T(8,128)(2,1)S(1)}, u32[]{:S(2)}, u32[]{:S(2)}) collective-permute-start(bf16[144,256]{1,0:T(8,128)(2,1)S(1)} %get-tuple-element.22), channel_id=1, source_target_pairs={{0,2},{2,0},{1,3},{3,1},{4,6},{6,4},{5,7},{7,5},{8,10},{10,8},{9,1... | collective-permute-start | bytes 221192 | tf_op jit(solution)/shard_map/ppermute | solution.py:150
  14.8 13.0 %copy-start.2 = (bf16[256,512]{1,0:T(8,128)(2,1)S(1)}, bf16[256,512]{1,0:T(8,128)(2,1)}, u32[]{:S(2)}) copy-start(bf16[256,512]{1,0:T(8,128)(2,1)} %constant.5.clone.turned_ref) | copy-start | bytes 786436
  14.8 13.0 %copy-start.5 = (f32[256]{0:T(256)S(1)}, f32[256]{0:T(256)}, u32[]{:S(2)}) copy-start(f32[256]{0:T(256)} %param.10) | copy-start | bytes 3076
  14.8 8.5 %collective-permute-start.12 = (bf16[4,128,128]{2,1,0:T(8,128)(2,1)S(1)}, bf16[4,128,128]{2,1,0:T(8,128)(2,1)S(1)}, u32[]{:S(2)}, u32[]{:S(2)}) collective-permute-start(bf16[4,128,128]{2,1,0:T(8,128)(2,1)S(1)} %get-tuple-element.26), channel_id=1, source_target_pairs={{0,2},{2,0},{1,3},{3,1},{4,6},{6,4},{5,7},{7,5},{8,10},{10,8},{9,1... | collective-permute-start | bytes 393224 | tf_op jit(solution)/shard_map/ppermute | solution.py:150
  16.4 6.8 %collective-permute-start.13 = (f32[144,128]{1,0:T(8,128)S(1)}, f32[144,128]{1,0:T(8,128)S(1)}, u32[]{:S(2)}, u32[]{:S(2)}) collective-permute-start(f32[144,128]{1,0:T(8,128)S(1)} %get-tuple-element.30), channel_id=1, source_target_pairs={{0,2},{2,0},{1,3},{3,1},{4,6},{6,4},{5,7},{7,5},{8,10},{10,8},{9,1... | collective-permute-start | bytes 221192 | tf_op jit(solution)/shard_map/ppermute | solution.py:150
  18.4 6.6 %collective-permute-start.10 = (bf16[256,128]{1,0:T(8,128)(2,1)S(1)}, bf16[256,128]{1,0:T(8,128)(2,1)S(1)}, u32[]{:S(2)}, u32[]{:S(2)}) collective-permute-start(bf16[256,128]{1,0:T(8,128)(2,1)S(1)} %shard_map.78.own_ref), channel_id=1, source_target_pairs={{0,12},{4,8},{8,4},{12,0},{1,13},{5,9},{9,5},{13,1},{2,14},{6,10},... | collective-permute-start | bytes 196616 | tf_op jit(solution)/shard_map/ppermute | solution.py:467
  22.6 4.4 %collective-permute-start.11 = (bf16[256,128]{1,0:T(8,128)(2,1)S(1)}, bf16[256,128]{1,0:T(8,128)(2,1)S(1)}, u32[]{:S(2)}, u32[]{:S(2)}) collective-permute-start(bf16[256,128]{1,0:T(8,128)(2,1)S(1)} %shard_map.78.own_ref), channel_id=1, source_target_pairs={{0,4},{4,0},{8,12},{12,8},{1,5},{5,1},{9,13},{13,9},{2,6},{6,2},{1... | collective-permute-start | bytes 196616 | tf_op jit(solution)/shard_map/ppermute | solution.py:467
  22.6 5.2 %collective-permute-start.9 = (bf16[256,128]{1,0:T(8,128)(2,1)S(1)}, bf16[256,128]{1,0:T(8,128)(2,1)S(1)}, u32[]{:S(2)}, u32[]{:S(2)}) collective-permute-start(bf16[256,128]{1,0:T(8,128)(2,1)S(1)} %shard_map.78.own_ref), channel_id=1, source_target_pairs={{0,8},{4,12},{8,0},{12,4},{1,9},{5,13},{9,1},{13,5},{2,10},{6,14},... | collective-permute-start | bytes 196616 | tf_op jit(solution)/shard_map/ppermute | solution.py:467
  28.2 4.0 %collective-permute-start.14 = (bf16[128,128]{1,0:T(8,128)(2,1)S(1)}, bf16[128,128]{1,0:T(8,128)(2,1)S(1)}, u32[]{:S(2)}, u32[]{:S(2)}) collective-permute-start(bf16[128,128]{1,0:T(8,128)(2,1)S(1)} %get-tuple-element.32), channel_id=1, source_target_pairs={{0,2},{2,0},{1,3},{3,1},{4,6},{6,4},{5,7},{7,5},{8,10},{10,8},{9,1... | collective-permute-start | bytes 98312 | tf_op jit(solution)/shard_map/ppermute | solution.py:150

commit v7 on v6

--- a/solution.py
+++ b/solution.py
@@ -194,27 +194,42 @@
         keep, send = split_channels(summed, own_half)
         lanes = slice(place * half, (place + 1) * half)
         keep_ref[:, lanes] = keep
-        send_ref[:, lanes] = send.astype(send_ref.dtype)
-
-
-def project_first_body(rows_ref, cycled_ref, weight_ref, keep_ref, send_ref):
+        send_ref[:, lanes] = send.astype(BF16)
+
+
+def project_first_body(
+    rows_ref, cycled_ref, weight_ref, keep_product, send_product, keep_query, send_query
+):
     here = lax.axis_index("chan") == lax.axis_index("fsdp")
     rows = jnp.where(here, rows_ref[...], cycled_ref[...])
-    project(rows, weight_ref, (0, 1, 2), keep_ref, send_ref)
-
-
-def project_second_body(
-    branches, cycled_ref, hop_ref, pack_ref, pack_hop_ref, weight_ref, keep_ref, send_ref, *done_refs
-):
+    project(rows, weight_ref, (1, 2), keep_product, send_product)
+    project(rows, weight_ref, (0,), keep_query, send_query)
+
+
+def arrived_rows(cycled_ref, hop_ref, pack_ref, pack_hop_ref):
     here = lax.axis_index("chan") == lax.axis_index("fsdp")
     pieces = cycled_ref.shape[1] // pack_ref.shape[1]
     rows = jnp.where(here, cycled_ref[...], hop_ref[...])
     halo = unpack_halo(jnp.where(here, pack_ref[...], pack_hop_ref[...]), pieces)
     halo = jnp.where(lax.axis_index("seq") > 0, halo, jnp.zeros_like(halo))
-    rows = jnp.concatenate([halo, rows], axis=0)
-    project(rows, weight_ref, branches, keep_ref, send_ref)
-    for done_ref in done_refs:
-        done_ref[...] = jnp.zeros_like(done_ref)
+    return jnp.concatenate([halo, rows], axis=0)
+
+
+def project_product_body(
+    cycled_ref, hop_ref, pack_ref, pack_hop_ref, weight_ref, keep_ref, send_ref, done_ref
+):
+    rows = arrived_rows(cycled_ref, hop_ref, pack_ref, pack_hop_ref)
+    project(rows, weight_ref, (1, 2), keep_ref, send_ref)
+    done_ref[...] = jnp.zeros_like(done_ref)
+
+
+def project_query_body(
+    cycled_ref, hop_ref, pack_ref, pack_hop_ref, weight_ref, first_ref, keep_ref, send_ref
+):
+    rows = arrived_rows(cycled_ref, hop_ref, pack_ref, pack_hop_ref)
+    count = first_ref.shape[0]
+    send_ref[:count, :] = first_ref[...]
+    project(rows, weight_ref, (0,), keep_ref, send_ref.at[count:, :])
 
 
 def sort_taps_body(*refs):
@@ -273,16 +288,11 @@
     own = lax.axis_index("fsdp")
     rows = keep_first.shape[0]
     half = keep_second.shape[1] // len(branches)
-    first_lanes = slice(branches[0] * half, (branches[-1] + 1) * half)
     joined[:HALO, :] = keep_second[:HALO, :] + got_second[:HALO, :].astype(F32)
     own_start = pl.multiple_of(HALO + own * rows, HALO)
     other_start = pl.multiple_of(HALO + (1 - own) * rows, HALO)
-    joined[pl.ds(own_start, rows), :] = (
-        keep_first[:, first_lanes] + got_second[HALO:, :].astype(F32)
-    )
-    joined[pl.ds(other_start, rows), :] = (
-        keep_second[HALO:, :] + got_first[:, first_lanes].astype(F32)
-    )
+    joined[pl.ds(own_start, rows), :] = keep_first[...] + got_second[HALO:, :].astype(F32)
+    joined[pl.ds(other_start, rows), :] = keep_second[HALO:, :] + got_first[...].astype(F32)
     mixed = []
     for place, branch in enumerate(branches):
         lanes = slice(place * half, (place + 1) * half)
@@ -305,9 +315,10 @@
     product_ref[...] = (key * value).astype(BF16)
 
 
-def query_body(keep_first, keep_second, got_first, got_second, short_ref, query_ref, joined):
+def query_body(keep_first, keep_second, got_ref, short_ref, query_ref, joined):
+    rows = keep_first.shape[0]
     (query,) = mixed_branches(
-        (0,), keep_first, keep_second, got_first, got_second, short_ref, joined
+        (0,), keep_first, keep_second, got_ref.at[:rows, :], got_ref.at[rows:, :], short_ref, joined
     )
     query_ref[...] = query
 
@@ -412,16 +423,22 @@
     cycled = after(cycled, pack_got)
     hop = exchange(cycled, "chan")
     pack_hop = exchange(pack_got, "chan")
-    keep_first, send_first = call(
+    keep_first, send_first, keep_first_query, send_first_query = call(
         project_first_body,
         cost_estimate=LONG,
         in_specs=whole_specs(3),
-        out_specs=whole_specs(2),
-        out_shape=(shape((rows, 3 * half), F32), shape((rows, 3 * half), BF16)),
+        out_specs=whole_specs(4),
+        out_shape=(
+            shape((rows, 2 * half), F32),
+            shape((rows, 2 * half), BF16),
+            shape((rows, half), F32),
+            shape((rows, half), BF16),
+        ),
     )(tokens, cycled, weight)
     got_first = exchange(send_first, "fsdp")
-    keep_product, send_product, second_done = call(
-        functools.partial(project_second_body, (1, 2)),
+    arrived = (cycled, hop, pack_got, pack_hop, weight)
+    keep_second, send_second, second_done = call(
+        project_product_body,
         in_specs=whole_specs(5),
         out_specs=whole_specs(3),
         out_shape=(
@@ -429,13 +446,16 @@
             shape((HALO + rows, 2 * half), BF16),
             token,
         ),
-    )(cycled, hop, pack_got, pack_hop, weight)
-    keep_query, send_query = call(
-        functools.partial(project_second_body, (0,)),
-        in_specs=whole_specs(5),
+    )(*arrived)
+    keep_second_query, send_query = call(
+        project_query_body,
+        in_specs=whole_specs(6),
         out_specs=whole_specs(2),
-        out_shape=(shape((HALO + rows, half), F32), shape((HALO + rows, half), F32)),
-    )(cycled, hop, pack_got, pack_hop, weight)
+        out_shape=(
+            shape((HALO + rows, half), F32),
+            shape((rows + HALO + rows, half), BF16),
+        ),
+    )(*arrived, send_first_query)
     tap_keep, tap_send, tap_done = call(
         sort_taps_body,
         in_specs=whole_specs(1 + blocks),
@@ -446,7 +466,7 @@
             token,
         ),
     )(*tap_blocks, second_done)
-    got_product = exchange(send_product, "fsdp")
+    got_second = exchange(send_second, "fsdp")
     got_query = exchange(send_query, "fsdp")
 
     product = call(
@@ -455,15 +475,15 @@
         out_specs=whole_specs(1)[0],
         out_shape=shape((size, half), BF16),
         scratch_shapes=[pltpu.VMEM((HALO + size, 2 * half), F32)],
-    )(keep_first, keep_product, got_first, got_product, short_weight, tap_done)
+    )(keep_first, keep_second, got_first, got_second, short_weight, tap_done)
     query = call(
         query_body,
-        in_specs=whole_specs(5),
+        in_specs=whole_specs(4),
         out_specs=whole_specs(1)[0],
         out_shape=shape((size, half), F32),
         scratch_shapes=[pltpu.VMEM((HALO + size, half), F32)],
-    )(keep_first, keep_query, got_first, got_query, short_weight)
-    tap_got = exchange(tap_send, "fsdp")
+    )(keep_first_query, keep_second_query, got_query, short_weight)
+    tap_got = exchange(after(tap_send, got_first, keep_second_query), "fsdp")
     last, far, near = (lax.ppermute(product, "seq", pairs[step]) for step in (2, 3, 1))
     table = wave_table(size)
     forward = jnp.asarray(table, dtype=BF16)

time: 33 us -> 32.4 us (0.982)
  waiting for transfers between devices: 8.73 us -> 8.29 us
    ppermute x3, waiting for transfers between devices: 0.47 us -> 0.01 us  [pair_mesh(): lax.ppermute(filter_taps, 'seq', pairs[step])]
  transfers between devices with their start and end apart: 15 -> 15, of which waited for: 8 -> 7; matrix products, arithmetic and copies ran while one was open for 0% -> 0% of each run, Pallas kernels for 9% -> 9%
where the time goes in v7:
time: 32.4 us; the launch traced here: 32.2 us
  starting transfers between devices  18.4 us (57%)
  waiting for transfers between devices  8.29 us (26%)
  Pallas kernels  4.12 us (13%)
  local copies, waits for them, and re-layouts  1.3 us (4%)
    ppermute x7, starting transfers between devices, exchange(): return lax.ppermute(value, axis, [(0, 1), (1, 0)])  4.85 us
    ppermute x7, waiting for transfers between devices, exchange(): return lax.ppermute(value, axis, [(0, 1), (1, 0)])  4.65 us
    ppermute x3, starting transfers between devices, pair_mesh(): lax.ppermute(product, 'seq', pairs[step])  4.58 us
    ppermute x3, starting transfers between devices, pair_mesh(): lax.ppermute(filter_taps, 'seq', pairs[step])  4.39 us
    ppermute x1, starting transfers between devices, pair_mesh(): lax.ppermute(pack, ('seq', 'fsdp', 'chan'), [(4 * s + 2 * f + c, 4 * ((s...  4.09 us
    ppermute x3, waiting for transfers between devices, pair_mesh(): lax.ppermute(product, 'seq', pairs[step])  3.59 us
    unnamed x14, local copies, waits for them, and re-layouts  1.3 us
  transfers between devices with their start and end apart: 15, of which 7 were waited for; matrix products, arithmetic and copies ran while one was open for 0% of the time, Pallas kernels for 9%

profile of v7, /device:TPU:0, one launch (start us, length us, event | category | flops | bytes accessed | tf_op | source)
XLA Modules:
  0.0 32.2 jit_solution(10512976349994627191)
XLA Ops:
  0.0 0.5 %collective-permute-start = (bf16[128,2048]{1,0:T(8,128)(2,1)}, bf16[128,2048]{1,0:T(8,128)(2,1)S(1)}, u32[]{:S(2)}, u32[]{:S(2)}) collective-permute-start(bf16[128,2048]{1,0:T(8,128)(2,1)} %rows_ref.3), channel_id=1, source_target_pairs={{1,3},{3,2},{2,0},{0,1},{5,7},{7,6},{6,4},{4,5},{9,11},{11,10},{10... | collective-permute-start | bytes 1572872 | tf_op jit(solution)/shard_map/ppermute | solution.py:401
  0.5 1.3 %copy-done.6 = bf16[128,2048]{1,0:T(8,128)(2,1)S(1)} copy-done((bf16[128,2048]{1,0:T(8,128)(2,1)S(1)}, bf16[128,2048]{1,0:T(8,128)(2,1)}, u32[]{:S(2)}) %copy-start.6) | copy-done | bytes 524312
  1.7 0.1 shard_map.73
  1.9 4.1 %collective-permute-start.1 = (bf16[16,256]{1,0:T(8,128)(2,1)S(1)}, bf16[16,256]{1,0:T(8,128)(2,1)S(1)}, u32[]{:S(2)}, u32[]{:S(2)}) collective-permute-start(bf16[16,256]{1,0:T(8,128)(2,1)S(1)} %shard_map.73), channel_id=1, source_target_pairs={{0,6},{1,5},{2,4},{3,7},{4,10},{5,9},{6,8},{7,11},{8,14},{9,13},{1... | collective-permute-start | bytes 24584 | tf_op jit(solution)/shard_map/ppermute | solution.py:410
  6.0 1.6 %collective-permute-start.6 = (bf16[128,256]{1,0:T(8,128)(2,1)S(1)}, bf16[128,256]{1,0:T(8,128)(2,1)S(1)}, u32[]{:S(2)}, u32[]{:S(2)}) collective-permute-start(bf16[128,256]{1,0:T(8,128)(2,1)S(1)} %copy-done.3), channel_id=1, source_target_pairs={{0,4},{4,0},{8,12},{12,8},{1,5},{5,1},{9,13},{13,9},{2,6},{6,2},{1... | collective-permute-start | bytes 196616 | tf_op jit(solution)/shard_map/ppermute | solution.py:421
  7.5 1.0 %collective-permute-start.7 = (bf16[128,256]{1,0:T(8,128)(2,1)S(1)}, bf16[128,256]{1,0:T(8,128)(2,1)S(1)}, u32[]{:S(2)}, u32[]{:S(2)}) collective-permute-start(bf16[128,256]{1,0:T(8,128)(2,1)S(1)} %copy-done.3), channel_id=1, source_target_pairs={{0,8},{4,12},{8,0},{12,4},{1,9},{5,13},{9,1},{13,5},{2,10},{6,14},... | collective-permute-start | bytes 196616 | tf_op jit(solution)/shard_map/ppermute | solution.py:421
  8.6 1.8 %collective-permute-start.8 = (bf16[128,256]{1,0:T(8,128)(2,1)S(1)}, bf16[128,256]{1,0:T(8,128)(2,1)S(1)}, u32[]{:S(2)}, u32[]{:S(2)}) collective-permute-start(bf16[128,256]{1,0:T(8,128)(2,1)S(1)} %copy-done.3), channel_id=1, source_target_pairs={{0,12},{4,8},{8,4},{12,0},{1,13},{5,9},{9,5},{13,1},{2,14},{6,10},... | collective-permute-start | bytes 196616 | tf_op jit(solution)/shard_map/ppermute | solution.py:421
  10.4 0.5 %collective-permute-start.2 = (bf16[128,2048]{1,0:T(8,128)(2,1)S(1)}, bf16[128,2048]{1,0:T(8,128)(2,1)S(1)}, u32[]{:S(2)}, u32[]{:S(2)}) collective-permute-start(bf16[128,2048]{1,0:T(8,128)(2,1)S(1)} %shard_map.74.cycled_ref), channel_id=1, source_target_pairs={{0,1},{1,0},{2,3},{3,2},{4,5},{5,4},{6,7},{7,6},{8,9},{9,8},{10,11... | collective-permute-start | bytes 1572872 | tf_op jit(solution)/shard_map/ppermute | solution.py:150
  10.9 0.6 %shard_map.75 = (f32[128,256]{1,0:T(8,128)S(1)}, bf16[128,256]{1,0:T(8,128)(2,1)S(1)}, f32[128,128]{1,0:T(8,128)S(1)}, bf16[128,128]{1,0:T(8,128)(2,1)S(1)}) custom-call(bf16[128,2048]{1,0:T(8,128)(2,1)S(1)} %copy-done.6, bf16[128,2048]{1,0:T(8,128)(2,1)S(1)} %shard_map.74.cycled_ref, bf16[3,2048,256]{2,1,0:T(8,128)(2,1)S(1)} %bitcast.2), custom_call_target="tpu_custom_call" | custom-call | flops 10000000000 | bytes 40000000 | tf_op jit(solution)/shard_map/pallas_call | solution.py:426
  11.5 0.1 collective-permute-done.3.pack_hop_ref
  11.5 0.4 %collective-permute-start.4 = (bf16[128,256]{1,0:T(8,128)(2,1)S(1)}, bf16[128,256]{1,0:T(8,128)(2,1)S(1)}, u32[]{:S(2)}, u32[]{:S(2)}) collective-permute-start(bf16[128,256]{1,0:T(8,128)(2,1)S(1)} %get-tuple-element.23), channel_id=1, source_target_pairs={{0,2},{2,0},{1,3},{3,1},{4,6},{6,4},{5,7},{7,5},{8,10},{10,8},{9,1... | collective-permute-start | bytes 196616 | tf_op jit(solution)/shard_map/ppermute | solution.py:150
  11.9 0.5 %collective-permute-done.2.hop_ref = bf16[128,2048]{1,0:T(8,128)(2,1)S(1)} collective-permute-done((bf16[128,2048]{1,0:T(8,128)(2,1)S(1)}, bf16[128,2048]{1,0:T(8,128)(2,1)S(1)}, u32[]{:S(2)}, u32[]{:S(2)}) %collective-permute-start.2) | collective-permute-done | bytes 524320 | tf_op jit(solution)/shard_map/ppermute | solution.py:150
  12.4 0.6 %shard_map.76 = (f32[144,256]{1,0:T(8,128)S(1)}, bf16[144,256]{1,0:T(8,128)(2,1)S(1)}, f32[8,128]{1,0:T(8,128)S(1)}) custom-call(bf16[128,2048]{1,0:T(8,128)(2,1)S(1)} %shard_map.74.cycled_ref, bf16[128,2048]{1,0:T(8,128)(2,1)S(1)} %collective-permute-done.2.hop_ref, bf16[16,256]{1,0:T(8,128)(2,1)S(1)} %collective-permute-done.1.refs_1_.pack_ref, ...), custom_call_target="tpu_custom_call" | custom-call | tf_op jit(solution)/shard_map/pallas_call | solution.py:440
  13.0 1.2 %collective-permute-start.5 = (bf16[144,256]{1,0:T(8,128)(2,1)S(1)}, bf16[144,256]{1,0:T(8,128)(2,1)S(1)}, u32[]{:S(2)}, u32[]{:S(2)}) collective-permute-start(bf16[144,256]{1,0:T(8,128)(2,1)S(1)} %get-tuple-element.24), channel_id=1, source_target_pairs={{0,2},{2,0},{1,3},{3,1},{4,6},{6,4},{5,7},{7,5},{8,10},{10,8},{9,1... | collective-permute-start | bytes 221192 | tf_op jit(solution)/shard_map/ppermute | solution.py:150
  14.3 0.5 %shard_map.79 = (f32[144,128]{1,0:T(8,128)S(1)}, bf16[272,128]{1,0:T(8,128)(2,1)S(1)}) custom-call(bf16[128,2048]{1,0:T(8,128)(2,1)S(1)} %shard_map.74.cycled_ref, bf16[128,2048]{1,0:T(8,128)(2,1)S(1)} %collective-permute-done.2.hop_ref, bf16[16,256]{1,0:T(8,128)(2,1)S(1)} %collective-permute-done.1.refs_1_.pack_ref, ...), custom_call_target="tpu_custom_call" | custom-call | tf_op jit(solution)/shard_map/pallas_call | solution.py:450
  14.8 0.1 shard_map.77
  14.8 1.0 %collective-permute-done.4.got_first.refs_1_ = bf16[128,256]{1,0:T(8,128)(2,1)S(1)} collective-permute-done((bf16[128,256]{1,0:T(8,128)(2,1)S(1)}, bf16[128,256]{1,0:T(8,128)(2,1)S(1)}, u32[]{:S(2)}, u32[]{:S(2)}) %collective-permute-start.4) | collective-permute-done | bytes 65568 | tf_op jit(solution)/shard_map/ppermute | solution.py:150
  15.8 0.4 %collective-permute-start.12 = (bf16[4,128,128]{2,1,0:T(8,128)(2,1)S(1)}, bf16[4,128,128]{2,1,0:T(8,128)(2,1)S(1)}, u32[]{:S(2)}, u32[]{:S(2)}) collective-permute-start(bf16[4,128,128]{2,1,0:T(8,128)(2,1)S(1)} %shard_map.80), channel_id=1, source_target_pairs={{0,2},{2,0},{1,3},{3,1},{4,6},{6,4},{5,7},{7,5},{8,10},{10,8},{9,1... | collective-permute-start | bytes 393224 | tf_op jit(solution)/shard_map/ppermute | solution.py:150
  16.2 1.6 %collective-permute-start.13 = (bf16[272,128]{1,0:T(8,128)(2,1)S(1)}, bf16[272,128]{1,0:T(8,128)(2,1)S(1)}, u32[]{:S(2)}, u32[]{:S(2)}) collective-permute-start(bf16[272,128]{1,0:T(8,128)(2,1)S(1)} %get-tuple-element.34), channel_id=1, source_target_pairs={{0,2},{2,0},{1,3},{3,1},{4,6},{6,4},{5,7},{7,5},{8,10},{10,8},{9,1... | collective-permute-start | bytes 208904 | tf_op jit(solution)/shard_map/ppermute | solution.py:150
  17.9 0.1 shard_map.78.own_ref
  18.0 3.9 %collective-permute-start.10 = (bf16[256,128]{1,0:T(8,128)(2,1)S(1)}, bf16[256,128]{1,0:T(8,128)(2,1)S(1)}, u32[]{:S(2)}, u32[]{:S(2)}) collective-permute-start(bf16[256,128]{1,0:T(8,128)(2,1)S(1)} %shard_map.78.own_ref), channel_id=1, source_target_pairs={{0,12},{4,8},{8,4},{12,0},{1,13},{5,9},{9,5},{13,1},{2,14},{6,10},... | collective-permute-start | bytes 196616 | tf_op jit(solution)/shard_map/ppermute | solution.py:487
  22.0 0.6 %collective-permute-start.9 = (bf16[256,128]{1,0:T(8,128)(2,1)S(1)}, bf16[256,128]{1,0:T(8,128)(2,1)S(1)}, u32[]{:S(2)}, u32[]{:S(2)}) collective-permute-start(bf16[256,128]{1,0:T(8,128)(2,1)S(1)} %shard_map.78.own_ref), channel_id=1, source_target_pairs={{0,8},{4,12},{8,0},{12,4},{1,9},{5,13},{9,1},{13,5},{2,10},{6,14},... | collective-permute-start | bytes 196616 | tf_op jit(solution)/shard_map/ppermute | solution.py:487
  22.7 0.4 %shard_map.81 = (f32[4,256,128]{2,1,0:T(8,128)S(1)}, f32[4,256,128]{2,1,0:T(8,128)S(1)}) custom-call(bf16[512,256]{1,0:T(8,128)(2,1)S(1)} %copy-done.1, bf16[4,128,128]{2,1,0:T(8,128)(2,1)S(1)} %get-tuple-element.27.keep_ref, bf16[4,128,128]{2,1,0:T(8,128)(2,1)S(1)} %collective-permute-done.12.got_ref), custom_call_target="tpu_custom_call" | custom-call | tf_op jit(solution)/shard_map/pallas_call | solution.py:491
  23.1 1.2 %collective-permute-done.10.far_ref = bf16[256,128]{1,0:T(8,128)(2,1)S(1)} collective-permute-done((bf16[256,128]{1,0:T(8,128)(2,1)S(1)}, bf16[256,128]{1,0:T(8,128)(2,1)S(1)}, u32[]{:S(2)}, u32[]{:S(2)}) %collective-permute-start.10) | collective-permute-done | bytes 65568 | tf_op jit(solution)/shard_map/ppermute | solution.py:487
  24.4 1.9 %collective-permute-done.11.near_ref = bf16[256,128]{1,0:T(8,128)(2,1)S(1)} collective-permute-done((bf16[256,128]{1,0:T(8,128)(2,1)S(1)}, bf16[256,128]{1,0:T(8,128)(2,1)S(1)}, u32[]{:S(2)}, u32[]{:S(2)}) %collective-permute-start.11) | collective-permute-done | bytes 65568 | tf_op jit(solution)/shard_map/ppermute | solution.py:487
  26.2 0.4 %shard_map.82.total_ref = f32[2,256,128]{2,1,0:T(8,128)S(1)} custom-call(bf16[256,128]{1,0:T(8,128)(2,1)S(1)} %shard_map.78.own_ref, bf16[256,128]{1,0:T(8,128)(2,1)S(1)} %collective-permute-done.10.far_ref, bf16[256,128]{1,0:T(8,128)(2,1)S(1)} %collective-permute-done.11.near_ref, f32[4,256,128]{2,1,0:T(8,128)S(1)} %get-tuple-element.31.real_ref, ...), custom_call_target="tpu_custom_call" | custom-call | tf_op jit(solution)/shard_map/pallas_call | solution.py:497
  26.6 0.5 %collective-permute-done.9.last_ref = bf16[256,128]{1,0:T(8,128)(2,1)S(1)} collective-permute-done((bf16[256,128]{1,0:T(8,128)(2,1)S(1)}, bf16[256,128]{1,0:T(8,128)(2,1)S(1)}, u32[]{:S(2)}, u32[]{:S(2)}) %collective-permute-start.9) | collective-permute-done | bytes 65568 | tf_op jit(solution)/shard_map/ppermute | solution.py:487
  27.1 0.5 %shard_map.84 = (bf16[128,128]{1,0:T(8,128)(2,1)S(1)}, bf16[512,128]{1,0:T(8,128)(2,1)S(1)}) custom-call(bf16[256,128]{1,0:T(8,128)(2,1)S(1)} %collective-permute-done.9.last_ref, f32[2,256,128]{2,1,0:T(8,128)S(1)} %shard_map.82.total_ref, f32[4,256,128]{2,1,0:T(8,128)S(1)} %get-tuple-element.31.real_ref, f32[4,256,128]{2,1,0:T(8,128)S(1)} %get-tuple-element.32.imag_ref, ...), custom_call_target="tpu_custom_call" | custom-call | tf_op jit(solution)/shard_map/pallas_call | solution.py:504
  27.6 0.7 %collective-permute-start.14 = (bf16[128,128]{1,0:T(8,128)(2,1)S(1)}, bf16[128,128]{1,0:T(8,128)(2,1)S(1)}, u32[]{:S(2)}, u32[]{:S(2)}) collective-permute-start(bf16[128,128]{1,0:T(8,128)(2,1)S(1)} %get-tuple-element.36), channel_id=1, source_target_pairs={{0,2},{2,0},{1,3},{3,1},{4,6},{6,4},{5,7},{7,5},{8,10},{10,8},{9,1... | collective-permute-start | bytes 98312 | tf_op jit(solution)/shard_map/ppermute | solution.py:150
  28.3 0.2 shard_map.85.stay_ref
  28.5 3.1 %collective-permute-done.14.got_ref = bf16[128,128]{1,0:T(8,128)(2,1)S(1)} collective-permute-done((bf16[128,128]{1,0:T(8,128)(2,1)S(1)}, bf16[128,128]{1,0:T(8,128)(2,1)S(1)}, u32[]{:S(2)}, u32[]{:S(2)}) %collective-permute-start.14) | collective-permute-done | bytes 32800 | tf_op jit(solution)/shard_map/ppermute | solution.py:150
  31.6 0.6 %shard_map.86 = bf16[128,256]{1,0:T(8,128)(2,1)} custom-call(bf16[128,128]{1,0:T(8,128)(2,1)S(1)} %shard_map.85.stay_ref, bf16[128,128]{1,0:T(8,128)(2,1)S(1)} %collective-permute-done.14.got_ref), custom_call_target="tpu_custom_call" | custom-call | tf_op jit(solution)/shard_map/pallas_call | solution.py:517
  (26 shorter events, 0.2 us)
Async XLA Ops:
  0.0 6.0 %copy-start.3 = (bf16[128,256]{1,0:T(8,128)(2,1)S(1)}, bf16[128,256]{1,0:T(8,128)(2,1)}, u32[]{:S(2)}) copy-start(bf16[128,256]{1,0:T(8,128)(2,1)} %refs_0_.1) | copy-start | bytes 196612
  0.0 10.9 %copy-start = (bf16[2048,3,256]{2,0,1:T(8,128)(2,1)S(1)}, bf16[2048,3,256]{2,0,1:T(8,128)(2,1)}, u32[]{:S(2)}) copy-start(bf16[2048,3,256]{2,0,1:T(8,128)(2,1)} %param.8) | copy-start | bytes 9437188
  0.0 10.4 %collective-permute-start = (bf16[128,2048]{1,0:T(8,128)(2,1)}, bf16[128,2048]{1,0:T(8,128)(2,1)S(1)}, u32[]{:S(2)}, u32[]{:S(2)}) collective-permute-start(bf16[128,2048]{1,0:T(8,128)(2,1)} %rows_ref.3), channel_id=1, source_target_pairs={{1,3},{3,2},{2,0},{0,1},{5,7},{7,6},{6,4},{4,5},{9,11},{11,10},{10... | collective-permute-start | bytes 1572872 | tf_op jit(solution)/shard_map/ppermute | solution.py:401
  0.5 1.3 %copy-start.6 = (bf16[128,2048]{1,0:T(8,128)(2,1)S(1)}, bf16[128,2048]{1,0:T(8,128)(2,1)}, u32[]{:S(2)}) copy-start(bf16[128,2048]{1,0:T(8,128)(2,1)} %rows_ref.3) | copy-start | bytes 1572868
  1.9 8.5 %collective-permute-start.1 = (bf16[16,256]{1,0:T(8,128)(2,1)S(1)}, bf16[16,256]{1,0:T(8,128)(2,1)S(1)}, u32[]{:S(2)}, u32[]{:S(2)}) collective-permute-start(bf16[16,256]{1,0:T(8,128)(2,1)S(1)} %shard_map.73), channel_id=1, source_target_pairs={{0,6},{1,5},{2,4},{3,7},{4,10},{5,9},{6,8},{7,11},{8,14},{9,13},{1... | collective-permute-start | bytes 24584 | tf_op jit(solution)/shard_map/ppermute | solution.py:410
  6.0 8.8 %collective-permute-start.6 = (bf16[128,256]{1,0:T(8,128)(2,1)S(1)}, bf16[128,256]{1,0:T(8,128)(2,1)S(1)}, u32[]{:S(2)}, u32[]{:S(2)}) collective-permute-start(bf16[128,256]{1,0:T(8,128)(2,1)S(1)} %copy-done.3), channel_id=1, source_target_pairs={{0,4},{4,0},{8,12},{12,8},{1,5},{5,1},{9,13},{13,9},{2,6},{6,2},{1... | collective-permute-start | bytes 196616 | tf_op jit(solution)/shard_map/ppermute | solution.py:421
  7.5 7.2 %collective-permute-start.7 = (bf16[128,256]{1,0:T(8,128)(2,1)S(1)}, bf16[128,256]{1,0:T(8,128)(2,1)S(1)}, u32[]{:S(2)}, u32[]{:S(2)}) collective-permute-start(bf16[128,256]{1,0:T(8,128)(2,1)S(1)} %copy-done.3), channel_id=1, source_target_pairs={{0,8},{4,12},{8,0},{12,4},{1,9},{5,13},{9,1},{13,5},{2,10},{6,14},... | collective-permute-start | bytes 196616 | tf_op jit(solution)/shard_map/ppermute | solution.py:421
  8.6 6.2 %collective-permute-start.8 = (bf16[128,256]{1,0:T(8,128)(2,1)S(1)}, bf16[128,256]{1,0:T(8,128)(2,1)S(1)}, u32[]{:S(2)}, u32[]{:S(2)}) collective-permute-start(bf16[128,256]{1,0:T(8,128)(2,1)S(1)} %copy-done.3), channel_id=1, source_target_pairs={{0,12},{4,8},{8,4},{12,0},{1,13},{5,9},{9,5},{13,1},{2,14},{6,10},... | collective-permute-start | bytes 196616 | tf_op jit(solution)/shard_map/ppermute | solution.py:421
  10.4 1.2 %collective-permute-start.3 = (bf16[16,256]{1,0:T(8,128)(2,1)S(1)}, bf16[16,256]{1,0:T(8,128)(2,1)S(1)}, u32[]{:S(2)}, u32[]{:S(2)}) collective-permute-start(bf16[16,256]{1,0:T(8,128)(2,1)S(1)} %collective-permute-done.1.refs_1_.pack_ref), channel_id=1, source_target_pairs={{0,1},{1,0},{2,3},{3,2},{4,5},{5,4},{6,7},{7,6},{8,9},{9,8},{10,11... | collective-permute-start | bytes 24584 | tf_op jit(solution)/shard_map/ppermute | solution.py:150
  10.4 2.0 %collective-permute-start.2 = (bf16[128,2048]{1,0:T(8,128)(2,1)S(1)}, bf16[128,2048]{1,0:T(8,128)(2,1)S(1)}, u32[]{:S(2)}, u32[]{:S(2)}) collective-permute-start(bf16[128,2048]{1,0:T(8,128)(2,1)S(1)} %shard_map.74.cycled_ref), channel_id=1, source_target_pairs={{0,1},{1,0},{2,3},{3,2},{4,5},{5,4},{6,7},{7,6},{8,9},{9,8},{10,11... | collective-permute-start | bytes 1572872 | tf_op jit(solution)/shard_map/ppermute | solution.py:150
  11.5 4.3 %collective-permute-start.4 = (bf16[128,256]{1,0:T(8,128)(2,1)S(1)}, bf16[128,256]{1,0:T(8,128)(2,1)S(1)}, u32[]{:S(2)}, u32[]{:S(2)}) collective-permute-start(bf16[128,256]{1,0:T(8,128)(2,1)S(1)} %get-tuple-element.23), channel_id=1, source_target_pairs={{0,2},{2,0},{1,3},{3,1},{4,6},{6,4},{5,7},{7,5},{8,10},{10,8},{9,1... | collective-permute-start | bytes 196616 | tf_op jit(solution)/shard_map/ppermute | solution.py:150
  13.0 4.9 %copy-start.4 = (f32[3,3,256]{2,1,0:T(4,128)S(1)}, f32[3,3,256]{2,1,0:T(4,128)}, u32[]{:S(2)}) copy-start(f32[3,3,256]{2,1,0:T(4,128)} %short_ref.3) | copy-start | bytes 27652
  13.0 9.7 %copy-start.1 = (bf16[512,256]{1,0:T(8,128)(2,1)S(1)}, bf16[512,256]{1,0:T(8,128)(2,1)}, u32[]{:S(2)}) copy-start(bf16[512,256]{1,0:T(8,128)(2,1)} %constant.4.clone.table_ref) | copy-start | bytes 786436
  13.0 4.8 %collective-permute-start.5 = (bf16[144,256]{1,0:T(8,128)(2,1)S(1)}, bf16[144,256]{1,0:T(8,128)(2,1)S(1)}, u32[]{:S(2)}, u32[]{:S(2)}) collective-permute-start(bf16[144,256]{1,0:T(8,128)(2,1)S(1)} %get-tuple-element.24), channel_id=1, source_target_pairs={{0,2},{2,0},{1,3},{3,1},{4,6},{6,4},{5,7},{7,5},{8,10},{10,8},{9,1... | collective-permute-start | bytes 221192 | tf_op jit(solution)/shard_map/ppermute | solution.py:150
  14.3 12.9 %copy-start.2 = (bf16[256,512]{1,0:T(8,128)(2,1)S(1)}, bf16[256,512]{1,0:T(8,128)(2,1)}, u32[]{:S(2)}) copy-start(bf16[256,512]{1,0:T(8,128)(2,1)} %constant.5.clone.turned_ref) | copy-start | bytes 786436
  14.3 12.9 %copy-start.5 = (f32[256]{0:T(256)S(1)}, f32[256]{0:T(256)}, u32[]{:S(2)}) copy-start(f32[256]{0:T(256)} %param.10) | copy-start | bytes 3076
  15.8 6.8 %collective-permute-start.12 = (bf16[4,128,128]{2,1,0:T(8,128)(2,1)S(1)}, bf16[4,128,128]{2,1,0:T(8,128)(2,1)S(1)}, u32[]{:S(2)}, u32[]{:S(2)}) collective-permute-start(bf16[4,128,128]{2,1,0:T(8,128)(2,1)S(1)} %shard_map.80), channel_id=1, source_target_pairs={{0,2},{2,0},{1,3},{3,1},{4,6},{6,4},{5,7},{7,5},{8,10},{10,8},{9,1... | collective-permute-start | bytes 393224 | tf_op jit(solution)/shard_map/ppermute | solution.py:150
  16.2 6.4 %collective-permute-start.13 = (bf16[272,128]{1,0:T(8,128)(2,1)S(1)}, bf16[272,128]{1,0:T(8,128)(2,1)S(1)}, u32[]{:S(2)}, u32[]{:S(2)}) collective-permute-start(bf16[272,128]{1,0:T(8,128)(2,1)S(1)} %get-tuple-element.34), channel_id=1, source_target_pairs={{0,2},{2,0},{1,3},{3,1},{4,6},{6,4},{5,7},{7,5},{8,10},{10,8},{9,1... | collective-permute-start | bytes 208904 | tf_op jit(solution)/shard_map/ppermute | solution.py:150
  18.0 6.3 %collective-permute-start.10 = (bf16[256,128]{1,0:T(8,128)(2,1)S(1)}, bf16[256,128]{1,0:T(8,128)(2,1)S(1)}, u32[]{:S(2)}, u32[]{:S(2)}) collective-permute-start(bf16[256,128]{1,0:T(8,128)(2,1)S(1)} %shard_map.78.own_ref), channel_id=1, source_target_pairs={{0,12},{4,8},{8,4},{12,0},{1,13},{5,9},{9,5},{13,1},{2,14},{6,10},... | collective-permute-start | bytes 196616 | tf_op jit(solution)/shard_map/ppermute | solution.py:487
  22.0 4.3 %collective-permute-start.11 = (bf16[256,128]{1,0:T(8,128)(2,1)S(1)}, bf16[256,128]{1,0:T(8,128)(2,1)S(1)}, u32[]{:S(2)}, u32[]{:S(2)}) collective-permute-start(bf16[256,128]{1,0:T(8,128)(2,1)S(1)} %shard_map.78.own_ref), channel_id=1, source_target_pairs={{0,4},{4,0},{8,12},{12,8},{1,5},{5,1},{9,13},{13,9},{2,6},{6,2},{1... | collective-permute-start | bytes 196616 | tf_op jit(solution)/shard_map/ppermute | solution.py:487
  22.0 5.2 %collective-permute-start.9 = (bf16[256,128]{1,0:T(8,128)(2,1)S(1)}, bf16[256,128]{1,0:T(8,128)(2,1)S(1)}, u32[]{:S(2)}, u32[]{:S(2)}) collective-permute-start(bf16[256,128]{1,0:T(8,128)(2,1)S(1)} %shard_map.78.own_ref), channel_id=1, source_target_pairs={{0,8},{4,12},{8,0},{12,4},{1,9},{5,13},{9,1},{13,5},{2,10},{6,14},... | collective-permute-start | bytes 196616 | tf_op jit(solution)/shard_map/ppermute | solution.py:487
  27.6 4.0 %collective-permute-start.14 = (bf16[128,128]{1,0:T(8,128)(2,1)S(1)}, bf16[128,128]{1,0:T(8,128)(2,1)S(1)}, u32[]{:S(2)}, u32[]{:S(2)}) collective-permute-start(bf16[128,128]{1,0:T(8,128)(2,1)S(1)} %get-tuple-element.36), channel_id=1, source_target_pairs={{0,2},{2,0},{1,3},{3,1},{4,6},{6,4},{5,7},{7,5},{8,10},{10,8},{9,1... | collective-permute-start | bytes 98312 | tf_op jit(solution)/shard_map/ppermute | solution.py:150

commit v8 on v7

--- a/solution.py
+++ b/solution.py
@@ -224,25 +224,23 @@
 
 
 def project_query_body(
-    cycled_ref, hop_ref, pack_ref, pack_hop_ref, weight_ref, first_ref, keep_ref, send_ref
+    cycled_ref, hop_ref, pack_ref, pack_hop_ref, weight_ref, first_ref, order_ref,
+    own_ref, one_ref, two_ref, three_ref, keep_ref, taps_ref, send_ref, done_ref
 ):
     rows = arrived_rows(cycled_ref, hop_ref, pack_ref, pack_hop_ref)
     count = first_ref.shape[0]
     send_ref[:count, :] = first_ref[...]
-    project(rows, weight_ref, (0,), keep_ref, send_ref.at[count:, :])
-
-
-def sort_taps_body(*refs):
-    keep_ref, send_ref, done_ref = refs[-3:]
+    after_query = count + rows.shape[0]
+    project(rows, weight_ref, (0,), keep_ref, send_ref.at[count:after_query, :])
     position = lax.axis_index("seq")
     first = lax.axis_index("fsdp") == 0
-    blocks, _, half = keep_ref.shape
-    for step in range(blocks):
+    _, tap_rows, half = taps_ref.shape
+    for step, tap_ref in enumerate((own_ref, one_ref, two_ref, three_ref)):
         block = position ^ step
-        taps = refs[step][...]
-        low, high = (taps[:, :half], taps[:, half:])
-        keep_ref[block] = jnp.where(first, low, high)
-        send_ref[block] = jnp.where(first, high, low)
+        low, high = (tap_ref[:, :half], tap_ref[:, half:])
+        taps_ref[block] = jnp.where(first, low, high)
+        start = pl.multiple_of(after_query + block * tap_rows, HALO)
+        send_ref[pl.ds(start, tap_rows), :] = jnp.where(first, high, low)
     done_ref[...] = jnp.zeros_like(done_ref)
 
 
@@ -250,13 +248,14 @@
     pass
 
 
-def after(value, *orders):
+def after(value, *orders, cost_estimate=None):
     return pl.pallas_call(
         after_body,
         in_specs=whole_specs(1 + len(orders)),
         out_specs=whole_specs(1)[0],
         out_shape=shape(value.shape, value.dtype),
         input_output_aliases={0: 0},
+        cost_estimate=cost_estimate,
         compiler_params=pltpu.CompilerParams(vmem_limit_bytes=32 * 1024 * 1024),
     )(value, *orders)
 
@@ -269,7 +268,8 @@
     sign = sign * (1.0 / size)
     before_real = before_imag = None
     for block in range(blocks):
-        keep, got = (keep_ref[block], got_ref[block])
+        start = got_ref.shape[0] - (blocks - block) * keep_ref.shape[1]
+        keep, got = (keep_ref[block], got_ref[start : start + keep_ref.shape[1], :])
         taps = jnp.concatenate(
             [jnp.where(first, keep, got), jnp.where(first, got, keep)], axis=0
         )
@@ -318,7 +318,7 @@
 def query_body(keep_first, keep_second, got_ref, short_ref, query_ref, joined):
     rows = keep_first.shape[0]
     (query,) = mixed_branches(
-        (0,), keep_first, keep_second, got_ref.at[:rows, :], got_ref.at[rows:, :], short_ref, joined
+        (0,), keep_first, keep_second, got_ref.at[:rows, :], got_ref.at[rows : 2 * rows + HALO, :], short_ref, joined
     )
     query_ref[...] = query
 
@@ -337,9 +337,9 @@
     return (real * tap_real - imag * tap_imag, real * tap_imag + imag * tap_real)
 
 
-def conv_early_body(own_ref, far_ref, near_ref, real_ref, imag_ref, table_ref, total_ref):
+def conv_early_body(own_ref, near_ref, far_ref, real_ref, imag_ref, table_ref, total_ref):
     total_ref[0], total_ref[1] = spectrum_term(0, own_ref, real_ref, imag_ref, table_ref)
-    for step, block_ref in ((3, far_ref), (1, near_ref)):
+    for step, block_ref in ((1, near_ref), (3, far_ref)):
         real, imag = spectrum_term(step, block_ref, real_ref, imag_ref, table_ref)
         total_ref[0] += real
         total_ref[1] += imag
@@ -447,44 +447,36 @@
             token,
         ),
     )(*arrived)
-    keep_second_query, send_query = call(
+    keep_second_query, tap_keep, send_late, late_done = call(
         project_query_body,
-        in_specs=whole_specs(6),
-        out_specs=whole_specs(2),
+        in_specs=whole_specs(7 + blocks),
+        out_specs=whole_specs(4),
         out_shape=(
             shape((HALO + rows, half), F32),
-            shape((rows + HALO + rows, half), BF16),
-        ),
-    )(*arrived, send_first_query)
-    tap_keep, tap_send, tap_done = call(
-        sort_taps_body,
-        in_specs=whole_specs(1 + blocks),
-        out_specs=whole_specs(3),
-        out_shape=(
             shape((blocks, rows, half), BF16),
-            shape((blocks, rows, half), BF16),
+            shape((rows + HALO + rows + blocks * rows, half), BF16),
             token,
         ),
-    )(*tap_blocks, second_done)
+    )(*arrived, send_first_query, second_done, *tap_blocks)
     got_second = exchange(send_second, "fsdp")
-    got_query = exchange(send_query, "fsdp")
 
     product = call(
         product_body,
+        cost_estimate=LONG,
         in_specs=whole_specs(6),
         out_specs=whole_specs(1)[0],
         out_shape=shape((size, half), BF16),
         scratch_shapes=[pltpu.VMEM((HALO + size, 2 * half), F32)],
-    )(keep_first, keep_second, got_first, got_second, short_weight, tap_done)
+    )(keep_first, keep_second, got_first, got_second, short_weight, late_done)
+    got_late = exchange(after(send_late, got_first, cost_estimate=LONG), "fsdp")
     query = call(
         query_body,
         in_specs=whole_specs(4),
         out_specs=whole_specs(1)[0],
         out_shape=shape((size, half), F32),
         scratch_shapes=[pltpu.VMEM((HALO + size, half), F32)],
-    )(keep_first_query, keep_second_query, got_query, short_weight)
-    tap_got = exchange(after(tap_send, got_first, keep_second_query), "fsdp")
-    last, far, near = (lax.ppermute(product, "seq", pairs[step]) for step in (2, 3, 1))
+    )(keep_first_query, keep_second_query, got_late, short_weight)
+    last, near, far = (lax.ppermute(product, "seq", pairs[step]) for step in (2, 1, 3))
     table = wave_table(size)
     forward = jnp.asarray(table, dtype=BF16)
     inverse = jnp.asarray(table.T, dtype=BF16)
@@ -493,13 +485,13 @@
         in_specs=whole_specs(3),
         out_specs=whole_specs(2),
         out_shape=(shape((blocks, size, half), F32), shape((blocks, size, half), F32)),
-    )(forward, tap_keep, tap_got)
+    )(forward, tap_keep, got_late)
     total = call(
         conv_early_body,
         in_specs=whole_specs(6),
         out_specs=whole_specs(1)[0],
         out_shape=shape((2, size, half), F32),
-    )(product, far, near, tap_real, tap_imag, forward)
+    )(product, near, far, tap_real, tap_imag, forward)
     ending = (inverse, query, skip_gain.reshape(1, width), product)
     go, stacked = call(
         conv_last_body,

time: 32.4 us -> 32.1 us (level)
  starting transfers between devices: 18.4 us -> 17.3 us
  waiting for transfers between devices: 8.29 us -> 9.16 us
    ppermute x7 -> x6, starting transfers between devices: 4.85 us -> 3.88 us  [exchange(): return lax.ppermute(value, axis, [(0, 1), (1, 0)])]
    ppermute x7 -> x6, waiting for transfers between devices: 4.65 us -> 5.26 us  [exchange(): return lax.ppermute(value, axis, [(0, 1), (1, 0)])]
    ppermute x3, waiting for transfers between devices: 0.01 us -> 0.42 us  [pair_mesh(): lax.ppermute(filter_taps, 'seq', pairs[step])]
  transfers between devices with their start and end apart: 15 -> 14, of which waited for: 7 -> 8; matrix products, arithmetic and copies ran while one was open for 0% -> 0% of each run, Pallas kernels for 9% -> 10%
where the time goes in v8:
time: 32.1 us; the launch traced here: 32 us
  starting transfers between devices  17.3 us (54%)
  waiting for transfers between devices  9.16 us (29%)
  Pallas kernels  4.15 us (13%)
  local copies, waits for them, and re-layouts  1.3 us (4%)
    ppermute x6, waiting for transfers between devices, exchange(): return lax.ppermute(value, axis, [(0, 1), (1, 0)])  5.26 us
    ppermute x3, starting transfers between devices, pair_mesh(): lax.ppermute(product, 'seq', pairs[step])  4.45 us
    ppermute x3, starting transfers between devices, pair_mesh(): lax.ppermute(filter_taps, 'seq', pairs[step])  4.39 us
    ppermute x1, starting transfers between devices, pair_mesh(): lax.ppermute(pack, ('seq', 'fsdp', 'chan'), [(4 * s + 2 * f + c, 4 * ((s...  4.09 us
    ppermute x6, starting transfers between devices, exchange(): return lax.ppermute(value, axis, [(0, 1), (1, 0)])  3.88 us
    ppermute x3, waiting for transfers between devices, pair_mesh(): lax.ppermute(product, 'seq', pairs[step])  3.42 us
    unnamed x14, local copies, waits for them, and re-layouts  1.3 us
    pallas_call x1, Pallas kernels, pair_mesh(): call(join_body, in_specs=whole_specs(2), out_specs=whole_specs(1)[0], out...  0.65 us
  transfers between devices with their start and end apart: 14, of which 8 were waited for; matrix products, arithmetic and copies ran while one was open for 0% of the time, Pallas kernels for 10%

profile of v8, /device:TPU:0, one launch (start us, length us, event | category | flops | bytes accessed | tf_op | source)
XLA Modules:
  0.0 32.0 jit_solution(16576883970541287553)
XLA Ops:
  0.0 0.5 %collective-permute-start = (bf16[128,2048]{1,0:T(8,128)(2,1)}, bf16[128,2048]{1,0:T(8,128)(2,1)S(1)}, u32[]{:S(2)}, u32[]{:S(2)}) collective-permute-start(bf16[128,2048]{1,0:T(8,128)(2,1)} %rows_ref.3), channel_id=1, source_target_pairs={{1,3},{3,2},{2,0},{0,1},{5,7},{7,6},{6,4},{4,5},{9,11},{11,10},{10... | collective-permute-start | bytes 1572872 | tf_op jit(solution)/shard_map/ppermute | solution.py:401
  0.5 1.3 %copy-done.6 = bf16[128,2048]{1,0:T(8,128)(2,1)S(1)} copy-done((bf16[128,2048]{1,0:T(8,128)(2,1)S(1)}, bf16[128,2048]{1,0:T(8,128)(2,1)}, u32[]{:S(2)}) %copy-start.6) | copy-done | bytes 524312
  1.7 0.1 shard_map.73
  1.9 4.1 %collective-permute-start.1 = (bf16[16,256]{1,0:T(8,128)(2,1)S(1)}, bf16[16,256]{1,0:T(8,128)(2,1)S(1)}, u32[]{:S(2)}, u32[]{:S(2)}) collective-permute-start(bf16[16,256]{1,0:T(8,128)(2,1)S(1)} %shard_map.73), channel_id=1, source_target_pairs={{0,6},{1,5},{2,4},{3,7},{4,10},{5,9},{6,8},{7,11},{8,14},{9,13},{1... | collective-permute-start | bytes 24584 | tf_op jit(solution)/shard_map/ppermute | solution.py:410
  6.0 2.6 %collective-permute-start.7 = (bf16[128,256]{1,0:T(8,128)(2,1)S(1)}, bf16[128,256]{1,0:T(8,128)(2,1)S(1)}, u32[]{:S(2)}, u32[]{:S(2)}) collective-permute-start(bf16[128,256]{1,0:T(8,128)(2,1)S(1)} %copy-done.3), channel_id=1, source_target_pairs={{0,8},{4,12},{8,0},{12,4},{1,9},{5,13},{9,1},{13,5},{2,10},{6,14},... | collective-permute-start | bytes 196616 | tf_op jit(solution)/shard_map/ppermute | solution.py:421
  8.6 1.8 %collective-permute-start.8 = (bf16[128,256]{1,0:T(8,128)(2,1)S(1)}, bf16[128,256]{1,0:T(8,128)(2,1)S(1)}, u32[]{:S(2)}, u32[]{:S(2)}) collective-permute-start(bf16[128,256]{1,0:T(8,128)(2,1)S(1)} %copy-done.3), channel_id=1, source_target_pairs={{0,12},{4,8},{8,4},{12,0},{1,13},{5,9},{9,5},{13,1},{2,14},{6,10},... | collective-permute-start | bytes 196616 | tf_op jit(solution)/shard_map/ppermute | solution.py:421
  10.4 0.0 collective-permute-done.refs_0_
  10.4 0.5 %collective-permute-start.2 = (bf16[128,2048]{1,0:T(8,128)(2,1)S(1)}, bf16[128,2048]{1,0:T(8,128)(2,1)S(1)}, u32[]{:S(2)}, u32[]{:S(2)}) collective-permute-start(bf16[128,2048]{1,0:T(8,128)(2,1)S(1)} %shard_map.74.cycled_ref), channel_id=1, source_target_pairs={{0,1},{1,0},{2,3},{3,2},{4,5},{5,4},{6,7},{7,6},{8,9},{9,8},{10,11... | collective-permute-start | bytes 1572872 | tf_op jit(solution)/shard_map/ppermute | solution.py:150
  10.9 0.6 %shard_map.75 = (f32[128,256]{1,0:T(8,128)S(1)}, bf16[128,256]{1,0:T(8,128)(2,1)S(1)}, f32[128,128]{1,0:T(8,128)S(1)}, bf16[128,128]{1,0:T(8,128)(2,1)S(1)}) custom-call(bf16[128,2048]{1,0:T(8,128)(2,1)S(1)} %copy-done.6, bf16[128,2048]{1,0:T(8,128)(2,1)S(1)} %shard_map.74.cycled_ref, bf16[3,2048,256]{2,1,0:T(8,128)(2,1)S(1)} %bitcast.2), custom_call_target="tpu_custom_call" | custom-call | flops 10000000000 | bytes 40000000 | tf_op jit(solution)/shard_map/pallas_call | solution.py:426
  11.5 0.6 %collective-permute-start.4 = (bf16[128,256]{1,0:T(8,128)(2,1)S(1)}, bf16[128,256]{1,0:T(8,128)(2,1)S(1)}, u32[]{:S(2)}, u32[]{:S(2)}) collective-permute-start(bf16[128,256]{1,0:T(8,128)(2,1)S(1)} %get-tuple-element.22), channel_id=1, source_target_pairs={{0,2},{2,0},{1,3},{3,1},{4,6},{6,4},{5,7},{7,5},{8,10},{10,8},{9,1... | collective-permute-start | bytes 196616 | tf_op jit(solution)/shard_map/ppermute | solution.py:150
  12.1 0.3 collective-permute-done.2.hop_ref
  12.4 0.6 %shard_map.76 = (f32[144,256]{1,0:T(8,128)S(1)}, bf16[144,256]{1,0:T(8,128)(2,1)S(1)}, f32[8,128]{1,0:T(8,128)S(1)}) custom-call(bf16[128,2048]{1,0:T(8,128)(2,1)S(1)} %shard_map.74.cycled_ref, bf16[128,2048]{1,0:T(8,128)(2,1)S(1)} %collective-permute-done.2.hop_ref, bf16[16,256]{1,0:T(8,128)(2,1)S(1)} %collective-permute-done.1.refs_1_.pack_ref, ...), custom_call_target="tpu_custom_call" | custom-call | tf_op jit(solution)/shard_map/pallas_call | solution.py:440
  13.0 1.3 %collective-permute-start.5 = (bf16[144,256]{1,0:T(8,128)(2,1)S(1)}, bf16[144,256]{1,0:T(8,128)(2,1)S(1)}, u32[]{:S(2)}, u32[]{:S(2)}) collective-permute-start(bf16[144,256]{1,0:T(8,128)(2,1)S(1)} %get-tuple-element.23), channel_id=1, source_target_pairs={{0,2},{2,0},{1,3},{3,1},{4,6},{6,4},{5,7},{7,5},{8,10},{10,8},{9,1... | collective-permute-start | bytes 221192 | tf_op jit(solution)/shard_map/ppermute | solution.py:150
  14.3 0.4 %collective-permute-done.8.three_ref = bf16[128,256]{1,0:T(8,128)(2,1)S(1)} collective-permute-done((bf16[128,256]{1,0:T(8,128)(2,1)S(1)}, bf16[128,256]{1,0:T(8,128)(2,1)S(1)}, u32[]{:S(2)}, u32[]{:S(2)}) %collective-permute-start.8) | collective-permute-done | bytes 65568 | tf_op jit(solution)/shard_map/ppermute | solution.py:421
  14.7 0.5 %shard_map.77 = (f32[144,128]{1,0:T(8,128)S(1)}, bf16[4,128,128]{2,1,0:T(8,128)(2,1)S(1)}, bf16[784,128]{1,0:T(8,128)(2,1)S(1)}, f32[8,128]{1,0:T(8,128)S(1)}) custom-call(bf16[128,2048]{1,0:T(8,128)(2,1)S(1)} %shard_map.74.cycled_ref, bf16[128,2048]{1,0:T(8,128)(2,1)S(1)} %collective-permute-done.2.hop_ref, ...), custom_call_target="tpu_custom_call" | custom-call | tf_op jit(solution)/shard_map/pallas_call | solution.py:450
  15.2 0.6 %collective-permute-done.4.got_first.refs_1_ = bf16[128,256]{1,0:T(8,128)(2,1)S(1)} collective-permute-done((bf16[128,256]{1,0:T(8,128)(2,1)S(1)}, bf16[128,256]{1,0:T(8,128)(2,1)S(1)}, u32[]{:S(2)}, u32[]{:S(2)}) %collective-permute-start.4) | collective-permute-done | bytes 65568 | tf_op jit(solution)/shard_map/ppermute | solution.py:150
  15.9 0.5 %collective-permute-start.12 = (bf16[784,128]{1,0:T(8,128)(2,1)S(1)}, bf16[784,128]{1,0:T(8,128)(2,1)S(1)}, u32[]{:S(2)}, u32[]{:S(2)}) collective-permute-start(bf16[784,128]{1,0:T(8,128)(2,1)S(1)} %shard_map.79), channel_id=1, source_target_pairs={{0,2},{2,0},{1,3},{3,1},{4,6},{6,4},{5,7},{7,5},{8,10},{10,8},{9,1... | collective-permute-start | bytes 602120 | tf_op jit(solution)/shard_map/ppermute | solution.py:150
  16.4 1.5 %collective-permute-done.5.got_second = bf16[144,256]{1,0:T(8,128)(2,1)S(1)} collective-permute-done((bf16[144,256]{1,0:T(8,128)(2,1)S(1)}, bf16[144,256]{1,0:T(8,128)(2,1)S(1)}, u32[]{:S(2)}, u32[]{:S(2)}) %collective-permute-start.5) | collective-permute-done | bytes 73760 | tf_op jit(solution)/shard_map/ppermute | solution.py:150
  17.9 0.1 shard_map.78.own_ref
  18.1 3.6 %collective-permute-start.11 = (bf16[256,128]{1,0:T(8,128)(2,1)S(1)}, bf16[256,128]{1,0:T(8,128)(2,1)S(1)}, u32[]{:S(2)}, u32[]{:S(2)}) collective-permute-start(bf16[256,128]{1,0:T(8,128)(2,1)S(1)} %shard_map.78.own_ref), channel_id=1, source_target_pairs={{0,12},{4,8},{8,4},{12,0},{1,13},{5,9},{9,5},{13,1},{2,14},{6,10},... | collective-permute-start | bytes 196616 | tf_op jit(solution)/shard_map/ppermute | solution.py:479
  21.7 0.8 %collective-permute-start.9 = (bf16[256,128]{1,0:T(8,128)(2,1)S(1)}, bf16[256,128]{1,0:T(8,128)(2,1)S(1)}, u32[]{:S(2)}, u32[]{:S(2)}) collective-permute-start(bf16[256,128]{1,0:T(8,128)(2,1)S(1)} %shard_map.78.own_ref), channel_id=1, source_target_pairs={{0,8},{4,12},{8,0},{12,4},{1,9},{5,13},{9,1},{13,5},{2,10},{6,14},... | collective-permute-start | bytes 196616 | tf_op jit(solution)/shard_map/ppermute | solution.py:479
  22.5 0.1 shard_map.82.query_ref
  22.6 0.5 %shard_map.80 = (f32[4,256,128]{2,1,0:T(8,128)S(1)}, f32[4,256,128]{2,1,0:T(8,128)S(1)}) custom-call(bf16[512,256]{1,0:T(8,128)(2,1)S(1)} %copy-done.1, bf16[4,128,128]{2,1,0:T(8,128)(2,1)S(1)} %get-tuple-element.27.keep_ref, bf16[784,128]{1,0:T(8,128)(2,1)S(1)} %collective-permute-done.12.got_ref), custom_call_target="tpu_custom_call" | custom-call | tf_op jit(solution)/shard_map/pallas_call | solution.py:483
  23.0 1.3 %collective-permute-done.11.far_ref = bf16[256,128]{1,0:T(8,128)(2,1)S(1)} collective-permute-done((bf16[256,128]{1,0:T(8,128)(2,1)S(1)}, bf16[256,128]{1,0:T(8,128)(2,1)S(1)}, u32[]{:S(2)}, u32[]{:S(2)}) %collective-permute-start.11) | collective-permute-done | bytes 65568 | tf_op jit(solution)/shard_map/ppermute | solution.py:479
  24.3 1.6 %collective-permute-done.10.near_ref = bf16[256,128]{1,0:T(8,128)(2,1)S(1)} collective-permute-done((bf16[256,128]{1,0:T(8,128)(2,1)S(1)}, bf16[256,128]{1,0:T(8,128)(2,1)S(1)}, u32[]{:S(2)}, u32[]{:S(2)}) %collective-permute-start.10) | collective-permute-done | bytes 65568 | tf_op jit(solution)/shard_map/ppermute | solution.py:479
  26.0 0.4 %shard_map.81.total_ref = f32[2,256,128]{2,1,0:T(8,128)S(1)} custom-call(bf16[256,128]{1,0:T(8,128)(2,1)S(1)} %shard_map.78.own_ref, bf16[256,128]{1,0:T(8,128)(2,1)S(1)} %collective-permute-done.10.near_ref, bf16[256,128]{1,0:T(8,128)(2,1)S(1)} %collective-permute-done.11.far_ref, f32[4,256,128]{2,1,0:T(8,128)S(1)} %get-tuple-element.29.real_ref, ...), custom_call_target="tpu_custom_call" | custom-call | tf_op jit(solution)/shard_map/pallas_call | solution.py:489
  26.4 0.5 %collective-permute-done.9.last_ref = bf16[256,128]{1,0:T(8,128)(2,1)S(1)} collective-permute-done((bf16[256,128]{1,0:T(8,128)(2,1)S(1)}, bf16[256,128]{1,0:T(8,128)(2,1)S(1)}, u32[]{:S(2)}, u32[]{:S(2)}) %collective-permute-start.9) | collective-permute-done | bytes 65568 | tf_op jit(solution)/shard_map/ppermute | solution.py:479
  26.9 0.5 %shard_map.83 = (bf16[128,128]{1,0:T(8,128)(2,1)S(1)}, bf16[512,128]{1,0:T(8,128)(2,1)S(1)}) custom-call(bf16[256,128]{1,0:T(8,128)(2,1)S(1)} %collective-permute-done.9.last_ref, f32[2,256,128]{2,1,0:T(8,128)S(1)} %shard_map.81.total_ref, f32[4,256,128]{2,1,0:T(8,128)S(1)} %get-tuple-element.29.real_ref, f32[4,256,128]{2,1,0:T(8,128)S(1)} %get-tuple-element.30.imag_ref, ...), custom_call_target="tpu_custom_call" | custom-call | tf_op jit(solution)/shard_map/pallas_call | solution.py:496
  27.3 1.0 %collective-permute-start.13 = (bf16[128,128]{1,0:T(8,128)(2,1)S(1)}, bf16[128,128]{1,0:T(8,128)(2,1)S(1)}, u32[]{:S(2)}, u32[]{:S(2)}) collective-permute-start(bf16[128,128]{1,0:T(8,128)(2,1)S(1)} %get-tuple-element.34), channel_id=1, source_target_pairs={{0,2},{2,0},{1,3},{3,1},{4,6},{6,4},{5,7},{7,5},{8,10},{10,8},{9,1... | collective-permute-start | bytes 98312 | tf_op jit(solution)/shard_map/ppermute | solution.py:150
  28.3 0.2 shard_map.84.stay_ref
  28.5 2.8 %collective-permute-done.13.got_ref = bf16[128,128]{1,0:T(8,128)(2,1)S(1)} collective-permute-done((bf16[128,128]{1,0:T(8,128)(2,1)S(1)}, bf16[128,128]{1,0:T(8,128)(2,1)S(1)}, u32[]{:S(2)}, u32[]{:S(2)}) %collective-permute-start.13) | collective-permute-done | bytes 32800 | tf_op jit(solution)/shard_map/ppermute | solution.py:150
  31.3 0.6 %shard_map.85 = bf16[128,256]{1,0:T(8,128)(2,1)} custom-call(bf16[128,128]{1,0:T(8,128)(2,1)S(1)} %shard_map.84.stay_ref, bf16[128,128]{1,0:T(8,128)(2,1)S(1)} %collective-permute-done.13.got_ref), custom_call_target="tpu_custom_call" | custom-call | tf_op jit(solution)/shard_map/pallas_call | solution.py:509
  (23 shorter events, 0.1 us)
Async XLA Ops:
  0.0 6.0 %copy-start.3 = (bf16[128,256]{1,0:T(8,128)(2,1)S(1)}, bf16[128,256]{1,0:T(8,128)(2,1)}, u32[]{:S(2)}) copy-start(bf16[128,256]{1,0:T(8,128)(2,1)} %own_ref.1) | copy-start | bytes 196612
  0.0 10.9 %copy-start = (bf16[2048,3,256]{2,0,1:T(8,128)(2,1)S(1)}, bf16[2048,3,256]{2,0,1:T(8,128)(2,1)}, u32[]{:S(2)}) copy-start(bf16[2048,3,256]{2,0,1:T(8,128)(2,1)} %param.8) | copy-start | bytes 9437188
  0.0 10.4 %collective-permute-start = (bf16[128,2048]{1,0:T(8,128)(2,1)}, bf16[128,2048]{1,0:T(8,128)(2,1)S(1)}, u32[]{:S(2)}, u32[]{:S(2)}) collective-permute-start(bf16[128,2048]{1,0:T(8,128)(2,1)} %rows_ref.3), channel_id=1, source_target_pairs={{1,3},{3,2},{2,0},{0,1},{5,7},{7,6},{6,4},{4,5},{9,11},{11,10},{10... | collective-permute-start | bytes 1572872 | tf_op jit(solution)/shard_map/ppermute | solution.py:401
  0.5 1.3 %copy-start.6 = (bf16[128,2048]{1,0:T(8,128)(2,1)S(1)}, bf16[128,2048]{1,0:T(8,128)(2,1)}, u32[]{:S(2)}) copy-start(bf16[128,2048]{1,0:T(8,128)(2,1)} %rows_ref.3) | copy-start | bytes 1572868
  1.9 8.5 %collective-permute-start.1 = (bf16[16,256]{1,0:T(8,128)(2,1)S(1)}, bf16[16,256]{1,0:T(8,128)(2,1)S(1)}, u32[]{:S(2)}, u32[]{:S(2)}) collective-permute-start(bf16[16,256]{1,0:T(8,128)(2,1)S(1)} %shard_map.73), channel_id=1, source_target_pairs={{0,6},{1,5},{2,4},{3,7},{4,10},{5,9},{6,8},{7,11},{8,14},{9,13},{1... | collective-permute-start | bytes 24584 | tf_op jit(solution)/shard_map/ppermute | solution.py:410
  6.0 8.3 %collective-permute-start.7 = (bf16[128,256]{1,0:T(8,128)(2,1)S(1)}, bf16[128,256]{1,0:T(8,128)(2,1)S(1)}, u32[]{:S(2)}, u32[]{:S(2)}) collective-permute-start(bf16[128,256]{1,0:T(8,128)(2,1)S(1)} %copy-done.3), channel_id=1, source_target_pairs={{0,8},{4,12},{8,0},{12,4},{1,9},{5,13},{9,1},{13,5},{2,10},{6,14},... | collective-permute-start | bytes 196616 | tf_op jit(solution)/shard_map/ppermute | solution.py:421
  8.6 5.8 %collective-permute-start.6 = (bf16[128,256]{1,0:T(8,128)(2,1)S(1)}, bf16[128,256]{1,0:T(8,128)(2,1)S(1)}, u32[]{:S(2)}, u32[]{:S(2)}) collective-permute-start(bf16[128,256]{1,0:T(8,128)(2,1)S(1)} %copy-done.3), channel_id=1, source_target_pairs={{0,4},{4,0},{8,12},{12,8},{1,5},{5,1},{9,13},{13,9},{2,6},{6,2},{1... | collective-permute-start | bytes 196616 | tf_op jit(solution)/shard_map/ppermute | solution.py:421
  8.6 6.2 %collective-permute-start.8 = (bf16[128,256]{1,0:T(8,128)(2,1)S(1)}, bf16[128,256]{1,0:T(8,128)(2,1)S(1)}, u32[]{:S(2)}, u32[]{:S(2)}) collective-permute-start(bf16[128,256]{1,0:T(8,128)(2,1)S(1)} %copy-done.3), channel_id=1, source_target_pairs={{0,12},{4,8},{8,4},{12,0},{1,13},{5,9},{9,5},{13,1},{2,14},{6,10},... | collective-permute-start | bytes 196616 | tf_op jit(solution)/shard_map/ppermute | solution.py:421
  10.4 1.2 %collective-permute-start.3 = (bf16[16,256]{1,0:T(8,128)(2,1)S(1)}, bf16[16,256]{1,0:T(8,128)(2,1)S(1)}, u32[]{:S(2)}, u32[]{:S(2)}) collective-permute-start(bf16[16,256]{1,0:T(8,128)(2,1)S(1)} %collective-permute-done.1.refs_1_.pack_ref), channel_id=1, source_target_pairs={{0,1},{1,0},{2,3},{3,2},{4,5},{5,4},{6,7},{7,6},{8,9},{9,8},{10,11... | collective-permute-start | bytes 24584 | tf_op jit(solution)/shard_map/ppermute | solution.py:150
  10.4 2.0 %collective-permute-start.2 = (bf16[128,2048]{1,0:T(8,128)(2,1)S(1)}, bf16[128,2048]{1,0:T(8,128)(2,1)S(1)}, u32[]{:S(2)}, u32[]{:S(2)}) collective-permute-start(bf16[128,2048]{1,0:T(8,128)(2,1)S(1)} %shard_map.74.cycled_ref), channel_id=1, source_target_pairs={{0,1},{1,0},{2,3},{3,2},{4,5},{5,4},{6,7},{7,6},{8,9},{9,8},{10,11... | collective-permute-start | bytes 1572872 | tf_op jit(solution)/shard_map/ppermute | solution.py:150
  11.5 4.3 %collective-permute-start.4 = (bf16[128,256]{1,0:T(8,128)(2,1)S(1)}, bf16[128,256]{1,0:T(8,128)(2,1)S(1)}, u32[]{:S(2)}, u32[]{:S(2)}) collective-permute-start(bf16[128,256]{1,0:T(8,128)(2,1)S(1)} %get-tuple-element.22), channel_id=1, source_target_pairs={{0,2},{2,0},{1,3},{3,1},{4,6},{6,4},{5,7},{7,5},{8,10},{10,8},{9,1... | collective-permute-start | bytes 196616 | tf_op jit(solution)/shard_map/ppermute | solution.py:150
  13.0 4.9 %collective-permute-start.5 = (bf16[144,256]{1,0:T(8,128)(2,1)S(1)}, bf16[144,256]{1,0:T(8,128)(2,1)S(1)}, u32[]{:S(2)}, u32[]{:S(2)}) collective-permute-start(bf16[144,256]{1,0:T(8,128)(2,1)S(1)} %get-tuple-element.23), channel_id=1, source_target_pairs={{0,2},{2,0},{1,3},{3,1},{4,6},{6,4},{5,7},{7,5},{8,10},{10,8},{9,1... | collective-permute-start | bytes 221192 | tf_op jit(solution)/shard_map/ppermute | solution.py:150
  15.8 2.1 %copy-start.4 = (f32[3,3,256]{2,1,0:T(4,128)S(1)}, f32[3,3,256]{2,1,0:T(4,128)}, u32[]{:S(2)}) copy-start(f32[3,3,256]{2,1,0:T(4,128)} %short_ref.3) | copy-start | bytes 27652
  15.9 6.7 %collective-permute-start.12 = (bf16[784,128]{1,0:T(8,128)(2,1)S(1)}, bf16[784,128]{1,0:T(8,128)(2,1)S(1)}, u32[]{:S(2)}, u32[]{:S(2)}) collective-permute-start(bf16[784,128]{1,0:T(8,128)(2,1)S(1)} %shard_map.79), channel_id=1, source_target_pairs={{0,2},{2,0},{1,3},{3,1},{4,6},{6,4},{5,7},{7,5},{8,10},{10,8},{9,1... | collective-permute-start | bytes 602120 | tf_op jit(solution)/shard_map/ppermute | solution.py:150
  17.9 4.7 %copy-start.1 = (bf16[512,256]{1,0:T(8,128)(2,1)S(1)}, bf16[512,256]{1,0:T(8,128)(2,1)}, u32[]{:S(2)}) copy-start(bf16[512,256]{1,0:T(8,128)(2,1)} %constant.4.clone.table_ref) | copy-start | bytes 786436
  17.9 9.0 %copy-start.2 = (bf16[256,512]{1,0:T(8,128)(2,1)S(1)}, bf16[256,512]{1,0:T(8,128)(2,1)}, u32[]{:S(2)}) copy-start(bf16[256,512]{1,0:T(8,128)(2,1)} %constant.5.clone.turned_ref) | copy-start | bytes 786436
  17.9 9.0 %copy-start.5 = (f32[256]{0:T(256)S(1)}, f32[256]{0:T(256)}, u32[]{:S(2)}) copy-start(f32[256]{0:T(256)} %param.10) | copy-start | bytes 3076
  18.1 6.3 %collective-permute-start.11 = (bf16[256,128]{1,0:T(8,128)(2,1)S(1)}, bf16[256,128]{1,0:T(8,128)(2,1)S(1)}, u32[]{:S(2)}, u32[]{:S(2)}) collective-permute-start(bf16[256,128]{1,0:T(8,128)(2,1)S(1)} %shard_map.78.own_ref), channel_id=1, source_target_pairs={{0,12},{4,8},{8,4},{12,0},{1,13},{5,9},{9,5},{13,1},{2,14},{6,10},... | collective-permute-start | bytes 196616 | tf_op jit(solution)/shard_map/ppermute | solution.py:479
  21.7 4.3 %collective-permute-start.10 = (bf16[256,128]{1,0:T(8,128)(2,1)S(1)}, bf16[256,128]{1,0:T(8,128)(2,1)S(1)}, u32[]{:S(2)}, u32[]{:S(2)}) collective-permute-start(bf16[256,128]{1,0:T(8,128)(2,1)S(1)} %shard_map.78.own_ref), channel_id=1, source_target_pairs={{0,4},{4,0},{8,12},{12,8},{1,5},{5,1},{9,13},{13,9},{2,6},{6,2},{1... | collective-permute-start | bytes 196616 | tf_op jit(solution)/shard_map/ppermute | solution.py:479
  21.7 5.2 %collective-permute-start.9 = (bf16[256,128]{1,0:T(8,128)(2,1)S(1)}, bf16[256,128]{1,0:T(8,128)(2,1)S(1)}, u32[]{:S(2)}, u32[]{:S(2)}) collective-permute-start(bf16[256,128]{1,0:T(8,128)(2,1)S(1)} %shard_map.78.own_ref), channel_id=1, source_target_pairs={{0,8},{4,12},{8,0},{12,4},{1,9},{5,13},{9,1},{13,5},{2,10},{6,14},... | collective-permute-start | bytes 196616 | tf_op jit(solution)/shard_map/ppermute | solution.py:479
  27.3 4.0 %collective-permute-start.13 = (bf16[128,128]{1,0:T(8,128)(2,1)S(1)}, bf16[128,128]{1,0:T(8,128)(2,1)S(1)}, u32[]{:S(2)}, u32[]{:S(2)}) collective-permute-start(bf16[128,128]{1,0:T(8,128)(2,1)S(1)} %get-tuple-element.34), channel_id=1, source_target_pairs={{0,2},{2,0},{1,3},{3,1},{4,6},{6,4},{5,7},{7,5},{8,10},{10,8},{9,1... | collective-permute-start | bytes 98312 | tf_op jit(solution)/shard_map/ppermute | solution.py:150

commit v9 on v8

--- a/solution.py
+++ b/solution.py
@@ -206,28 +206,32 @@
     project(rows, weight_ref, (0,), keep_query, send_query)
 
 
-def arrived_rows(cycled_ref, hop_ref, pack_ref, pack_hop_ref):
+def halo_body(pack_ref, pack_hop_ref, halo_ref):
     here = lax.axis_index("chan") == lax.axis_index("fsdp")
-    pieces = cycled_ref.shape[1] // pack_ref.shape[1]
+    pieces = halo_ref.shape[1] // pack_ref.shape[1]
+    halo = unpack_halo(jnp.where(here, pack_ref[...], pack_hop_ref[...]), pieces)
+    halo_ref[...] = jnp.where(lax.axis_index("seq") > 0, halo, jnp.zeros_like(halo))
+
+
+def arrived_rows(cycled_ref, hop_ref, halo_ref):
+    here = lax.axis_index("chan") == lax.axis_index("fsdp")
     rows = jnp.where(here, cycled_ref[...], hop_ref[...])
-    halo = unpack_halo(jnp.where(here, pack_ref[...], pack_hop_ref[...]), pieces)
-    halo = jnp.where(lax.axis_index("seq") > 0, halo, jnp.zeros_like(halo))
-    return jnp.concatenate([halo, rows], axis=0)
+    return jnp.concatenate([halo_ref[...], rows], axis=0)
 
 
 def project_product_body(
-    cycled_ref, hop_ref, pack_ref, pack_hop_ref, weight_ref, keep_ref, send_ref, done_ref
+    cycled_ref, hop_ref, halo_ref, weight_ref, keep_ref, send_ref, done_ref
 ):
-    rows = arrived_rows(cycled_ref, hop_ref, pack_ref, pack_hop_ref)
+    rows = arrived_rows(cycled_ref, hop_ref, halo_ref)
     project(rows, weight_ref, (1, 2), keep_ref, send_ref)
     done_ref[...] = jnp.zeros_like(done_ref)
 
 
 def project_query_body(
-    cycled_ref, hop_ref, pack_ref, pack_hop_ref, weight_ref, first_ref, order_ref,
+    cycled_ref, hop_ref, halo_ref, weight_ref, first_ref, order_ref,
     own_ref, one_ref, two_ref, three_ref, keep_ref, taps_ref, send_ref, done_ref
 ):
-    rows = arrived_rows(cycled_ref, hop_ref, pack_ref, pack_hop_ref)
+    rows = arrived_rows(cycled_ref, hop_ref, halo_ref)
     count = first_ref.shape[0]
     send_ref[:count, :] = first_ref[...]
     after_query = count + rows.shape[0]
@@ -317,8 +321,10 @@
 
 def query_body(keep_first, keep_second, got_ref, short_ref, query_ref, joined):
     rows = keep_first.shape[0]
+    got_first = got_ref.at[:rows, :]
+    got_second = got_ref.at[rows : rows + keep_second.shape[0], :]
     (query,) = mixed_branches(
-        (0,), keep_first, keep_second, got_ref.at[:rows, :], got_ref.at[rows : 2 * rows + HALO, :], short_ref, joined
+        (0,), keep_first, keep_second, got_first, got_second, short_ref, joined
     )
     query_ref[...] = query
 
@@ -436,10 +442,16 @@
         ),
     )(tokens, cycled, weight)
     got_first = exchange(send_first, "fsdp")
-    arrived = (cycled, hop, pack_got, pack_hop, weight)
+    halo = call(
+        halo_body,
+        in_specs=whole_specs(2),
+        out_specs=whole_specs(1)[0],
+        out_shape=shape((HALO, tokens.shape[1]), BF16),
+    )(pack_got, pack_hop)
+    arrived = (cycled, hop, halo, weight)
     keep_second, send_second, second_done = call(
         project_product_body,
-        in_specs=whole_specs(5),
+        in_specs=whole_specs(4),
         out_specs=whole_specs(3),
         out_shape=(
             shape((HALO + rows, 2 * half), F32),
@@ -449,7 +461,7 @@
     )(*arrived)
     keep_second_query, tap_keep, send_late, late_done = call(
         project_query_body,
-        in_specs=whole_specs(7 + blocks),
+        in_specs=whole_specs(6 + blocks),
         out_specs=whole_specs(4),
         out_shape=(
             shape((HALO + rows, half), F32),

time: 32.1 us -> 32 us (level)
  waiting for transfers between devices: 9.16 us -> 8.76 us
    ppermute x6, waiting for transfers between devices: 5.26 us -> 4.79 us  [exchange(): return lax.ppermute(value, axis, [(0, 1), (1, 0)])]
    ppermute x6, starting transfers between devices: 3.88 us -> 4.22 us  [exchange(): return lax.ppermute(value, axis, [(0, 1), (1, 0)])]
    pallas_call x2 -> x3, Pallas kernels: 1.08 us -> 1.02 us  [the longest x1 0.5 us: pair_mesh(): call(project_product_body, in_specs=whole_specs(4), out_specs=whole_specs...]
  transfers between devices with their start and end apart: 14 -> 14, of which waited for: 8 -> 8; matrix products, arithmetic and copies ran while one was open for 0% -> 0% of each run, Pallas kernels for 10% -> 9%
where the time goes in v9:
time: 32 us; the launch traced here: 31.9 us
  starting transfers between devices  17.6 us (55%)
  waiting for transfers between devices  8.76 us (27%)
  Pallas kernels  4.09 us (13%)
  local copies, waits for them, and re-layouts  1.3 us (4%)
    ppermute x6, waiting for transfers between devices, exchange(): return lax.ppermute(value, axis, [(0, 1), (1, 0)])  4.79 us
    ppermute x3, starting transfers between devices, pair_mesh(): lax.ppermute(product, 'seq', pairs[step])  4.45 us
    ppermute x3, starting transfers between devices, pair_mesh(): lax.ppermute(filter_taps, 'seq', pairs[step])  4.39 us
    ppermute x6, starting transfers between devices, exchange(): return lax.ppermute(value, axis, [(0, 1), (1, 0)])  4.22 us
    ppermute x1, starting transfers between devices, pair_mesh(): lax.ppermute(pack, ('seq', 'fsdp', 'chan'), [(4 * s + 2 * f + c, 4 * ((s...  4.09 us
    ppermute x3, waiting for transfers between devices, pair_mesh(): lax.ppermute(product, 'seq', pairs[step])  3.55 us
    unnamed x14, local copies, waits for them, and re-layouts  1.3 us
    pallas_call x1, Pallas kernels, pair_mesh(): call(join_body, in_specs=whole_specs(2), out_specs=whole_specs(1)[0], out...  0.65 us
  transfers between devices with their start and end apart: 14, of which 8 were waited for; matrix products, arithmetic and copies ran while one was open for 0% of the time, Pallas kernels for 9%

profile of v9, /device:TPU:0, one launch (start us, length us, event | category | flops | bytes accessed | tf_op | source)
XLA Modules:
  0.0 31.9 jit_solution(17057544802516340385)
XLA Ops:
  0.0 0.5 %collective-permute-start = (bf16[128,2048]{1,0:T(8,128)(2,1)}, bf16[128,2048]{1,0:T(8,128)(2,1)S(1)}, u32[]{:S(2)}, u32[]{:S(2)}) collective-permute-start(bf16[128,2048]{1,0:T(8,128)(2,1)} %rows_ref.3), channel_id=1, source_target_pairs={{1,3},{3,2},{2,0},{0,1},{5,7},{7,6},{6,4},{4,5},{9,11},{11,10},{10... | collective-permute-start | bytes 1572872 | tf_op jit(solution)/shard_map/ppermute | solution.py:407
  0.5 1.3 %copy-done.6 = bf16[128,2048]{1,0:T(8,128)(2,1)S(1)} copy-done((bf16[128,2048]{1,0:T(8,128)(2,1)S(1)}, bf16[128,2048]{1,0:T(8,128)(2,1)}, u32[]{:S(2)}) %copy-start.6) | copy-done | bytes 524312
  1.7 0.1 shard_map.73
  1.9 4.1 %collective-permute-start.1 = (bf16[16,256]{1,0:T(8,128)(2,1)S(1)}, bf16[16,256]{1,0:T(8,128)(2,1)S(1)}, u32[]{:S(2)}, u32[]{:S(2)}) collective-permute-start(bf16[16,256]{1,0:T(8,128)(2,1)S(1)} %shard_map.73), channel_id=1, source_target_pairs={{0,6},{1,5},{2,4},{3,7},{4,10},{5,9},{6,8},{7,11},{8,14},{9,13},{1... | collective-permute-start | bytes 24584 | tf_op jit(solution)/shard_map/ppermute | solution.py:416
  6.0 2.6 %collective-permute-start.7 = (bf16[128,256]{1,0:T(8,128)(2,1)S(1)}, bf16[128,256]{1,0:T(8,128)(2,1)S(1)}, u32[]{:S(2)}, u32[]{:S(2)}) collective-permute-start(bf16[128,256]{1,0:T(8,128)(2,1)S(1)} %copy-done.3), channel_id=1, source_target_pairs={{0,8},{4,12},{8,0},{12,4},{1,9},{5,13},{9,1},{13,5},{2,10},{6,14},... | collective-permute-start | bytes 196616 | tf_op jit(solution)/shard_map/ppermute | solution.py:427
  8.6 1.8 %collective-permute-start.8 = (bf16[128,256]{1,0:T(8,128)(2,1)S(1)}, bf16[128,256]{1,0:T(8,128)(2,1)S(1)}, u32[]{:S(2)}, u32[]{:S(2)}) collective-permute-start(bf16[128,256]{1,0:T(8,128)(2,1)S(1)} %copy-done.3), channel_id=1, source_target_pairs={{0,12},{4,8},{8,4},{12,0},{1,13},{5,9},{9,5},{13,1},{2,14},{6,10},... | collective-permute-start | bytes 196616 | tf_op jit(solution)/shard_map/ppermute | solution.py:427
  10.4 0.5 %collective-permute-start.2 = (bf16[128,2048]{1,0:T(8,128)(2,1)S(1)}, bf16[128,2048]{1,0:T(8,128)(2,1)S(1)}, u32[]{:S(2)}, u32[]{:S(2)}) collective-permute-start(bf16[128,2048]{1,0:T(8,128)(2,1)S(1)} %shard_map.74.cycled_ref), channel_id=1, source_target_pairs={{0,1},{1,0},{2,3},{3,2},{4,5},{5,4},{6,7},{7,6},{8,9},{9,8},{10,11... | collective-permute-start | bytes 1572872 | tf_op jit(solution)/shard_map/ppermute | solution.py:150
  10.9 0.6 %shard_map.75 = (f32[128,256]{1,0:T(8,128)S(1)}, bf16[128,256]{1,0:T(8,128)(2,1)S(1)}, f32[128,128]{1,0:T(8,128)S(1)}, bf16[128,128]{1,0:T(8,128)(2,1)S(1)}) custom-call(bf16[128,2048]{1,0:T(8,128)(2,1)S(1)} %copy-done.6, bf16[128,2048]{1,0:T(8,128)(2,1)S(1)} %shard_map.74.cycled_ref, bf16[3,2048,256]{2,1,0:T(8,128)(2,1)S(1)} %bitcast.2), custom_call_target="tpu_custom_call" | custom-call | flops 10000000000 | bytes 40000000 | tf_op jit(solution)/shard_map/pallas_call | solution.py:432
  11.5 0.6 %collective-permute-start.4 = (bf16[128,256]{1,0:T(8,128)(2,1)S(1)}, bf16[128,256]{1,0:T(8,128)(2,1)S(1)}, u32[]{:S(2)}, u32[]{:S(2)}) collective-permute-start(bf16[128,256]{1,0:T(8,128)(2,1)S(1)} %get-tuple-element.22), channel_id=1, source_target_pairs={{0,2},{2,0},{1,3},{3,1},{4,6},{6,4},{5,7},{7,5},{8,10},{10,8},{9,1... | collective-permute-start | bytes 196616 | tf_op jit(solution)/shard_map/ppermute | solution.py:150
  12.1 0.1 shard_map.76.halo_ref
  12.3 0.1 collective-permute-done.2.hop_ref
  12.4 0.5 %shard_map.77 = (f32[144,256]{1,0:T(8,128)S(1)}, bf16[144,256]{1,0:T(8,128)(2,1)S(1)}, f32[8,128]{1,0:T(8,128)S(1)}) custom-call(bf16[128,2048]{1,0:T(8,128)(2,1)S(1)} %shard_map.74.cycled_ref, bf16[128,2048]{1,0:T(8,128)(2,1)S(1)} %collective-permute-done.2.hop_ref, bf16[16,2048]{1,0:T(8,128)(2,1)S(1)} %shard_map.76.halo_ref, bf16[3,2048,256]{2,1,0:T(8,128)(2,1)S(1)} %bitcast.3), custom_call_target="tpu_custom_call" | custom-call | tf_op jit(solution)/shard_map/pallas_call | solution.py:452
  12.9 1.4 %collective-permute-start.5 = (bf16[144,256]{1,0:T(8,128)(2,1)S(1)}, bf16[144,256]{1,0:T(8,128)(2,1)S(1)}, u32[]{:S(2)}, u32[]{:S(2)}) collective-permute-start(bf16[144,256]{1,0:T(8,128)(2,1)S(1)} %get-tuple-element.23), channel_id=1, source_target_pairs={{0,2},{2,0},{1,3},{3,1},{4,6},{6,4},{5,7},{7,5},{8,10},{10,8},{9,1... | collective-permute-start | bytes 221192 | tf_op jit(solution)/shard_map/ppermute | solution.py:150
  14.4 0.4 %collective-permute-done.8.three_ref = bf16[128,256]{1,0:T(8,128)(2,1)S(1)} collective-permute-done((bf16[128,256]{1,0:T(8,128)(2,1)S(1)}, bf16[128,256]{1,0:T(8,128)(2,1)S(1)}, u32[]{:S(2)}, u32[]{:S(2)}) %collective-permute-start.8) | collective-permute-done | bytes 65568 | tf_op jit(solution)/shard_map/ppermute | solution.py:427
  14.7 0.4 %shard_map.78 = (f32[144,128]{1,0:T(8,128)S(1)}, bf16[4,128,128]{2,1,0:T(8,128)(2,1)S(1)}, bf16[784,128]{1,0:T(8,128)(2,1)S(1)}, f32[8,128]{1,0:T(8,128)S(1)}) custom-call(bf16[128,2048]{1,0:T(8,128)(2,1)S(1)} %shard_map.74.cycled_ref, bf16[128,2048]{1,0:T(8,128)(2,1)S(1)} %collective-permute-done.2.hop_ref, bf16[16,2048]{1,0:T(8,128)(2,1)S(1)} %shard_map.76.halo_ref, ...), custom_call_target="tpu_custom_call" | custom-call | tf_op jit(solution)/shard_map/pallas_call | solution.py:462
  15.1 0.7 %collective-permute-done.4.got_first.refs_1_ = bf16[128,256]{1,0:T(8,128)(2,1)S(1)} collective-permute-done((bf16[128,256]{1,0:T(8,128)(2,1)S(1)}, bf16[128,256]{1,0:T(8,128)(2,1)S(1)}, u32[]{:S(2)}, u32[]{:S(2)}) %collective-permute-start.4) | collective-permute-done | bytes 65568 | tf_op jit(solution)/shard_map/ppermute | solution.py:150
  15.9 0.5 %collective-permute-start.12 = (bf16[784,128]{1,0:T(8,128)(2,1)S(1)}, bf16[784,128]{1,0:T(8,128)(2,1)S(1)}, u32[]{:S(2)}, u32[]{:S(2)}) collective-permute-start(bf16[784,128]{1,0:T(8,128)(2,1)S(1)} %shard_map.80), channel_id=1, source_target_pairs={{0,2},{2,0},{1,3},{3,1},{4,6},{6,4},{5,7},{7,5},{8,10},{10,8},{9,1... | collective-permute-start | bytes 602120 | tf_op jit(solution)/shard_map/ppermute | solution.py:150
  16.4 1.3 %collective-permute-done.5.got_second = bf16[144,256]{1,0:T(8,128)(2,1)S(1)} collective-permute-done((bf16[144,256]{1,0:T(8,128)(2,1)S(1)}, bf16[144,256]{1,0:T(8,128)(2,1)S(1)}, u32[]{:S(2)}, u32[]{:S(2)}) %collective-permute-start.5) | collective-permute-done | bytes 73760 | tf_op jit(solution)/shard_map/ppermute | solution.py:150
  17.7 0.1 shard_map.79.own_ref
  17.8 3.8 %collective-permute-start.11 = (bf16[256,128]{1,0:T(8,128)(2,1)S(1)}, bf16[256,128]{1,0:T(8,128)(2,1)S(1)}, u32[]{:S(2)}, u32[]{:S(2)}) collective-permute-start(bf16[256,128]{1,0:T(8,128)(2,1)S(1)} %shard_map.79.own_ref), channel_id=1, source_target_pairs={{0,12},{4,8},{8,4},{12,0},{1,13},{5,9},{9,5},{13,1},{2,14},{6,10},... | collective-permute-start | bytes 196616 | tf_op jit(solution)/shard_map/ppermute | solution.py:491
  21.6 0.7 %collective-permute-start.9 = (bf16[256,128]{1,0:T(8,128)(2,1)S(1)}, bf16[256,128]{1,0:T(8,128)(2,1)S(1)}, u32[]{:S(2)}, u32[]{:S(2)}) collective-permute-start(bf16[256,128]{1,0:T(8,128)(2,1)S(1)} %shard_map.79.own_ref), channel_id=1, source_target_pairs={{0,8},{4,12},{8,0},{12,4},{1,9},{5,13},{9,1},{13,5},{2,10},{6,14},... | collective-permute-start | bytes 196616 | tf_op jit(solution)/shard_map/ppermute | solution.py:491
  22.3 0.1 shard_map.83.query_ref
  22.3 0.5 %shard_map.81 = (f32[4,256,128]{2,1,0:T(8,128)S(1)}, f32[4,256,128]{2,1,0:T(8,128)S(1)}) custom-call(bf16[512,256]{1,0:T(8,128)(2,1)S(1)} %copy-done.1, bf16[4,128,128]{2,1,0:T(8,128)(2,1)S(1)} %get-tuple-element.27.keep_ref, bf16[784,128]{1,0:T(8,128)(2,1)S(1)} %collective-permute-done.12.got_ref), custom_call_target="tpu_custom_call" | custom-call | tf_op jit(solution)/shard_map/pallas_call | solution.py:495
  22.8 1.3 %collective-permute-done.11.far_ref = bf16[256,128]{1,0:T(8,128)(2,1)S(1)} collective-permute-done((bf16[256,128]{1,0:T(8,128)(2,1)S(1)}, bf16[256,128]{1,0:T(8,128)(2,1)S(1)}, u32[]{:S(2)}, u32[]{:S(2)}) %collective-permute-start.11) | collective-permute-done | bytes 65568 | tf_op jit(solution)/shard_map/ppermute | solution.py:491
  24.1 1.8 %collective-permute-done.10.near_ref = bf16[256,128]{1,0:T(8,128)(2,1)S(1)} collective-permute-done((bf16[256,128]{1,0:T(8,128)(2,1)S(1)}, bf16[256,128]{1,0:T(8,128)(2,1)S(1)}, u32[]{:S(2)}, u32[]{:S(2)}) %collective-permute-start.10) | collective-permute-done | bytes 65568 | tf_op jit(solution)/shard_map/ppermute | solution.py:491
  25.9 0.4 %shard_map.82.total_ref = f32[2,256,128]{2,1,0:T(8,128)S(1)} custom-call(bf16[256,128]{1,0:T(8,128)(2,1)S(1)} %shard_map.79.own_ref, bf16[256,128]{1,0:T(8,128)(2,1)S(1)} %collective-permute-done.10.near_ref, bf16[256,128]{1,0:T(8,128)(2,1)S(1)} %collective-permute-done.11.far_ref, f32[4,256,128]{2,1,0:T(8,128)S(1)} %get-tuple-element.29.real_ref, ...), custom_call_target="tpu_custom_call" | custom-call | tf_op jit(solution)/shard_map/pallas_call | solution.py:501
  26.3 0.5 %collective-permute-done.9.last_ref = bf16[256,128]{1,0:T(8,128)(2,1)S(1)} collective-permute-done((bf16[256,128]{1,0:T(8,128)(2,1)S(1)}, bf16[256,128]{1,0:T(8,128)(2,1)S(1)}, u32[]{:S(2)}, u32[]{:S(2)}) %collective-permute-start.9) | collective-permute-done | bytes 65568 | tf_op jit(solution)/shard_map/ppermute | solution.py:491
  26.8 0.5 %shard_map.84 = (bf16[128,128]{1,0:T(8,128)(2,1)S(1)}, bf16[512,128]{1,0:T(8,128)(2,1)S(1)}) custom-call(bf16[256,128]{1,0:T(8,128)(2,1)S(1)} %collective-permute-done.9.last_ref, f32[2,256,128]{2,1,0:T(8,128)S(1)} %shard_map.82.total_ref, f32[4,256,128]{2,1,0:T(8,128)S(1)} %get-tuple-element.29.real_ref, f32[4,256,128]{2,1,0:T(8,128)S(1)} %get-tuple-element.30.imag_ref, ...), custom_call_target="tpu_custom_call" | custom-call | tf_op jit(solution)/shard_map/pallas_call | solution.py:508
  27.2 1.2 %collective-permute-start.13 = (bf16[128,128]{1,0:T(8,128)(2,1)S(1)}, bf16[128,128]{1,0:T(8,128)(2,1)S(1)}, u32[]{:S(2)}, u32[]{:S(2)}) collective-permute-start(bf16[128,128]{1,0:T(8,128)(2,1)S(1)} %get-tuple-element.34), channel_id=1, source_target_pairs={{0,2},{2,0},{1,3},{3,1},{4,6},{6,4},{5,7},{7,5},{8,10},{10,8},{9,1... | collective-permute-start | bytes 98312 | tf_op jit(solution)/shard_map/ppermute | solution.py:150
  28.4 0.2 shard_map.85.stay_ref
  28.6 2.6 %collective-permute-done.13.got_ref = bf16[128,128]{1,0:T(8,128)(2,1)S(1)} collective-permute-done((bf16[128,128]{1,0:T(8,128)(2,1)S(1)}, bf16[128,128]{1,0:T(8,128)(2,1)S(1)}, u32[]{:S(2)}, u32[]{:S(2)}) %collective-permute-start.13) | collective-permute-done | bytes 32800 | tf_op jit(solution)/shard_map/ppermute | solution.py:150
  31.2 0.6 %shard_map.86 = bf16[128,256]{1,0:T(8,128)(2,1)} custom-call(bf16[128,128]{1,0:T(8,128)(2,1)S(1)} %shard_map.85.stay_ref, bf16[128,128]{1,0:T(8,128)(2,1)S(1)} %collective-permute-done.13.got_ref), custom_call_target="tpu_custom_call" | custom-call | tf_op jit(solution)/shard_map/pallas_call | solution.py:521
  (24 shorter events, 0.1 us)
Async XLA Ops:
  0.0 6.0 %copy-start.3 = (bf16[128,256]{1,0:T(8,128)(2,1)S(1)}, bf16[128,256]{1,0:T(8,128)(2,1)}, u32[]{:S(2)}) copy-start(bf16[128,256]{1,0:T(8,128)(2,1)} %own_ref.1) | copy-start | bytes 196612
  0.0 10.9 %copy-start = (bf16[2048,3,256]{2,0,1:T(8,128)(2,1)S(1)}, bf16[2048,3,256]{2,0,1:T(8,128)(2,1)}, u32[]{:S(2)}) copy-start(bf16[2048,3,256]{2,0,1:T(8,128)(2,1)} %param.8) | copy-start | bytes 9437188
  0.0 10.4 %collective-permute-start = (bf16[128,2048]{1,0:T(8,128)(2,1)}, bf16[128,2048]{1,0:T(8,128)(2,1)S(1)}, u32[]{:S(2)}, u32[]{:S(2)}) collective-permute-start(bf16[128,2048]{1,0:T(8,128)(2,1)} %rows_ref.3), channel_id=1, source_target_pairs={{1,3},{3,2},{2,0},{0,1},{5,7},{7,6},{6,4},{4,5},{9,11},{11,10},{10... | collective-permute-start | bytes 1572872 | tf_op jit(solution)/shard_map/ppermute | solution.py:407
  0.5 1.3 %copy-start.6 = (bf16[128,2048]{1,0:T(8,128)(2,1)S(1)}, bf16[128,2048]{1,0:T(8,128)(2,1)}, u32[]{:S(2)}) copy-start(bf16[128,2048]{1,0:T(8,128)(2,1)} %rows_ref.3) | copy-start | bytes 1572868
  1.9 8.5 %collective-permute-start.1 = (bf16[16,256]{1,0:T(8,128)(2,1)S(1)}, bf16[16,256]{1,0:T(8,128)(2,1)S(1)}, u32[]{:S(2)}, u32[]{:S(2)}) collective-permute-start(bf16[16,256]{1,0:T(8,128)(2,1)S(1)} %shard_map.73), channel_id=1, source_target_pairs={{0,6},{1,5},{2,4},{3,7},{4,10},{5,9},{6,8},{7,11},{8,14},{9,13},{1... | collective-permute-start | bytes 24584 | tf_op jit(solution)/shard_map/ppermute | solution.py:416
  6.0 8.4 %collective-permute-start.7 = (bf16[128,256]{1,0:T(8,128)(2,1)S(1)}, bf16[128,256]{1,0:T(8,128)(2,1)S(1)}, u32[]{:S(2)}, u32[]{:S(2)}) collective-permute-start(bf16[128,256]{1,0:T(8,128)(2,1)S(1)} %copy-done.3), channel_id=1, source_target_pairs={{0,8},{4,12},{8,0},{12,4},{1,9},{5,13},{9,1},{13,5},{2,10},{6,14},... | collective-permute-start | bytes 196616 | tf_op jit(solution)/shard_map/ppermute | solution.py:427
  8.6 5.8 %collective-permute-start.6 = (bf16[128,256]{1,0:T(8,128)(2,1)S(1)}, bf16[128,256]{1,0:T(8,128)(2,1)S(1)}, u32[]{:S(2)}, u32[]{:S(2)}) collective-permute-start(bf16[128,256]{1,0:T(8,128)(2,1)S(1)} %copy-done.3), channel_id=1, source_target_pairs={{0,4},{4,0},{8,12},{12,8},{1,5},{5,1},{9,13},{13,9},{2,6},{6,2},{1... | collective-permute-start | bytes 196616 | tf_op jit(solution)/shard_map/ppermute | solution.py:427
  8.6 6.2 %collective-permute-start.8 = (bf16[128,256]{1,0:T(8,128)(2,1)S(1)}, bf16[128,256]{1,0:T(8,128)(2,1)S(1)}, u32[]{:S(2)}, u32[]{:S(2)}) collective-permute-start(bf16[128,256]{1,0:T(8,128)(2,1)S(1)} %copy-done.3), channel_id=1, source_target_pairs={{0,12},{4,8},{8,4},{12,0},{1,13},{5,9},{9,5},{13,1},{2,14},{6,10},... | collective-permute-start | bytes 196616 | tf_op jit(solution)/shard_map/ppermute | solution.py:427
  10.4 1.2 %collective-permute-start.3 = (bf16[16,256]{1,0:T(8,128)(2,1)S(1)}, bf16[16,256]{1,0:T(8,128)(2,1)S(1)}, u32[]{:S(2)}, u32[]{:S(2)}) collective-permute-start(bf16[16,256]{1,0:T(8,128)(2,1)S(1)} %collective-permute-done.1.refs_1_.pack_ref), channel_id=1, source_target_pairs={{0,1},{1,0},{2,3},{3,2},{4,5},{5,4},{6,7},{7,6},{8,9},{9,8},{10,11... | collective-permute-start | bytes 24584 | tf_op jit(solution)/shard_map/ppermute | solution.py:150
  10.4 2.0 %collective-permute-start.2 = (bf16[128,2048]{1,0:T(8,128)(2,1)S(1)}, bf16[128,2048]{1,0:T(8,128)(2,1)S(1)}, u32[]{:S(2)}, u32[]{:S(2)}) collective-permute-start(bf16[128,2048]{1,0:T(8,128)(2,1)S(1)} %shard_map.74.cycled_ref), channel_id=1, source_target_pairs={{0,1},{1,0},{2,3},{3,2},{4,5},{5,4},{6,7},{7,6},{8,9},{9,8},{10,11... | collective-permute-start | bytes 1572872 | tf_op jit(solution)/shard_map/ppermute | solution.py:150
  11.5 4.3 %collective-permute-start.4 = (bf16[128,256]{1,0:T(8,128)(2,1)S(1)}, bf16[128,256]{1,0:T(8,128)(2,1)S(1)}, u32[]{:S(2)}, u32[]{:S(2)}) collective-permute-start(bf16[128,256]{1,0:T(8,128)(2,1)S(1)} %get-tuple-element.22), channel_id=1, source_target_pairs={{0,2},{2,0},{1,3},{3,1},{4,6},{6,4},{5,7},{7,5},{8,10},{10,8},{9,1... | collective-permute-start | bytes 196616 | tf_op jit(solution)/shard_map/ppermute | solution.py:150
  12.9 4.8 %collective-permute-start.5 = (bf16[144,256]{1,0:T(8,128)(2,1)S(1)}, bf16[144,256]{1,0:T(8,128)(2,1)S(1)}, u32[]{:S(2)}, u32[]{:S(2)}) collective-permute-start(bf16[144,256]{1,0:T(8,128)(2,1)S(1)} %get-tuple-element.23), channel_id=1, source_target_pairs={{0,2},{2,0},{1,3},{3,1},{4,6},{6,4},{5,7},{7,5},{8,10},{10,8},{9,1... | collective-permute-start | bytes 221192 | tf_op jit(solution)/shard_map/ppermute | solution.py:150
  15.8 1.8 %copy-start.4 = (f32[3,3,256]{2,1,0:T(4,128)S(1)}, f32[3,3,256]{2,1,0:T(4,128)}, u32[]{:S(2)}) copy-start(f32[3,3,256]{2,1,0:T(4,128)} %short_ref.3) | copy-start | bytes 27652
  15.9 6.4 %collective-permute-start.12 = (bf16[784,128]{1,0:T(8,128)(2,1)S(1)}, bf16[784,128]{1,0:T(8,128)(2,1)S(1)}, u32[]{:S(2)}, u32[]{:S(2)}) collective-permute-start(bf16[784,128]{1,0:T(8,128)(2,1)S(1)} %shard_map.80), channel_id=1, source_target_pairs={{0,2},{2,0},{1,3},{3,1},{4,6},{6,4},{5,7},{7,5},{8,10},{10,8},{9,1... | collective-permute-start | bytes 602120 | tf_op jit(solution)/shard_map/ppermute | solution.py:150
  17.7 4.7 %copy-start.1 = (bf16[512,256]{1,0:T(8,128)(2,1)S(1)}, bf16[512,256]{1,0:T(8,128)(2,1)}, u32[]{:S(2)}) copy-start(bf16[512,256]{1,0:T(8,128)(2,1)} %constant.4.clone.table_ref) | copy-start | bytes 786436
  17.7 9.1 %copy-start.2 = (bf16[256,512]{1,0:T(8,128)(2,1)S(1)}, bf16[256,512]{1,0:T(8,128)(2,1)}, u32[]{:S(2)}) copy-start(bf16[256,512]{1,0:T(8,128)(2,1)} %constant.5.clone.turned_ref) | copy-start | bytes 786436
  17.7 9.1 %copy-start.5 = (f32[256]{0:T(256)S(1)}, f32[256]{0:T(256)}, u32[]{:S(2)}) copy-start(f32[256]{0:T(256)} %param.10) | copy-start | bytes 3076
  17.8 6.2 %collective-permute-start.11 = (bf16[256,128]{1,0:T(8,128)(2,1)S(1)}, bf16[256,128]{1,0:T(8,128)(2,1)S(1)}, u32[]{:S(2)}, u32[]{:S(2)}) collective-permute-start(bf16[256,128]{1,0:T(8,128)(2,1)S(1)} %shard_map.79.own_ref), channel_id=1, source_target_pairs={{0,12},{4,8},{8,4},{12,0},{1,13},{5,9},{9,5},{13,1},{2,14},{6,10},... | collective-permute-start | bytes 196616 | tf_op jit(solution)/shard_map/ppermute | solution.py:491
  21.6 4.3 %collective-permute-start.10 = (bf16[256,128]{1,0:T(8,128)(2,1)S(1)}, bf16[256,128]{1,0:T(8,128)(2,1)S(1)}, u32[]{:S(2)}, u32[]{:S(2)}) collective-permute-start(bf16[256,128]{1,0:T(8,128)(2,1)S(1)} %shard_map.79.own_ref), channel_id=1, source_target_pairs={{0,4},{4,0},{8,12},{12,8},{1,5},{5,1},{9,13},{13,9},{2,6},{6,2},{1... | collective-permute-start | bytes 196616 | tf_op jit(solution)/shard_map/ppermute | solution.py:491
  21.6 5.2 %collective-permute-start.9 = (bf16[256,128]{1,0:T(8,128)(2,1)S(1)}, bf16[256,128]{1,0:T(8,128)(2,1)S(1)}, u32[]{:S(2)}, u32[]{:S(2)}) collective-permute-start(bf16[256,128]{1,0:T(8,128)(2,1)S(1)} %shard_map.79.own_ref), channel_id=1, source_target_pairs={{0,8},{4,12},{8,0},{12,4},{1,9},{5,13},{9,1},{13,5},{2,10},{6,14},... | collective-permute-start | bytes 196616 | tf_op jit(solution)/shard_map/ppermute | solution.py:491
  27.2 4.0 %collective-permute-start.13 = (bf16[128,128]{1,0:T(8,128)(2,1)S(1)}, bf16[128,128]{1,0:T(8,128)(2,1)S(1)}, u32[]{:S(2)}, u32[]{:S(2)}) collective-permute-start(bf16[128,128]{1,0:T(8,128)(2,1)S(1)} %get-tuple-element.34), channel_id=1, source_target_pairs={{0,2},{2,0},{1,3},{3,1},{4,6},{6,4},{5,7},{7,5},{8,10},{10,8},{9,1... | collective-permute-start | bytes 98312 | tf_op jit(solution)/shard_map/ppermute | solution.py:150

commit v10 on v9

--- a/solution.py
+++ b/solution.py
@@ -190,7 +190,9 @@
     own_half = lax.axis_index("fsdp")
     half = weight_ref.shape[2] // 2
     for place, branch in enumerate(branches):
-        summed = jnp.dot(rows, weight_ref[branch], preferred_element_type=F32)
+        depth = rows.shape[1] // 2
+        summed = jnp.dot(rows[:, :depth], weight_ref[branch, :depth, :], preferred_element_type=F32)
+        summed += jnp.dot(rows[:, depth:], weight_ref[branch, depth:, :], preferred_element_type=F32)
         keep, send = split_channels(summed, own_half)
         lanes = slice(place * half, (place + 1) * half)
         keep_ref[:, lanes] = keep
@@ -337,8 +339,13 @@
     block = block_ref[...]
     if step:
         block = jnp.where(source < position, block, jnp.zeros_like(block))
-    waves = jnp.dot(table_ref[...], block, preferred_element_type=F32)
-    real, imag = (waves[:size], -waves[size:])
+    part = size // 2
+    waves = [
+        jnp.dot(table_ref[start : start + part, :], block, preferred_element_type=F32)
+        for start in range(0, 2 * size, part)
+    ]
+    real = jnp.concatenate(waves[:2], axis=0)
+    imag = -jnp.concatenate(waves[2:], axis=0)
     tap_real, tap_imag = (real_ref[back], imag_ref[back])
     return (real * tap_real - imag * tap_imag, real * tap_imag + imag * tap_real)
 
@@ -354,7 +361,9 @@
 def gated_rows(place, rows, stacked, turned_ref, query_ref, gain_ref, own_ref):
     half = own_ref.shape[1]
     lines = pl.ds(pl.multiple_of(place * rows, rows), rows)
-    conv = jnp.dot(turned_ref[lines, :], stacked, preferred_element_type=F32)
+    size = stacked.shape[0] // 2
+    conv = jnp.dot(turned_ref[lines, :size], stacked[:size], preferred_element_type=F32)
+    conv += jnp.dot(turned_ref[lines, size:], stacked[size:], preferred_element_type=F32)
     first = lax.axis_index("fsdp") == 0
     gain = jnp.where(first, gain_ref[:, :half], gain_ref[:, half:])
     gated = query_ref[lines, :] * (conv + gain * own_ref[lines, :].astype(F32))

time: 32 us -> 31.9 us (level)
  no operation moved by 1% of the time
where the time goes in v10:
time: 31.9 us; the launch traced here: 31.8 us
  starting transfers between devices  17.6 us (55%)
  waiting for transfers between devices  8.79 us (28%)
  Pallas kernels  4.01 us (13%)
  local copies, waits for them, and re-layouts  1.3 us (4%)
    ppermute x6, waiting for transfers between devices, exchange(): return lax.ppermute(value, axis, [(0, 1), (1, 0)])  4.79 us
    ppermute x3, starting transfers between devices, pair_mesh(): lax.ppermute(product, 'seq', pairs[step])  4.45 us
    ppermute x3, starting transfers between devices, pair_mesh(): lax.ppermute(filter_taps, 'seq', pairs[step])  4.39 us
    ppermute x6, starting transfers between devices, exchange(): return lax.ppermute(value, axis, [(0, 1), (1, 0)])  4.22 us
    ppermute x1, starting transfers between devices, pair_mesh(): lax.ppermute(pack, ('seq', 'fsdp', 'chan'), [(4 * s + 2 * f + c, 4 * ((s...  4.09 us
    ppermute x3, waiting for transfers between devices, pair_mesh(): lax.ppermute(product, 'seq', pairs[step])  3.57 us
    unnamed x14, local copies, waits for them, and re-layouts  1.3 us
    pallas_call x1, Pallas kernels, pair_mesh(): call(join_body, in_specs=whole_specs(2), out_specs=whole_specs(1)[0], out...  0.65 us
  transfers between devices with their start and end apart: 14, of which 8 were waited for; matrix products, arithmetic and copies ran while one was open for 0% of the time, Pallas kernels for 9%

profile of v10, /device:TPU:0, one launch (start us, length us, event | category | flops | bytes accessed | tf_op | source)
XLA Modules:
  0.0 31.8 jit_solution(4291920542110369973)
XLA Ops:
  0.0 0.5 %collective-permute-start = (bf16[128,2048]{1,0:T(8,128)(2,1)}, bf16[128,2048]{1,0:T(8,128)(2,1)S(1)}, u32[]{:S(2)}, u32[]{:S(2)}) collective-permute-start(bf16[128,2048]{1,0:T(8,128)(2,1)} %rows_ref.3), channel_id=1, source_target_pairs={{1,3},{3,2},{2,0},{0,1},{5,7},{7,6},{6,4},{4,5},{9,11},{11,10},{10... | collective-permute-start | bytes 1572872 | tf_op jit(solution)/shard_map/ppermute | solution.py:416
  0.5 1.3 %copy-done.6 = bf16[128,2048]{1,0:T(8,128)(2,1)S(1)} copy-done((bf16[128,2048]{1,0:T(8,128)(2,1)S(1)}, bf16[128,2048]{1,0:T(8,128)(2,1)}, u32[]{:S(2)}) %copy-start.6) | copy-done | bytes 524312
  1.7 0.1 shard_map.73
  1.9 4.1 %collective-permute-start.1 = (bf16[16,256]{1,0:T(8,128)(2,1)S(1)}, bf16[16,256]{1,0:T(8,128)(2,1)S(1)}, u32[]{:S(2)}, u32[]{:S(2)}) collective-permute-start(bf16[16,256]{1,0:T(8,128)(2,1)S(1)} %shard_map.73), channel_id=1, source_target_pairs={{0,6},{1,5},{2,4},{3,7},{4,10},{5,9},{6,8},{7,11},{8,14},{9,13},{1... | collective-permute-start | bytes 24584 | tf_op jit(solution)/shard_map/ppermute | solution.py:425
  6.0 2.6 %collective-permute-start.7 = (bf16[128,256]{1,0:T(8,128)(2,1)S(1)}, bf16[128,256]{1,0:T(8,128)(2,1)S(1)}, u32[]{:S(2)}, u32[]{:S(2)}) collective-permute-start(bf16[128,256]{1,0:T(8,128)(2,1)S(1)} %copy-done.3), channel_id=1, source_target_pairs={{0,8},{4,12},{8,0},{12,4},{1,9},{5,13},{9,1},{13,5},{2,10},{6,14},... | collective-permute-start | bytes 196616 | tf_op jit(solution)/shard_map/ppermute | solution.py:436
  8.6 1.8 %collective-permute-start.8 = (bf16[128,256]{1,0:T(8,128)(2,1)S(1)}, bf16[128,256]{1,0:T(8,128)(2,1)S(1)}, u32[]{:S(2)}, u32[]{:S(2)}) collective-permute-start(bf16[128,256]{1,0:T(8,128)(2,1)S(1)} %copy-done.3), channel_id=1, source_target_pairs={{0,12},{4,8},{8,4},{12,0},{1,13},{5,9},{9,5},{13,1},{2,14},{6,10},... | collective-permute-start | bytes 196616 | tf_op jit(solution)/shard_map/ppermute | solution.py:436
  10.4 0.5 %collective-permute-start.2 = (bf16[128,2048]{1,0:T(8,128)(2,1)S(1)}, bf16[128,2048]{1,0:T(8,128)(2,1)S(1)}, u32[]{:S(2)}, u32[]{:S(2)}) collective-permute-start(bf16[128,2048]{1,0:T(8,128)(2,1)S(1)} %shard_map.74.cycled_ref), channel_id=1, source_target_pairs={{0,1},{1,0},{2,3},{3,2},{4,5},{5,4},{6,7},{7,6},{8,9},{9,8},{10,11... | collective-permute-start | bytes 1572872 | tf_op jit(solution)/shard_map/ppermute | solution.py:150
  10.9 0.6 %shard_map.75 = (f32[128,256]{1,0:T(8,128)S(1)}, bf16[128,256]{1,0:T(8,128)(2,1)S(1)}, f32[128,128]{1,0:T(8,128)S(1)}, bf16[128,128]{1,0:T(8,128)(2,1)S(1)}) custom-call(bf16[128,2048]{1,0:T(8,128)(2,1)S(1)} %copy-done.6, bf16[128,2048]{1,0:T(8,128)(2,1)S(1)} %shard_map.74.cycled_ref, bf16[3,2048,256]{2,1,0:T(8,128)(2,1)S(1)} %bitcast.2), custom_call_target="tpu_custom_call" | custom-call | flops 10000000000 | bytes 40000000 | tf_op jit(solution)/shard_map/pallas_call | solution.py:441
  11.5 0.6 %collective-permute-start.4 = (bf16[128,256]{1,0:T(8,128)(2,1)S(1)}, bf16[128,256]{1,0:T(8,128)(2,1)S(1)}, u32[]{:S(2)}, u32[]{:S(2)}) collective-permute-start(bf16[128,256]{1,0:T(8,128)(2,1)S(1)} %get-tuple-element.22), channel_id=1, source_target_pairs={{0,2},{2,0},{1,3},{3,1},{4,6},{6,4},{5,7},{7,5},{8,10},{10,8},{9,1... | collective-permute-start | bytes 196616 | tf_op jit(solution)/shard_map/ppermute | solution.py:150
  12.1 0.1 shard_map.76.halo_ref
  12.3 0.1 collective-permute-done.2.hop_ref
  12.4 0.5 %shard_map.77 = (f32[144,256]{1,0:T(8,128)S(1)}, bf16[144,256]{1,0:T(8,128)(2,1)S(1)}, f32[8,128]{1,0:T(8,128)S(1)}) custom-call(bf16[128,2048]{1,0:T(8,128)(2,1)S(1)} %shard_map.74.cycled_ref, bf16[128,2048]{1,0:T(8,128)(2,1)S(1)} %collective-permute-done.2.hop_ref, bf16[16,2048]{1,0:T(8,128)(2,1)S(1)} %shard_map.76.halo_ref, bf16[3,2048,256]{2,1,0:T(8,128)(2,1)S(1)} %bitcast.3), custom_call_target="tpu_custom_call" | custom-call | tf_op jit(solution)/shard_map/pallas_call | solution.py:461
  12.9 1.4 %collective-permute-start.5 = (bf16[144,256]{1,0:T(8,128)(2,1)S(1)}, bf16[144,256]{1,0:T(8,128)(2,1)S(1)}, u32[]{:S(2)}, u32[]{:S(2)}) collective-permute-start(bf16[144,256]{1,0:T(8,128)(2,1)S(1)} %get-tuple-element.23), channel_id=1, source_target_pairs={{0,2},{2,0},{1,3},{3,1},{4,6},{6,4},{5,7},{7,5},{8,10},{10,8},{9,1... | collective-permute-start | bytes 221192 | tf_op jit(solution)/shard_map/ppermute | solution.py:150
  14.4 0.4 %collective-permute-done.8.three_ref = bf16[128,256]{1,0:T(8,128)(2,1)S(1)} collective-permute-done((bf16[128,256]{1,0:T(8,128)(2,1)S(1)}, bf16[128,256]{1,0:T(8,128)(2,1)S(1)}, u32[]{:S(2)}, u32[]{:S(2)}) %collective-permute-start.8) | collective-permute-done | bytes 65568 | tf_op jit(solution)/shard_map/ppermute | solution.py:436
  14.7 0.4 %shard_map.78 = (f32[144,128]{1,0:T(8,128)S(1)}, bf16[4,128,128]{2,1,0:T(8,128)(2,1)S(1)}, bf16[784,128]{1,0:T(8,128)(2,1)S(1)}, f32[8,128]{1,0:T(8,128)S(1)}) custom-call(bf16[128,2048]{1,0:T(8,128)(2,1)S(1)} %shard_map.74.cycled_ref, bf16[128,2048]{1,0:T(8,128)(2,1)S(1)} %collective-permute-done.2.hop_ref, bf16[16,2048]{1,0:T(8,128)(2,1)S(1)} %shard_map.76.halo_ref, ...), custom_call_target="tpu_custom_call" | custom-call | tf_op jit(solution)/shard_map/pallas_call | solution.py:471
  15.1 0.7 %collective-permute-done.4.got_first.refs_1_ = bf16[128,256]{1,0:T(8,128)(2,1)S(1)} collective-permute-done((bf16[128,256]{1,0:T(8,128)(2,1)S(1)}, bf16[128,256]{1,0:T(8,128)(2,1)S(1)}, u32[]{:S(2)}, u32[]{:S(2)}) %collective-permute-start.4) | collective-permute-done | bytes 65568 | tf_op jit(solution)/shard_map/ppermute | solution.py:150
  15.9 0.5 %collective-permute-start.12 = (bf16[784,128]{1,0:T(8,128)(2,1)S(1)}, bf16[784,128]{1,0:T(8,128)(2,1)S(1)}, u32[]{:S(2)}, u32[]{:S(2)}) collective-permute-start(bf16[784,128]{1,0:T(8,128)(2,1)S(1)} %shard_map.80), channel_id=1, source_target_pairs={{0,2},{2,0},{1,3},{3,1},{4,6},{6,4},{5,7},{7,5},{8,10},{10,8},{9,1... | collective-permute-start | bytes 602120 | tf_op jit(solution)/shard_map/ppermute | solution.py:150
  16.4 1.3 %collective-permute-done.5.got_second = bf16[144,256]{1,0:T(8,128)(2,1)S(1)} collective-permute-done((bf16[144,256]{1,0:T(8,128)(2,1)S(1)}, bf16[144,256]{1,0:T(8,128)(2,1)S(1)}, u32[]{:S(2)}, u32[]{:S(2)}) %collective-permute-start.5) | collective-permute-done | bytes 73760 | tf_op jit(solution)/shard_map/ppermute | solution.py:150
  17.7 0.1 shard_map.79.own_ref
  17.8 3.8 %collective-permute-start.11 = (bf16[256,128]{1,0:T(8,128)(2,1)S(1)}, bf16[256,128]{1,0:T(8,128)(2,1)S(1)}, u32[]{:S(2)}, u32[]{:S(2)}) collective-permute-start(bf16[256,128]{1,0:T(8,128)(2,1)S(1)} %shard_map.79.own_ref), channel_id=1, source_target_pairs={{0,12},{4,8},{8,4},{12,0},{1,13},{5,9},{9,5},{13,1},{2,14},{6,10},... | collective-permute-start | bytes 196616 | tf_op jit(solution)/shard_map/ppermute | solution.py:500
  21.6 0.7 %collective-permute-start.9 = (bf16[256,128]{1,0:T(8,128)(2,1)S(1)}, bf16[256,128]{1,0:T(8,128)(2,1)S(1)}, u32[]{:S(2)}, u32[]{:S(2)}) collective-permute-start(bf16[256,128]{1,0:T(8,128)(2,1)S(1)} %shard_map.79.own_ref), channel_id=1, source_target_pairs={{0,8},{4,12},{8,0},{12,4},{1,9},{5,13},{9,1},{13,5},{2,10},{6,14},... | collective-permute-start | bytes 196616 | tf_op jit(solution)/shard_map/ppermute | solution.py:500
  22.3 0.1 shard_map.83.query_ref
  22.3 0.5 %shard_map.81 = (f32[4,256,128]{2,1,0:T(8,128)S(1)}, f32[4,256,128]{2,1,0:T(8,128)S(1)}) custom-call(bf16[512,256]{1,0:T(8,128)(2,1)S(1)} %copy-done.1, bf16[4,128,128]{2,1,0:T(8,128)(2,1)S(1)} %get-tuple-element.27.keep_ref, bf16[784,128]{1,0:T(8,128)(2,1)S(1)} %collective-permute-done.12.got_ref), custom_call_target="tpu_custom_call" | custom-call | tf_op jit(solution)/shard_map/pallas_call | solution.py:504
  22.8 1.3 %collective-permute-done.11.far_ref = bf16[256,128]{1,0:T(8,128)(2,1)S(1)} collective-permute-done((bf16[256,128]{1,0:T(8,128)(2,1)S(1)}, bf16[256,128]{1,0:T(8,128)(2,1)S(1)}, u32[]{:S(2)}, u32[]{:S(2)}) %collective-permute-start.11) | collective-permute-done | bytes 65568 | tf_op jit(solution)/shard_map/ppermute | solution.py:500
  24.1 1.8 %collective-permute-done.10.near_ref = bf16[256,128]{1,0:T(8,128)(2,1)S(1)} collective-permute-done((bf16[256,128]{1,0:T(8,128)(2,1)S(1)}, bf16[256,128]{1,0:T(8,128)(2,1)S(1)}, u32[]{:S(2)}, u32[]{:S(2)}) %collective-permute-start.10) | collective-permute-done | bytes 65568 | tf_op jit(solution)/shard_map/ppermute | solution.py:500
  25.9 0.4 %shard_map.82.total_ref = f32[2,256,128]{2,1,0:T(8,128)S(1)} custom-call(bf16[256,128]{1,0:T(8,128)(2,1)S(1)} %shard_map.79.own_ref, bf16[256,128]{1,0:T(8,128)(2,1)S(1)} %collective-permute-done.10.near_ref, bf16[256,128]{1,0:T(8,128)(2,1)S(1)} %collective-permute-done.11.far_ref, f32[4,256,128]{2,1,0:T(8,128)S(1)} %get-tuple-element.29.real_ref, ...), custom_call_target="tpu_custom_call" | custom-call | tf_op jit(solution)/shard_map/pallas_call | solution.py:510
  26.2 0.5 %collective-permute-done.9.last_ref = bf16[256,128]{1,0:T(8,128)(2,1)S(1)} collective-permute-done((bf16[256,128]{1,0:T(8,128)(2,1)S(1)}, bf16[256,128]{1,0:T(8,128)(2,1)S(1)}, u32[]{:S(2)}, u32[]{:S(2)}) %collective-permute-start.9) | collective-permute-done | bytes 65568 | tf_op jit(solution)/shard_map/ppermute | solution.py:500
  26.8 0.4 %shard_map.84 = (bf16[128,128]{1,0:T(8,128)(2,1)S(1)}, bf16[512,128]{1,0:T(8,128)(2,1)S(1)}) custom-call(bf16[256,128]{1,0:T(8,128)(2,1)S(1)} %collective-permute-done.9.last_ref, f32[2,256,128]{2,1,0:T(8,128)S(1)} %shard_map.82.total_ref, f32[4,256,128]{2,1,0:T(8,128)S(1)} %get-tuple-element.29.real_ref, f32[4,256,128]{2,1,0:T(8,128)S(1)} %get-tuple-element.30.imag_ref, ...), custom_call_target="tpu_custom_call" | custom-call | tf_op jit(solution)/shard_map/pallas_call | solution.py:517
  27.2 1.2 %collective-permute-start.13 = (bf16[128,128]{1,0:T(8,128)(2,1)S(1)}, bf16[128,128]{1,0:T(8,128)(2,1)S(1)}, u32[]{:S(2)}, u32[]{:S(2)}) collective-permute-start(bf16[128,128]{1,0:T(8,128)(2,1)S(1)} %get-tuple-element.34), channel_id=1, source_target_pairs={{0,2},{2,0},{1,3},{3,1},{4,6},{6,4},{5,7},{7,5},{8,10},{10,8},{9,1... | collective-permute-start | bytes 98312 | tf_op jit(solution)/shard_map/ppermute | solution.py:150
  28.4 0.2 shard_map.85.stay_ref
  28.5 2.6 %collective-permute-done.13.got_ref = bf16[128,128]{1,0:T(8,128)(2,1)S(1)} collective-permute-done((bf16[128,128]{1,0:T(8,128)(2,1)S(1)}, bf16[128,128]{1,0:T(8,128)(2,1)S(1)}, u32[]{:S(2)}, u32[]{:S(2)}) %collective-permute-start.13) | collective-permute-done | bytes 32800 | tf_op jit(solution)/shard_map/ppermute | solution.py:150
  31.1 0.6 %shard_map.86 = bf16[128,256]{1,0:T(8,128)(2,1)} custom-call(bf16[128,128]{1,0:T(8,128)(2,1)S(1)} %shard_map.85.stay_ref, bf16[128,128]{1,0:T(8,128)(2,1)S(1)} %collective-permute-done.13.got_ref), custom_call_target="tpu_custom_call" | custom-call | tf_op jit(solution)/shard_map/pallas_call | solution.py:530
  (24 shorter events, 0.1 us)
Async XLA Ops:
  0.0 6.0 %copy-start.3 = (bf16[128,256]{1,0:T(8,128)(2,1)S(1)}, bf16[128,256]{1,0:T(8,128)(2,1)}, u32[]{:S(2)}) copy-start(bf16[128,256]{1,0:T(8,128)(2,1)} %own_ref.1) | copy-start | bytes 196612
  0.0 10.9 %copy-start = (bf16[2048,3,256]{2,0,1:T(8,128)(2,1)S(1)}, bf16[2048,3,256]{2,0,1:T(8,128)(2,1)}, u32[]{:S(2)}) copy-start(bf16[2048,3,256]{2,0,1:T(8,128)(2,1)} %param.8) | copy-start | bytes 9437188
  0.0 10.4 %collective-permute-start = (bf16[128,2048]{1,0:T(8,128)(2,1)}, bf16[128,2048]{1,0:T(8,128)(2,1)S(1)}, u32[]{:S(2)}, u32[]{:S(2)}) collective-permute-start(bf16[128,2048]{1,0:T(8,128)(2,1)} %rows_ref.3), channel_id=1, source_target_pairs={{1,3},{3,2},{2,0},{0,1},{5,7},{7,6},{6,4},{4,5},{9,11},{11,10},{10... | collective-permute-start | bytes 1572872 | tf_op jit(solution)/shard_map/ppermute | solution.py:416
  0.5 1.3 %copy-start.6 = (bf16[128,2048]{1,0:T(8,128)(2,1)S(1)}, bf16[128,2048]{1,0:T(8,128)(2,1)}, u32[]{:S(2)}) copy-start(bf16[128,2048]{1,0:T(8,128)(2,1)} %rows_ref.3) | copy-start | bytes 1572868
  1.9 8.5 %collective-permute-start.1 = (bf16[16,256]{1,0:T(8,128)(2,1)S(1)}, bf16[16,256]{1,0:T(8,128)(2,1)S(1)}, u32[]{:S(2)}, u32[]{:S(2)}) collective-permute-start(bf16[16,256]{1,0:T(8,128)(2,1)S(1)} %shard_map.73), channel_id=1, source_target_pairs={{0,6},{1,5},{2,4},{3,7},{4,10},{5,9},{6,8},{7,11},{8,14},{9,13},{1... | collective-permute-start | bytes 24584 | tf_op jit(solution)/shard_map/ppermute | solution.py:425
  6.0 8.4 %collective-permute-start.7 = (bf16[128,256]{1,0:T(8,128)(2,1)S(1)}, bf16[128,256]{1,0:T(8,128)(2,1)S(1)}, u32[]{:S(2)}, u32[]{:S(2)}) collective-permute-start(bf16[128,256]{1,0:T(8,128)(2,1)S(1)} %copy-done.3), channel_id=1, source_target_pairs={{0,8},{4,12},{8,0},{12,4},{1,9},{5,13},{9,1},{13,5},{2,10},{6,14},... | collective-permute-start | bytes 196616 | tf_op jit(solution)/shard_map/ppermute | solution.py:436
  8.6 5.8 %collective-permute-start.6 = (bf16[128,256]{1,0:T(8,128)(2,1)S(1)}, bf16[128,256]{1,0:T(8,128)(2,1)S(1)}, u32[]{:S(2)}, u32[]{:S(2)}) collective-permute-start(bf16[128,256]{1,0:T(8,128)(2,1)S(1)} %copy-done.3), channel_id=1, source_target_pairs={{0,4},{4,0},{8,12},{12,8},{1,5},{5,1},{9,13},{13,9},{2,6},{6,2},{1... | collective-permute-start | bytes 196616 | tf_op jit(solution)/shard_map/ppermute | solution.py:436
  8.6 6.2 %collective-permute-start.8 = (bf16[128,256]{1,0:T(8,128)(2,1)S(1)}, bf16[128,256]{1,0:T(8,128)(2,1)S(1)}, u32[]{:S(2)}, u32[]{:S(2)}) collective-permute-start(bf16[128,256]{1,0:T(8,128)(2,1)S(1)} %copy-done.3), channel_id=1, source_target_pairs={{0,12},{4,8},{8,4},{12,0},{1,13},{5,9},{9,5},{13,1},{2,14},{6,10},... | collective-permute-start | bytes 196616 | tf_op jit(solution)/shard_map/ppermute | solution.py:436
  10.4 1.2 %collective-permute-start.3 = (bf16[16,256]{1,0:T(8,128)(2,1)S(1)}, bf16[16,256]{1,0:T(8,128)(2,1)S(1)}, u32[]{:S(2)}, u32[]{:S(2)}) collective-permute-start(bf16[16,256]{1,0:T(8,128)(2,1)S(1)} %collective-permute-done.1.refs_1_.pack_ref), channel_id=1, source_target_pairs={{0,1},{1,0},{2,3},{3,2},{4,5},{5,4},{6,7},{7,6},{8,9},{9,8},{10,11... | collective-permute-start | bytes 24584 | tf_op jit(solution)/shard_map/ppermute | solution.py:150
  10.4 2.0 %collective-permute-start.2 = (bf16[128,2048]{1,0:T(8,128)(2,1)S(1)}, bf16[128,2048]{1,0:T(8,128)(2,1)S(1)}, u32[]{:S(2)}, u32[]{:S(2)}) collective-permute-start(bf16[128,2048]{1,0:T(8,128)(2,1)S(1)} %shard_map.74.cycled_ref), channel_id=1, source_target_pairs={{0,1},{1,0},{2,3},{3,2},{4,5},{5,4},{6,7},{7,6},{8,9},{9,8},{10,11... | collective-permute-start | bytes 1572872 | tf_op jit(solution)/shard_map/ppermute | solution.py:150
  11.5 4.3 %collective-permute-start.4 = (bf16[128,256]{1,0:T(8,128)(2,1)S(1)}, bf16[128,256]{1,0:T(8,128)(2,1)S(1)}, u32[]{:S(2)}, u32[]{:S(2)}) collective-permute-start(bf16[128,256]{1,0:T(8,128)(2,1)S(1)} %get-tuple-element.22), channel_id=1, source_target_pairs={{0,2},{2,0},{1,3},{3,1},{4,6},{6,4},{5,7},{7,5},{8,10},{10,8},{9,1... | collective-permute-start | bytes 196616 | tf_op jit(solution)/shard_map/ppermute | solution.py:150
  12.9 4.8 %collective-permute-start.5 = (bf16[144,256]{1,0:T(8,128)(2,1)S(1)}, bf16[144,256]{1,0:T(8,128)(2,1)S(1)}, u32[]{:S(2)}, u32[]{:S(2)}) collective-permute-start(bf16[144,256]{1,0:T(8,128)(2,1)S(1)} %get-tuple-element.23), channel_id=1, source_target_pairs={{0,2},{2,0},{1,3},{3,1},{4,6},{6,4},{5,7},{7,5},{8,10},{10,8},{9,1... | collective-permute-start | bytes 221192 | tf_op jit(solution)/shard_map/ppermute | solution.py:150
  15.8 1.8 %copy-start.4 = (f32[3,3,256]{2,1,0:T(4,128)S(1)}, f32[3,3,256]{2,1,0:T(4,128)}, u32[]{:S(2)}) copy-start(f32[3,3,256]{2,1,0:T(4,128)} %short_ref.3) | copy-start | bytes 27652
  15.9 6.4 %collective-permute-start.12 = (bf16[784,128]{1,0:T(8,128)(2,1)S(1)}, bf16[784,128]{1,0:T(8,128)(2,1)S(1)}, u32[]{:S(2)}, u32[]{:S(2)}) collective-permute-start(bf16[784,128]{1,0:T(8,128)(2,1)S(1)} %shard_map.80), channel_id=1, source_target_pairs={{0,2},{2,0},{1,3},{3,1},{4,6},{6,4},{5,7},{7,5},{8,10},{10,8},{9,1... | collective-permute-start | bytes 602120 | tf_op jit(solution)/shard_map/ppermute | solution.py:150
  17.7 4.7 %copy-start.1 = (bf16[512,256]{1,0:T(8,128)(2,1)S(1)}, bf16[512,256]{1,0:T(8,128)(2,1)}, u32[]{:S(2)}) copy-start(bf16[512,256]{1,0:T(8,128)(2,1)} %constant.4.clone.table_ref) | copy-start | bytes 786436
  17.7 9.1 %copy-start.2 = (bf16[256,512]{1,0:T(8,128)(2,1)S(1)}, bf16[256,512]{1,0:T(8,128)(2,1)}, u32[]{:S(2)}) copy-start(bf16[256,512]{1,0:T(8,128)(2,1)} %constant.5.clone.turned_ref) | copy-start | bytes 786436
  17.7 9.1 %copy-start.5 = (f32[256]{0:T(256)S(1)}, f32[256]{0:T(256)}, u32[]{:S(2)}) copy-start(f32[256]{0:T(256)} %param.10) | copy-start | bytes 3076
  17.8 6.2 %collective-permute-start.11 = (bf16[256,128]{1,0:T(8,128)(2,1)S(1)}, bf16[256,128]{1,0:T(8,128)(2,1)S(1)}, u32[]{:S(2)}, u32[]{:S(2)}) collective-permute-start(bf16[256,128]{1,0:T(8,128)(2,1)S(1)} %shard_map.79.own_ref), channel_id=1, source_target_pairs={{0,12},{4,8},{8,4},{12,0},{1,13},{5,9},{9,5},{13,1},{2,14},{6,10},... | collective-permute-start | bytes 196616 | tf_op jit(solution)/shard_map/ppermute | solution.py:500
  21.6 4.3 %collective-permute-start.10 = (bf16[256,128]{1,0:T(8,128)(2,1)S(1)}, bf16[256,128]{1,0:T(8,128)(2,1)S(1)}, u32[]{:S(2)}, u32[]{:S(2)}) collective-permute-start(bf16[256,128]{1,0:T(8,128)(2,1)S(1)} %shard_map.79.own_ref), channel_id=1, source_target_pairs={{0,4},{4,0},{8,12},{12,8},{1,5},{5,1},{9,13},{13,9},{2,6},{6,2},{1... | collective-permute-start | bytes 196616 | tf_op jit(solution)/shard_map/ppermute | solution.py:500
  21.6 5.2 %collective-permute-start.9 = (bf16[256,128]{1,0:T(8,128)(2,1)S(1)}, bf16[256,128]{1,0:T(8,128)(2,1)S(1)}, u32[]{:S(2)}, u32[]{:S(2)}) collective-permute-start(bf16[256,128]{1,0:T(8,128)(2,1)S(1)} %shard_map.79.own_ref), channel_id=1, source_target_pairs={{0,8},{4,12},{8,0},{12,4},{1,9},{5,13},{9,1},{13,5},{2,10},{6,14},... | collective-permute-start | bytes 196616 | tf_op jit(solution)/shard_map/ppermute | solution.py:500
  27.2 4.0 %collective-permute-start.13 = (bf16[128,128]{1,0:T(8,128)(2,1)S(1)}, bf16[128,128]{1,0:T(8,128)(2,1)S(1)}, u32[]{:S(2)}, u32[]{:S(2)}) collective-permute-start(bf16[128,128]{1,0:T(8,128)(2,1)S(1)} %get-tuple-element.34), channel_id=1, source_target_pairs={{0,2},{2,0},{1,3},{3,1},{4,6},{6,4},{5,7},{7,5},{8,10},{10,8},{9,1... | collective-permute-start | bytes 98312 | tf_op jit(solution)/shard_map/ppermute | solution.py:150

commit v11 on v9

--- a/solution.py
+++ b/solution.py
@@ -197,13 +197,10 @@
         send_ref[:, lanes] = send.astype(BF16)
 
 
-def project_first_body(
-    rows_ref, cycled_ref, weight_ref, keep_product, send_product, keep_query, send_query
-):
+def project_first_body(rows_ref, cycled_ref, weight_ref, keep_ref, send_ref):
     here = lax.axis_index("chan") == lax.axis_index("fsdp")
     rows = jnp.where(here, rows_ref[...], cycled_ref[...])
-    project(rows, weight_ref, (1, 2), keep_product, send_product)
-    project(rows, weight_ref, (0,), keep_query, send_query)
+    project(rows, weight_ref, (1, 2), keep_ref, send_ref)
 
 
 def halo_body(pack_ref, pack_hop_ref, halo_ref):
@@ -228,14 +225,14 @@
 
 
 def project_query_body(
-    cycled_ref, hop_ref, halo_ref, weight_ref, first_ref, order_ref,
+    cycled_ref, hop_ref, halo_ref, weight_ref, rows_ref, order_ref,
     own_ref, one_ref, two_ref, three_ref, keep_ref, taps_ref, send_ref, done_ref
 ):
-    rows = arrived_rows(cycled_ref, hop_ref, halo_ref)
-    count = first_ref.shape[0]
-    send_ref[:count, :] = first_ref[...]
-    after_query = count + rows.shape[0]
-    project(rows, weight_ref, (0,), keep_ref, send_ref.at[count:after_query, :])
+    here = lax.axis_index("chan") == lax.axis_index("fsdp")
+    own = jnp.where(here, rows_ref[...], cycled_ref[...])
+    rows = jnp.concatenate([own, arrived_rows(cycled_ref, hop_ref, halo_ref)], axis=0)
+    after_query = rows.shape[0]
+    project(rows, weight_ref, (0,), keep_ref, send_ref.at[:after_query, :])
     position = lax.axis_index("seq")
     first = lax.axis_index("fsdp") == 0
     _, tap_rows, half = taps_ref.shape
@@ -319,12 +316,17 @@
     product_ref[...] = (key * value).astype(BF16)
 
 
-def query_body(keep_first, keep_second, got_ref, short_ref, query_ref, joined):
-    rows = keep_first.shape[0]
-    got_first = got_ref.at[:rows, :]
-    got_second = got_ref.at[rows : rows + keep_second.shape[0], :]
+def query_body(keep_ref, got_ref, short_ref, query_ref, joined):
+    rows = (keep_ref.shape[0] - HALO) // 2
+    first, second = (pl.ds(0, rows), pl.ds(rows, HALO + rows))
     (query,) = mixed_branches(
-        (0,), keep_first, keep_second, got_first, got_second, short_ref, joined
+        (0,),
+        keep_ref.at[first, :],
+        keep_ref.at[second, :],
+        got_ref.at[first, :],
+        got_ref.at[second, :],
+        short_ref,
+        joined,
     )
     query_ref[...] = query
 
@@ -343,9 +345,9 @@
     return (real * tap_real - imag * tap_imag, real * tap_imag + imag * tap_real)
 
 
-def conv_early_body(own_ref, near_ref, far_ref, real_ref, imag_ref, table_ref, total_ref):
+def conv_early_body(own_ref, far_ref, near_ref, real_ref, imag_ref, table_ref, total_ref):
     total_ref[0], total_ref[1] = spectrum_term(0, own_ref, real_ref, imag_ref, table_ref)
-    for step, block_ref in ((1, near_ref), (3, far_ref)):
+    for step, block_ref in ((3, far_ref), (1, near_ref)):
         real, imag = spectrum_term(step, block_ref, real_ref, imag_ref, table_ref)
         total_ref[0] += real
         total_ref[1] += imag
@@ -429,17 +431,12 @@
     cycled = after(cycled, pack_got)
     hop = exchange(cycled, "chan")
     pack_hop = exchange(pack_got, "chan")
-    keep_first, send_first, keep_first_query, send_first_query = call(
+    keep_first, send_first = call(
         project_first_body,
         cost_estimate=LONG,
         in_specs=whole_specs(3),
-        out_specs=whole_specs(4),
-        out_shape=(
-            shape((rows, 2 * half), F32),
-            shape((rows, 2 * half), BF16),
-            shape((rows, half), F32),
-            shape((rows, half), BF16),
-        ),
+        out_specs=whole_specs(2),
+        out_shape=(shape((rows, 2 * half), F32), shape((rows, 2 * half), BF16)),
     )(tokens, cycled, weight)
     got_first = exchange(send_first, "fsdp")
     halo = call(
@@ -459,17 +456,17 @@
             token,
         ),
     )(*arrived)
-    keep_second_query, tap_keep, send_late, late_done = call(
+    keep_query, tap_keep, send_late, late_done = call(
         project_query_body,
         in_specs=whole_specs(6 + blocks),
         out_specs=whole_specs(4),
         out_shape=(
-            shape((HALO + rows, half), F32),
+            shape((rows + HALO + rows, half), F32),
             shape((blocks, rows, half), BF16),
             shape((rows + HALO + rows + blocks * rows, half), BF16),
             token,
         ),
-    )(*arrived, send_first_query, second_done, *tap_blocks)
+    )(*arrived, tokens, second_done, *tap_blocks)
     got_second = exchange(send_second, "fsdp")
 
     product = call(
@@ -483,12 +480,12 @@
     got_late = exchange(after(send_late, got_first, cost_estimate=LONG), "fsdp")
     query = call(
         query_body,
-        in_specs=whole_specs(4),
+        in_specs=whole_specs(3),
         out_specs=whole_specs(1)[0],
         out_shape=shape((size, half), F32),
         scratch_shapes=[pltpu.VMEM((HALO + size, half), F32)],
-    )(keep_first_query, keep_second_query, got_late, short_weight)
-    last, near, far = (lax.ppermute(product, "seq", pairs[step]) for step in (2, 1, 3))
+    )(keep_query, got_late, short_weight)
+    last, far, near = (lax.ppermute(product, "seq", pairs[step]) for step in (2, 3, 1))
     table = wave_table(size)
     forward = jnp.asarray(table, dtype=BF16)
     inverse = jnp.asarray(table.T, dtype=BF16)
@@ -503,7 +500,7 @@
         in_specs=whole_specs(6),
         out_specs=whole_specs(1)[0],
         out_shape=shape((2, size, half), F32),
-    )(product, near, far, tap_real, tap_imag, forward)
+    )(product, far, near, tap_real, tap_imag, forward)
     ending = (inverse, query, skip_gain.reshape(1, width), product)
     go, stacked = call(
         conv_last_body,

time: 32 us -> 32 us (level)
    unnamed x14 -> x16, local copies, waits for them, and re-layouts: 1.3 us -> 1.3 us
  transfers between devices with their start and end apart: 14 -> 14, of which waited for: 8 -> 9; matrix products, arithmetic and copies ran while one was open for 0% -> 0% of each run, Pallas kernels for 9% -> 9%
where the time goes in v11:
time: 32 us; the launch traced here: 31.9 us
  starting transfers between devices  17.6 us (55%)
  waiting for transfers between devices  8.81 us (28%)
  Pallas kernels  4.09 us (13%)
  local copies, waits for them, and re-layouts  1.3 us (4%)
    ppermute x6, waiting for transfers between devices, exchange(): return lax.ppermute(value, axis, [(0, 1), (1, 0)])  4.65 us
    ppermute x3, starting transfers between devices, pair_mesh(): lax.ppermute(product, 'seq', pairs[step])  4.55 us
    ppermute x3, starting transfers between devices, pair_mesh(): lax.ppermute(filter_taps, 'seq', pairs[step])  4.39 us
    ppermute x1, starting transfers between devices, pair_mesh(): lax.ppermute(pack, ('seq', 'fsdp', 'chan'), [(4 * s + 2 * f + c, 4 * ((s...  4.09 us
    ppermute x6, starting transfers between devices, exchange(): return lax.ppermute(value, axis, [(0, 1), (1, 0)])  4.08 us
    ppermute x3, waiting for transfers between devices, pair_mesh(): lax.ppermute(product, 'seq', pairs[step])  3.59 us
    unnamed x16, local copies, waits for them, and re-layouts  1.3 us
    pallas_call x1, Pallas kernels, pair_mesh(): call(join_body, in_specs=whole_specs(2), out_specs=whole_specs(1)[0], out...  0.65 us
  transfers between devices with their start and end apart: 14, of which 9 were waited for; matrix products, arithmetic and copies ran while one was open for 0% of the time, Pallas kernels for 9%

profile of v11, /device:TPU:0, one launch (start us, length us, event | category | flops | bytes accessed | tf_op | source)
XLA Modules:
  0.0 31.9 jit_solution(16320360350612040772)
XLA Ops:
  0.0 0.5 %collective-permute-start = (bf16[128,2048]{1,0:T(8,128)(2,1)}, bf16[128,2048]{1,0:T(8,128)(2,1)S(1)}, u32[]{:S(2)}, u32[]{:S(2)}) collective-permute-start(bf16[128,2048]{1,0:T(8,128)(2,1)} %rows_ref.5), channel_id=1, source_target_pairs={{1,3},{3,2},{2,0},{0,1},{5,7},{7,6},{6,4},{4,5},{9,11},{11,10},{10... | collective-permute-start | bytes 1572872 | tf_op jit(solution)/shard_map/ppermute | solution.py:409
  0.5 1.3 %copy-done.3 = bf16[128,2048]{1,0:T(8,128)(2,1)S(1)} copy-done((bf16[128,2048]{1,0:T(8,128)(2,1)S(1)}, bf16[128,2048]{1,0:T(8,128)(2,1)}, u32[]{:S(2)}) %copy-start.3) | copy-done | bytes 524312
  1.7 0.1 shard_map.73
  1.9 4.1 %collective-permute-start.1 = (bf16[16,256]{1,0:T(8,128)(2,1)S(1)}, bf16[16,256]{1,0:T(8,128)(2,1)S(1)}, u32[]{:S(2)}, u32[]{:S(2)}) collective-permute-start(bf16[16,256]{1,0:T(8,128)(2,1)S(1)} %shard_map.73), channel_id=1, source_target_pairs={{0,6},{1,5},{2,4},{3,7},{4,10},{5,9},{6,8},{7,11},{8,14},{9,13},{1... | collective-permute-start | bytes 24584 | tf_op jit(solution)/shard_map/ppermute | solution.py:418
  6.0 1.6 %collective-permute-start.6 = (bf16[128,256]{1,0:T(8,128)(2,1)S(1)}, bf16[128,256]{1,0:T(8,128)(2,1)S(1)}, u32[]{:S(2)}, u32[]{:S(2)}) collective-permute-start(bf16[128,256]{1,0:T(8,128)(2,1)S(1)} %copy-done.5), channel_id=1, source_target_pairs={{0,4},{4,0},{8,12},{12,8},{1,5},{5,1},{9,13},{13,9},{2,6},{6,2},{1... | collective-permute-start | bytes 196616 | tf_op jit(solution)/shard_map/ppermute | solution.py:429
  7.5 1.0 %collective-permute-start.7 = (bf16[128,256]{1,0:T(8,128)(2,1)S(1)}, bf16[128,256]{1,0:T(8,128)(2,1)S(1)}, u32[]{:S(2)}, u32[]{:S(2)}) collective-permute-start(bf16[128,256]{1,0:T(8,128)(2,1)S(1)} %copy-done.5), channel_id=1, source_target_pairs={{0,8},{4,12},{8,0},{12,4},{1,9},{5,13},{9,1},{13,5},{2,10},{6,14},... | collective-permute-start | bytes 196616 | tf_op jit(solution)/shard_map/ppermute | solution.py:429
  8.5 1.8 %collective-permute-start.8 = (bf16[128,256]{1,0:T(8,128)(2,1)S(1)}, bf16[128,256]{1,0:T(8,128)(2,1)S(1)}, u32[]{:S(2)}, u32[]{:S(2)}) collective-permute-start(bf16[128,256]{1,0:T(8,128)(2,1)S(1)} %copy-done.5), channel_id=1, source_target_pairs={{0,12},{4,8},{8,4},{12,0},{1,13},{5,9},{9,5},{13,1},{2,14},{6,10},... | collective-permute-start | bytes 196616 | tf_op jit(solution)/shard_map/ppermute | solution.py:429
  10.4 0.5 %collective-permute-start.2 = (bf16[128,2048]{1,0:T(8,128)(2,1)S(1)}, bf16[128,2048]{1,0:T(8,128)(2,1)S(1)}, u32[]{:S(2)}, u32[]{:S(2)}) collective-permute-start(bf16[128,2048]{1,0:T(8,128)(2,1)S(1)} %shard_map.74.cycled_ref), channel_id=1, source_target_pairs={{0,1},{1,0},{2,3},{3,2},{4,5},{5,4},{6,7},{7,6},{8,9},{9,8},{10,11... | collective-permute-start | bytes 1572872 | tf_op jit(solution)/shard_map/ppermute | solution.py:150
  10.9 0.5 %shard_map.75 = (f32[128,256]{1,0:T(8,128)S(1)}, bf16[128,256]{1,0:T(8,128)(2,1)S(1)}) custom-call(bf16[128,2048]{1,0:T(8,128)(2,1)S(1)} %copy-done.3, bf16[128,2048]{1,0:T(8,128)(2,1)S(1)} %shard_map.74.cycled_ref, bf16[3,2048,256]{2,1,0:T(8,128)(2,1)S(1)} %bitcast.2), custom_call_target="tpu_custom_call" | custom-call | flops 10000000000 | bytes 40000000 | tf_op jit(solution)/shard_map/pallas_call | solution.py:434
  11.4 0.2 collective-permute-done.3.pack_hop_ref
  11.5 0.4 %collective-permute-start.4 = (bf16[128,256]{1,0:T(8,128)(2,1)S(1)}, bf16[128,256]{1,0:T(8,128)(2,1)S(1)}, u32[]{:S(2)}, u32[]{:S(2)}) collective-permute-start(bf16[128,256]{1,0:T(8,128)(2,1)S(1)} %get-tuple-element.20), channel_id=1, source_target_pairs={{0,2},{2,0},{1,3},{3,1},{4,6},{6,4},{5,7},{7,5},{8,10},{10,8},{9,1... | collective-permute-start | bytes 196616 | tf_op jit(solution)/shard_map/ppermute | solution.py:150
  11.9 0.1 shard_map.76.halo_ref
  12.1 0.3 %collective-permute-done.2.hop_ref = bf16[128,2048]{1,0:T(8,128)(2,1)S(1)} collective-permute-done((bf16[128,2048]{1,0:T(8,128)(2,1)S(1)}, bf16[128,2048]{1,0:T(8,128)(2,1)S(1)}, u32[]{:S(2)}, u32[]{:S(2)}) %collective-permute-start.2) | collective-permute-done | bytes 524320 | tf_op jit(solution)/shard_map/ppermute | solution.py:150
  12.4 0.5 %shard_map.77 = (f32[144,256]{1,0:T(8,128)S(1)}, bf16[144,256]{1,0:T(8,128)(2,1)S(1)}, f32[8,128]{1,0:T(8,128)S(1)}) custom-call(bf16[128,2048]{1,0:T(8,128)(2,1)S(1)} %shard_map.74.cycled_ref, bf16[128,2048]{1,0:T(8,128)(2,1)S(1)} %collective-permute-done.2.hop_ref, bf16[16,2048]{1,0:T(8,128)(2,1)S(1)} %shard_map.76.halo_ref, bf16[3,2048,256]{2,1,0:T(8,128)(2,1)S(1)} %bitcast.3), custom_call_target="tpu_custom_call" | custom-call | tf_op jit(solution)/shard_map/pallas_call | solution.py:449
  12.9 1.4 %collective-permute-start.5 = (bf16[144,256]{1,0:T(8,128)(2,1)S(1)}, bf16[144,256]{1,0:T(8,128)(2,1)S(1)}, u32[]{:S(2)}, u32[]{:S(2)}) collective-permute-start(bf16[144,256]{1,0:T(8,128)(2,1)S(1)} %get-tuple-element.21), channel_id=1, source_target_pairs={{0,2},{2,0},{1,3},{3,1},{4,6},{6,4},{5,7},{7,5},{8,10},{10,8},{9,1... | collective-permute-start | bytes 221192 | tf_op jit(solution)/shard_map/ppermute | solution.py:150
  14.3 0.5 %collective-permute-done.7.two_ref = bf16[128,256]{1,0:T(8,128)(2,1)S(1)} collective-permute-done((bf16[128,256]{1,0:T(8,128)(2,1)S(1)}, bf16[128,256]{1,0:T(8,128)(2,1)S(1)}, u32[]{:S(2)}, u32[]{:S(2)}) %collective-permute-start.7) | collective-permute-done | bytes 65568 | tf_op jit(solution)/shard_map/ppermute | solution.py:429
  14.8 0.5 %shard_map.78 = (f32[272,128]{1,0:T(8,128)S(1)}, bf16[4,128,128]{2,1,0:T(8,128)(2,1)S(1)}, bf16[784,128]{1,0:T(8,128)(2,1)S(1)}, f32[8,128]{1,0:T(8,128)S(1)}) custom-call(bf16[128,2048]{1,0:T(8,128)(2,1)S(1)} %shard_map.74.cycled_ref, bf16[128,2048]{1,0:T(8,128)(2,1)S(1)} %collective-permute-done.2.hop_ref, bf16[16,2048]{1,0:T(8,128)(2,1)S(1)} %shard_map.76.halo_ref, ...), custom_call_target="tpu_custom_call" | custom-call | tf_op jit(solution)/shard_map/pallas_call | solution.py:459
  15.3 0.4 %collective-permute-done.4.got_first.refs_1_ = bf16[128,256]{1,0:T(8,128)(2,1)S(1)} collective-permute-done((bf16[128,256]{1,0:T(8,128)(2,1)S(1)}, bf16[128,256]{1,0:T(8,128)(2,1)S(1)}, u32[]{:S(2)}, u32[]{:S(2)}) %collective-permute-start.4) | collective-permute-done | bytes 65568 | tf_op jit(solution)/shard_map/ppermute | solution.py:150
  15.8 0.8 %collective-permute-start.12 = (bf16[784,128]{1,0:T(8,128)(2,1)S(1)}, bf16[784,128]{1,0:T(8,128)(2,1)S(1)}, u32[]{:S(2)}, u32[]{:S(2)}) collective-permute-start(bf16[784,128]{1,0:T(8,128)(2,1)S(1)} %shard_map.80), channel_id=1, source_target_pairs={{0,2},{2,0},{1,3},{3,1},{4,6},{6,4},{5,7},{7,5},{8,10},{10,8},{9,1... | collective-permute-start | bytes 602120 | tf_op jit(solution)/shard_map/ppermute | solution.py:150
  16.6 0.9 %collective-permute-done.5.got_second = bf16[144,256]{1,0:T(8,128)(2,1)S(1)} collective-permute-done((bf16[144,256]{1,0:T(8,128)(2,1)S(1)}, bf16[144,256]{1,0:T(8,128)(2,1)S(1)}, u32[]{:S(2)}, u32[]{:S(2)}) %collective-permute-start.5) | collective-permute-done | bytes 73760 | tf_op jit(solution)/shard_map/ppermute | solution.py:150
  17.7 3.9 %collective-permute-start.10 = (bf16[256,128]{1,0:T(8,128)(2,1)S(1)}, bf16[256,128]{1,0:T(8,128)(2,1)S(1)}, u32[]{:S(2)}, u32[]{:S(2)}) collective-permute-start(bf16[256,128]{1,0:T(8,128)(2,1)S(1)} %shard_map.79.own_ref), channel_id=1, source_target_pairs={{0,12},{4,8},{8,4},{12,0},{1,13},{5,9},{9,5},{13,1},{2,14},{6,10},... | collective-permute-start | bytes 196616 | tf_op jit(solution)/shard_map/ppermute | solution.py:488
  21.6 0.6 %collective-permute-start.9 = (bf16[256,128]{1,0:T(8,128)(2,1)S(1)}, bf16[256,128]{1,0:T(8,128)(2,1)S(1)}, u32[]{:S(2)}, u32[]{:S(2)}) collective-permute-start(bf16[256,128]{1,0:T(8,128)(2,1)S(1)} %shard_map.79.own_ref), channel_id=1, source_target_pairs={{0,8},{4,12},{8,0},{12,4},{1,9},{5,13},{9,1},{13,5},{2,10},{6,14},... | collective-permute-start | bytes 196616 | tf_op jit(solution)/shard_map/ppermute | solution.py:488
  22.3 0.5 %shard_map.81 = (f32[4,256,128]{2,1,0:T(8,128)S(1)}, f32[4,256,128]{2,1,0:T(8,128)S(1)}) custom-call(bf16[512,256]{1,0:T(8,128)(2,1)S(1)} %copy-done.1, bf16[4,128,128]{2,1,0:T(8,128)(2,1)S(1)} %get-tuple-element.24.keep_ref, bf16[784,128]{1,0:T(8,128)(2,1)S(1)} %collective-permute-done.12.got_ref), custom_call_target="tpu_custom_call" | custom-call | tf_op jit(solution)/shard_map/pallas_call | solution.py:492
  22.8 1.2 %collective-permute-done.10.far_ref = bf16[256,128]{1,0:T(8,128)(2,1)S(1)} collective-permute-done((bf16[256,128]{1,0:T(8,128)(2,1)S(1)}, bf16[256,128]{1,0:T(8,128)(2,1)S(1)}, u32[]{:S(2)}, u32[]{:S(2)}) %collective-permute-start.10) | collective-permute-done | bytes 65568 | tf_op jit(solution)/shard_map/ppermute | solution.py:488
  24.0 1.9 %collective-permute-done.11.near_ref = bf16[256,128]{1,0:T(8,128)(2,1)S(1)} collective-permute-done((bf16[256,128]{1,0:T(8,128)(2,1)S(1)}, bf16[256,128]{1,0:T(8,128)(2,1)S(1)}, u32[]{:S(2)}, u32[]{:S(2)}) %collective-permute-start.11) | collective-permute-done | bytes 65568 | tf_op jit(solution)/shard_map/ppermute | solution.py:488
  25.9 0.4 %shard_map.82.total_ref = f32[2,256,128]{2,1,0:T(8,128)S(1)} custom-call(bf16[256,128]{1,0:T(8,128)(2,1)S(1)} %shard_map.79.own_ref, bf16[256,128]{1,0:T(8,128)(2,1)S(1)} %collective-permute-done.10.far_ref, bf16[256,128]{1,0:T(8,128)(2,1)S(1)} %collective-permute-done.11.near_ref, f32[4,256,128]{2,1,0:T(8,128)S(1)} %get-tuple-element.26.real_ref, ...), custom_call_target="tpu_custom_call" | custom-call | tf_op jit(solution)/shard_map/pallas_call | solution.py:498
  26.3 0.5 %collective-permute-done.9.last_ref = bf16[256,128]{1,0:T(8,128)(2,1)S(1)} collective-permute-done((bf16[256,128]{1,0:T(8,128)(2,1)S(1)}, bf16[256,128]{1,0:T(8,128)(2,1)S(1)}, u32[]{:S(2)}, u32[]{:S(2)}) %collective-permute-start.9) | collective-permute-done | bytes 65568 | tf_op jit(solution)/shard_map/ppermute | solution.py:488
  26.8 0.5 %shard_map.84 = (bf16[128,128]{1,0:T(8,128)(2,1)S(1)}, bf16[512,128]{1,0:T(8,128)(2,1)S(1)}) custom-call(bf16[256,128]{1,0:T(8,128)(2,1)S(1)} %collective-permute-done.9.last_ref, f32[2,256,128]{2,1,0:T(8,128)S(1)} %shard_map.82.total_ref, f32[4,256,128]{2,1,0:T(8,128)S(1)} %get-tuple-element.26.real_ref, f32[4,256,128]{2,1,0:T(8,128)S(1)} %get-tuple-element.27.imag_ref, ...), custom_call_target="tpu_custom_call" | custom-call | tf_op jit(solution)/shard_map/pallas_call | solution.py:505
  27.2 1.0 %collective-permute-start.13 = (bf16[128,128]{1,0:T(8,128)(2,1)S(1)}, bf16[128,128]{1,0:T(8,128)(2,1)S(1)}, u32[]{:S(2)}, u32[]{:S(2)}) collective-permute-start(bf16[128,128]{1,0:T(8,128)(2,1)S(1)} %get-tuple-element.30), channel_id=1, source_target_pairs={{0,2},{2,0},{1,3},{3,1},{4,6},{6,4},{5,7},{7,5},{8,10},{10,8},{9,1... | collective-permute-start | bytes 98312 | tf_op jit(solution)/shard_map/ppermute | solution.py:150
  28.3 0.2 shard_map.85.stay_ref
  28.4 2.8 %collective-permute-done.13.got_ref = bf16[128,128]{1,0:T(8,128)(2,1)S(1)} collective-permute-done((bf16[128,128]{1,0:T(8,128)(2,1)S(1)}, bf16[128,128]{1,0:T(8,128)(2,1)S(1)}, u32[]{:S(2)}, u32[]{:S(2)}) %collective-permute-start.13) | collective-permute-done | bytes 32800 | tf_op jit(solution)/shard_map/ppermute | solution.py:150
  31.2 0.6 %shard_map.86 = bf16[128,256]{1,0:T(8,128)(2,1)} custom-call(bf16[128,128]{1,0:T(8,128)(2,1)S(1)} %shard_map.85.stay_ref, bf16[128,128]{1,0:T(8,128)(2,1)S(1)} %collective-permute-done.13.got_ref), custom_call_target="tpu_custom_call" | custom-call | tf_op jit(solution)/shard_map/pallas_call | solution.py:518
  (26 shorter events, 0.3 us)
Async XLA Ops:
  0.0 10.9 %copy-start = (bf16[2048,3,256]{2,0,1:T(8,128)(2,1)S(1)}, bf16[2048,3,256]{2,0,1:T(8,128)(2,1)}, u32[]{:S(2)}) copy-start(bf16[2048,3,256]{2,0,1:T(8,128)(2,1)} %param.8) | copy-start | bytes 9437188
  0.0 10.4 %collective-permute-start = (bf16[128,2048]{1,0:T(8,128)(2,1)}, bf16[128,2048]{1,0:T(8,128)(2,1)S(1)}, u32[]{:S(2)}, u32[]{:S(2)}) collective-permute-start(bf16[128,2048]{1,0:T(8,128)(2,1)} %rows_ref.5), channel_id=1, source_target_pairs={{1,3},{3,2},{2,0},{0,1},{5,7},{7,6},{6,4},{4,5},{9,11},{11,10},{10... | collective-permute-start | bytes 1572872 | tf_op jit(solution)/shard_map/ppermute | solution.py:409
  0.5 1.3 %copy-start.3 = (bf16[128,2048]{1,0:T(8,128)(2,1)S(1)}, bf16[128,2048]{1,0:T(8,128)(2,1)}, u32[]{:S(2)}) copy-start(bf16[128,2048]{1,0:T(8,128)(2,1)} %rows_ref.5) | copy-start | bytes 1572868
  1.7 4.2 %copy-start.5 = (bf16[128,256]{1,0:T(8,128)(2,1)S(1)}, bf16[128,256]{1,0:T(8,128)(2,1)}, u32[]{:S(2)}) copy-start(bf16[128,256]{1,0:T(8,128)(2,1)} %own_ref.1) | copy-start | bytes 196612
  1.9 8.5 %collective-permute-start.1 = (bf16[16,256]{1,0:T(8,128)(2,1)S(1)}, bf16[16,256]{1,0:T(8,128)(2,1)S(1)}, u32[]{:S(2)}, u32[]{:S(2)}) collective-permute-start(bf16[16,256]{1,0:T(8,128)(2,1)S(1)} %shard_map.73), channel_id=1, source_target_pairs={{0,6},{1,5},{2,4},{3,7},{4,10},{5,9},{6,8},{7,11},{8,14},{9,13},{1... | collective-permute-start | bytes 24584 | tf_op jit(solution)/shard_map/ppermute | solution.py:418
  6.0 8.3 %collective-permute-start.6 = (bf16[128,256]{1,0:T(8,128)(2,1)S(1)}, bf16[128,256]{1,0:T(8,128)(2,1)S(1)}, u32[]{:S(2)}, u32[]{:S(2)}) collective-permute-start(bf16[128,256]{1,0:T(8,128)(2,1)S(1)} %copy-done.5), channel_id=1, source_target_pairs={{0,4},{4,0},{8,12},{12,8},{1,5},{5,1},{9,13},{13,9},{2,6},{6,2},{1... | collective-permute-start | bytes 196616 | tf_op jit(solution)/shard_map/ppermute | solution.py:429
  7.5 7.3 %collective-permute-start.7 = (bf16[128,256]{1,0:T(8,128)(2,1)S(1)}, bf16[128,256]{1,0:T(8,128)(2,1)S(1)}, u32[]{:S(2)}, u32[]{:S(2)}) collective-permute-start(bf16[128,256]{1,0:T(8,128)(2,1)S(1)} %copy-done.5), channel_id=1, source_target_pairs={{0,8},{4,12},{8,0},{12,4},{1,9},{5,13},{9,1},{13,5},{2,10},{6,14},... | collective-permute-start | bytes 196616 | tf_op jit(solution)/shard_map/ppermute | solution.py:429
  8.5 6.3 %collective-permute-start.8 = (bf16[128,256]{1,0:T(8,128)(2,1)S(1)}, bf16[128,256]{1,0:T(8,128)(2,1)S(1)}, u32[]{:S(2)}, u32[]{:S(2)}) collective-permute-start(bf16[128,256]{1,0:T(8,128)(2,1)S(1)} %copy-done.5), channel_id=1, source_target_pairs={{0,12},{4,8},{8,4},{12,0},{1,13},{5,9},{9,5},{13,1},{2,14},{6,10},... | collective-permute-start | bytes 196616 | tf_op jit(solution)/shard_map/ppermute | solution.py:429
  10.3 1.2 %collective-permute-start.3 = (bf16[16,256]{1,0:T(8,128)(2,1)S(1)}, bf16[16,256]{1,0:T(8,128)(2,1)S(1)}, u32[]{:S(2)}, u32[]{:S(2)}) collective-permute-start(bf16[16,256]{1,0:T(8,128)(2,1)S(1)} %collective-permute-done.1.refs_1_.pack_ref), channel_id=1, source_target_pairs={{0,1},{1,0},{2,3},{3,2},{4,5},{5,4},{6,7},{7,6},{8,9},{9,8},{10,11... | collective-permute-start | bytes 24584 | tf_op jit(solution)/shard_map/ppermute | solution.py:150
  10.4 2.0 %collective-permute-start.2 = (bf16[128,2048]{1,0:T(8,128)(2,1)S(1)}, bf16[128,2048]{1,0:T(8,128)(2,1)S(1)}, u32[]{:S(2)}, u32[]{:S(2)}) collective-permute-start(bf16[128,2048]{1,0:T(8,128)(2,1)S(1)} %shard_map.74.cycled_ref), channel_id=1, source_target_pairs={{0,1},{1,0},{2,3},{3,2},{4,5},{5,4},{6,7},{7,6},{8,9},{9,8},{10,11... | collective-permute-start | bytes 1572872 | tf_op jit(solution)/shard_map/ppermute | solution.py:150
  11.3 3.5 %copy-start.4 = (bf16[128,2048]{1,0:T(8,128)(2,1)S(1)}, bf16[128,2048]{1,0:T(8,128)(2,1)}, u32[]{:S(2)}) copy-start(bf16[128,2048]{1,0:T(8,128)(2,1)} %rows_ref.5) | copy-start | bytes 1572868
  11.5 4.3 %collective-permute-start.4 = (bf16[128,256]{1,0:T(8,128)(2,1)S(1)}, bf16[128,256]{1,0:T(8,128)(2,1)S(1)}, u32[]{:S(2)}, u32[]{:S(2)}) collective-permute-start(bf16[128,256]{1,0:T(8,128)(2,1)S(1)} %get-tuple-element.20), channel_id=1, source_target_pairs={{0,2},{2,0},{1,3},{3,1},{4,6},{6,4},{5,7},{7,5},{8,10},{10,8},{9,1... | collective-permute-start | bytes 196616 | tf_op jit(solution)/shard_map/ppermute | solution.py:150
  12.9 4.6 %collective-permute-start.5 = (bf16[144,256]{1,0:T(8,128)(2,1)S(1)}, bf16[144,256]{1,0:T(8,128)(2,1)S(1)}, u32[]{:S(2)}, u32[]{:S(2)}) collective-permute-start(bf16[144,256]{1,0:T(8,128)(2,1)S(1)} %get-tuple-element.21), channel_id=1, source_target_pairs={{0,2},{2,0},{1,3},{3,1},{4,6},{6,4},{5,7},{7,5},{8,10},{10,8},{9,1... | collective-permute-start | bytes 221192 | tf_op jit(solution)/shard_map/ppermute | solution.py:150
  15.8 1.8 %copy-start.6 = (f32[3,3,256]{2,1,0:T(4,128)S(1)}, f32[3,3,256]{2,1,0:T(4,128)}, u32[]{:S(2)}) copy-start(f32[3,3,256]{2,1,0:T(4,128)} %short_ref.3) | copy-start | bytes 27652
  15.8 6.5 %collective-permute-start.12 = (bf16[784,128]{1,0:T(8,128)(2,1)S(1)}, bf16[784,128]{1,0:T(8,128)(2,1)S(1)}, u32[]{:S(2)}, u32[]{:S(2)}) collective-permute-start(bf16[784,128]{1,0:T(8,128)(2,1)S(1)} %shard_map.80), channel_id=1, source_target_pairs={{0,2},{2,0},{1,3},{3,1},{4,6},{6,4},{5,7},{7,5},{8,10},{10,8},{9,1... | collective-permute-start | bytes 602120 | tf_op jit(solution)/shard_map/ppermute | solution.py:150
  17.5 4.8 %copy-start.1 = (bf16[512,256]{1,0:T(8,128)(2,1)S(1)}, bf16[512,256]{1,0:T(8,128)(2,1)}, u32[]{:S(2)}) copy-start(bf16[512,256]{1,0:T(8,128)(2,1)} %constant.4.clone.table_ref) | copy-start | bytes 786436
  17.5 9.2 %copy-start.2 = (bf16[256,512]{1,0:T(8,128)(2,1)S(1)}, bf16[256,512]{1,0:T(8,128)(2,1)}, u32[]{:S(2)}) copy-start(bf16[256,512]{1,0:T(8,128)(2,1)} %constant.5.clone.turned_ref) | copy-start | bytes 786436
  17.5 9.2 %copy-start.7 = (f32[256]{0:T(256)S(1)}, f32[256]{0:T(256)}, u32[]{:S(2)}) copy-start(f32[256]{0:T(256)} %param.10) | copy-start | bytes 3076
  17.7 6.3 %collective-permute-start.10 = (bf16[256,128]{1,0:T(8,128)(2,1)S(1)}, bf16[256,128]{1,0:T(8,128)(2,1)S(1)}, u32[]{:S(2)}, u32[]{:S(2)}) collective-permute-start(bf16[256,128]{1,0:T(8,128)(2,1)S(1)} %shard_map.79.own_ref), channel_id=1, source_target_pairs={{0,12},{4,8},{8,4},{12,0},{1,13},{5,9},{9,5},{13,1},{2,14},{6,10},... | collective-permute-start | bytes 196616 | tf_op jit(solution)/shard_map/ppermute | solution.py:488
  21.6 4.3 %collective-permute-start.11 = (bf16[256,128]{1,0:T(8,128)(2,1)S(1)}, bf16[256,128]{1,0:T(8,128)(2,1)S(1)}, u32[]{:S(2)}, u32[]{:S(2)}) collective-permute-start(bf16[256,128]{1,0:T(8,128)(2,1)S(1)} %shard_map.79.own_ref), channel_id=1, source_target_pairs={{0,4},{4,0},{8,12},{12,8},{1,5},{5,1},{9,13},{13,9},{2,6},{6,2},{1... | collective-permute-start | bytes 196616 | tf_op jit(solution)/shard_map/ppermute | solution.py:488
  21.6 5.2 %collective-permute-start.9 = (bf16[256,128]{1,0:T(8,128)(2,1)S(1)}, bf16[256,128]{1,0:T(8,128)(2,1)S(1)}, u32[]{:S(2)}, u32[]{:S(2)}) collective-permute-start(bf16[256,128]{1,0:T(8,128)(2,1)S(1)} %shard_map.79.own_ref), channel_id=1, source_target_pairs={{0,8},{4,12},{8,0},{12,4},{1,9},{5,13},{9,1},{13,5},{2,10},{6,14},... | collective-permute-start | bytes 196616 | tf_op jit(solution)/shard_map/ppermute | solution.py:488
  27.2 4.0 %collective-permute-start.13 = (bf16[128,128]{1,0:T(8,128)(2,1)S(1)}, bf16[128,128]{1,0:T(8,128)(2,1)S(1)}, u32[]{:S(2)}, u32[]{:S(2)}) collective-permute-start(bf16[128,128]{1,0:T(8,128)(2,1)S(1)} %get-tuple-element.30), channel_id=1, source_target_pairs={{0,2},{2,0},{1,3},{3,1},{4,6},{6,4},{5,7},{7,5},{8,10},{10,8},{9,1... | collective-permute-start | bytes 98312 | tf_op jit(solution)/shard_map/ppermute | solution.py:150

commit v12 on v9

--- a/solution.py
+++ b/solution.py
@@ -426,7 +426,7 @@
     tap_blocks = [filter_taps] + [
         lax.ppermute(filter_taps, "seq", pairs[step]) for step in range(1, blocks)
     ]
-    cycled = after(cycled, pack_got)
+    cycled = after(cycled, pack)
     hop = exchange(cycled, "chan")
     pack_hop = exchange(pack_got, "chan")
     keep_first, send_first, keep_first_query, send_first_query = call(

time: 32 us -> 32 us (level)
  no operation moved by 1% of the time
where the time goes in v12:
time: 32 us; the launch traced here: 31.9 us
  starting transfers between devices  17.6 us (55%)
  waiting for transfers between devices  8.76 us (27%)
  Pallas kernels  4.09 us (13%)
  local copies, waits for them, and re-layouts  1.3 us (4%)
    ppermute x6, waiting for transfers between devices, exchange(): return lax.ppermute(value, axis, [(0, 1), (1, 0)])  4.79 us
    ppermute x3, starting transfers between devices, pair_mesh(): lax.ppermute(product, 'seq', pairs[step])  4.45 us
    ppermute x3, starting transfers between devices, pair_mesh(): lax.ppermute(filter_taps, 'seq', pairs[step])  4.39 us
    ppermute x6, starting transfers between devices, exchange(): return lax.ppermute(value, axis, [(0, 1), (1, 0)])  4.22 us
    ppermute x1, starting transfers between devices, pair_mesh(): lax.ppermute(pack, ('seq', 'fsdp', 'chan'), [(4 * s + 2 * f + c, 4 * ((s...  4.09 us
    ppermute x3, waiting for transfers between devices, pair_mesh(): lax.ppermute(product, 'seq', pairs[step])  3.55 us
    unnamed x14, local copies, waits for them, and re-layouts  1.3 us
    pallas_call x1, Pallas kernels, pair_mesh(): call(join_body, in_specs=whole_specs(2), out_specs=whole_specs(1)[0], out...  0.65 us
  transfers between devices with their start and end apart: 14, of which 8 were waited for; matrix products, arithmetic and copies ran while one was open for 0% of the time, Pallas kernels for 9%

profile of v12, /device:TPU:0, one launch (start us, length us, event | category | flops | bytes accessed | tf_op | source)
XLA Modules:
  0.0 31.9 jit_solution(5328743655258047251)
XLA Ops:
  0.0 0.5 %collective-permute-start = (bf16[128,2048]{1,0:T(8,128)(2,1)}, bf16[128,2048]{1,0:T(8,128)(2,1)S(1)}, u32[]{:S(2)}, u32[]{:S(2)}) collective-permute-start(bf16[128,2048]{1,0:T(8,128)(2,1)} %rows_ref.3), channel_id=1, source_target_pairs={{1,3},{3,2},{2,0},{0,1},{5,7},{7,6},{6,4},{4,5},{9,11},{11,10},{10... | collective-permute-start | bytes 1572872 | tf_op jit(solution)/shard_map/ppermute | solution.py:407
  0.5 1.3 %copy-done.6 = bf16[128,2048]{1,0:T(8,128)(2,1)S(1)} copy-done((bf16[128,2048]{1,0:T(8,128)(2,1)S(1)}, bf16[128,2048]{1,0:T(8,128)(2,1)}, u32[]{:S(2)}) %copy-start.6) | copy-done | bytes 524312
  1.7 0.1 shard_map.73.refs_1_
  1.9 4.1 %collective-permute-start.2 = (bf16[16,256]{1,0:T(8,128)(2,1)S(1)}, bf16[16,256]{1,0:T(8,128)(2,1)S(1)}, u32[]{:S(2)}, u32[]{:S(2)}) collective-permute-start(bf16[16,256]{1,0:T(8,128)(2,1)S(1)} %shard_map.73.refs_1_), channel_id=1, source_target_pairs={{0,6},{1,5},{2,4},{3,7},{4,10},{5,9},{6,8},{7,11},{8,14},{9,13},{1... | collective-permute-start | bytes 24584 | tf_op jit(solution)/shard_map/ppermute | solution.py:416
  6.0 2.6 %collective-permute-start.7 = (bf16[128,256]{1,0:T(8,128)(2,1)S(1)}, bf16[128,256]{1,0:T(8,128)(2,1)S(1)}, u32[]{:S(2)}, u32[]{:S(2)}) collective-permute-start(bf16[128,256]{1,0:T(8,128)(2,1)S(1)} %copy-done.3), channel_id=1, source_target_pairs={{0,8},{4,12},{8,0},{12,4},{1,9},{5,13},{9,1},{13,5},{2,10},{6,14},... | collective-permute-start | bytes 196616 | tf_op jit(solution)/shard_map/ppermute | solution.py:427
  8.6 1.8 %collective-permute-start.8 = (bf16[128,256]{1,0:T(8,128)(2,1)S(1)}, bf16[128,256]{1,0:T(8,128)(2,1)S(1)}, u32[]{:S(2)}, u32[]{:S(2)}) collective-permute-start(bf16[128,256]{1,0:T(8,128)(2,1)S(1)} %copy-done.3), channel_id=1, source_target_pairs={{0,12},{4,8},{8,4},{12,0},{1,13},{5,9},{9,5},{13,1},{2,14},{6,10},... | collective-permute-start | bytes 196616 | tf_op jit(solution)/shard_map/ppermute | solution.py:427
  10.4 0.5 %collective-permute-start.1 = (bf16[128,2048]{1,0:T(8,128)(2,1)S(1)}, bf16[128,2048]{1,0:T(8,128)(2,1)S(1)}, u32[]{:S(2)}, u32[]{:S(2)}) collective-permute-start(bf16[128,2048]{1,0:T(8,128)(2,1)S(1)} %shard_map.74.cycled_ref), channel_id=1, source_target_pairs={{0,1},{1,0},{2,3},{3,2},{4,5},{5,4},{6,7},{7,6},{8,9},{9,8},{10,11... | collective-permute-start | bytes 1572872 | tf_op jit(solution)/shard_map/ppermute | solution.py:150
  10.9 0.6 %shard_map.75 = (f32[128,256]{1,0:T(8,128)S(1)}, bf16[128,256]{1,0:T(8,128)(2,1)S(1)}, f32[128,128]{1,0:T(8,128)S(1)}, bf16[128,128]{1,0:T(8,128)(2,1)S(1)}) custom-call(bf16[128,2048]{1,0:T(8,128)(2,1)S(1)} %copy-done.6, bf16[128,2048]{1,0:T(8,128)(2,1)S(1)} %shard_map.74.cycled_ref, bf16[3,2048,256]{2,1,0:T(8,128)(2,1)S(1)} %bitcast.2), custom_call_target="tpu_custom_call" | custom-call | flops 10000000000 | bytes 40000000 | tf_op jit(solution)/shard_map/pallas_call | solution.py:432
  11.5 0.6 %collective-permute-start.4 = (bf16[128,256]{1,0:T(8,128)(2,1)S(1)}, bf16[128,256]{1,0:T(8,128)(2,1)S(1)}, u32[]{:S(2)}, u32[]{:S(2)}) collective-permute-start(bf16[128,256]{1,0:T(8,128)(2,1)S(1)} %get-tuple-element.22), channel_id=1, source_target_pairs={{0,2},{2,0},{1,3},{3,1},{4,6},{6,4},{5,7},{7,5},{8,10},{10,8},{9,1... | collective-permute-start | bytes 196616 | tf_op jit(solution)/shard_map/ppermute | solution.py:150
  12.1 0.1 shard_map.76.halo_ref
  12.3 0.1 collective-permute-done.1.hop_ref
  12.4 0.5 %shard_map.77 = (f32[144,256]{1,0:T(8,128)S(1)}, bf16[144,256]{1,0:T(8,128)(2,1)S(1)}, f32[8,128]{1,0:T(8,128)S(1)}) custom-call(bf16[128,2048]{1,0:T(8,128)(2,1)S(1)} %shard_map.74.cycled_ref, bf16[128,2048]{1,0:T(8,128)(2,1)S(1)} %collective-permute-done.1.hop_ref, bf16[16,2048]{1,0:T(8,128)(2,1)S(1)} %shard_map.76.halo_ref, bf16[3,2048,256]{2,1,0:T(8,128)(2,1)S(1)} %bitcast.3), custom_call_target="tpu_custom_call" | custom-call | tf_op jit(solution)/shard_map/pallas_call | solution.py:452
  12.9 1.4 %collective-permute-start.5 = (bf16[144,256]{1,0:T(8,128)(2,1)S(1)}, bf16[144,256]{1,0:T(8,128)(2,1)S(1)}, u32[]{:S(2)}, u32[]{:S(2)}) collective-permute-start(bf16[144,256]{1,0:T(8,128)(2,1)S(1)} %get-tuple-element.23), channel_id=1, source_target_pairs={{0,2},{2,0},{1,3},{3,1},{4,6},{6,4},{5,7},{7,5},{8,10},{10,8},{9,1... | collective-permute-start | bytes 221192 | tf_op jit(solution)/shard_map/ppermute | solution.py:150
  14.4 0.4 %collective-permute-done.8.three_ref = bf16[128,256]{1,0:T(8,128)(2,1)S(1)} collective-permute-done((bf16[128,256]{1,0:T(8,128)(2,1)S(1)}, bf16[128,256]{1,0:T(8,128)(2,1)S(1)}, u32[]{:S(2)}, u32[]{:S(2)}) %collective-permute-start.8) | collective-permute-done | bytes 65568 | tf_op jit(solution)/shard_map/ppermute | solution.py:427
  14.7 0.4 %shard_map.78 = (f32[144,128]{1,0:T(8,128)S(1)}, bf16[4,128,128]{2,1,0:T(8,128)(2,1)S(1)}, bf16[784,128]{1,0:T(8,128)(2,1)S(1)}, f32[8,128]{1,0:T(8,128)S(1)}) custom-call(bf16[128,2048]{1,0:T(8,128)(2,1)S(1)} %shard_map.74.cycled_ref, bf16[128,2048]{1,0:T(8,128)(2,1)S(1)} %collective-permute-done.1.hop_ref, bf16[16,2048]{1,0:T(8,128)(2,1)S(1)} %shard_map.76.halo_ref, ...), custom_call_target="tpu_custom_call" | custom-call | tf_op jit(solution)/shard_map/pallas_call | solution.py:462
  15.1 0.7 %collective-permute-done.4.got_first.refs_1_ = bf16[128,256]{1,0:T(8,128)(2,1)S(1)} collective-permute-done((bf16[128,256]{1,0:T(8,128)(2,1)S(1)}, bf16[128,256]{1,0:T(8,128)(2,1)S(1)}, u32[]{:S(2)}, u32[]{:S(2)}) %collective-permute-start.4) | collective-permute-done | bytes 65568 | tf_op jit(solution)/shard_map/ppermute | solution.py:150
  15.9 0.5 %collective-permute-start.12 = (bf16[784,128]{1,0:T(8,128)(2,1)S(1)}, bf16[784,128]{1,0:T(8,128)(2,1)S(1)}, u32[]{:S(2)}, u32[]{:S(2)}) collective-permute-start(bf16[784,128]{1,0:T(8,128)(2,1)S(1)} %shard_map.80), channel_id=1, source_target_pairs={{0,2},{2,0},{1,3},{3,1},{4,6},{6,4},{5,7},{7,5},{8,10},{10,8},{9,1... | collective-permute-start | bytes 602120 | tf_op jit(solution)/shard_map/ppermute | solution.py:150
  16.4 1.3 %collective-permute-done.5.got_second = bf16[144,256]{1,0:T(8,128)(2,1)S(1)} collective-permute-done((bf16[144,256]{1,0:T(8,128)(2,1)S(1)}, bf16[144,256]{1,0:T(8,128)(2,1)S(1)}, u32[]{:S(2)}, u32[]{:S(2)}) %collective-permute-start.5) | collective-permute-done | bytes 73760 | tf_op jit(solution)/shard_map/ppermute | solution.py:150
  17.7 0.1 shard_map.79.own_ref
  17.8 3.8 %collective-permute-start.11 = (bf16[256,128]{1,0:T(8,128)(2,1)S(1)}, bf16[256,128]{1,0:T(8,128)(2,1)S(1)}, u32[]{:S(2)}, u32[]{:S(2)}) collective-permute-start(bf16[256,128]{1,0:T(8,128)(2,1)S(1)} %shard_map.79.own_ref), channel_id=1, source_target_pairs={{0,12},{4,8},{8,4},{12,0},{1,13},{5,9},{9,5},{13,1},{2,14},{6,10},... | collective-permute-start | bytes 196616 | tf_op jit(solution)/shard_map/ppermute | solution.py:491
  21.6 0.7 %collective-permute-start.9 = (bf16[256,128]{1,0:T(8,128)(2,1)S(1)}, bf16[256,128]{1,0:T(8,128)(2,1)S(1)}, u32[]{:S(2)}, u32[]{:S(2)}) collective-permute-start(bf16[256,128]{1,0:T(8,128)(2,1)S(1)} %shard_map.79.own_ref), channel_id=1, source_target_pairs={{0,8},{4,12},{8,0},{12,4},{1,9},{5,13},{9,1},{13,5},{2,10},{6,14},... | collective-permute-start | bytes 196616 | tf_op jit(solution)/shard_map/ppermute | solution.py:491
  22.3 0.1 shard_map.83.query_ref
  22.3 0.5 %shard_map.81 = (f32[4,256,128]{2,1,0:T(8,128)S(1)}, f32[4,256,128]{2,1,0:T(8,128)S(1)}) custom-call(bf16[512,256]{1,0:T(8,128)(2,1)S(1)} %copy-done.1, bf16[4,128,128]{2,1,0:T(8,128)(2,1)S(1)} %get-tuple-element.27.keep_ref, bf16[784,128]{1,0:T(8,128)(2,1)S(1)} %collective-permute-done.12.got_ref), custom_call_target="tpu_custom_call" | custom-call | tf_op jit(solution)/shard_map/pallas_call | solution.py:495
  22.8 1.3 %collective-permute-done.11.far_ref = bf16[256,128]{1,0:T(8,128)(2,1)S(1)} collective-permute-done((bf16[256,128]{1,0:T(8,128)(2,1)S(1)}, bf16[256,128]{1,0:T(8,128)(2,1)S(1)}, u32[]{:S(2)}, u32[]{:S(2)}) %collective-permute-start.11) | collective-permute-done | bytes 65568 | tf_op jit(solution)/shard_map/ppermute | solution.py:491
  24.1 1.8 %collective-permute-done.10.near_ref = bf16[256,128]{1,0:T(8,128)(2,1)S(1)} collective-permute-done((bf16[256,128]{1,0:T(8,128)(2,1)S(1)}, bf16[256,128]{1,0:T(8,128)(2,1)S(1)}, u32[]{:S(2)}, u32[]{:S(2)}) %collective-permute-start.10) | collective-permute-done | bytes 65568 | tf_op jit(solution)/shard_map/ppermute | solution.py:491
  25.9 0.4 %shard_map.82.total_ref = f32[2,256,128]{2,1,0:T(8,128)S(1)} custom-call(bf16[256,128]{1,0:T(8,128)(2,1)S(1)} %shard_map.79.own_ref, bf16[256,128]{1,0:T(8,128)(2,1)S(1)} %collective-permute-done.10.near_ref, bf16[256,128]{1,0:T(8,128)(2,1)S(1)} %collective-permute-done.11.far_ref, f32[4,256,128]{2,1,0:T(8,128)S(1)} %get-tuple-element.29.real_ref, ...), custom_call_target="tpu_custom_call" | custom-call | tf_op jit(solution)/shard_map/pallas_call | solution.py:501
  26.3 0.5 %collective-permute-done.9.last_ref = bf16[256,128]{1,0:T(8,128)(2,1)S(1)} collective-permute-done((bf16[256,128]{1,0:T(8,128)(2,1)S(1)}, bf16[256,128]{1,0:T(8,128)(2,1)S(1)}, u32[]{:S(2)}, u32[]{:S(2)}) %collective-permute-start.9) | collective-permute-done | bytes 65568 | tf_op jit(solution)/shard_map/ppermute | solution.py:491
  26.8 0.5 %shard_map.84 = (bf16[128,128]{1,0:T(8,128)(2,1)S(1)}, bf16[512,128]{1,0:T(8,128)(2,1)S(1)}) custom-call(bf16[256,128]{1,0:T(8,128)(2,1)S(1)} %collective-permute-done.9.last_ref, f32[2,256,128]{2,1,0:T(8,128)S(1)} %shard_map.82.total_ref, f32[4,256,128]{2,1,0:T(8,128)S(1)} %get-tuple-element.29.real_ref, f32[4,256,128]{2,1,0:T(8,128)S(1)} %get-tuple-element.30.imag_ref, ...), custom_call_target="tpu_custom_call" | custom-call | tf_op jit(solution)/shard_map/pallas_call | solution.py:508
  27.2 1.2 %collective-permute-start.13 = (bf16[128,128]{1,0:T(8,128)(2,1)S(1)}, bf16[128,128]{1,0:T(8,128)(2,1)S(1)}, u32[]{:S(2)}, u32[]{:S(2)}) collective-permute-start(bf16[128,128]{1,0:T(8,128)(2,1)S(1)} %get-tuple-element.34), channel_id=1, source_target_pairs={{0,2},{2,0},{1,3},{3,1},{4,6},{6,4},{5,7},{7,5},{8,10},{10,8},{9,1... | collective-permute-start | bytes 98312 | tf_op jit(solution)/shard_map/ppermute | solution.py:150
  28.4 0.2 shard_map.85.stay_ref
  28.6 2.6 %collective-permute-done.13.got_ref = bf16[128,128]{1,0:T(8,128)(2,1)S(1)} collective-permute-done((bf16[128,128]{1,0:T(8,128)(2,1)S(1)}, bf16[128,128]{1,0:T(8,128)(2,1)S(1)}, u32[]{:S(2)}, u32[]{:S(2)}) %collective-permute-start.13) | collective-permute-done | bytes 32800 | tf_op jit(solution)/shard_map/ppermute | solution.py:150
  31.2 0.6 %shard_map.86 = bf16[128,256]{1,0:T(8,128)(2,1)} custom-call(bf16[128,128]{1,0:T(8,128)(2,1)S(1)} %shard_map.85.stay_ref, bf16[128,128]{1,0:T(8,128)(2,1)S(1)} %collective-permute-done.13.got_ref), custom_call_target="tpu_custom_call" | custom-call | tf_op jit(solution)/shard_map/pallas_call | solution.py:521
  (24 shorter events, 0.1 us)
Async XLA Ops:
  0.0 6.0 %copy-start.3 = (bf16[128,256]{1,0:T(8,128)(2,1)S(1)}, bf16[128,256]{1,0:T(8,128)(2,1)}, u32[]{:S(2)}) copy-start(bf16[128,256]{1,0:T(8,128)(2,1)} %own_ref.1) | copy-start | bytes 196612
  0.0 10.9 %copy-start = (bf16[2048,3,256]{2,0,1:T(8,128)(2,1)S(1)}, bf16[2048,3,256]{2,0,1:T(8,128)(2,1)}, u32[]{:S(2)}) copy-start(bf16[2048,3,256]{2,0,1:T(8,128)(2,1)} %param.8) | copy-start | bytes 9437188
  0.0 10.4 %collective-permute-start = (bf16[128,2048]{1,0:T(8,128)(2,1)}, bf16[128,2048]{1,0:T(8,128)(2,1)S(1)}, u32[]{:S(2)}, u32[]{:S(2)}) collective-permute-start(bf16[128,2048]{1,0:T(8,128)(2,1)} %rows_ref.3), channel_id=1, source_target_pairs={{1,3},{3,2},{2,0},{0,1},{5,7},{7,6},{6,4},{4,5},{9,11},{11,10},{10... | collective-permute-start | bytes 1572872 | tf_op jit(solution)/shard_map/ppermute | solution.py:407
  0.5 1.3 %copy-start.6 = (bf16[128,2048]{1,0:T(8,128)(2,1)S(1)}, bf16[128,2048]{1,0:T(8,128)(2,1)}, u32[]{:S(2)}) copy-start(bf16[128,2048]{1,0:T(8,128)(2,1)} %rows_ref.3) | copy-start | bytes 1572868
  1.9 8.5 %collective-permute-start.2 = (bf16[16,256]{1,0:T(8,128)(2,1)S(1)}, bf16[16,256]{1,0:T(8,128)(2,1)S(1)}, u32[]{:S(2)}, u32[]{:S(2)}) collective-permute-start(bf16[16,256]{1,0:T(8,128)(2,1)S(1)} %shard_map.73.refs_1_), channel_id=1, source_target_pairs={{0,6},{1,5},{2,4},{3,7},{4,10},{5,9},{6,8},{7,11},{8,14},{9,13},{1... | collective-permute-start | bytes 24584 | tf_op jit(solution)/shard_map/ppermute | solution.py:416
  6.0 8.4 %collective-permute-start.7 = (bf16[128,256]{1,0:T(8,128)(2,1)S(1)}, bf16[128,256]{1,0:T(8,128)(2,1)S(1)}, u32[]{:S(2)}, u32[]{:S(2)}) collective-permute-start(bf16[128,256]{1,0:T(8,128)(2,1)S(1)} %copy-done.3), channel_id=1, source_target_pairs={{0,8},{4,12},{8,0},{12,4},{1,9},{5,13},{9,1},{13,5},{2,10},{6,14},... | collective-permute-start | bytes 196616 | tf_op jit(solution)/shard_map/ppermute | solution.py:427
  8.6 5.8 %collective-permute-start.6 = (bf16[128,256]{1,0:T(8,128)(2,1)S(1)}, bf16[128,256]{1,0:T(8,128)(2,1)S(1)}, u32[]{:S(2)}, u32[]{:S(2)}) collective-permute-start(bf16[128,256]{1,0:T(8,128)(2,1)S(1)} %copy-done.3), channel_id=1, source_target_pairs={{0,4},{4,0},{8,12},{12,8},{1,5},{5,1},{9,13},{13,9},{2,6},{6,2},{1... | collective-permute-start | bytes 196616 | tf_op jit(solution)/shard_map/ppermute | solution.py:427
  8.6 6.2 %collective-permute-start.8 = (bf16[128,256]{1,0:T(8,128)(2,1)S(1)}, bf16[128,256]{1,0:T(8,128)(2,1)S(1)}, u32[]{:S(2)}, u32[]{:S(2)}) collective-permute-start(bf16[128,256]{1,0:T(8,128)(2,1)S(1)} %copy-done.3), channel_id=1, source_target_pairs={{0,12},{4,8},{8,4},{12,0},{1,13},{5,9},{9,5},{13,1},{2,14},{6,10},... | collective-permute-start | bytes 196616 | tf_op jit(solution)/shard_map/ppermute | solution.py:427
  10.4 1.2 %collective-permute-start.3 = (bf16[16,256]{1,0:T(8,128)(2,1)S(1)}, bf16[16,256]{1,0:T(8,128)(2,1)S(1)}, u32[]{:S(2)}, u32[]{:S(2)}) collective-permute-start(bf16[16,256]{1,0:T(8,128)(2,1)S(1)} %collective-permute-done.2.pack_ref), channel_id=1, source_target_pairs={{0,1},{1,0},{2,3},{3,2},{4,5},{5,4},{6,7},{7,6},{8,9},{9,8},{10,11... | collective-permute-start | bytes 24584 | tf_op jit(solution)/shard_map/ppermute | solution.py:150
  10.4 2.0 %collective-permute-start.1 = (bf16[128,2048]{1,0:T(8,128)(2,1)S(1)}, bf16[128,2048]{1,0:T(8,128)(2,1)S(1)}, u32[]{:S(2)}, u32[]{:S(2)}) collective-permute-start(bf16[128,2048]{1,0:T(8,128)(2,1)S(1)} %shard_map.74.cycled_ref), channel_id=1, source_target_pairs={{0,1},{1,0},{2,3},{3,2},{4,5},{5,4},{6,7},{7,6},{8,9},{9,8},{10,11... | collective-permute-start | bytes 1572872 | tf_op jit(solution)/shard_map/ppermute | solution.py:150
  11.5 4.3 %collective-permute-start.4 = (bf16[128,256]{1,0:T(8,128)(2,1)S(1)}, bf16[128,256]{1,0:T(8,128)(2,1)S(1)}, u32[]{:S(2)}, u32[]{:S(2)}) collective-permute-start(bf16[128,256]{1,0:T(8,128)(2,1)S(1)} %get-tuple-element.22), channel_id=1, source_target_pairs={{0,2},{2,0},{1,3},{3,1},{4,6},{6,4},{5,7},{7,5},{8,10},{10,8},{9,1... | collective-permute-start | bytes 196616 | tf_op jit(solution)/shard_map/ppermute | solution.py:150
  12.9 4.8 %collective-permute-start.5 = (bf16[144,256]{1,0:T(8,128)(2,1)S(1)}, bf16[144,256]{1,0:T(8,128)(2,1)S(1)}, u32[]{:S(2)}, u32[]{:S(2)}) collective-permute-start(bf16[144,256]{1,0:T(8,128)(2,1)S(1)} %get-tuple-element.23), channel_id=1, source_target_pairs={{0,2},{2,0},{1,3},{3,1},{4,6},{6,4},{5,7},{7,5},{8,10},{10,8},{9,1... | collective-permute-start | bytes 221192 | tf_op jit(solution)/shard_map/ppermute | solution.py:150
  15.8 1.8 %copy-start.4 = (f32[3,3,256]{2,1,0:T(4,128)S(1)}, f32[3,3,256]{2,1,0:T(4,128)}, u32[]{:S(2)}) copy-start(f32[3,3,256]{2,1,0:T(4,128)} %short_ref.3) | copy-start | bytes 27652
  15.9 6.4 %collective-permute-start.12 = (bf16[784,128]{1,0:T(8,128)(2,1)S(1)}, bf16[784,128]{1,0:T(8,128)(2,1)S(1)}, u32[]{:S(2)}, u32[]{:S(2)}) collective-permute-start(bf16[784,128]{1,0:T(8,128)(2,1)S(1)} %shard_map.80), channel_id=1, source_target_pairs={{0,2},{2,0},{1,3},{3,1},{4,6},{6,4},{5,7},{7,5},{8,10},{10,8},{9,1... | collective-permute-start | bytes 602120 | tf_op jit(solution)/shard_map/ppermute | solution.py:150
  17.7 4.7 %copy-start.1 = (bf16[512,256]{1,0:T(8,128)(2,1)S(1)}, bf16[512,256]{1,0:T(8,128)(2,1)}, u32[]{:S(2)}) copy-start(bf16[512,256]{1,0:T(8,128)(2,1)} %constant.4.clone.table_ref) | copy-start | bytes 786436
  17.7 9.1 %copy-start.2 = (bf16[256,512]{1,0:T(8,128)(2,1)S(1)}, bf16[256,512]{1,0:T(8,128)(2,1)}, u32[]{:S(2)}) copy-start(bf16[256,512]{1,0:T(8,128)(2,1)} %constant.5.clone.turned_ref) | copy-start | bytes 786436
  17.7 9.1 %copy-start.5 = (f32[256]{0:T(256)S(1)}, f32[256]{0:T(256)}, u32[]{:S(2)}) copy-start(f32[256]{0:T(256)} %param.10) | copy-start | bytes 3076
  17.8 6.2 %collective-permute-start.11 = (bf16[256,128]{1,0:T(8,128)(2,1)S(1)}, bf16[256,128]{1,0:T(8,128)(2,1)S(1)}, u32[]{:S(2)}, u32[]{:S(2)}) collective-permute-start(bf16[256,128]{1,0:T(8,128)(2,1)S(1)} %shard_map.79.own_ref), channel_id=1, source_target_pairs={{0,12},{4,8},{8,4},{12,0},{1,13},{5,9},{9,5},{13,1},{2,14},{6,10},... | collective-permute-start | bytes 196616 | tf_op jit(solution)/shard_map/ppermute | solution.py:491
  21.6 4.3 %collective-permute-start.10 = (bf16[256,128]{1,0:T(8,128)(2,1)S(1)}, bf16[256,128]{1,0:T(8,128)(2,1)S(1)}, u32[]{:S(2)}, u32[]{:S(2)}) collective-permute-start(bf16[256,128]{1,0:T(8,128)(2,1)S(1)} %shard_map.79.own_ref), channel_id=1, source_target_pairs={{0,4},{4,0},{8,12},{12,8},{1,5},{5,1},{9,13},{13,9},{2,6},{6,2},{1... | collective-permute-start | bytes 196616 | tf_op jit(solution)/shard_map/ppermute | solution.py:491
  21.6 5.2 %collective-permute-start.9 = (bf16[256,128]{1,0:T(8,128)(2,1)S(1)}, bf16[256,128]{1,0:T(8,128)(2,1)S(1)}, u32[]{:S(2)}, u32[]{:S(2)}) collective-permute-start(bf16[256,128]{1,0:T(8,128)(2,1)S(1)} %shard_map.79.own_ref), channel_id=1, source_target_pairs={{0,8},{4,12},{8,0},{12,4},{1,9},{5,13},{9,1},{13,5},{2,10},{6,14},... | collective-permute-start | bytes 196616 | tf_op jit(solution)/shard_map/ppermute | solution.py:491
  27.2 4.0 %collective-permute-start.13 = (bf16[128,128]{1,0:T(8,128)(2,1)S(1)}, bf16[128,128]{1,0:T(8,128)(2,1)S(1)}, u32[]{:S(2)}, u32[]{:S(2)}) collective-permute-start(bf16[128,128]{1,0:T(8,128)(2,1)S(1)} %get-tuple-element.34), channel_id=1, source_target_pairs={{0,2},{2,0},{1,3},{3,1},{4,6},{6,4},{5,7},{7,5},{8,10},{10,8},{9,1... | collective-permute-start | bytes 98312 | tf_op jit(solution)/shard_map/ppermute | solution.py:150

commit v13 on v9

--- a/solution.py
+++ b/solution.py
@@ -423,9 +423,10 @@
             for c in range(2)
         ],
     )
-    tap_blocks = [filter_taps] + [
-        lax.ppermute(filter_taps, "seq", pairs[step]) for step in range(1, blocks)
-    ]
+    arrived_taps = {
+        step: lax.ppermute(filter_taps, "seq", pairs[step]) for step in (2, 1, 3)
+    }
+    tap_blocks = [filter_taps] + [arrived_taps[step] for step in range(1, blocks)]
     cycled = after(cycled, pack_got)
     hop = exchange(cycled, "chan")
     pack_hop = exchange(pack_got, "chan")

time: 32 us -> 32 us (level)
  no operation moved by 1% of the time
where the time goes in v13:
time: 32 us; the launch traced here: 31.9 us
  starting transfers between devices  17.6 us (55%)
  waiting for transfers between devices  8.76 us (27%)
  Pallas kernels  4.09 us (13%)
  local copies, waits for them, and re-layouts  1.3 us (4%)
    ppermute x6, waiting for transfers between devices, exchange(): return lax.ppermute(value, axis, [(0, 1), (1, 0)])  4.79 us
    ppermute x3, starting transfers between devices, pair_mesh(): lax.ppermute(product, 'seq', pairs[step])  4.45 us
    ppermute x3, starting transfers between devices, pair_mesh(): lax.ppermute(filter_taps, 'seq', pairs[step])  4.39 us
    ppermute x6, starting transfers between devices, exchange(): return lax.ppermute(value, axis, [(0, 1), (1, 0)])  4.22 us
    ppermute x1, starting transfers between devices, pair_mesh(): lax.ppermute(pack, ('seq', 'fsdp', 'chan'), [(4 * s + 2 * f + c, 4 * ((s...  4.09 us
    ppermute x3, waiting for transfers between devices, pair_mesh(): lax.ppermute(product, 'seq', pairs[step])  3.55 us
    unnamed x14, local copies, waits for them, and re-layouts  1.3 us
    pallas_call x1, Pallas kernels, pair_mesh(): call(join_body, in_specs=whole_specs(2), out_specs=whole_specs(1)[0], out...  0.65 us
  transfers between devices with their start and end apart: 14, of which 8 were waited for; matrix products, arithmetic and copies ran while one was open for 0% of the time, Pallas kernels for 9%

profile of v13, /device:TPU:0, one launch (start us, length us, event | category | flops | bytes accessed | tf_op | source)
XLA Modules:
  0.0 31.9 jit_solution(17057544802516340385)
XLA Ops:
  0.0 0.5 %collective-permute-start = (bf16[128,2048]{1,0:T(8,128)(2,1)}, bf16[128,2048]{1,0:T(8,128)(2,1)S(1)}, u32[]{:S(2)}, u32[]{:S(2)}) collective-permute-start(bf16[128,2048]{1,0:T(8,128)(2,1)} %rows_ref.3), channel_id=1, source_target_pairs={{1,3},{3,2},{2,0},{0,1},{5,7},{7,6},{6,4},{4,5},{9,11},{11,10},{10... | collective-permute-start | bytes 1572872 | tf_op jit(solution)/shard_map/ppermute | solution.py:407
  0.5 1.3 %copy-done.6 = bf16[128,2048]{1,0:T(8,128)(2,1)S(1)} copy-done((bf16[128,2048]{1,0:T(8,128)(2,1)S(1)}, bf16[128,2048]{1,0:T(8,128)(2,1)}, u32[]{:S(2)}) %copy-start.6) | copy-done | bytes 524312
  1.7 0.1 shard_map.73
  1.9 4.1 %collective-permute-start.1 = (bf16[16,256]{1,0:T(8,128)(2,1)S(1)}, bf16[16,256]{1,0:T(8,128)(2,1)S(1)}, u32[]{:S(2)}, u32[]{:S(2)}) collective-permute-start(bf16[16,256]{1,0:T(8,128)(2,1)S(1)} %shard_map.73), channel_id=1, source_target_pairs={{0,6},{1,5},{2,4},{3,7},{4,10},{5,9},{6,8},{7,11},{8,14},{9,13},{1... | collective-permute-start | bytes 24584 | tf_op jit(solution)/shard_map/ppermute | solution.py:416
  6.0 2.6 %collective-permute-start.7 = (bf16[128,256]{1,0:T(8,128)(2,1)S(1)}, bf16[128,256]{1,0:T(8,128)(2,1)S(1)}, u32[]{:S(2)}, u32[]{:S(2)}) collective-permute-start(bf16[128,256]{1,0:T(8,128)(2,1)S(1)} %copy-done.3), channel_id=1, source_target_pairs={{0,8},{4,12},{8,0},{12,4},{1,9},{5,13},{9,1},{13,5},{2,10},{6,14},... | collective-permute-start | bytes 196616 | tf_op jit(solution)/shard_map/ppermute | solution.py:427
  8.6 1.8 %collective-permute-start.8 = (bf16[128,256]{1,0:T(8,128)(2,1)S(1)}, bf16[128,256]{1,0:T(8,128)(2,1)S(1)}, u32[]{:S(2)}, u32[]{:S(2)}) collective-permute-start(bf16[128,256]{1,0:T(8,128)(2,1)S(1)} %copy-done.3), channel_id=1, source_target_pairs={{0,12},{4,8},{8,4},{12,0},{1,13},{5,9},{9,5},{13,1},{2,14},{6,10},... | collective-permute-start | bytes 196616 | tf_op jit(solution)/shard_map/ppermute | solution.py:427
  10.4 0.5 %collective-permute-start.2 = (bf16[128,2048]{1,0:T(8,128)(2,1)S(1)}, bf16[128,2048]{1,0:T(8,128)(2,1)S(1)}, u32[]{:S(2)}, u32[]{:S(2)}) collective-permute-start(bf16[128,2048]{1,0:T(8,128)(2,1)S(1)} %shard_map.74.cycled_ref), channel_id=1, source_target_pairs={{0,1},{1,0},{2,3},{3,2},{4,5},{5,4},{6,7},{7,6},{8,9},{9,8},{10,11... | collective-permute-start | bytes 1572872 | tf_op jit(solution)/shard_map/ppermute | solution.py:150
  10.9 0.6 %shard_map.75 = (f32[128,256]{1,0:T(8,128)S(1)}, bf16[128,256]{1,0:T(8,128)(2,1)S(1)}, f32[128,128]{1,0:T(8,128)S(1)}, bf16[128,128]{1,0:T(8,128)(2,1)S(1)}) custom-call(bf16[128,2048]{1,0:T(8,128)(2,1)S(1)} %copy-done.6, bf16[128,2048]{1,0:T(8,128)(2,1)S(1)} %shard_map.74.cycled_ref, bf16[3,2048,256]{2,1,0:T(8,128)(2,1)S(1)} %bitcast.2), custom_call_target="tpu_custom_call" | custom-call | flops 10000000000 | bytes 40000000 | tf_op jit(solution)/shard_map/pallas_call | solution.py:433
  11.5 0.6 %collective-permute-start.4 = (bf16[128,256]{1,0:T(8,128)(2,1)S(1)}, bf16[128,256]{1,0:T(8,128)(2,1)S(1)}, u32[]{:S(2)}, u32[]{:S(2)}) collective-permute-start(bf16[128,256]{1,0:T(8,128)(2,1)S(1)} %get-tuple-element.22), channel_id=1, source_target_pairs={{0,2},{2,0},{1,3},{3,1},{4,6},{6,4},{5,7},{7,5},{8,10},{10,8},{9,1... | collective-permute-start | bytes 196616 | tf_op jit(solution)/shard_map/ppermute | solution.py:150
  12.1 0.1 shard_map.76.halo_ref
  12.3 0.1 collective-permute-done.2.hop_ref
  12.4 0.5 %shard_map.77 = (f32[144,256]{1,0:T(8,128)S(1)}, bf16[144,256]{1,0:T(8,128)(2,1)S(1)}, f32[8,128]{1,0:T(8,128)S(1)}) custom-call(bf16[128,2048]{1,0:T(8,128)(2,1)S(1)} %shard_map.74.cycled_ref, bf16[128,2048]{1,0:T(8,128)(2,1)S(1)} %collective-permute-done.2.hop_ref, bf16[16,2048]{1,0:T(8,128)(2,1)S(1)} %shard_map.76.halo_ref, bf16[3,2048,256]{2,1,0:T(8,128)(2,1)S(1)} %bitcast.3), custom_call_target="tpu_custom_call" | custom-call | tf_op jit(solution)/shard_map/pallas_call | solution.py:453
  12.9 1.4 %collective-permute-start.5 = (bf16[144,256]{1,0:T(8,128)(2,1)S(1)}, bf16[144,256]{1,0:T(8,128)(2,1)S(1)}, u32[]{:S(2)}, u32[]{:S(2)}) collective-permute-start(bf16[144,256]{1,0:T(8,128)(2,1)S(1)} %get-tuple-element.23), channel_id=1, source_target_pairs={{0,2},{2,0},{1,3},{3,1},{4,6},{6,4},{5,7},{7,5},{8,10},{10,8},{9,1... | collective-permute-start | bytes 221192 | tf_op jit(solution)/shard_map/ppermute | solution.py:150
  14.4 0.4 %collective-permute-done.8.three_ref = bf16[128,256]{1,0:T(8,128)(2,1)S(1)} collective-permute-done((bf16[128,256]{1,0:T(8,128)(2,1)S(1)}, bf16[128,256]{1,0:T(8,128)(2,1)S(1)}, u32[]{:S(2)}, u32[]{:S(2)}) %collective-permute-start.8) | collective-permute-done | bytes 65568 | tf_op jit(solution)/shard_map/ppermute | solution.py:427
  14.7 0.4 %shard_map.78 = (f32[144,128]{1,0:T(8,128)S(1)}, bf16[4,128,128]{2,1,0:T(8,128)(2,1)S(1)}, bf16[784,128]{1,0:T(8,128)(2,1)S(1)}, f32[8,128]{1,0:T(8,128)S(1)}) custom-call(bf16[128,2048]{1,0:T(8,128)(2,1)S(1)} %shard_map.74.cycled_ref, bf16[128,2048]{1,0:T(8,128)(2,1)S(1)} %collective-permute-done.2.hop_ref, bf16[16,2048]{1,0:T(8,128)(2,1)S(1)} %shard_map.76.halo_ref, ...), custom_call_target="tpu_custom_call" | custom-call | tf_op jit(solution)/shard_map/pallas_call | solution.py:463
  15.1 0.7 %collective-permute-done.4.got_first.refs_1_ = bf16[128,256]{1,0:T(8,128)(2,1)S(1)} collective-permute-done((bf16[128,256]{1,0:T(8,128)(2,1)S(1)}, bf16[128,256]{1,0:T(8,128)(2,1)S(1)}, u32[]{:S(2)}, u32[]{:S(2)}) %collective-permute-start.4) | collective-permute-done | bytes 65568 | tf_op jit(solution)/shard_map/ppermute | solution.py:150
  15.9 0.5 %collective-permute-start.12 = (bf16[784,128]{1,0:T(8,128)(2,1)S(1)}, bf16[784,128]{1,0:T(8,128)(2,1)S(1)}, u32[]{:S(2)}, u32[]{:S(2)}) collective-permute-start(bf16[784,128]{1,0:T(8,128)(2,1)S(1)} %shard_map.80), channel_id=1, source_target_pairs={{0,2},{2,0},{1,3},{3,1},{4,6},{6,4},{5,7},{7,5},{8,10},{10,8},{9,1... | collective-permute-start | bytes 602120 | tf_op jit(solution)/shard_map/ppermute | solution.py:150
  16.4 1.3 %collective-permute-done.5.got_second = bf16[144,256]{1,0:T(8,128)(2,1)S(1)} collective-permute-done((bf16[144,256]{1,0:T(8,128)(2,1)S(1)}, bf16[144,256]{1,0:T(8,128)(2,1)S(1)}, u32[]{:S(2)}, u32[]{:S(2)}) %collective-permute-start.5) | collective-permute-done | bytes 73760 | tf_op jit(solution)/shard_map/ppermute | solution.py:150
  17.7 0.1 shard_map.79.own_ref
  17.8 3.8 %collective-permute-start.11 = (bf16[256,128]{1,0:T(8,128)(2,1)S(1)}, bf16[256,128]{1,0:T(8,128)(2,1)S(1)}, u32[]{:S(2)}, u32[]{:S(2)}) collective-permute-start(bf16[256,128]{1,0:T(8,128)(2,1)S(1)} %shard_map.79.own_ref), channel_id=1, source_target_pairs={{0,12},{4,8},{8,4},{12,0},{1,13},{5,9},{9,5},{13,1},{2,14},{6,10},... | collective-permute-start | bytes 196616 | tf_op jit(solution)/shard_map/ppermute | solution.py:492
  21.6 0.7 %collective-permute-start.9 = (bf16[256,128]{1,0:T(8,128)(2,1)S(1)}, bf16[256,128]{1,0:T(8,128)(2,1)S(1)}, u32[]{:S(2)}, u32[]{:S(2)}) collective-permute-start(bf16[256,128]{1,0:T(8,128)(2,1)S(1)} %shard_map.79.own_ref), channel_id=1, source_target_pairs={{0,8},{4,12},{8,0},{12,4},{1,9},{5,13},{9,1},{13,5},{2,10},{6,14},... | collective-permute-start | bytes 196616 | tf_op jit(solution)/shard_map/ppermute | solution.py:492
  22.3 0.1 shard_map.83.query_ref
  22.3 0.5 %shard_map.81 = (f32[4,256,128]{2,1,0:T(8,128)S(1)}, f32[4,256,128]{2,1,0:T(8,128)S(1)}) custom-call(bf16[512,256]{1,0:T(8,128)(2,1)S(1)} %copy-done.1, bf16[4,128,128]{2,1,0:T(8,128)(2,1)S(1)} %get-tuple-element.27.keep_ref, bf16[784,128]{1,0:T(8,128)(2,1)S(1)} %collective-permute-done.12.got_ref), custom_call_target="tpu_custom_call" | custom-call | tf_op jit(solution)/shard_map/pallas_call | solution.py:496
  22.8 1.3 %collective-permute-done.11.far_ref = bf16[256,128]{1,0:T(8,128)(2,1)S(1)} collective-permute-done((bf16[256,128]{1,0:T(8,128)(2,1)S(1)}, bf16[256,128]{1,0:T(8,128)(2,1)S(1)}, u32[]{:S(2)}, u32[]{:S(2)}) %collective-permute-start.11) | collective-permute-done | bytes 65568 | tf_op jit(solution)/shard_map/ppermute | solution.py:492
  24.1 1.8 %collective-permute-done.10.near_ref = bf16[256,128]{1,0:T(8,128)(2,1)S(1)} collective-permute-done((bf16[256,128]{1,0:T(8,128)(2,1)S(1)}, bf16[256,128]{1,0:T(8,128)(2,1)S(1)}, u32[]{:S(2)}, u32[]{:S(2)}) %collective-permute-start.10) | collective-permute-done | bytes 65568 | tf_op jit(solution)/shard_map/ppermute | solution.py:492
  25.9 0.4 %shard_map.82.total_ref = f32[2,256,128]{2,1,0:T(8,128)S(1)} custom-call(bf16[256,128]{1,0:T(8,128)(2,1)S(1)} %shard_map.79.own_ref, bf16[256,128]{1,0:T(8,128)(2,1)S(1)} %collective-permute-done.10.near_ref, bf16[256,128]{1,0:T(8,128)(2,1)S(1)} %collective-permute-done.11.far_ref, f32[4,256,128]{2,1,0:T(8,128)S(1)} %get-tuple-element.29.real_ref, ...), custom_call_target="tpu_custom_call" | custom-call | tf_op jit(solution)/shard_map/pallas_call | solution.py:502
  26.3 0.5 %collective-permute-done.9.last_ref = bf16[256,128]{1,0:T(8,128)(2,1)S(1)} collective-permute-done((bf16[256,128]{1,0:T(8,128)(2,1)S(1)}, bf16[256,128]{1,0:T(8,128)(2,1)S(1)}, u32[]{:S(2)}, u32[]{:S(2)}) %collective-permute-start.9) | collective-permute-done | bytes 65568 | tf_op jit(solution)/shard_map/ppermute | solution.py:492
  26.8 0.5 %shard_map.84 = (bf16[128,128]{1,0:T(8,128)(2,1)S(1)}, bf16[512,128]{1,0:T(8,128)(2,1)S(1)}) custom-call(bf16[256,128]{1,0:T(8,128)(2,1)S(1)} %collective-permute-done.9.last_ref, f32[2,256,128]{2,1,0:T(8,128)S(1)} %shard_map.82.total_ref, f32[4,256,128]{2,1,0:T(8,128)S(1)} %get-tuple-element.29.real_ref, f32[4,256,128]{2,1,0:T(8,128)S(1)} %get-tuple-element.30.imag_ref, ...), custom_call_target="tpu_custom_call" | custom-call | tf_op jit(solution)/shard_map/pallas_call | solution.py:509
  27.2 1.2 %collective-permute-start.13 = (bf16[128,128]{1,0:T(8,128)(2,1)S(1)}, bf16[128,128]{1,0:T(8,128)(2,1)S(1)}, u32[]{:S(2)}, u32[]{:S(2)}) collective-permute-start(bf16[128,128]{1,0:T(8,128)(2,1)S(1)} %get-tuple-element.34), channel_id=1, source_target_pairs={{0,2},{2,0},{1,3},{3,1},{4,6},{6,4},{5,7},{7,5},{8,10},{10,8},{9,1... | collective-permute-start | bytes 98312 | tf_op jit(solution)/shard_map/ppermute | solution.py:150
  28.4 0.2 shard_map.85.stay_ref
  28.6 2.6 %collective-permute-done.13.got_ref = bf16[128,128]{1,0:T(8,128)(2,1)S(1)} collective-permute-done((bf16[128,128]{1,0:T(8,128)(2,1)S(1)}, bf16[128,128]{1,0:T(8,128)(2,1)S(1)}, u32[]{:S(2)}, u32[]{:S(2)}) %collective-permute-start.13) | collective-permute-done | bytes 32800 | tf_op jit(solution)/shard_map/ppermute | solution.py:150
  31.2 0.6 %shard_map.86 = bf16[128,256]{1,0:T(8,128)(2,1)} custom-call(bf16[128,128]{1,0:T(8,128)(2,1)S(1)} %shard_map.85.stay_ref, bf16[128,128]{1,0:T(8,128)(2,1)S(1)} %collective-permute-done.13.got_ref), custom_call_target="tpu_custom_call" | custom-call | tf_op jit(solution)/shard_map/pallas_call | solution.py:522
  (24 shorter events, 0.1 us)
Async XLA Ops:
  0.0 6.0 %copy-start.3 = (bf16[128,256]{1,0:T(8,128)(2,1)S(1)}, bf16[128,256]{1,0:T(8,128)(2,1)}, u32[]{:S(2)}) copy-start(bf16[128,256]{1,0:T(8,128)(2,1)} %own_ref.1) | copy-start | bytes 196612
  0.0 10.9 %copy-start = (bf16[2048,3,256]{2,0,1:T(8,128)(2,1)S(1)}, bf16[2048,3,256]{2,0,1:T(8,128)(2,1)}, u32[]{:S(2)}) copy-start(bf16[2048,3,256]{2,0,1:T(8,128)(2,1)} %param.8) | copy-start | bytes 9437188
  0.0 10.4 %collective-permute-start = (bf16[128,2048]{1,0:T(8,128)(2,1)}, bf16[128,2048]{1,0:T(8,128)(2,1)S(1)}, u32[]{:S(2)}, u32[]{:S(2)}) collective-permute-start(bf16[128,2048]{1,0:T(8,128)(2,1)} %rows_ref.3), channel_id=1, source_target_pairs={{1,3},{3,2},{2,0},{0,1},{5,7},{7,6},{6,4},{4,5},{9,11},{11,10},{10... | collective-permute-start | bytes 1572872 | tf_op jit(solution)/shard_map/ppermute | solution.py:407
  0.5 1.3 %copy-start.6 = (bf16[128,2048]{1,0:T(8,128)(2,1)S(1)}, bf16[128,2048]{1,0:T(8,128)(2,1)}, u32[]{:S(2)}) copy-start(bf16[128,2048]{1,0:T(8,128)(2,1)} %rows_ref.3) | copy-start | bytes 1572868
  1.9 8.5 %collective-permute-start.1 = (bf16[16,256]{1,0:T(8,128)(2,1)S(1)}, bf16[16,256]{1,0:T(8,128)(2,1)S(1)}, u32[]{:S(2)}, u32[]{:S(2)}) collective-permute-start(bf16[16,256]{1,0:T(8,128)(2,1)S(1)} %shard_map.73), channel_id=1, source_target_pairs={{0,6},{1,5},{2,4},{3,7},{4,10},{5,9},{6,8},{7,11},{8,14},{9,13},{1... | collective-permute-start | bytes 24584 | tf_op jit(solution)/shard_map/ppermute | solution.py:416
  6.0 8.4 %collective-permute-start.7 = (bf16[128,256]{1,0:T(8,128)(2,1)S(1)}, bf16[128,256]{1,0:T(8,128)(2,1)S(1)}, u32[]{:S(2)}, u32[]{:S(2)}) collective-permute-start(bf16[128,256]{1,0:T(8,128)(2,1)S(1)} %copy-done.3), channel_id=1, source_target_pairs={{0,8},{4,12},{8,0},{12,4},{1,9},{5,13},{9,1},{13,5},{2,10},{6,14},... | collective-permute-start | bytes 196616 | tf_op jit(solution)/shard_map/ppermute | solution.py:427
  8.6 5.8 %collective-permute-start.6 = (bf16[128,256]{1,0:T(8,128)(2,1)S(1)}, bf16[128,256]{1,0:T(8,128)(2,1)S(1)}, u32[]{:S(2)}, u32[]{:S(2)}) collective-permute-start(bf16[128,256]{1,0:T(8,128)(2,1)S(1)} %copy-done.3), channel_id=1, source_target_pairs={{0,4},{4,0},{8,12},{12,8},{1,5},{5,1},{9,13},{13,9},{2,6},{6,2},{1... | collective-permute-start | bytes 196616 | tf_op jit(solution)/shard_map/ppermute | solution.py:427
  8.6 6.2 %collective-permute-start.8 = (bf16[128,256]{1,0:T(8,128)(2,1)S(1)}, bf16[128,256]{1,0:T(8,128)(2,1)S(1)}, u32[]{:S(2)}, u32[]{:S(2)}) collective-permute-start(bf16[128,256]{1,0:T(8,128)(2,1)S(1)} %copy-done.3), channel_id=1, source_target_pairs={{0,12},{4,8},{8,4},{12,0},{1,13},{5,9},{9,5},{13,1},{2,14},{6,10},... | collective-permute-start | bytes 196616 | tf_op jit(solution)/shard_map/ppermute | solution.py:427
  10.4 1.2 %collective-permute-start.3 = (bf16[16,256]{1,0:T(8,128)(2,1)S(1)}, bf16[16,256]{1,0:T(8,128)(2,1)S(1)}, u32[]{:S(2)}, u32[]{:S(2)}) collective-permute-start(bf16[16,256]{1,0:T(8,128)(2,1)S(1)} %collective-permute-done.1.refs_1_.pack_ref), channel_id=1, source_target_pairs={{0,1},{1,0},{2,3},{3,2},{4,5},{5,4},{6,7},{7,6},{8,9},{9,8},{10,11... | collective-permute-start | bytes 24584 | tf_op jit(solution)/shard_map/ppermute | solution.py:150
  10.4 2.0 %collective-permute-start.2 = (bf16[128,2048]{1,0:T(8,128)(2,1)S(1)}, bf16[128,2048]{1,0:T(8,128)(2,1)S(1)}, u32[]{:S(2)}, u32[]{:S(2)}) collective-permute-start(bf16[128,2048]{1,0:T(8,128)(2,1)S(1)} %shard_map.74.cycled_ref), channel_id=1, source_target_pairs={{0,1},{1,0},{2,3},{3,2},{4,5},{5,4},{6,7},{7,6},{8,9},{9,8},{10,11... | collective-permute-start | bytes 1572872 | tf_op jit(solution)/shard_map/ppermute | solution.py:150
  11.5 4.3 %collective-permute-start.4 = (bf16[128,256]{1,0:T(8,128)(2,1)S(1)}, bf16[128,256]{1,0:T(8,128)(2,1)S(1)}, u32[]{:S(2)}, u32[]{:S(2)}) collective-permute-start(bf16[128,256]{1,0:T(8,128)(2,1)S(1)} %get-tuple-element.22), channel_id=1, source_target_pairs={{0,2},{2,0},{1,3},{3,1},{4,6},{6,4},{5,7},{7,5},{8,10},{10,8},{9,1... | collective-permute-start | bytes 196616 | tf_op jit(solution)/shard_map/ppermute | solution.py:150
  12.9 4.8 %collective-permute-start.5 = (bf16[144,256]{1,0:T(8,128)(2,1)S(1)}, bf16[144,256]{1,0:T(8,128)(2,1)S(1)}, u32[]{:S(2)}, u32[]{:S(2)}) collective-permute-start(bf16[144,256]{1,0:T(8,128)(2,1)S(1)} %get-tuple-element.23), channel_id=1, source_target_pairs={{0,2},{2,0},{1,3},{3,1},{4,6},{6,4},{5,7},{7,5},{8,10},{10,8},{9,1... | collective-permute-start | bytes 221192 | tf_op jit(solution)/shard_map/ppermute | solution.py:150
  15.8 1.8 %copy-start.4 = (f32[3,3,256]{2,1,0:T(4,128)S(1)}, f32[3,3,256]{2,1,0:T(4,128)}, u32[]{:S(2)}) copy-start(f32[3,3,256]{2,1,0:T(4,128)} %short_ref.3) | copy-start | bytes 27652
  15.9 6.4 %collective-permute-start.12 = (bf16[784,128]{1,0:T(8,128)(2,1)S(1)}, bf16[784,128]{1,0:T(8,128)(2,1)S(1)}, u32[]{:S(2)}, u32[]{:S(2)}) collective-permute-start(bf16[784,128]{1,0:T(8,128)(2,1)S(1)} %shard_map.80), channel_id=1, source_target_pairs={{0,2},{2,0},{1,3},{3,1},{4,6},{6,4},{5,7},{7,5},{8,10},{10,8},{9,1... | collective-permute-start | bytes 602120 | tf_op jit(solution)/shard_map/ppermute | solution.py:150
  17.7 4.7 %copy-start.1 = (bf16[512,256]{1,0:T(8,128)(2,1)S(1)}, bf16[512,256]{1,0:T(8,128)(2,1)}, u32[]{:S(2)}) copy-start(bf16[512,256]{1,0:T(8,128)(2,1)} %constant.4.clone.table_ref) | copy-start | bytes 786436
  17.7 9.1 %copy-start.2 = (bf16[256,512]{1,0:T(8,128)(2,1)S(1)}, bf16[256,512]{1,0:T(8,128)(2,1)}, u32[]{:S(2)}) copy-start(bf16[256,512]{1,0:T(8,128)(2,1)} %constant.5.clone.turned_ref) | copy-start | bytes 786436
  17.7 9.1 %copy-start.5 = (f32[256]{0:T(256)S(1)}, f32[256]{0:T(256)}, u32[]{:S(2)}) copy-start(f32[256]{0:T(256)} %param.10) | copy-start | bytes 3076
  17.8 6.2 %collective-permute-start.11 = (bf16[256,128]{1,0:T(8,128)(2,1)S(1)}, bf16[256,128]{1,0:T(8,128)(2,1)S(1)}, u32[]{:S(2)}, u32[]{:S(2)}) collective-permute-start(bf16[256,128]{1,0:T(8,128)(2,1)S(1)} %shard_map.79.own_ref), channel_id=1, source_target_pairs={{0,12},{4,8},{8,4},{12,0},{1,13},{5,9},{9,5},{13,1},{2,14},{6,10},... | collective-permute-start | bytes 196616 | tf_op jit(solution)/shard_map/ppermute | solution.py:492
  21.6 4.3 %collective-permute-start.10 = (bf16[256,128]{1,0:T(8,128)(2,1)S(1)}, bf16[256,128]{1,0:T(8,128)(2,1)S(1)}, u32[]{:S(2)}, u32[]{:S(2)}) collective-permute-start(bf16[256,128]{1,0:T(8,128)(2,1)S(1)} %shard_map.79.own_ref), channel_id=1, source_target_pairs={{0,4},{4,0},{8,12},{12,8},{1,5},{5,1},{9,13},{13,9},{2,6},{6,2},{1... | collective-permute-start | bytes 196616 | tf_op jit(solution)/shard_map/ppermute | solution.py:492
  21.6 5.2 %collective-permute-start.9 = (bf16[256,128]{1,0:T(8,128)(2,1)S(1)}, bf16[256,128]{1,0:T(8,128)(2,1)S(1)}, u32[]{:S(2)}, u32[]{:S(2)}) collective-permute-start(bf16[256,128]{1,0:T(8,128)(2,1)S(1)} %shard_map.79.own_ref), channel_id=1, source_target_pairs={{0,8},{4,12},{8,0},{12,4},{1,9},{5,13},{9,1},{13,5},{2,10},{6,14},... | collective-permute-start | bytes 196616 | tf_op jit(solution)/shard_map/ppermute | solution.py:492
  27.2 4.0 %collective-permute-start.13 = (bf16[128,128]{1,0:T(8,128)(2,1)S(1)}, bf16[128,128]{1,0:T(8,128)(2,1)S(1)}, u32[]{:S(2)}, u32[]{:S(2)}) collective-permute-start(bf16[128,128]{1,0:T(8,128)(2,1)S(1)} %get-tuple-element.34), channel_id=1, source_target_pairs={{0,2},{2,0},{1,3},{3,1},{4,6},{6,4},{5,7},{7,5},{8,10},{10,8},{9,1... | collective-permute-start | bytes 98312 | tf_op jit(solution)/shard_map/ppermute | solution.py:150

commit v14 on v13

--- a/solution.py
+++ b/solution.py
@@ -337,8 +337,13 @@
     block = block_ref[...]
     if step:
         block = jnp.where(source < position, block, jnp.zeros_like(block))
-    waves = jnp.dot(table_ref[...], block, preferred_element_type=F32)
-    real, imag = (waves[:size], -waves[size:])
+    part = size // 2
+    waves = [
+        jnp.dot(table_ref[start : start + part, :], block, preferred_element_type=F32)
+        for start in range(0, 2 * size, part)
+    ]
+    real = jnp.concatenate(waves[:2], axis=0)
+    imag = -jnp.concatenate(waves[2:], axis=0)
     tap_real, tap_imag = (real_ref[back], imag_ref[back])
     return (real * tap_real - imag * tap_imag, real * tap_imag + imag * tap_real)
 

time: 32 us -> 31.9 us (level)
  no operation moved by 1% of the time
where the time goes in v14:
time: 31.9 us; the launch traced here: 31.8 us
  starting transfers between devices  17.6 us (55%)
  waiting for transfers between devices  8.79 us (28%)
  Pallas kernels  4.01 us (13%)
  local copies, waits for them, and re-layouts  1.3 us (4%)
    ppermute x6, waiting for transfers between devices, exchange(): return lax.ppermute(value, axis, [(0, 1), (1, 0)])  4.79 us
    ppermute x3, starting transfers between devices, pair_mesh(): lax.ppermute(product, 'seq', pairs[step])  4.45 us
    ppermute x3, starting transfers between devices, pair_mesh(): lax.ppermute(filter_taps, 'seq', pairs[step])  4.39 us
    ppermute x6, starting transfers between devices, exchange(): return lax.ppermute(value, axis, [(0, 1), (1, 0)])  4.22 us
    ppermute x1, starting transfers between devices, pair_mesh(): lax.ppermute(pack, ('seq', 'fsdp', 'chan'), [(4 * s + 2 * f + c, 4 * ((s...  4.09 us
    ppermute x3, waiting for transfers between devices, pair_mesh(): lax.ppermute(product, 'seq', pairs[step])  3.57 us
    unnamed x14, local copies, waits for them, and re-layouts  1.3 us
    pallas_call x1, Pallas kernels, pair_mesh(): call(join_body, in_specs=whole_specs(2), out_specs=whole_specs(1)[0], out...  0.65 us
  transfers between devices with their start and end apart: 14, of which 8 were waited for; matrix products, arithmetic and copies ran while one was open for 0% of the time, Pallas kernels for 9%

profile of v14, /device:TPU:0, one launch (start us, length us, event | category | flops | bytes accessed | tf_op | source)
XLA Modules:
  0.0 31.8 jit_solution(4574962151553326843)
XLA Ops:
  0.0 0.5 %collective-permute-start = (bf16[128,2048]{1,0:T(8,128)(2,1)}, bf16[128,2048]{1,0:T(8,128)(2,1)S(1)}, u32[]{:S(2)}, u32[]{:S(2)}) collective-permute-start(bf16[128,2048]{1,0:T(8,128)(2,1)} %rows_ref.3), channel_id=1, source_target_pairs={{1,3},{3,2},{2,0},{0,1},{5,7},{7,6},{6,4},{4,5},{9,11},{11,10},{10... | collective-permute-start | bytes 1572872 | tf_op jit(solution)/shard_map/ppermute | solution.py:412
  0.5 1.3 %copy-done.6 = bf16[128,2048]{1,0:T(8,128)(2,1)S(1)} copy-done((bf16[128,2048]{1,0:T(8,128)(2,1)S(1)}, bf16[128,2048]{1,0:T(8,128)(2,1)}, u32[]{:S(2)}) %copy-start.6) | copy-done | bytes 524312
  1.7 0.1 shard_map.73
  1.9 4.1 %collective-permute-start.1 = (bf16[16,256]{1,0:T(8,128)(2,1)S(1)}, bf16[16,256]{1,0:T(8,128)(2,1)S(1)}, u32[]{:S(2)}, u32[]{:S(2)}) collective-permute-start(bf16[16,256]{1,0:T(8,128)(2,1)S(1)} %shard_map.73), channel_id=1, source_target_pairs={{0,6},{1,5},{2,4},{3,7},{4,10},{5,9},{6,8},{7,11},{8,14},{9,13},{1... | collective-permute-start | bytes 24584 | tf_op jit(solution)/shard_map/ppermute | solution.py:421
  6.0 2.6 %collective-permute-start.7 = (bf16[128,256]{1,0:T(8,128)(2,1)S(1)}, bf16[128,256]{1,0:T(8,128)(2,1)S(1)}, u32[]{:S(2)}, u32[]{:S(2)}) collective-permute-start(bf16[128,256]{1,0:T(8,128)(2,1)S(1)} %copy-done.3), channel_id=1, source_target_pairs={{0,8},{4,12},{8,0},{12,4},{1,9},{5,13},{9,1},{13,5},{2,10},{6,14},... | collective-permute-start | bytes 196616 | tf_op jit(solution)/shard_map/ppermute | solution.py:432
  8.6 1.8 %collective-permute-start.8 = (bf16[128,256]{1,0:T(8,128)(2,1)S(1)}, bf16[128,256]{1,0:T(8,128)(2,1)S(1)}, u32[]{:S(2)}, u32[]{:S(2)}) collective-permute-start(bf16[128,256]{1,0:T(8,128)(2,1)S(1)} %copy-done.3), channel_id=1, source_target_pairs={{0,12},{4,8},{8,4},{12,0},{1,13},{5,9},{9,5},{13,1},{2,14},{6,10},... | collective-permute-start | bytes 196616 | tf_op jit(solution)/shard_map/ppermute | solution.py:432
  10.4 0.5 %collective-permute-start.2 = (bf16[128,2048]{1,0:T(8,128)(2,1)S(1)}, bf16[128,2048]{1,0:T(8,128)(2,1)S(1)}, u32[]{:S(2)}, u32[]{:S(2)}) collective-permute-start(bf16[128,2048]{1,0:T(8,128)(2,1)S(1)} %shard_map.74.cycled_ref), channel_id=1, source_target_pairs={{0,1},{1,0},{2,3},{3,2},{4,5},{5,4},{6,7},{7,6},{8,9},{9,8},{10,11... | collective-permute-start | bytes 1572872 | tf_op jit(solution)/shard_map/ppermute | solution.py:150
  10.9 0.6 %shard_map.75 = (f32[128,256]{1,0:T(8,128)S(1)}, bf16[128,256]{1,0:T(8,128)(2,1)S(1)}, f32[128,128]{1,0:T(8,128)S(1)}, bf16[128,128]{1,0:T(8,128)(2,1)S(1)}) custom-call(bf16[128,2048]{1,0:T(8,128)(2,1)S(1)} %copy-done.6, bf16[128,2048]{1,0:T(8,128)(2,1)S(1)} %shard_map.74.cycled_ref, bf16[3,2048,256]{2,1,0:T(8,128)(2,1)S(1)} %bitcast.2), custom_call_target="tpu_custom_call" | custom-call | flops 10000000000 | bytes 40000000 | tf_op jit(solution)/shard_map/pallas_call | solution.py:438
  11.5 0.6 %collective-permute-start.4 = (bf16[128,256]{1,0:T(8,128)(2,1)S(1)}, bf16[128,256]{1,0:T(8,128)(2,1)S(1)}, u32[]{:S(2)}, u32[]{:S(2)}) collective-permute-start(bf16[128,256]{1,0:T(8,128)(2,1)S(1)} %get-tuple-element.22), channel_id=1, source_target_pairs={{0,2},{2,0},{1,3},{3,1},{4,6},{6,4},{5,7},{7,5},{8,10},{10,8},{9,1... | collective-permute-start | bytes 196616 | tf_op jit(solution)/shard_map/ppermute | solution.py:150
  12.1 0.1 shard_map.76.halo_ref
  12.3 0.1 collective-permute-done.2.hop_ref
  12.4 0.5 %shard_map.77 = (f32[144,256]{1,0:T(8,128)S(1)}, bf16[144,256]{1,0:T(8,128)(2,1)S(1)}, f32[8,128]{1,0:T(8,128)S(1)}) custom-call(bf16[128,2048]{1,0:T(8,128)(2,1)S(1)} %shard_map.74.cycled_ref, bf16[128,2048]{1,0:T(8,128)(2,1)S(1)} %collective-permute-done.2.hop_ref, bf16[16,2048]{1,0:T(8,128)(2,1)S(1)} %shard_map.76.halo_ref, bf16[3,2048,256]{2,1,0:T(8,128)(2,1)S(1)} %bitcast.3), custom_call_target="tpu_custom_call" | custom-call | tf_op jit(solution)/shard_map/pallas_call | solution.py:458
  12.9 1.4 %collective-permute-start.5 = (bf16[144,256]{1,0:T(8,128)(2,1)S(1)}, bf16[144,256]{1,0:T(8,128)(2,1)S(1)}, u32[]{:S(2)}, u32[]{:S(2)}) collective-permute-start(bf16[144,256]{1,0:T(8,128)(2,1)S(1)} %get-tuple-element.23), channel_id=1, source_target_pairs={{0,2},{2,0},{1,3},{3,1},{4,6},{6,4},{5,7},{7,5},{8,10},{10,8},{9,1... | collective-permute-start | bytes 221192 | tf_op jit(solution)/shard_map/ppermute | solution.py:150
  14.4 0.4 %collective-permute-done.8.three_ref = bf16[128,256]{1,0:T(8,128)(2,1)S(1)} collective-permute-done((bf16[128,256]{1,0:T(8,128)(2,1)S(1)}, bf16[128,256]{1,0:T(8,128)(2,1)S(1)}, u32[]{:S(2)}, u32[]{:S(2)}) %collective-permute-start.8) | collective-permute-done | bytes 65568 | tf_op jit(solution)/shard_map/ppermute | solution.py:432
  14.7 0.4 %shard_map.78 = (f32[144,128]{1,0:T(8,128)S(1)}, bf16[4,128,128]{2,1,0:T(8,128)(2,1)S(1)}, bf16[784,128]{1,0:T(8,128)(2,1)S(1)}, f32[8,128]{1,0:T(8,128)S(1)}) custom-call(bf16[128,2048]{1,0:T(8,128)(2,1)S(1)} %shard_map.74.cycled_ref, bf16[128,2048]{1,0:T(8,128)(2,1)S(1)} %collective-permute-done.2.hop_ref, bf16[16,2048]{1,0:T(8,128)(2,1)S(1)} %shard_map.76.halo_ref, ...), custom_call_target="tpu_custom_call" | custom-call | tf_op jit(solution)/shard_map/pallas_call | solution.py:468
  15.1 0.7 %collective-permute-done.4.got_first.refs_1_ = bf16[128,256]{1,0:T(8,128)(2,1)S(1)} collective-permute-done((bf16[128,256]{1,0:T(8,128)(2,1)S(1)}, bf16[128,256]{1,0:T(8,128)(2,1)S(1)}, u32[]{:S(2)}, u32[]{:S(2)}) %collective-permute-start.4) | collective-permute-done | bytes 65568 | tf_op jit(solution)/shard_map/ppermute | solution.py:150
  15.9 0.5 %collective-permute-start.12 = (bf16[784,128]{1,0:T(8,128)(2,1)S(1)}, bf16[784,128]{1,0:T(8,128)(2,1)S(1)}, u32[]{:S(2)}, u32[]{:S(2)}) collective-permute-start(bf16[784,128]{1,0:T(8,128)(2,1)S(1)} %shard_map.80), channel_id=1, source_target_pairs={{0,2},{2,0},{1,3},{3,1},{4,6},{6,4},{5,7},{7,5},{8,10},{10,8},{9,1... | collective-permute-start | bytes 602120 | tf_op jit(solution)/shard_map/ppermute | solution.py:150
  16.4 1.3 %collective-permute-done.5.got_second = bf16[144,256]{1,0:T(8,128)(2,1)S(1)} collective-permute-done((bf16[144,256]{1,0:T(8,128)(2,1)S(1)}, bf16[144,256]{1,0:T(8,128)(2,1)S(1)}, u32[]{:S(2)}, u32[]{:S(2)}) %collective-permute-start.5) | collective-permute-done | bytes 73760 | tf_op jit(solution)/shard_map/ppermute | solution.py:150
  17.7 0.1 shard_map.79.own_ref
  17.8 3.8 %collective-permute-start.11 = (bf16[256,128]{1,0:T(8,128)(2,1)S(1)}, bf16[256,128]{1,0:T(8,128)(2,1)S(1)}, u32[]{:S(2)}, u32[]{:S(2)}) collective-permute-start(bf16[256,128]{1,0:T(8,128)(2,1)S(1)} %shard_map.79.own_ref), channel_id=1, source_target_pairs={{0,12},{4,8},{8,4},{12,0},{1,13},{5,9},{9,5},{13,1},{2,14},{6,10},... | collective-permute-start | bytes 196616 | tf_op jit(solution)/shard_map/ppermute | solution.py:497
  21.6 0.7 %collective-permute-start.9 = (bf16[256,128]{1,0:T(8,128)(2,1)S(1)}, bf16[256,128]{1,0:T(8,128)(2,1)S(1)}, u32[]{:S(2)}, u32[]{:S(2)}) collective-permute-start(bf16[256,128]{1,0:T(8,128)(2,1)S(1)} %shard_map.79.own_ref), channel_id=1, source_target_pairs={{0,8},{4,12},{8,0},{12,4},{1,9},{5,13},{9,1},{13,5},{2,10},{6,14},... | collective-permute-start | bytes 196616 | tf_op jit(solution)/shard_map/ppermute | solution.py:497
  22.3 0.1 shard_map.83.query_ref
  22.3 0.5 %shard_map.81 = (f32[4,256,128]{2,1,0:T(8,128)S(1)}, f32[4,256,128]{2,1,0:T(8,128)S(1)}) custom-call(bf16[512,256]{1,0:T(8,128)(2,1)S(1)} %copy-done.1, bf16[4,128,128]{2,1,0:T(8,128)(2,1)S(1)} %get-tuple-element.27.keep_ref, bf16[784,128]{1,0:T(8,128)(2,1)S(1)} %collective-permute-done.12.got_ref), custom_call_target="tpu_custom_call" | custom-call | tf_op jit(solution)/shard_map/pallas_call | solution.py:501
  22.8 1.3 %collective-permute-done.11.far_ref = bf16[256,128]{1,0:T(8,128)(2,1)S(1)} collective-permute-done((bf16[256,128]{1,0:T(8,128)(2,1)S(1)}, bf16[256,128]{1,0:T(8,128)(2,1)S(1)}, u32[]{:S(2)}, u32[]{:S(2)}) %collective-permute-start.11) | collective-permute-done | bytes 65568 | tf_op jit(solution)/shard_map/ppermute | solution.py:497
  24.1 1.8 %collective-permute-done.10.near_ref = bf16[256,128]{1,0:T(8,128)(2,1)S(1)} collective-permute-done((bf16[256,128]{1,0:T(8,128)(2,1)S(1)}, bf16[256,128]{1,0:T(8,128)(2,1)S(1)}, u32[]{:S(2)}, u32[]{:S(2)}) %collective-permute-start.10) | collective-permute-done | bytes 65568 | tf_op jit(solution)/shard_map/ppermute | solution.py:497
  25.9 0.4 %shard_map.82.total_ref = f32[2,256,128]{2,1,0:T(8,128)S(1)} custom-call(bf16[256,128]{1,0:T(8,128)(2,1)S(1)} %shard_map.79.own_ref, bf16[256,128]{1,0:T(8,128)(2,1)S(1)} %collective-permute-done.10.near_ref, bf16[256,128]{1,0:T(8,128)(2,1)S(1)} %collective-permute-done.11.far_ref, f32[4,256,128]{2,1,0:T(8,128)S(1)} %get-tuple-element.29.real_ref, ...), custom_call_target="tpu_custom_call" | custom-call | tf_op jit(solution)/shard_map/pallas_call | solution.py:507
  26.2 0.5 %collective-permute-done.9.last_ref = bf16[256,128]{1,0:T(8,128)(2,1)S(1)} collective-permute-done((bf16[256,128]{1,0:T(8,128)(2,1)S(1)}, bf16[256,128]{1,0:T(8,128)(2,1)S(1)}, u32[]{:S(2)}, u32[]{:S(2)}) %collective-permute-start.9) | collective-permute-done | bytes 65568 | tf_op jit(solution)/shard_map/ppermute | solution.py:497
  26.8 0.4 %shard_map.84 = (bf16[128,128]{1,0:T(8,128)(2,1)S(1)}, bf16[512,128]{1,0:T(8,128)(2,1)S(1)}) custom-call(bf16[256,128]{1,0:T(8,128)(2,1)S(1)} %collective-permute-done.9.last_ref, f32[2,256,128]{2,1,0:T(8,128)S(1)} %shard_map.82.total_ref, f32[4,256,128]{2,1,0:T(8,128)S(1)} %get-tuple-element.29.real_ref, f32[4,256,128]{2,1,0:T(8,128)S(1)} %get-tuple-element.30.imag_ref, ...), custom_call_target="tpu_custom_call" | custom-call | tf_op jit(solution)/shard_map/pallas_call | solution.py:514
  27.2 1.2 %collective-permute-start.13 = (bf16[128,128]{1,0:T(8,128)(2,1)S(1)}, bf16[128,128]{1,0:T(8,128)(2,1)S(1)}, u32[]{:S(2)}, u32[]{:S(2)}) collective-permute-start(bf16[128,128]{1,0:T(8,128)(2,1)S(1)} %get-tuple-element.34), channel_id=1, source_target_pairs={{0,2},{2,0},{1,3},{3,1},{4,6},{6,4},{5,7},{7,5},{8,10},{10,8},{9,1... | collective-permute-start | bytes 98312 | tf_op jit(solution)/shard_map/ppermute | solution.py:150
  28.4 0.2 shard_map.85.stay_ref
  28.5 2.6 %collective-permute-done.13.got_ref = bf16[128,128]{1,0:T(8,128)(2,1)S(1)} collective-permute-done((bf16[128,128]{1,0:T(8,128)(2,1)S(1)}, bf16[128,128]{1,0:T(8,128)(2,1)S(1)}, u32[]{:S(2)}, u32[]{:S(2)}) %collective-permute-start.13) | collective-permute-done | bytes 32800 | tf_op jit(solution)/shard_map/ppermute | solution.py:150
  31.1 0.6 %shard_map.86 = bf16[128,256]{1,0:T(8,128)(2,1)} custom-call(bf16[128,128]{1,0:T(8,128)(2,1)S(1)} %shard_map.85.stay_ref, bf16[128,128]{1,0:T(8,128)(2,1)S(1)} %collective-permute-done.13.got_ref), custom_call_target="tpu_custom_call" | custom-call | tf_op jit(solution)/shard_map/pallas_call | solution.py:527
  (24 shorter events, 0.1 us)
Async XLA Ops:
  0.0 6.0 %copy-start.3 = (bf16[128,256]{1,0:T(8,128)(2,1)S(1)}, bf16[128,256]{1,0:T(8,128)(2,1)}, u32[]{:S(2)}) copy-start(bf16[128,256]{1,0:T(8,128)(2,1)} %own_ref.1) | copy-start | bytes 196612
  0.0 10.9 %copy-start = (bf16[2048,3,256]{2,0,1:T(8,128)(2,1)S(1)}, bf16[2048,3,256]{2,0,1:T(8,128)(2,1)}, u32[]{:S(2)}) copy-start(bf16[2048,3,256]{2,0,1:T(8,128)(2,1)} %param.8) | copy-start | bytes 9437188
  0.0 10.4 %collective-permute-start = (bf16[128,2048]{1,0:T(8,128)(2,1)}, bf16[128,2048]{1,0:T(8,128)(2,1)S(1)}, u32[]{:S(2)}, u32[]{:S(2)}) collective-permute-start(bf16[128,2048]{1,0:T(8,128)(2,1)} %rows_ref.3), channel_id=1, source_target_pairs={{1,3},{3,2},{2,0},{0,1},{5,7},{7,6},{6,4},{4,5},{9,11},{11,10},{10... | collective-permute-start | bytes 1572872 | tf_op jit(solution)/shard_map/ppermute | solution.py:412
  0.5 1.3 %copy-start.6 = (bf16[128,2048]{1,0:T(8,128)(2,1)S(1)}, bf16[128,2048]{1,0:T(8,128)(2,1)}, u32[]{:S(2)}) copy-start(bf16[128,2048]{1,0:T(8,128)(2,1)} %rows_ref.3) | copy-start | bytes 1572868
  1.9 8.5 %collective-permute-start.1 = (bf16[16,256]{1,0:T(8,128)(2,1)S(1)}, bf16[16,256]{1,0:T(8,128)(2,1)S(1)}, u32[]{:S(2)}, u32[]{:S(2)}) collective-permute-start(bf16[16,256]{1,0:T(8,128)(2,1)S(1)} %shard_map.73), channel_id=1, source_target_pairs={{0,6},{1,5},{2,4},{3,7},{4,10},{5,9},{6,8},{7,11},{8,14},{9,13},{1... | collective-permute-start | bytes 24584 | tf_op jit(solution)/shard_map/ppermute | solution.py:421
  6.0 8.4 %collective-permute-start.7 = (bf16[128,256]{1,0:T(8,128)(2,1)S(1)}, bf16[128,256]{1,0:T(8,128)(2,1)S(1)}, u32[]{:S(2)}, u32[]{:S(2)}) collective-permute-start(bf16[128,256]{1,0:T(8,128)(2,1)S(1)} %copy-done.3), channel_id=1, source_target_pairs={{0,8},{4,12},{8,0},{12,4},{1,9},{5,13},{9,1},{13,5},{2,10},{6,14},... | collective-permute-start | bytes 196616 | tf_op jit(solution)/shard_map/ppermute | solution.py:432
  8.6 5.8 %collective-permute-start.6 = (bf16[128,256]{1,0:T(8,128)(2,1)S(1)}, bf16[128,256]{1,0:T(8,128)(2,1)S(1)}, u32[]{:S(2)}, u32[]{:S(2)}) collective-permute-start(bf16[128,256]{1,0:T(8,128)(2,1)S(1)} %copy-done.3), channel_id=1, source_target_pairs={{0,4},{4,0},{8,12},{12,8},{1,5},{5,1},{9,13},{13,9},{2,6},{6,2},{1... | collective-permute-start | bytes 196616 | tf_op jit(solution)/shard_map/ppermute | solution.py:432
  8.6 6.2 %collective-permute-start.8 = (bf16[128,256]{1,0:T(8,128)(2,1)S(1)}, bf16[128,256]{1,0:T(8,128)(2,1)S(1)}, u32[]{:S(2)}, u32[]{:S(2)}) collective-permute-start(bf16[128,256]{1,0:T(8,128)(2,1)S(1)} %copy-done.3), channel_id=1, source_target_pairs={{0,12},{4,8},{8,4},{12,0},{1,13},{5,9},{9,5},{13,1},{2,14},{6,10},... | collective-permute-start | bytes 196616 | tf_op jit(solution)/shard_map/ppermute | solution.py:432
  10.4 1.2 %collective-permute-start.3 = (bf16[16,256]{1,0:T(8,128)(2,1)S(1)}, bf16[16,256]{1,0:T(8,128)(2,1)S(1)}, u32[]{:S(2)}, u32[]{:S(2)}) collective-permute-start(bf16[16,256]{1,0:T(8,128)(2,1)S(1)} %collective-permute-done.1.refs_1_.pack_ref), channel_id=1, source_target_pairs={{0,1},{1,0},{2,3},{3,2},{4,5},{5,4},{6,7},{7,6},{8,9},{9,8},{10,11... | collective-permute-start | bytes 24584 | tf_op jit(solution)/shard_map/ppermute | solution.py:150
  10.4 2.0 %collective-permute-start.2 = (bf16[128,2048]{1,0:T(8,128)(2,1)S(1)}, bf16[128,2048]{1,0:T(8,128)(2,1)S(1)}, u32[]{:S(2)}, u32[]{:S(2)}) collective-permute-start(bf16[128,2048]{1,0:T(8,128)(2,1)S(1)} %shard_map.74.cycled_ref), channel_id=1, source_target_pairs={{0,1},{1,0},{2,3},{3,2},{4,5},{5,4},{6,7},{7,6},{8,9},{9,8},{10,11... | collective-permute-start | bytes 1572872 | tf_op jit(solution)/shard_map/ppermute | solution.py:150
  11.5 4.3 %collective-permute-start.4 = (bf16[128,256]{1,0:T(8,128)(2,1)S(1)}, bf16[128,256]{1,0:T(8,128)(2,1)S(1)}, u32[]{:S(2)}, u32[]{:S(2)}) collective-permute-start(bf16[128,256]{1,0:T(8,128)(2,1)S(1)} %get-tuple-element.22), channel_id=1, source_target_pairs={{0,2},{2,0},{1,3},{3,1},{4,6},{6,4},{5,7},{7,5},{8,10},{10,8},{9,1... | collective-permute-start | bytes 196616 | tf_op jit(solution)/shard_map/ppermute | solution.py:150
  12.9 4.8 %collective-permute-start.5 = (bf16[144,256]{1,0:T(8,128)(2,1)S(1)}, bf16[144,256]{1,0:T(8,128)(2,1)S(1)}, u32[]{:S(2)}, u32[]{:S(2)}) collective-permute-start(bf16[144,256]{1,0:T(8,128)(2,1)S(1)} %get-tuple-element.23), channel_id=1, source_target_pairs={{0,2},{2,0},{1,3},{3,1},{4,6},{6,4},{5,7},{7,5},{8,10},{10,8},{9,1... | collective-permute-start | bytes 221192 | tf_op jit(solution)/shard_map/ppermute | solution.py:150
  15.8 1.8 %copy-start.4 = (f32[3,3,256]{2,1,0:T(4,128)S(1)}, f32[3,3,256]{2,1,0:T(4,128)}, u32[]{:S(2)}) copy-start(f32[3,3,256]{2,1,0:T(4,128)} %short_ref.3) | copy-start | bytes 27652
  15.9 6.4 %collective-permute-start.12 = (bf16[784,128]{1,0:T(8,128)(2,1)S(1)}, bf16[784,128]{1,0:T(8,128)(2,1)S(1)}, u32[]{:S(2)}, u32[]{:S(2)}) collective-permute-start(bf16[784,128]{1,0:T(8,128)(2,1)S(1)} %shard_map.80), channel_id=1, source_target_pairs={{0,2},{2,0},{1,3},{3,1},{4,6},{6,4},{5,7},{7,5},{8,10},{10,8},{9,1... | collective-permute-start | bytes 602120 | tf_op jit(solution)/shard_map/ppermute | solution.py:150
  17.7 4.7 %copy-start.1 = (bf16[512,256]{1,0:T(8,128)(2,1)S(1)}, bf16[512,256]{1,0:T(8,128)(2,1)}, u32[]{:S(2)}) copy-start(bf16[512,256]{1,0:T(8,128)(2,1)} %constant.4.clone.table_ref) | copy-start | bytes 786436
  17.7 9.1 %copy-start.2 = (bf16[256,512]{1,0:T(8,128)(2,1)S(1)}, bf16[256,512]{1,0:T(8,128)(2,1)}, u32[]{:S(2)}) copy-start(bf16[256,512]{1,0:T(8,128)(2,1)} %constant.5.clone.turned_ref) | copy-start | bytes 786436
  17.7 9.1 %copy-start.5 = (f32[256]{0:T(256)S(1)}, f32[256]{0:T(256)}, u32[]{:S(2)}) copy-start(f32[256]{0:T(256)} %param.10) | copy-start | bytes 3076
  17.8 6.2 %collective-permute-start.11 = (bf16[256,128]{1,0:T(8,128)(2,1)S(1)}, bf16[256,128]{1,0:T(8,128)(2,1)S(1)}, u32[]{:S(2)}, u32[]{:S(2)}) collective-permute-start(bf16[256,128]{1,0:T(8,128)(2,1)S(1)} %shard_map.79.own_ref), channel_id=1, source_target_pairs={{0,12},{4,8},{8,4},{12,0},{1,13},{5,9},{9,5},{13,1},{2,14},{6,10},... | collective-permute-start | bytes 196616 | tf_op jit(solution)/shard_map/ppermute | solution.py:497
  21.6 4.3 %collective-permute-start.10 = (bf16[256,128]{1,0:T(8,128)(2,1)S(1)}, bf16[256,128]{1,0:T(8,128)(2,1)S(1)}, u32[]{:S(2)}, u32[]{:S(2)}) collective-permute-start(bf16[256,128]{1,0:T(8,128)(2,1)S(1)} %shard_map.79.own_ref), channel_id=1, source_target_pairs={{0,4},{4,0},{8,12},{12,8},{1,5},{5,1},{9,13},{13,9},{2,6},{6,2},{1... | collective-permute-start | bytes 196616 | tf_op jit(solution)/shard_map/ppermute | solution.py:497
  21.6 5.2 %collective-permute-start.9 = (bf16[256,128]{1,0:T(8,128)(2,1)S(1)}, bf16[256,128]{1,0:T(8,128)(2,1)S(1)}, u32[]{:S(2)}, u32[]{:S(2)}) collective-permute-start(bf16[256,128]{1,0:T(8,128)(2,1)S(1)} %shard_map.79.own_ref), channel_id=1, source_target_pairs={{0,8},{4,12},{8,0},{12,4},{1,9},{5,13},{9,1},{13,5},{2,10},{6,14},... | collective-permute-start | bytes 196616 | tf_op jit(solution)/shard_map/ppermute | solution.py:497
  27.2 4.0 %collective-permute-start.13 = (bf16[128,128]{1,0:T(8,128)(2,1)S(1)}, bf16[128,128]{1,0:T(8,128)(2,1)S(1)}, u32[]{:S(2)}, u32[]{:S(2)}) collective-permute-start(bf16[128,128]{1,0:T(8,128)(2,1)S(1)} %get-tuple-element.34), channel_id=1, source_target_pairs={{0,2},{2,0},{1,3},{3,1},{4,6},{6,4},{5,7},{7,5},{8,10},{10,8},{9,1... | collective-permute-start | bytes 98312 | tf_op jit(solution)/shard_map/ppermute | solution.py:150
